TPU v7x, 32 devices: a whole 2x2x4 slice. The times are simulated.
32 devices in a mesh: pair: 16 (over z, y, x), virt: 2 (over core).
Axes of the slice: x: 2, y: 2, z: 4, core: 2. Of those that a mesh axis runs over, the one named last changes fastest.
Arguments:
- t2_amplitudes: float32 [64, 2048], P('pair', 'virt'), may hold values from -6 to 6
- integral_tiles: float32 [16, 2, 32, 128, 128], P('pair', 'virt'), may hold values from -0.125 to 0.125
- out_tiles: int32 [16, 2, 32], P('pair', 'virt'), may hold values from 0 to 15, as said below
- in_tiles: int32 [16, 2, 32], P('pair', 'virt'), may hold values from 0 to 15
- tile_counts: int32 [16, 2], P('pair', 'virt'), may hold values from 1 to 32, as said below
Outputs:
- ladder: float32 [64, 2048], P('pair', 'virt')
Inputs may be any that keep to these rules, and one draw needn't show every extreme that they name: `out_tiles`: slots of the devices at virt index v name output tiles v * 8 to (v + 1) * 8 - 1 only. `tile_counts`: in every draw some device has all 32 slots live.
All inputs are finite; a program needn't handle non-finite values.
Results may differ from a plain program's by a relative error of at most 0.0003.
Values sent between devices are 32-bit elements; how exact they have to be, the bound alone decides.
No kernel may reach another device: no remote copies, remote signals or barrier semaphores. Data moves between devices by JAX's collectives and lax.ppermute only.
A program may use at most 64 MiB of HBM per device.

v0:
```python
import jax
import jax.numpy as jnp
from jax import lax
from jax.experimental import pallas as pl
from jax.experimental.pallas import tpu as pltpu
from jax.sharding import PartitionSpec as P

W = 128
COPY_GROUP = 8
GROUP = 16
NEAR = 4
SMEM = pl.BlockSpec(memory_space=pltpu.SMEM)
VMEM = pl.BlockSpec(memory_space=pltpu.VMEM)


def split(value):
    high = value.astype(jnp.bfloat16)
    low = (value - high.astype(jnp.float32)).astype(jnp.bfloat16)
    return high, low


def tile_kernel(out_tiles, live, ins, outs, tiles, mine, halves, codes, own, held, index_rows, arrived, singles):
    singles_of = ((ins, index_rows.at[0]), (outs, index_rows.at[1]), (mine, own))
    others = [pltpu.make_async_copy(here, there, singles.at[at]) for at, (here, there) in enumerate(singles_of)]
    for copy in others:
        copy.start()
    count = live[0, 0]
    groups = (count + COPY_GROUP - 1) // COPY_GROUP

    def tile_copy(index):
        part = pl.ds(index * COPY_GROUP, COPY_GROUP)
        return pltpu.make_async_copy(tiles.at[part], held.at[part], arrived.at[index])

    def begin(index, carry):
        tile_copy(index).start()
        return carry

    lax.fori_loop(0, groups, begin, 0)
    for copy in others:
        copy.wait()
    slots = lax.broadcasted_iota(jnp.int32, ins.shape, 1)
    tile_in = index_rows[0]
    owner = lax.bitwise_xor(lax.div(tile_in, out_tiles), lax.axis_index("virt"))
    codes[0:1, :] = owner * out_tiles + lax.rem(tile_in, out_tiles)
    codes[1:2, :] = jnp.where(slots < count, lax.rem(index_rows[1], out_tiles), out_tiles)
    codes[2:3, :] = jnp.full(ins.shape, count, jnp.int32)

    def one_group(index, carry):
        tile_copy(index).wait()
        for step in range(COPY_GROUP):
            slot = index * COPY_GROUP + step
            high, low = split(held[slot])
            halves[slot, :, :W] = high
            halves[slot, :, W:] = low
        return carry

    lax.fori_loop(0, groups, one_group, 0)


def prepare(tiles, ins, outs, live, mine, out_tiles):
    slots = tiles.shape[0]

    def kernel(*refs):
        tile_kernel(out_tiles, *refs)

    operands = [pltpu.with_memory_space_constraint(value, pltpu.HBM) for value in (ins, outs, tiles, mine)]
    return pl.pallas_call(
        kernel,
        out_shape=(
            jax.ShapeDtypeStruct((slots, W, 2 * W), jnp.bfloat16),
            jax.ShapeDtypeStruct((3, slots), jnp.int32),
            jax.ShapeDtypeStruct(mine.shape, mine.dtype),
        ),
        in_specs=[SMEM] + [pl.BlockSpec(memory_space=pltpu.HBM)] * 4,
        out_specs=(VMEM, VMEM, VMEM),
        scratch_shapes=[
            pltpu.VMEM((slots, W, W), jnp.float32),
            pltpu.VMEM((2, 1, slots), jnp.int32),
            pltpu.SemaphoreType.DMA((slots // COPY_GROUP,)),
            pltpu.SemaphoreType.DMA((3,)),
        ],
        compiler_params=pltpu.CompilerParams(vmem_limit_bytes=32 * 1024 * 1024),
        cost_estimate=pl.CostEstimate(flops=4 * slots * W * W, bytes_accessed=8 * slots * W * W, transcendentals=0),
    )(live, *operands)


def ladder_kernel(virts, codes_here, halves, *refs):
    blocks, (result, columns, flat, totals, codes, copied) = refs[: virts * NEAR], refs[virts * NEAR :]
    fetch = pltpu.make_async_copy(codes_here, codes, copied)
    fetch.start()
    far = blocks[0].shape[0]
    chunk_count = NEAR * far
    out_tiles = totals.shape[0] - 1
    rows = result.shape[1] // out_tiles
    total_rows = chunk_count * rows
    in_local = columns.shape[0] // virts
    totals[...] = jnp.zeros_like(totals)

    for owner in range(virts):
        for a in range(NEAR):
            for b in range(far):
                source = blocks[(owner ^ int((a > 0) != (b > 0))) * NEAR + a]
                place = pl.ds((a * far + b) * rows, rows)
                for tile in range(in_local):
                    flat[tile, place, :] = source[b, tile * rows : (tile + 1) * rows, :]
        for tile in range(in_local):
            high, low = split(flat[tile])
            columns[owner * in_local + tile, :total_rows, :] = high
            columns[owner * in_local + tile, total_rows:, :] = low

    fetch.wait()

    def one_group(index, carry):
        first = index * GROUP
        products = []
        for step in range(GROUP):
            got = jnp.dot(columns[codes[0, first + step]], halves[first + step], preferred_element_type=jnp.float32)
            upper, lower = got[:total_rows], got[total_rows:]
            products.append((upper[:, :W] + lower[:, :W]) + (upper[:, W:] + lower[:, W:]))
        for step in range(GROUP):
            place = codes[1, first + step]
            totals[place] = totals[place] + products[step]
        return carry

    lax.fori_loop(0, (codes[2, 0] + GROUP - 1) // GROUP, one_group, 0)
    def give(chunk, carry):
        for tile in range(out_tiles):
            result[chunk, tile * rows : (tile + 1) * rows, :] = totals[tile, pl.ds(chunk * rows, rows), :]
        return carry

    lax.fori_loop(0, chunk_count, give, 0, unroll=min(chunk_count, 16))


def local_terms(codes, blocks, halves, rows, out_tiles):
    far, chunk_rows, _ = blocks[0].shape
    virts = len(blocks) // NEAR
    total_rows = NEAR * far * rows
    in_local = chunk_rows // rows

    def kernel(*refs):
        ladder_kernel(virts, *refs)

    return pl.pallas_call(
        kernel,
        out_shape=jax.ShapeDtypeStruct((NEAR * far, out_tiles * rows, W), jnp.float32),
        in_specs=[VMEM, VMEM] + [VMEM] * len(blocks),
        out_specs=VMEM,
        scratch_shapes=[
            pltpu.VMEM((virts * in_local, 2 * total_rows, W), jnp.bfloat16),
            pltpu.VMEM((in_local, total_rows, W), jnp.float32),
            pltpu.VMEM((out_tiles + 1, total_rows, W), jnp.float32),
            pltpu.SMEM(codes.shape, jnp.int32),
            pltpu.SemaphoreType.DMA,
        ],
        compiler_params=pltpu.CompilerParams(vmem_limit_bytes=32 * 1024 * 1024),
    )(codes, halves, *blocks)


def swap(value, pairs, virts, mask, virt_mask):
    routes = [(a * virts + b, (a ^ mask) * virts + (b ^ virt_mask)) for a in range(pairs) for b in range(virts)]
    return lax.ppermute(value, ("pair", "virt"), routes)


def swap_sum(parts, pairs, virts, unit):
    last = len(parts) - 1
    received = [swap(parts[i], pairs, virts, i * unit, 1) for i in (0, last, *range(1, last))]
    return sum(received[1:], received[0])


def shards(t2_amplitudes, integral_tiles, out_tiles, in_tiles, tile_counts):
    rows, columns = t2_amplitudes.shape
    local_tiles = columns // W
    slots = integral_tiles.shape[2]
    pairs, virts = lax.axis_size("pair"), lax.axis_size("virt")
    mine = t2_amplitudes.reshape(rows, local_tiles, W).transpose(1, 0, 2).reshape(local_tiles * rows, W)
    halves, codes, own = prepare(
        integral_tiles.reshape(slots, W, W),
        in_tiles.reshape(1, slots),
        out_tiles.reshape(1, slots),
        tile_counts,
        mine,
        local_tiles,
    )
    line = jnp.stack([own] + [swap(mine, pairs, virts, mask, 1) for mask in range(NEAR, pairs, NEAR)])
    pieces = [line] + [swap(line, pairs, virts, mask, 1) for mask in range(1, NEAR)]
    blocks = pieces + [swap(piece, pairs, virts, 0, mask) for mask in range(1, virts) for piece in pieces]
    partial_sums = local_terms(codes, blocks, halves, rows, local_tiles)
    line_sums = swap_sum(partial_sums.reshape((NEAR, pairs // NEAR) + mine.shape), pairs, virts, 1)
    summed = swap_sum(line_sums, pairs, virts, NEAR)
    return summed.reshape(local_tiles, rows, W).transpose(1, 0, 2).reshape(rows, columns)


def solution(mesh):
    return jax.shard_map(
        shards,
        mesh=mesh,
        in_specs=(
            P("pair", "virt"),
            P("pair", "virt", None, None, None),
            P("pair", "virt", None),
            P("pair", "virt", None),
            P("pair", "virt"),
        ),
        out_specs=P("pair", "virt"),
        check_vma=False,
    )
```

profile of v0, /device:TPU:0, one launch (start us, length us, event | category | flops | bytes accessed | tf_op | source)
XLA Modules:
  0.0 31.5 jit_solution(423781020429510731)
XLA Ops:
  0.0 4.5 %collective-permute-start.2 = (f32[32,128]{1,0:T(8,128)}, f32[32,128]{1,0:T(8,128)S(1)}, u32[]{:S(2)}, u32[]{:S(2)}) collective-permute-start(f32[32,128]{1,0:T(8,128)} %bitcast.27), channel_id=1, source_target_pairs={{0,25},{1,24},{2,27},{3,26},{4,29},{5,28},{6,31},{7,30},{8,17},{9,... | collective-permute-start | bytes 49160 | tf_op jit(solution)/shard_map/ppermute | solution.py:161
  4.5 0.0 collective-permute-start.1
  4.5 0.8 %collective-permute-start = (f32[32,128]{1,0:T(8,128)}, f32[32,128]{1,0:T(8,128)S(1)}, u32[]{:S(2)}, u32[]{:S(2)}) collective-permute-start(f32[32,128]{1,0:T(8,128)} %bitcast.29), channel_id=1, source_target_pairs={{0,9},{1,8},{2,11},{3,10},{4,13},{5,12},{6,15},{7,14},{8,1},{9,0},... | collective-permute-start | bytes 49160 | tf_op jit(solution)/shard_map/ppermute | solution.py:161
  6.0 1.2 %shard_map.55 = (bf16[32,128,256]{2,1,0:T(8,128)(2,1)S(1)}, s32[3,32]{1,0:T(4,128)S(1)}, f32[32,128]{1,0:T(8,128)S(1)}) custom-call(s32[1,1]{1,0:T(1,128)S(6)} %copy.8.refs_0_, s32[1,32]{1,0:T(1,128)} %bitcast.34, s32[1,32]{1,0:T(1,128)} %bitcast.35, f32[32,128,128]{2,1,0:T(8,128)} %bitcast.26, f32[32,128]{1,0:T(8,128)} %bitcast.30), custom_call_target="tpu_custom_call" | custom-call | flops 2097152 | bytes 4194304 | tf_op jit(solution)/shard_map/pallas_call | solution.py:67
  7.2 0.0 collective-permute-done.2
  7.2 1.6 %collective-permute-done.1 = f32[32,128]{1,0:T(8,128)S(1)} collective-permute-done((f32[32,128]{1,0:T(8,128)}, f32[32,128]{1,0:T(8,128)S(1)}, u32[]{:S(2)}, u32[]{:S(2)}) %collective-permute-start.1) | collective-permute-done | bytes 16416 | tf_op jit(solution)/shard_map/ppermute | solution.py:161
  8.9 0.0 collective-permute-done
  8.9 2.7 %collective-permute-start.5 = (f32[4,32,128]{2,1,0:T(8,128)S(1)}, f32[4,32,128]{2,1,0:T(8,128)S(1)}, u32[]{:S(2)}, u32[]{:S(2)}) collective-permute-start(f32[4,32,128]{2,1,0:T(8,128)S(1)} %pad_maximum_fusion.refs_2_), channel_id=1, source_target_pairs={{0,7},{1,6},{2,5},{3,4},{4,3},{5,2},{6,1},{7,0},{8,15},{9,14},{10,... | collective-permute-start | bytes 196616 | tf_op jit(solution)/shard_map/ppermute | solution.py:161
  11.6 0.1 collective-permute-start.4
  11.6 0.7 %collective-permute-start.3 = (f32[4,32,128]{2,1,0:T(8,128)S(1)}, f32[4,32,128]{2,1,0:T(8,128)S(1)}, u32[]{:S(2)}, u32[]{:S(2)}) collective-permute-start(f32[4,32,128]{2,1,0:T(8,128)S(1)} %pad_maximum_fusion.refs_2_), channel_id=1, source_target_pairs={{0,3},{1,2},{2,1},{3,0},{4,7},{5,6},{6,5},{7,4},{8,11},{9,10},{10,... | collective-permute-start | bytes 196616 | tf_op jit(solution)/shard_map/ppermute | solution.py:161
  12.3 0.0 collective-permute-start.6
  12.3 1.6 %collective-permute-done.5.refs_5_ = f32[4,32,128]{2,1,0:T(8,128)S(1)} collective-permute-done((f32[4,32,128]{2,1,0:T(8,128)S(1)}, f32[4,32,128]{2,1,0:T(8,128)S(1)}, u32[]{:S(2)}, u32[]{:S(2)}) %collective-permute-start.5) | collective-permute-done | bytes 65568 | tf_op jit(solution)/shard_map/ppermute | solution.py:161
  14.0 0.1 collective-permute-start.9
  14.1 1.7 %collective-permute-done.4.refs_4_ = f32[4,32,128]{2,1,0:T(8,128)S(1)} collective-permute-done((f32[4,32,128]{2,1,0:T(8,128)S(1)}, f32[4,32,128]{2,1,0:T(8,128)S(1)}, u32[]{:S(2)}, u32[]{:S(2)}) %collective-permute-start.4) | collective-permute-done | bytes 65568 | tf_op jit(solution)/shard_map/ppermute | solution.py:161
  15.8 0.1 collective-permute-start.8
  15.9 0.0 collective-permute-done.3.refs_3_
  15.9 0.4 %collective-permute-start.7 = (f32[4,32,128]{2,1,0:T(8,128)S(1)}, f32[4,32,128]{2,1,0:T(8,128)S(1)}, u32[]{:S(2)}, u32[]{:S(2)}) collective-permute-start(f32[4,32,128]{2,1,0:T(8,128)S(1)} %collective-permute-done.3.refs_3_), channel_id=1, source_target_pairs={{0,1},{1,0},{2,3},{3,2},{4,5},{5,4},{6,7},{7,6},{8,9},{9,8},{10,11... | collective-permute-start | bytes 196616 | tf_op jit(solution)/shard_map/ppermute | solution.py:161
  16.3 0.0 collective-permute-done.6.refs_6_
  16.3 0.0 collective-permute-done.9.refs_9_
  16.3 0.7 %collective-permute-done.8.refs_8_ = f32[4,32,128]{2,1,0:T(8,128)S(1)} collective-permute-done((f32[4,32,128]{2,1,0:T(8,128)S(1)}, f32[4,32,128]{2,1,0:T(8,128)S(1)}, u32[]{:S(2)}, u32[]{:S(2)}) %collective-permute-start.8) | collective-permute-done | bytes 65568 | tf_op jit(solution)/shard_map/ppermute | solution.py:161
  17.1 0.2 collective-permute-done.7.refs_7_
  17.2 1.1 %shard_map.56 = f32[16,32,128]{2,1,0:T(8,128)S(1)} custom-call(s32[3,32]{1,0:T(4,128)S(1)} %get-tuple-element.8.refs_0_, bf16[32,128,256]{2,1,0:T(8,128)(2,1)S(1)} %get-tuple-element.9.refs_1_, f32[4,32,128]{2,1,0:T(8,128)S(1)} %pad_maximum_fusion.refs_2_, f32[4,32,128]{2,1,0:T(8,128)S(1)} %collective-permute-done.3.refs_3_, ...), custom_call_target="tpu_custom_call" | custom-call | tf_op jit(solution)/shard_map/pallas_call | solution.py:143
  18.3 1.9 %collective-permute-start.11 = (f32[4,32,128]{2,1,0:T(8,128)S(1)}, f32[4,32,128]{2,1,0:T(8,128)S(1)}, u32[]{:S(2)}, u32[]{:S(2)}) collective-permute-start(f32[4,32,128]{2,1,0:T(8,128)S(1)} %get-tuple-element.11), channel_id=1, source_target_pairs={{0,7},{1,6},{2,5},{3,4},{4,3},{5,2},{6,1},{7,0},{8,15},{9,14},{10,... | collective-permute-start | bytes 196616 | tf_op jit(solution)/shard_map/ppermute | solution.py:161
  20.2 0.7 %collective-permute-start.13 = (f32[4,32,128]{2,1,0:T(8,128)S(1)}, f32[4,32,128]{2,1,0:T(8,128)S(1)}, u32[]{:S(2)}, u32[]{:S(2)}) collective-permute-start(f32[4,32,128]{2,1,0:T(8,128)S(1)} %get-tuple-element.12), channel_id=1, source_target_pairs={{0,5},{1,4},{2,7},{3,6},{4,1},{5,0},{6,3},{7,2},{8,13},{9,12},{10,... | collective-permute-start | bytes 196616 | tf_op jit(solution)/shard_map/ppermute | solution.py:161
  20.9 1.1 %collective-permute-start.12 = (f32[4,32,128]{2,1,0:T(8,128)S(1)}, f32[4,32,128]{2,1,0:T(8,128)S(1)}, u32[]{:S(2)}, u32[]{:S(2)}) collective-permute-start(f32[4,32,128]{2,1,0:T(8,128)S(1)} %get-tuple-element.13), channel_id=1, source_target_pairs={{0,3},{1,2},{2,1},{3,0},{4,7},{5,6},{6,5},{7,4},{8,11},{9,10},{10,... | collective-permute-start | bytes 196616 | tf_op jit(solution)/shard_map/ppermute | solution.py:161
  22.0 0.0 collective-permute-start.10
  22.0 1.0 %collective-permute-done.11 = f32[4,32,128]{2,1,0:T(8,128)S(1)} collective-permute-done((f32[4,32,128]{2,1,0:T(8,128)S(1)}, f32[4,32,128]{2,1,0:T(8,128)S(1)}, u32[]{:S(2)}, u32[]{:S(2)}) %collective-permute-start.11) | collective-permute-done | bytes 65568 | tf_op jit(solution)/shard_map/ppermute | solution.py:161
  23.0 2.2 %collective-permute-done.13 = f32[4,32,128]{2,1,0:T(8,128)S(1)} collective-permute-done((f32[4,32,128]{2,1,0:T(8,128)S(1)}, f32[4,32,128]{2,1,0:T(8,128)S(1)}, u32[]{:S(2)}, u32[]{:S(2)}) %collective-permute-start.13) | collective-permute-done | bytes 65568 | tf_op jit(solution)/shard_map/ppermute | solution.py:161
  25.1 0.0 collective-permute-done.12
  25.1 0.0 collective-permute-done.10
  25.2 1.6 %collective-permute-start.15 = (f32[32,128]{1,0:T(8,128)S(1)}, f32[32,128]{1,0:T(8,128)S(1)}, u32[]{:S(2)}, u32[]{:S(2)}) collective-permute-start(f32[32,128]{1,0:T(8,128)S(1)} %get-tuple-element.15), channel_id=1, source_target_pairs={{0,25},{1,24},{2,27},{3,26},{4,29},{5,28},{6,31},{7,30},{8,17},{9,... | collective-permute-start | bytes 49160 | tf_op jit(solution)/shard_map/ppermute | solution.py:161
  26.8 0.3 collective-permute-start.17
  27.1 2.0 %collective-permute-start.16 = (f32[32,128]{1,0:T(8,128)S(1)}, f32[32,128]{1,0:T(8,128)S(1)}, u32[]{:S(2)}, u32[]{:S(2)}) collective-permute-start(f32[32,128]{1,0:T(8,128)S(1)} %get-tuple-element.17), channel_id=1, source_target_pairs={{0,9},{1,8},{2,11},{3,10},{4,13},{5,12},{6,15},{7,14},{8,1},{9,0},... | collective-permute-start | bytes 49160 | tf_op jit(solution)/shard_map/ppermute | solution.py:161
  29.1 0.4 %collective-permute-start.14 = (f32[32,128]{1,0:T(8,128)S(1)}, f32[32,128]{1,0:T(8,128)S(1)}, u32[]{:S(2)}, u32[]{:S(2)}) collective-permute-start(f32[32,128]{1,0:T(8,128)S(1)} %get-tuple-element.18), channel_id=1, source_target_pairs={{0,1},{1,0},{2,3},{3,2},{4,5},{5,4},{6,7},{7,6},{8,9},{9,8},{10,11... | collective-permute-start | bytes 49160 | tf_op jit(solution)/shard_map/ppermute | solution.py:161
  29.5 0.7 %collective-permute-done.15 = f32[32,128]{1,0:T(8,128)S(1)} collective-permute-done((f32[32,128]{1,0:T(8,128)S(1)}, f32[32,128]{1,0:T(8,128)S(1)}, u32[]{:S(2)}, u32[]{:S(2)}) %collective-permute-start.15) | collective-permute-done | bytes 16416 | tf_op jit(solution)/shard_map/ppermute | solution.py:161
  30.2 0.7 %collective-permute-done.17 = f32[32,128]{1,0:T(8,128)S(1)} collective-permute-done((f32[32,128]{1,0:T(8,128)S(1)}, f32[32,128]{1,0:T(8,128)S(1)}, u32[]{:S(2)}, u32[]{:S(2)}) %collective-permute-start.17) | collective-permute-done | bytes 16416 | tf_op jit(solution)/shard_map/ppermute | solution.py:161
  30.9 0.0 collective-permute-done.16
  30.9 0.0 collective-permute-done.14
  30.9 0.6 %add_add_fusion.1 = f32[32,128]{1,0:T(8,128)} fusion(f32[32,128]{1,0:T(8,128)S(1)} %collective-permute-done.17, f32[32,128]{1,0:T(8,128)S(1)} %collective-permute-done.16, f32[32,128]{1,0:T(8,128)S(1)} %collective-permute-done.14, f32[32,128]{1,0:T(8,128)S(1)} %collective-permute-done.15), kind=kLoop, calls=%fused_computation.6 | loop fusion | flops 12288 | bytes 81920 | tf_op jit(solution)/shard_map/add | solution.py:167
  (4 shorter events, 0.1 us)
Async XLA Ops:
  0.0 7.2 %collective-permute-start.2 = (f32[32,128]{1,0:T(8,128)}, f32[32,128]{1,0:T(8,128)S(1)}, u32[]{:S(2)}, u32[]{:S(2)}) collective-permute-start(f32[32,128]{1,0:T(8,128)} %bitcast.27), channel_id=1, source_target_pairs={{0,25},{1,24},{2,27},{3,26},{4,29},{5,28},{6,31},{7,30},{8,17},{9,... | collective-permute-start | bytes 49160 | tf_op jit(solution)/shard_map/ppermute | solution.py:161
  4.5 4.4 %collective-permute-start.1 = (f32[32,128]{1,0:T(8,128)}, f32[32,128]{1,0:T(8,128)S(1)}, u32[]{:S(2)}, u32[]{:S(2)}) collective-permute-start(f32[32,128]{1,0:T(8,128)} %bitcast.28), channel_id=1, source_target_pairs={{0,17},{1,16},{2,19},{3,18},{4,21},{5,20},{6,23},{7,22},{8,25},{9,... | collective-permute-start | bytes 49160 | tf_op jit(solution)/shard_map/ppermute | solution.py:161
  4.5 4.4 %collective-permute-start = (f32[32,128]{1,0:T(8,128)}, f32[32,128]{1,0:T(8,128)S(1)}, u32[]{:S(2)}, u32[]{:S(2)}) collective-permute-start(f32[32,128]{1,0:T(8,128)} %bitcast.29), channel_id=1, source_target_pairs={{0,9},{1,8},{2,11},{3,10},{4,13},{5,12},{6,15},{7,14},{8,1},{9,0},... | collective-permute-start | bytes 49160 | tf_op jit(solution)/shard_map/ppermute | solution.py:161
  8.9 5.1 %collective-permute-start.5 = (f32[4,32,128]{2,1,0:T(8,128)S(1)}, f32[4,32,128]{2,1,0:T(8,128)S(1)}, u32[]{:S(2)}, u32[]{:S(2)}) collective-permute-start(f32[4,32,128]{2,1,0:T(8,128)S(1)} %pad_maximum_fusion.refs_2_), channel_id=1, source_target_pairs={{0,7},{1,6},{2,5},{3,4},{4,3},{5,2},{6,1},{7,0},{8,15},{9,14},{10,... | collective-permute-start | bytes 196616 | tf_op jit(solution)/shard_map/ppermute | solution.py:161
  11.6 4.3 %collective-permute-start.4 = (f32[4,32,128]{2,1,0:T(8,128)S(1)}, f32[4,32,128]{2,1,0:T(8,128)S(1)}, u32[]{:S(2)}, u32[]{:S(2)}) collective-permute-start(f32[4,32,128]{2,1,0:T(8,128)S(1)} %pad_maximum_fusion.refs_2_), channel_id=1, source_target_pairs={{0,5},{1,4},{2,7},{3,6},{4,1},{5,0},{6,3},{7,2},{8,13},{9,12},{10,... | collective-permute-start | bytes 196616 | tf_op jit(solution)/shard_map/ppermute | solution.py:161
  11.6 4.3 %collective-permute-start.3 = (f32[4,32,128]{2,1,0:T(8,128)S(1)}, f32[4,32,128]{2,1,0:T(8,128)S(1)}, u32[]{:S(2)}, u32[]{:S(2)}) collective-permute-start(f32[4,32,128]{2,1,0:T(8,128)S(1)} %pad_maximum_fusion.refs_2_), channel_id=1, source_target_pairs={{0,3},{1,2},{2,1},{3,0},{4,7},{5,6},{6,5},{7,4},{8,11},{9,10},{10,... | collective-permute-start | bytes 196616 | tf_op jit(solution)/shard_map/ppermute | solution.py:161
  12.3 4.0 %collective-permute-start.6 = (f32[4,32,128]{2,1,0:T(8,128)S(1)}, f32[4,32,128]{2,1,0:T(8,128)S(1)}, u32[]{:S(2)}, u32[]{:S(2)}) collective-permute-start(f32[4,32,128]{2,1,0:T(8,128)S(1)} %pad_maximum_fusion.refs_2_), channel_id=1, source_target_pairs={{0,1},{1,0},{2,3},{3,2},{4,5},{5,4},{6,7},{7,6},{8,9},{9,8},{10,11... | collective-permute-start | bytes 196616 | tf_op jit(solution)/shard_map/ppermute | solution.py:161
  14.0 2.4 %collective-permute-start.9 = (f32[4,32,128]{2,1,0:T(8,128)S(1)}, f32[4,32,128]{2,1,0:T(8,128)S(1)}, u32[]{:S(2)}, u32[]{:S(2)}) collective-permute-start(f32[4,32,128]{2,1,0:T(8,128)S(1)} %collective-permute-done.5.refs_5_), channel_id=1, source_target_pairs={{0,1},{1,0},{2,3},{3,2},{4,5},{5,4},{6,7},{7,6},{8,9},{9,8},{10,11... | collective-permute-start | bytes 196616 | tf_op jit(solution)/shard_map/ppermute | solution.py:161
  15.8 1.3 %collective-permute-start.8 = (f32[4,32,128]{2,1,0:T(8,128)S(1)}, f32[4,32,128]{2,1,0:T(8,128)S(1)}, u32[]{:S(2)}, u32[]{:S(2)}) collective-permute-start(f32[4,32,128]{2,1,0:T(8,128)S(1)} %collective-permute-done.4.refs_4_), channel_id=1, source_target_pairs={{0,1},{1,0},{2,3},{3,2},{4,5},{5,4},{6,7},{7,6},{8,9},{9,8},{10,11... | collective-permute-start | bytes 196616 | tf_op jit(solution)/shard_map/ppermute | solution.py:161
  15.9 1.3 %collective-permute-start.7 = (f32[4,32,128]{2,1,0:T(8,128)S(1)}, f32[4,32,128]{2,1,0:T(8,128)S(1)}, u32[]{:S(2)}, u32[]{:S(2)}) collective-permute-start(f32[4,32,128]{2,1,0:T(8,128)S(1)} %collective-permute-done.3.refs_3_), channel_id=1, source_target_pairs={{0,1},{1,0},{2,3},{3,2},{4,5},{5,4},{6,7},{7,6},{8,9},{9,8},{10,11... | collective-permute-start | bytes 196616 | tf_op jit(solution)/shard_map/ppermute | solution.py:161
  18.3 4.7 %collective-permute-start.11 = (f32[4,32,128]{2,1,0:T(8,128)S(1)}, f32[4,32,128]{2,1,0:T(8,128)S(1)}, u32[]{:S(2)}, u32[]{:S(2)}) collective-permute-start(f32[4,32,128]{2,1,0:T(8,128)S(1)} %get-tuple-element.11), channel_id=1, source_target_pairs={{0,7},{1,6},{2,5},{3,4},{4,3},{5,2},{6,1},{7,0},{8,15},{9,14},{10,... | collective-permute-start | bytes 196616 | tf_op jit(solution)/shard_map/ppermute | solution.py:161
  20.2 4.9 %collective-permute-start.13 = (f32[4,32,128]{2,1,0:T(8,128)S(1)}, f32[4,32,128]{2,1,0:T(8,128)S(1)}, u32[]{:S(2)}, u32[]{:S(2)}) collective-permute-start(f32[4,32,128]{2,1,0:T(8,128)S(1)} %get-tuple-element.12), channel_id=1, source_target_pairs={{0,5},{1,4},{2,7},{3,6},{4,1},{5,0},{6,3},{7,2},{8,13},{9,12},{10,... | collective-permute-start | bytes 196616 | tf_op jit(solution)/shard_map/ppermute | solution.py:161
  20.9 4.2 %collective-permute-start.12 = (f32[4,32,128]{2,1,0:T(8,128)S(1)}, f32[4,32,128]{2,1,0:T(8,128)S(1)}, u32[]{:S(2)}, u32[]{:S(2)}) collective-permute-start(f32[4,32,128]{2,1,0:T(8,128)S(1)} %get-tuple-element.13), channel_id=1, source_target_pairs={{0,3},{1,2},{2,1},{3,0},{4,7},{5,6},{6,5},{7,4},{8,11},{9,10},{10,... | collective-permute-start | bytes 196616 | tf_op jit(solution)/shard_map/ppermute | solution.py:161
  22.0 3.2 %collective-permute-start.10 = (f32[4,32,128]{2,1,0:T(8,128)S(1)}, f32[4,32,128]{2,1,0:T(8,128)S(1)}, u32[]{:S(2)}, u32[]{:S(2)}) collective-permute-start(f32[4,32,128]{2,1,0:T(8,128)S(1)} %get-tuple-element.14), channel_id=1, source_target_pairs={{0,1},{1,0},{2,3},{3,2},{4,5},{5,4},{6,7},{7,6},{8,9},{9,8},{10,11... | collective-permute-start | bytes 196616 | tf_op jit(solution)/shard_map/ppermute | solution.py:161
  25.2 5.0 %collective-permute-start.15 = (f32[32,128]{1,0:T(8,128)S(1)}, f32[32,128]{1,0:T(8,128)S(1)}, u32[]{:S(2)}, u32[]{:S(2)}) collective-permute-start(f32[32,128]{1,0:T(8,128)S(1)} %get-tuple-element.15), channel_id=1, source_target_pairs={{0,25},{1,24},{2,27},{3,26},{4,29},{5,28},{6,31},{7,30},{8,17},{9,... | collective-permute-start | bytes 49160 | tf_op jit(solution)/shard_map/ppermute | solution.py:161
  26.8 4.1 %collective-permute-start.17 = (f32[32,128]{1,0:T(8,128)S(1)}, f32[32,128]{1,0:T(8,128)S(1)}, u32[]{:S(2)}, u32[]{:S(2)}) collective-permute-start(f32[32,128]{1,0:T(8,128)S(1)} %get-tuple-element.16), channel_id=1, source_target_pairs={{0,17},{1,16},{2,19},{3,18},{4,21},{5,20},{6,23},{7,22},{8,25},{9,... | collective-permute-start | bytes 49160 | tf_op jit(solution)/shard_map/ppermute | solution.py:161
  27.1 3.8 %collective-permute-start.16 = (f32[32,128]{1,0:T(8,128)S(1)}, f32[32,128]{1,0:T(8,128)S(1)}, u32[]{:S(2)}, u32[]{:S(2)}) collective-permute-start(f32[32,128]{1,0:T(8,128)S(1)} %get-tuple-element.17), channel_id=1, source_target_pairs={{0,9},{1,8},{2,11},{3,10},{4,13},{5,12},{6,15},{7,14},{8,1},{9,0},... | collective-permute-start | bytes 49160 | tf_op jit(solution)/shard_map/ppermute | solution.py:161
  29.1 1.8 %collective-permute-start.14 = (f32[32,128]{1,0:T(8,128)S(1)}, f32[32,128]{1,0:T(8,128)S(1)}, u32[]{:S(2)}, u32[]{:S(2)}) collective-permute-start(f32[32,128]{1,0:T(8,128)S(1)} %get-tuple-element.18), channel_id=1, source_target_pairs={{0,1},{1,0},{2,3},{3,2},{4,5},{5,4},{6,7},{7,6},{8,9},{9,8},{10,11... | collective-permute-start | bytes 49160 | tf_op jit(solution)/shard_map/ppermute | solution.py:161
where the time goes:
time: 31.8 us; the launch traced here: 31.5 us
  starting transfers between devices  17.4 us (55%)
  waiting for transfers between devices  10.4 us (33%)
  Pallas kernels  2.3 us (7%)
  between operations  0.72 us (2%)
  other arithmetic  0.64 us (2%)
    ppermute x18, starting transfers between devices, swap(): return lax.ppermute(value, ('pair', 'virt'), routes)  17.4 us
    ppermute x18, waiting for transfers between devices, swap(): return lax.ppermute(value, ('pair', 'virt'), routes)  10.4 us
    pallas_call x1, Pallas kernels, prepare(): pl.pallas_call(kernel, out_shape=(jax.ShapeDtypeStruct((slots, W, 2 * W),...  1.24 us
    pallas_call x1, Pallas kernels, local_terms(): pl.pallas_call(kernel, out_shape=jax.ShapeDtypeStruct((NEAR * far, out_ti...  1.06 us
  transfers between devices with their start and end apart: 18, of which 9 were waited for; matrix products, arithmetic and copies ran while one was open for 0% of the time, Pallas kernels for 4%

commit v1 on v0

--- a/solution.py
+++ b/solution.py
@@ -84,6 +84,18 @@
     )(live, *operands)
 
 
+def far_masks(far):
+    if far % 4:
+        return list(range(1, far)), []
+    singles = [mask for mask in range(1, far) if mask % 4 in (0, 3)]
+    return singles, [(mask, mask + 1) for mask in range(1, far, 4)]
+
+
+def turn(index):
+    far = index // NEAR
+    return (far ^ far // 2) % 2
+
+
 def ladder_kernel(virts, codes_here, halves, *refs):
     blocks, (result, columns, flat, totals, codes, copied) = refs[: virts * NEAR], refs[virts * NEAR :]
     fetch = pltpu.make_async_copy(codes_here, codes, copied)
@@ -96,13 +108,20 @@
     in_local = columns.shape[0] // virts
     totals[...] = jnp.zeros_like(totals)
 
+    singles, couples = far_masks(far)
+    base = 1 + len(singles)
     for owner in range(virts):
+        odd = owner % 2
         for a in range(NEAR):
-            for b in range(far):
-                source = blocks[(owner ^ int((a > 0) != (b > 0))) * NEAR + a]
+            same = blocks[(owner ^ int(a > 0)) * NEAR + a]
+            other = blocks[(owner ^ int(a == 0)) * NEAR + a]
+            sources = [(same, 0)] + [(other, at) for at in range(1, base)]
+            for at in range(base, far, 2):
+                sources += [(other, at), (same, at + 1)] if odd else [(same, at + 1), (other, at)]
+            for b, (source, at) in enumerate(sources):
                 place = pl.ds((a * far + b) * rows, rows)
                 for tile in range(in_local):
-                    flat[tile, place, :] = source[b, tile * rows : (tile + 1) * rows, :]
+                    flat[tile, place, :] = source[at, tile * rows : (tile + 1) * rows, :]
         for tile in range(in_local):
             high, low = split(flat[tile])
             columns[owner * in_local + tile, :total_rows, :] = high
@@ -123,12 +142,15 @@
         return carry
 
     lax.fori_loop(0, (codes[2, 0] + GROUP - 1) // GROUP, one_group, 0)
-    def give(chunk, carry):
-        for tile in range(out_tiles):
-            result[chunk, tile * rows : (tile + 1) * rows, :] = totals[tile, pl.ds(chunk * rows, rows), :]
-        return carry
-
-    lax.fori_loop(0, chunk_count, give, 0, unroll=min(chunk_count, 16))
+    swapped = lax.rem(lax.axis_index("virt"), 2) ^ turn(lax.axis_index("pair"))
+    masks = [0] + singles
+    for first, second in couples:
+        masks += [jnp.where(swapped == 0, first, second), jnp.where(swapped == 0, second, first)]
+    for a in range(NEAR):
+        for b, mask in enumerate(masks):
+            place = pl.ds((a * far + b) * rows, rows)
+            for tile in range(out_tiles):
+                result[a * far + mask, tile * rows : (tile + 1) * rows, :] = totals[tile, place, :]
 
 
 def local_terms(codes, blocks, halves, rows, out_tiles):
@@ -157,8 +179,39 @@
 
 
 def swap(value, pairs, virts, mask, virt_mask):
-    routes = [(a * virts + b, (a ^ mask) * virts + (b ^ virt_mask)) for a in range(pairs) for b in range(virts)]
+    mask_at = mask if callable(mask) else lambda a, b: mask
+    routes = [
+        (a * virts + b, (a ^ mask_at(a, b)) * virts + (b ^ virt_mask)) for a in range(pairs) for b in range(virts)
+    ]
     return lax.ppermute(value, ("pair", "virt"), routes)
+
+
+def gather_line(mine, own, pairs, virts):
+    singles, couples = far_masks(pairs // NEAR)
+    neighbour = swap(mine, pairs, virts, 0, 1)
+    near = copy_near(mine)
+    line = [own[None]] + [swap(near, pairs, virts, mask * NEAR, 1)[None] for mask in singles]
+    both = jnp.stack([near, neighbour])
+    for couple in couples:
+        line.append(swap(both, pairs, virts, lambda a, b: couple[turn(a) ^ b % 2] * NEAR, 1))
+    return jnp.concatenate(line)
+
+
+def copy_kernel(value, result, copied):
+    copy = pltpu.make_async_copy(value, result, copied)
+    copy.start()
+    copy.wait()
+
+
+def copy_near(value):
+    return pl.pallas_call(
+        copy_kernel,
+        out_shape=jax.ShapeDtypeStruct(value.shape, value.dtype),
+        in_specs=[pl.BlockSpec(memory_space=pltpu.HBM)],
+        out_specs=VMEM,
+        scratch_shapes=[pltpu.SemaphoreType.DMA],
+        cost_estimate=pl.CostEstimate(flops=0, bytes_accessed=1 << 22, transcendentals=0),
+    )(pltpu.with_memory_space_constraint(value, pltpu.HBM))
 
 
 def swap_sum(parts, pairs, virts, unit):
@@ -181,7 +234,7 @@
         mine,
         local_tiles,
     )
-    line = jnp.stack([own] + [swap(mine, pairs, virts, mask, 1) for mask in range(NEAR, pairs, NEAR)])
+    line = gather_line(mine, own, pairs, virts)
     pieces = [line] + [swap(line, pairs, virts, mask, 1) for mask in range(1, NEAR)]
     blocks = pieces + [swap(piece, pairs, virts, 0, mask) for mask in range(1, virts) for piece in pieces]
     partial_sums = local_terms(codes, blocks, halves, rows, local_tiles)

time: 31.8 us -> 34 us (1.069)
  Pallas kernels: 2.3 us -> 3.64 us
  other arithmetic: 0.64 us -> 1.36 us
    pallas_call x0 -> x1, Pallas kernels: none -> 1.33 us  [copy_near(): pl.pallas_call(copy_kernel, out_shape=jax.ShapeDtypeStruct(value.shape, v...]
    another operation x1, other arithmetic: 0.01 us -> 0.72 us  [gather_line(): both = jnp.stack([near, neighbour])]
  transfers between devices with their start and end apart: 18 -> 18, of which waited for: 9 -> 9; matrix products, arithmetic and copies ran while one was open for 0% -> 0% of each run, Pallas kernels for 4% -> 8%
where the time goes in v1:
time: 34 us; the launch traced here: 33.5 us
  starting transfers between devices  17.5 us (51%)
  waiting for transfers between devices  10.3 us (30%)
  Pallas kernels  3.64 us (11%)
  other arithmetic  1.36 us (4%)
  between operations  0.73 us (2%)
    ppermute x18, starting transfers between devices, swap(): return lax.ppermute(value, ('pair', 'virt'), routes)  17.5 us
    ppermute x18, waiting for transfers between devices, swap(): return lax.ppermute(value, ('pair', 'virt'), routes)  10.3 us
    pallas_call x1, Pallas kernels, copy_near(): pl.pallas_call(copy_kernel, out_shape=jax.ShapeDtypeStruct(value.shape, v...  1.33 us
    pallas_call x1, Pallas kernels, prepare(): pl.pallas_call(kernel, out_shape=(jax.ShapeDtypeStruct((slots, W, 2 * W),...  1.24 us
    pallas_call x1, Pallas kernels, local_terms(): pl.pallas_call(kernel, out_shape=jax.ShapeDtypeStruct((NEAR * far, out_ti...  1.07 us
    another operation x1, other arithmetic, gather_line(): both = jnp.stack([near, neighbour])  0.72 us
  transfers between devices with their start and end apart: 18, of which 9 were waited for; matrix products, arithmetic and copies ran while one was open for 0% of the time, Pallas kernels for 8%

profile of v1, /device:TPU:0, one launch (start us, length us, event | category | flops | bytes accessed | tf_op | source)
XLA Modules:
  0.0 33.5 jit_solution(10576075424430436042)
XLA Ops:
  0.0 0.5 %collective-permute-start.1 = (f32[32,128]{1,0:T(8,128)}, f32[32,128]{1,0:T(8,128)S(1)}, u32[]{:S(2)}, u32[]{:S(2)}) collective-permute-start(f32[32,128]{1,0:T(8,128)} %bitcast.27), channel_id=1, source_target_pairs={{0,1},{1,0},{2,3},{3,2},{4,5},{5,4},{6,7},{7,6},{8,9},{9,8},{10,11... | collective-permute-start | bytes 49160 | tf_op jit(solution)/shard_map/ppermute | solution.py:186
  0.5 1.3 %shard_map.56 = f32[32,128]{1,0:T(8,128)} custom-call(f32[32,128]{1,0:T(8,128)} %bitcast.28), custom_call_target="tpu_custom_call" | custom-call | bytes 4194304 | tf_op jit(solution)/shard_map/pallas_call | solution.py:207
  1.8 0.0 collective-permute-done.1
  1.8 0.7 %pad_maximum_fusion.1 = f32[2,32,128]{2,1,0:T(8,128)S(1)} fusion(f32[1,32,128]{2,1,0:T(8,128)S(1)} %bitcast.31, f32[1,32,128]{2,1,0:T(8,128)} %bitcast.30), kind=kLoop, calls=%fused_computation.2 | loop fusion | flops 8192 | bytes 65536 | tf_op jit(solution)/shard_map/stack | solution.py:194
  2.5 2.7 %collective-permute-start.2 = (f32[2,32,128]{2,1,0:T(8,128)S(1)}, f32[2,32,128]{2,1,0:T(8,128)S(1)}, u32[]{:S(2)}, u32[]{:S(2)}) collective-permute-start(f32[2,32,128]{2,1,0:T(8,128)S(1)} %pad_maximum_fusion.1), channel_id=1, source_target_pairs={{0,9},{1,16},{2,11},{3,18},{4,13},{5,20},{6,15},{7,22},{8,25},{9,0... | collective-permute-start | bytes 98312 | tf_op jit(solution)/shard_map/ppermute | solution.py:186
  5.2 2.0 %collective-permute-start = (f32[32,128]{1,0:T(8,128)}, f32[32,128]{1,0:T(8,128)S(1)}, u32[]{:S(2)}, u32[]{:S(2)}) collective-permute-start(f32[32,128]{1,0:T(8,128)} %shard_map.56), channel_id=1, source_target_pairs={{0,25},{1,24},{2,27},{3,26},{4,29},{5,28},{6,31},{7,30},{8,17},{9,... | collective-permute-start | bytes 49160 | tf_op jit(solution)/shard_map/ppermute | solution.py:186
  7.9 1.2 %shard_map.55 = (bf16[32,128,256]{2,1,0:T(8,128)(2,1)S(1)}, s32[3,32]{1,0:T(4,128)S(1)}, f32[32,128]{1,0:T(8,128)S(1)}) custom-call(s32[1,1]{1,0:T(1,128)S(6)} %copy.8.refs_0_, s32[1,32]{1,0:T(1,128)} %bitcast.33, s32[1,32]{1,0:T(1,128)} %bitcast.34, f32[32,128,128]{2,1,0:T(8,128)} %bitcast.26, f32[32,128]{1,0:T(8,128)} %bitcast.29), custom_call_target="tpu_custom_call" | custom-call | flops 2097152 | bytes 4194304 | tf_op jit(solution)/shard_map/pallas_call | solution.py:67
  9.1 1.2 %collective-permute-done = f32[32,128]{1,0:T(8,128)S(1)} collective-permute-done((f32[32,128]{1,0:T(8,128)}, f32[32,128]{1,0:T(8,128)S(1)}, u32[]{:S(2)}, u32[]{:S(2)}) %collective-permute-start) | collective-permute-done | bytes 16416 | tf_op jit(solution)/shard_map/ppermute | solution.py:186
  10.4 0.0 collective-permute-done.2
  10.4 3.2 %collective-permute-start.5 = (f32[4,32,128]{2,1,0:T(8,128)S(1)}, f32[4,32,128]{2,1,0:T(8,128)S(1)}, u32[]{:S(2)}, u32[]{:S(2)}) collective-permute-start(f32[4,32,128]{2,1,0:T(8,128)S(1)} %pad_maximum_fusion.refs_2_), channel_id=1, source_target_pairs={{0,7},{1,6},{2,5},{3,4},{4,3},{5,2},{6,1},{7,0},{8,15},{9,14},{10,... | collective-permute-start | bytes 196616 | tf_op jit(solution)/shard_map/ppermute | solution.py:186
  13.6 0.0 collective-permute-start.4
  13.6 0.8 %collective-permute-start.3 = (f32[4,32,128]{2,1,0:T(8,128)S(1)}, f32[4,32,128]{2,1,0:T(8,128)S(1)}, u32[]{:S(2)}, u32[]{:S(2)}) collective-permute-start(f32[4,32,128]{2,1,0:T(8,128)S(1)} %pad_maximum_fusion.refs_2_), channel_id=1, source_target_pairs={{0,3},{1,2},{2,1},{3,0},{4,7},{5,6},{6,5},{7,4},{8,11},{9,10},{10,... | collective-permute-start | bytes 196616 | tf_op jit(solution)/shard_map/ppermute | solution.py:186
  14.3 0.0 collective-permute-start.6
  14.3 1.6 %collective-permute-done.5.refs_5_ = f32[4,32,128]{2,1,0:T(8,128)S(1)} collective-permute-done((f32[4,32,128]{2,1,0:T(8,128)S(1)}, f32[4,32,128]{2,1,0:T(8,128)S(1)}, u32[]{:S(2)}, u32[]{:S(2)}) %collective-permute-start.5) | collective-permute-done | bytes 65568 | tf_op jit(solution)/shard_map/ppermute | solution.py:186
  16.0 0.1 collective-permute-start.9
  16.1 1.6 %collective-permute-done.4.refs_4_ = f32[4,32,128]{2,1,0:T(8,128)S(1)} collective-permute-done((f32[4,32,128]{2,1,0:T(8,128)S(1)}, f32[4,32,128]{2,1,0:T(8,128)S(1)}, u32[]{:S(2)}, u32[]{:S(2)}) %collective-permute-start.4) | collective-permute-done | bytes 65568 | tf_op jit(solution)/shard_map/ppermute | solution.py:186
  17.7 0.0 collective-permute-start.8
  17.7 0.0 collective-permute-done.3.refs_3_
  17.7 0.5 %collective-permute-start.7 = (f32[4,32,128]{2,1,0:T(8,128)S(1)}, f32[4,32,128]{2,1,0:T(8,128)S(1)}, u32[]{:S(2)}, u32[]{:S(2)}) collective-permute-start(f32[4,32,128]{2,1,0:T(8,128)S(1)} %collective-permute-done.3.refs_3_), channel_id=1, source_target_pairs={{0,1},{1,0},{2,3},{3,2},{4,5},{5,4},{6,7},{7,6},{8,9},{9,8},{10,11... | collective-permute-start | bytes 196616 | tf_op jit(solution)/shard_map/ppermute | solution.py:186
  18.2 0.0 collective-permute-done.6.refs_6_
  18.2 0.0 collective-permute-done.9.refs_9_
  18.2 0.7 %collective-permute-done.8.refs_8_ = f32[4,32,128]{2,1,0:T(8,128)S(1)} collective-permute-done((f32[4,32,128]{2,1,0:T(8,128)S(1)}, f32[4,32,128]{2,1,0:T(8,128)S(1)}, u32[]{:S(2)}, u32[]{:S(2)}) %collective-permute-start.8) | collective-permute-done | bytes 65568 | tf_op jit(solution)/shard_map/ppermute | solution.py:186
  18.9 0.2 collective-permute-done.7.refs_7_
  19.1 1.1 %shard_map.57 = f32[16,32,128]{2,1,0:T(8,128)S(1)} custom-call(s32[3,32]{1,0:T(4,128)S(1)} %get-tuple-element.8.refs_0_, bf16[32,128,256]{2,1,0:T(8,128)(2,1)S(1)} %get-tuple-element.9.refs_1_, f32[4,32,128]{2,1,0:T(8,128)S(1)} %pad_maximum_fusion.refs_2_, f32[4,32,128]{2,1,0:T(8,128)S(1)} %collective-permute-done.3.refs_3_, ...), custom_call_target="tpu_custom_call" | custom-call | tf_op jit(solution)/shard_map/pallas_call | solution.py:165
  20.2 1.9 %collective-permute-start.11 = (f32[4,32,128]{2,1,0:T(8,128)S(1)}, f32[4,32,128]{2,1,0:T(8,128)S(1)}, u32[]{:S(2)}, u32[]{:S(2)}) collective-permute-start(f32[4,32,128]{2,1,0:T(8,128)S(1)} %get-tuple-element.11), channel_id=1, source_target_pairs={{0,7},{1,6},{2,5},{3,4},{4,3},{5,2},{6,1},{7,0},{8,15},{9,14},{10,... | collective-permute-start | bytes 196616 | tf_op jit(solution)/shard_map/ppermute | solution.py:186
  22.1 0.5 %collective-permute-start.13 = (f32[4,32,128]{2,1,0:T(8,128)S(1)}, f32[4,32,128]{2,1,0:T(8,128)S(1)}, u32[]{:S(2)}, u32[]{:S(2)}) collective-permute-start(f32[4,32,128]{2,1,0:T(8,128)S(1)} %get-tuple-element.12), channel_id=1, source_target_pairs={{0,5},{1,4},{2,7},{3,6},{4,1},{5,0},{6,3},{7,2},{8,13},{9,12},{10,... | collective-permute-start | bytes 196616 | tf_op jit(solution)/shard_map/ppermute | solution.py:186
  22.6 0.8 %collective-permute-start.12 = (f32[4,32,128]{2,1,0:T(8,128)S(1)}, f32[4,32,128]{2,1,0:T(8,128)S(1)}, u32[]{:S(2)}, u32[]{:S(2)}) collective-permute-start(f32[4,32,128]{2,1,0:T(8,128)S(1)} %get-tuple-element.13), channel_id=1, source_target_pairs={{0,3},{1,2},{2,1},{3,0},{4,7},{5,6},{6,5},{7,4},{8,11},{9,10},{10,... | collective-permute-start | bytes 196616 | tf_op jit(solution)/shard_map/ppermute | solution.py:186
  23.4 0.2 collective-permute-start.10
  23.6 1.5 %collective-permute-done.11 = f32[4,32,128]{2,1,0:T(8,128)S(1)} collective-permute-done((f32[4,32,128]{2,1,0:T(8,128)S(1)}, f32[4,32,128]{2,1,0:T(8,128)S(1)}, u32[]{:S(2)}, u32[]{:S(2)}) %collective-permute-start.11) | collective-permute-done | bytes 65568 | tf_op jit(solution)/shard_map/ppermute | solution.py:186
  25.1 1.8 %collective-permute-done.13 = f32[4,32,128]{2,1,0:T(8,128)S(1)} collective-permute-done((f32[4,32,128]{2,1,0:T(8,128)S(1)}, f32[4,32,128]{2,1,0:T(8,128)S(1)}, u32[]{:S(2)}, u32[]{:S(2)}) %collective-permute-start.13) | collective-permute-done | bytes 65568 | tf_op jit(solution)/shard_map/ppermute | solution.py:186
  26.9 0.0 collective-permute-done.12
  26.9 0.0 collective-permute-done.10
  27.0 1.8 %collective-permute-start.15 = (f32[32,128]{1,0:T(8,128)S(1)}, f32[32,128]{1,0:T(8,128)S(1)}, u32[]{:S(2)}, u32[]{:S(2)}) collective-permute-start(f32[32,128]{1,0:T(8,128)S(1)} %get-tuple-element.15), channel_id=1, source_target_pairs={{0,25},{1,24},{2,27},{3,26},{4,29},{5,28},{6,31},{7,30},{8,17},{9,... | collective-permute-start | bytes 49160 | tf_op jit(solution)/shard_map/ppermute | solution.py:186
  28.8 0.0 collective-permute-start.17
  28.8 2.1 %collective-permute-start.16 = (f32[32,128]{1,0:T(8,128)S(1)}, f32[32,128]{1,0:T(8,128)S(1)}, u32[]{:S(2)}, u32[]{:S(2)}) collective-permute-start(f32[32,128]{1,0:T(8,128)S(1)} %get-tuple-element.17), channel_id=1, source_target_pairs={{0,9},{1,8},{2,11},{3,10},{4,13},{5,12},{6,15},{7,14},{8,1},{9,0},... | collective-permute-start | bytes 49160 | tf_op jit(solution)/shard_map/ppermute | solution.py:186
  30.9 0.4 %collective-permute-start.14 = (f32[32,128]{1,0:T(8,128)S(1)}, f32[32,128]{1,0:T(8,128)S(1)}, u32[]{:S(2)}, u32[]{:S(2)}) collective-permute-start(f32[32,128]{1,0:T(8,128)S(1)} %get-tuple-element.18), channel_id=1, source_target_pairs={{0,1},{1,0},{2,3},{3,2},{4,5},{5,4},{6,7},{7,6},{8,9},{9,8},{10,11... | collective-permute-start | bytes 49160 | tf_op jit(solution)/shard_map/ppermute | solution.py:186
  31.3 0.7 %collective-permute-done.15 = f32[32,128]{1,0:T(8,128)S(1)} collective-permute-done((f32[32,128]{1,0:T(8,128)S(1)}, f32[32,128]{1,0:T(8,128)S(1)}, u32[]{:S(2)}, u32[]{:S(2)}) %collective-permute-start.15) | collective-permute-done | bytes 16416 | tf_op jit(solution)/shard_map/ppermute | solution.py:186
  32.0 0.9 %collective-permute-done.17 = f32[32,128]{1,0:T(8,128)S(1)} collective-permute-done((f32[32,128]{1,0:T(8,128)S(1)}, f32[32,128]{1,0:T(8,128)S(1)}, u32[]{:S(2)}, u32[]{:S(2)}) %collective-permute-start.17) | collective-permute-done | bytes 16416 | tf_op jit(solution)/shard_map/ppermute | solution.py:186
  32.9 0.0 collective-permute-done.16
  32.9 0.0 collective-permute-done.14
  32.9 0.6 %add_add_fusion.1 = f32[32,128]{1,0:T(8,128)} fusion(f32[32,128]{1,0:T(8,128)S(1)} %collective-permute-done.17, f32[32,128]{1,0:T(8,128)S(1)} %collective-permute-done.16, f32[32,128]{1,0:T(8,128)S(1)} %collective-permute-done.14, f32[32,128]{1,0:T(8,128)S(1)} %collective-permute-done.15), kind=kLoop, calls=%fused_computation.7 | loop fusion | flops 12288 | bytes 81920 | tf_op jit(solution)/shard_map/add | solution.py:220
  (4 shorter events, 0.1 us)
Async XLA Ops:
  0.0 1.8 %collective-permute-start.1 = (f32[32,128]{1,0:T(8,128)}, f32[32,128]{1,0:T(8,128)S(1)}, u32[]{:S(2)}, u32[]{:S(2)}) collective-permute-start(f32[32,128]{1,0:T(8,128)} %bitcast.27), channel_id=1, source_target_pairs={{0,1},{1,0},{2,3},{3,2},{4,5},{5,4},{6,7},{7,6},{8,9},{9,8},{10,11... | collective-permute-start | bytes 49160 | tf_op jit(solution)/shard_map/ppermute | solution.py:186
  2.5 7.9 %collective-permute-start.2 = (f32[2,32,128]{2,1,0:T(8,128)S(1)}, f32[2,32,128]{2,1,0:T(8,128)S(1)}, u32[]{:S(2)}, u32[]{:S(2)}) collective-permute-start(f32[2,32,128]{2,1,0:T(8,128)S(1)} %pad_maximum_fusion.1), channel_id=1, source_target_pairs={{0,9},{1,16},{2,11},{3,18},{4,13},{5,20},{6,15},{7,22},{8,25},{9,0... | collective-permute-start | bytes 98312 | tf_op jit(solution)/shard_map/ppermute | solution.py:186
  5.2 5.2 %collective-permute-start = (f32[32,128]{1,0:T(8,128)}, f32[32,128]{1,0:T(8,128)S(1)}, u32[]{:S(2)}, u32[]{:S(2)}) collective-permute-start(f32[32,128]{1,0:T(8,128)} %shard_map.56), channel_id=1, source_target_pairs={{0,25},{1,24},{2,27},{3,26},{4,29},{5,28},{6,31},{7,30},{8,17},{9,... | collective-permute-start | bytes 49160 | tf_op jit(solution)/shard_map/ppermute | solution.py:186
  10.4 5.6 %collective-permute-start.5 = (f32[4,32,128]{2,1,0:T(8,128)S(1)}, f32[4,32,128]{2,1,0:T(8,128)S(1)}, u32[]{:S(2)}, u32[]{:S(2)}) collective-permute-start(f32[4,32,128]{2,1,0:T(8,128)S(1)} %pad_maximum_fusion.refs_2_), channel_id=1, source_target_pairs={{0,7},{1,6},{2,5},{3,4},{4,3},{5,2},{6,1},{7,0},{8,15},{9,14},{10,... | collective-permute-start | bytes 196616 | tf_op jit(solution)/shard_map/ppermute | solution.py:186
  13.6 4.1 %collective-permute-start.4 = (f32[4,32,128]{2,1,0:T(8,128)S(1)}, f32[4,32,128]{2,1,0:T(8,128)S(1)}, u32[]{:S(2)}, u32[]{:S(2)}) collective-permute-start(f32[4,32,128]{2,1,0:T(8,128)S(1)} %pad_maximum_fusion.refs_2_), channel_id=1, source_target_pairs={{0,5},{1,4},{2,7},{3,6},{4,1},{5,0},{6,3},{7,2},{8,13},{9,12},{10,... | collective-permute-start | bytes 196616 | tf_op jit(solution)/shard_map/ppermute | solution.py:186
  13.6 4.1 %collective-permute-start.3 = (f32[4,32,128]{2,1,0:T(8,128)S(1)}, f32[4,32,128]{2,1,0:T(8,128)S(1)}, u32[]{:S(2)}, u32[]{:S(2)}) collective-permute-start(f32[4,32,128]{2,1,0:T(8,128)S(1)} %pad_maximum_fusion.refs_2_), channel_id=1, source_target_pairs={{0,3},{1,2},{2,1},{3,0},{4,7},{5,6},{6,5},{7,4},{8,11},{9,10},{10,... | collective-permute-start | bytes 196616 | tf_op jit(solution)/shard_map/ppermute | solution.py:186
  14.3 3.9 %collective-permute-start.6 = (f32[4,32,128]{2,1,0:T(8,128)S(1)}, f32[4,32,128]{2,1,0:T(8,128)S(1)}, u32[]{:S(2)}, u32[]{:S(2)}) collective-permute-start(f32[4,32,128]{2,1,0:T(8,128)S(1)} %pad_maximum_fusion.refs_2_), channel_id=1, source_target_pairs={{0,1},{1,0},{2,3},{3,2},{4,5},{5,4},{6,7},{7,6},{8,9},{9,8},{10,11... | collective-permute-start | bytes 196616 | tf_op jit(solution)/shard_map/ppermute | solution.py:186
  16.0 2.2 %collective-permute-start.9 = (f32[4,32,128]{2,1,0:T(8,128)S(1)}, f32[4,32,128]{2,1,0:T(8,128)S(1)}, u32[]{:S(2)}, u32[]{:S(2)}) collective-permute-start(f32[4,32,128]{2,1,0:T(8,128)S(1)} %collective-permute-done.5.refs_5_), channel_id=1, source_target_pairs={{0,1},{1,0},{2,3},{3,2},{4,5},{5,4},{6,7},{7,6},{8,9},{9,8},{10,11... | collective-permute-start | bytes 196616 | tf_op jit(solution)/shard_map/ppermute | solution.py:186
  17.7 1.3 %collective-permute-start.8 = (f32[4,32,128]{2,1,0:T(8,128)S(1)}, f32[4,32,128]{2,1,0:T(8,128)S(1)}, u32[]{:S(2)}, u32[]{:S(2)}) collective-permute-start(f32[4,32,128]{2,1,0:T(8,128)S(1)} %collective-permute-done.4.refs_4_), channel_id=1, source_target_pairs={{0,1},{1,0},{2,3},{3,2},{4,5},{5,4},{6,7},{7,6},{8,9},{9,8},{10,11... | collective-permute-start | bytes 196616 | tf_op jit(solution)/shard_map/ppermute | solution.py:186
  17.7 1.4 %collective-permute-start.7 = (f32[4,32,128]{2,1,0:T(8,128)S(1)}, f32[4,32,128]{2,1,0:T(8,128)S(1)}, u32[]{:S(2)}, u32[]{:S(2)}) collective-permute-start(f32[4,32,128]{2,1,0:T(8,128)S(1)} %collective-permute-done.3.refs_3_), channel_id=1, source_target_pairs={{0,1},{1,0},{2,3},{3,2},{4,5},{5,4},{6,7},{7,6},{8,9},{9,8},{10,11... | collective-permute-start | bytes 196616 | tf_op jit(solution)/shard_map/ppermute | solution.py:186
  20.2 4.9 %collective-permute-start.11 = (f32[4,32,128]{2,1,0:T(8,128)S(1)}, f32[4,32,128]{2,1,0:T(8,128)S(1)}, u32[]{:S(2)}, u32[]{:S(2)}) collective-permute-start(f32[4,32,128]{2,1,0:T(8,128)S(1)} %get-tuple-element.11), channel_id=1, source_target_pairs={{0,7},{1,6},{2,5},{3,4},{4,3},{5,2},{6,1},{7,0},{8,15},{9,14},{10,... | collective-permute-start | bytes 196616 | tf_op jit(solution)/shard_map/ppermute | solution.py:186
  22.1 4.8 %collective-permute-start.13 = (f32[4,32,128]{2,1,0:T(8,128)S(1)}, f32[4,32,128]{2,1,0:T(8,128)S(1)}, u32[]{:S(2)}, u32[]{:S(2)}) collective-permute-start(f32[4,32,128]{2,1,0:T(8,128)S(1)} %get-tuple-element.12), channel_id=1, source_target_pairs={{0,5},{1,4},{2,7},{3,6},{4,1},{5,0},{6,3},{7,2},{8,13},{9,12},{10,... | collective-permute-start | bytes 196616 | tf_op jit(solution)/shard_map/ppermute | solution.py:186
  22.6 4.3 %collective-permute-start.12 = (f32[4,32,128]{2,1,0:T(8,128)S(1)}, f32[4,32,128]{2,1,0:T(8,128)S(1)}, u32[]{:S(2)}, u32[]{:S(2)}) collective-permute-start(f32[4,32,128]{2,1,0:T(8,128)S(1)} %get-tuple-element.13), channel_id=1, source_target_pairs={{0,3},{1,2},{2,1},{3,0},{4,7},{5,6},{6,5},{7,4},{8,11},{9,10},{10,... | collective-permute-start | bytes 196616 | tf_op jit(solution)/shard_map/ppermute | solution.py:186
  23.4 3.5 %collective-permute-start.10 = (f32[4,32,128]{2,1,0:T(8,128)S(1)}, f32[4,32,128]{2,1,0:T(8,128)S(1)}, u32[]{:S(2)}, u32[]{:S(2)}) collective-permute-start(f32[4,32,128]{2,1,0:T(8,128)S(1)} %get-tuple-element.14), channel_id=1, source_target_pairs={{0,1},{1,0},{2,3},{3,2},{4,5},{5,4},{6,7},{7,6},{8,9},{9,8},{10,11... | collective-permute-start | bytes 196616 | tf_op jit(solution)/shard_map/ppermute | solution.py:186
  27.0 5.0 %collective-permute-start.15 = (f32[32,128]{1,0:T(8,128)S(1)}, f32[32,128]{1,0:T(8,128)S(1)}, u32[]{:S(2)}, u32[]{:S(2)}) collective-permute-start(f32[32,128]{1,0:T(8,128)S(1)} %get-tuple-element.15), channel_id=1, source_target_pairs={{0,25},{1,24},{2,27},{3,26},{4,29},{5,28},{6,31},{7,30},{8,17},{9,... | collective-permute-start | bytes 49160 | tf_op jit(solution)/shard_map/ppermute | solution.py:186
  28.8 4.1 %collective-permute-start.17 = (f32[32,128]{1,0:T(8,128)S(1)}, f32[32,128]{1,0:T(8,128)S(1)}, u32[]{:S(2)}, u32[]{:S(2)}) collective-permute-start(f32[32,128]{1,0:T(8,128)S(1)} %get-tuple-element.16), channel_id=1, source_target_pairs={{0,17},{1,16},{2,19},{3,18},{4,21},{5,20},{6,23},{7,22},{8,25},{9,... | collective-permute-start | bytes 49160 | tf_op jit(solution)/shard_map/ppermute | solution.py:186
  28.8 4.1 %collective-permute-start.16 = (f32[32,128]{1,0:T(8,128)S(1)}, f32[32,128]{1,0:T(8,128)S(1)}, u32[]{:S(2)}, u32[]{:S(2)}) collective-permute-start(f32[32,128]{1,0:T(8,128)S(1)} %get-tuple-element.17), channel_id=1, source_target_pairs={{0,9},{1,8},{2,11},{3,10},{4,13},{5,12},{6,15},{7,14},{8,1},{9,0},... | collective-permute-start | bytes 49160 | tf_op jit(solution)/shard_map/ppermute | solution.py:186
  30.9 2.0 %collective-permute-start.14 = (f32[32,128]{1,0:T(8,128)S(1)}, f32[32,128]{1,0:T(8,128)S(1)}, u32[]{:S(2)}, u32[]{:S(2)}) collective-permute-start(f32[32,128]{1,0:T(8,128)S(1)} %get-tuple-element.18), channel_id=1, source_target_pairs={{0,1},{1,0},{2,3},{3,2},{4,5},{5,4},{6,7},{7,6},{8,9},{9,8},{10,11... | collective-permute-start | bytes 49160 | tf_op jit(solution)/shard_map/ppermute | solution.py:186

commit v2 on v0

--- a/solution.py
+++ b/solution.py
@@ -9,6 +9,7 @@
 COPY_GROUP = 8
 GROUP = 16
 NEAR = 4
+SWITCHED = (0, 2, 1, 3)
 SMEM = pl.BlockSpec(memory_space=pltpu.SMEM)
 VMEM = pl.BlockSpec(memory_space=pltpu.VMEM)
 
@@ -99,7 +100,8 @@
     for owner in range(virts):
         for a in range(NEAR):
             for b in range(far):
-                source = blocks[(owner ^ int((a > 0) != (b > 0))) * NEAR + a]
+                from_virt = owner ^ int((a > 0) != (b > 0))
+                source = blocks[from_virt * NEAR + (SWITCHED[a] if from_virt % 2 else a)]
                 place = pl.ds((a * far + b) * rows, rows)
                 for tile in range(in_local):
                     flat[tile, place, :] = source[b, tile * rows : (tile + 1) * rows, :]
@@ -156,14 +158,22 @@
     )(codes, halves, *blocks)
 
 
-def swap(value, pairs, virts, mask, virt_mask):
-    routes = [(a * virts + b, (a ^ mask) * virts + (b ^ virt_mask)) for a in range(pairs) for b in range(virts)]
+def near_mask(step, a, b):
+    return SWITCHED[step] if (a ^ a // 2 ^ b) % 2 else step
+
+
+def swap(value, pairs, virts, virt_mask, step=0, far=0):
+    routes = [
+        (a * virts + b, (a ^ far * NEAR ^ near_mask(step, a, b)) * virts + (b ^ virt_mask))
+        for a in range(pairs)
+        for b in range(virts)
+    ]
     return lax.ppermute(value, ("pair", "virt"), routes)
 
 
-def swap_sum(parts, pairs, virts, unit):
+def swap_sum(parts, pairs, virts, which):
     last = len(parts) - 1
-    received = [swap(parts[i], pairs, virts, i * unit, 1) for i in (0, last, *range(1, last))]
+    received = [swap(parts[i], pairs, virts, 1, **{which: i}) for i in (0, last, *range(1, last))]
     return sum(received[1:], received[0])
 
 
@@ -181,12 +191,12 @@
         mine,
         local_tiles,
     )
-    line = jnp.stack([own] + [swap(mine, pairs, virts, mask, 1) for mask in range(NEAR, pairs, NEAR)])
-    pieces = [line] + [swap(line, pairs, virts, mask, 1) for mask in range(1, NEAR)]
-    blocks = pieces + [swap(piece, pairs, virts, 0, mask) for mask in range(1, virts) for piece in pieces]
+    line = jnp.stack([own] + [swap(mine, pairs, virts, 1, far=mask) for mask in range(1, pairs // NEAR)])
+    pieces = [line] + [swap(line, pairs, virts, 1, step=step) for step in range(1, NEAR)]
+    blocks = pieces + [swap(piece, pairs, virts, mask) for mask in range(1, virts) for piece in pieces]
     partial_sums = local_terms(codes, blocks, halves, rows, local_tiles)
-    line_sums = swap_sum(partial_sums.reshape((NEAR, pairs // NEAR) + mine.shape), pairs, virts, 1)
-    summed = swap_sum(line_sums, pairs, virts, NEAR)
+    line_sums = swap_sum(partial_sums.reshape((NEAR, pairs // NEAR) + mine.shape), pairs, virts, "step")
+    summed = swap_sum(line_sums, pairs, virts, "far")
     return summed.reshape(local_tiles, rows, W).transpose(1, 0, 2).reshape(rows, columns)
 
 

time: 31.8 us -> 31.5 us (level)
  transfers between devices with their start and end apart: 18 -> 18, of which waited for: 9 -> 11; matrix products, arithmetic and copies ran while one was open for 0% -> 0% of each run, Pallas kernels for 4% -> 4%
where the time goes in v2:
time: 31.5 us; the launch traced here: 31.3 us
  starting transfers between devices  17.4 us (55%)
  waiting for transfers between devices  10.2 us (32%)
  Pallas kernels  2.3 us (7%)
  between operations  0.73 us (2%)
  other arithmetic  0.64 us (2%)
    ppermute x18, starting transfers between devices, swap(): return lax.ppermute(value, ('pair', 'virt'), routes)  17.4 us
    ppermute x18, waiting for transfers between devices, swap(): return lax.ppermute(value, ('pair', 'virt'), routes)  10.2 us
    pallas_call x1, Pallas kernels, prepare(): pl.pallas_call(kernel, out_shape=(jax.ShapeDtypeStruct((slots, W, 2 * W),...  1.24 us
    pallas_call x1, Pallas kernels, local_terms(): pl.pallas_call(kernel, out_shape=jax.ShapeDtypeStruct((NEAR * far, out_ti...  1.06 us
    add x2, other arithmetic, swap_sum(): return sum(received[1:], received[0])  0.63 us
  transfers between devices with their start and end apart: 18, of which 11 were waited for; matrix products, arithmetic and copies ran while one was open for 0% of the time, Pallas kernels for 4%

profile of v2, /device:TPU:0, one launch (start us, length us, event | category | flops | bytes accessed | tf_op | source)
XLA Modules:
  0.0 31.3 jit_solution(113263537829540207)
XLA Ops:
  0.0 4.5 %collective-permute-start.2 = (f32[32,128]{1,0:T(8,128)}, f32[32,128]{1,0:T(8,128)S(1)}, u32[]{:S(2)}, u32[]{:S(2)}) collective-permute-start(f32[32,128]{1,0:T(8,128)} %bitcast.27), channel_id=1, source_target_pairs={{0,25},{1,24},{2,27},{3,26},{4,29},{5,28},{6,31},{7,30},{8,17},{9,... | collective-permute-start | bytes 49160 | tf_op jit(solution)/shard_map/ppermute | solution.py:171
  4.5 0.0 collective-permute-start.1
  4.5 0.8 %collective-permute-start = (f32[32,128]{1,0:T(8,128)}, f32[32,128]{1,0:T(8,128)S(1)}, u32[]{:S(2)}, u32[]{:S(2)}) collective-permute-start(f32[32,128]{1,0:T(8,128)} %bitcast.29), channel_id=1, source_target_pairs={{0,9},{1,8},{2,11},{3,10},{4,13},{5,12},{6,15},{7,14},{8,1},{9,0},... | collective-permute-start | bytes 49160 | tf_op jit(solution)/shard_map/ppermute | solution.py:171
  6.0 1.2 %shard_map.55 = (bf16[32,128,256]{2,1,0:T(8,128)(2,1)S(1)}, s32[3,32]{1,0:T(4,128)S(1)}, f32[32,128]{1,0:T(8,128)S(1)}) custom-call(s32[1,1]{1,0:T(1,128)S(6)} %copy.8.refs_0_, s32[1,32]{1,0:T(1,128)} %bitcast.34, s32[1,32]{1,0:T(1,128)} %bitcast.35, f32[32,128,128]{2,1,0:T(8,128)} %bitcast.26, f32[32,128]{1,0:T(8,128)} %bitcast.30), custom_call_target="tpu_custom_call" | custom-call | flops 2097152 | bytes 4194304 | tf_op jit(solution)/shard_map/pallas_call | solution.py:68
  7.2 0.0 collective-permute-done.2
  7.2 1.6 %collective-permute-done.1 = f32[32,128]{1,0:T(8,128)S(1)} collective-permute-done((f32[32,128]{1,0:T(8,128)}, f32[32,128]{1,0:T(8,128)S(1)}, u32[]{:S(2)}, u32[]{:S(2)}) %collective-permute-start.1) | collective-permute-done | bytes 16416 | tf_op jit(solution)/shard_map/ppermute | solution.py:171
  8.9 0.0 collective-permute-done
  8.9 2.7 %collective-permute-start.5 = (f32[4,32,128]{2,1,0:T(8,128)S(1)}, f32[4,32,128]{2,1,0:T(8,128)S(1)}, u32[]{:S(2)}, u32[]{:S(2)}) collective-permute-start(f32[4,32,128]{2,1,0:T(8,128)S(1)} %pad_maximum_fusion.refs_2_), channel_id=1, source_target_pairs={{0,7},{1,6},{2,5},{3,4},{4,3},{5,2},{6,1},{7,0},{8,15},{9,14},{10,... | collective-permute-start | bytes 196616 | tf_op jit(solution)/shard_map/ppermute | solution.py:171
  11.6 0.1 collective-permute-start.4
  11.6 0.7 %collective-permute-start.3 = (f32[4,32,128]{2,1,0:T(8,128)S(1)}, f32[4,32,128]{2,1,0:T(8,128)S(1)}, u32[]{:S(2)}, u32[]{:S(2)}) collective-permute-start(f32[4,32,128]{2,1,0:T(8,128)S(1)} %pad_maximum_fusion.refs_2_), channel_id=1, source_target_pairs={{0,3},{1,4},{2,7},{3,0},{4,1},{5,6},{6,5},{7,2},{8,11},{9,12},{10,... | collective-permute-start | bytes 196616 | tf_op jit(solution)/shard_map/ppermute | solution.py:171
  12.3 0.0 collective-permute-start.6
  12.3 1.7 %collective-permute-done.5.refs_5_ = f32[4,32,128]{2,1,0:T(8,128)S(1)} collective-permute-done((f32[4,32,128]{2,1,0:T(8,128)S(1)}, f32[4,32,128]{2,1,0:T(8,128)S(1)}, u32[]{:S(2)}, u32[]{:S(2)}) %collective-permute-start.5) | collective-permute-done | bytes 65568 | tf_op jit(solution)/shard_map/ppermute | solution.py:171
  14.0 0.1 collective-permute-start.9
  14.1 1.2 %collective-permute-done.4.refs_4_ = f32[4,32,128]{2,1,0:T(8,128)S(1)} collective-permute-done((f32[4,32,128]{2,1,0:T(8,128)S(1)}, f32[4,32,128]{2,1,0:T(8,128)S(1)}, u32[]{:S(2)}, u32[]{:S(2)}) %collective-permute-start.4) | collective-permute-done | bytes 65568 | tf_op jit(solution)/shard_map/ppermute | solution.py:171
  15.3 0.8 %collective-permute-start.8 = (f32[4,32,128]{2,1,0:T(8,128)S(1)}, f32[4,32,128]{2,1,0:T(8,128)S(1)}, u32[]{:S(2)}, u32[]{:S(2)}) collective-permute-start(f32[4,32,128]{2,1,0:T(8,128)S(1)} %collective-permute-done.4.refs_4_), channel_id=1, source_target_pairs={{0,1},{1,0},{2,3},{3,2},{4,5},{5,4},{6,7},{7,6},{8,9},{9,8},{10,11... | collective-permute-start | bytes 196616 | tf_op jit(solution)/shard_map/ppermute | solution.py:171
  16.1 0.0 collective-permute-done.3.refs_3_
  16.1 0.0 collective-permute-start.7
  16.1 0.0 collective-permute-done.6.refs_6_
  16.1 0.0 collective-permute-done.9.refs_9_
  16.1 0.9 %collective-permute-done.8.refs_8_ = f32[4,32,128]{2,1,0:T(8,128)S(1)} collective-permute-done((f32[4,32,128]{2,1,0:T(8,128)S(1)}, f32[4,32,128]{2,1,0:T(8,128)S(1)}, u32[]{:S(2)}, u32[]{:S(2)}) %collective-permute-start.8) | collective-permute-done | bytes 65568 | tf_op jit(solution)/shard_map/ppermute | solution.py:171
  17.0 0.4 %collective-permute-done.7.refs_7_ = f32[4,32,128]{2,1,0:T(8,128)S(1)} collective-permute-done((f32[4,32,128]{2,1,0:T(8,128)S(1)}, f32[4,32,128]{2,1,0:T(8,128)S(1)}, u32[]{:S(2)}, u32[]{:S(2)}) %collective-permute-start.7) | collective-permute-done | bytes 65568 | tf_op jit(solution)/shard_map/ppermute | solution.py:171
  17.3 1.1 %shard_map.56 = f32[16,32,128]{2,1,0:T(8,128)S(1)} custom-call(s32[3,32]{1,0:T(4,128)S(1)} %get-tuple-element.8.refs_0_, bf16[32,128,256]{2,1,0:T(8,128)(2,1)S(1)} %get-tuple-element.9.refs_1_, f32[4,32,128]{2,1,0:T(8,128)S(1)} %pad_maximum_fusion.refs_2_, f32[4,32,128]{2,1,0:T(8,128)S(1)} %collective-permute-done.3.refs_3_, ...), custom_call_target="tpu_custom_call" | custom-call | tf_op jit(solution)/shard_map/pallas_call | solution.py:145
  18.4 1.3 %collective-permute-start.11 = (f32[4,32,128]{2,1,0:T(8,128)S(1)}, f32[4,32,128]{2,1,0:T(8,128)S(1)}, u32[]{:S(2)}, u32[]{:S(2)}) collective-permute-start(f32[4,32,128]{2,1,0:T(8,128)S(1)} %get-tuple-element.11), channel_id=1, source_target_pairs={{0,7},{1,6},{2,5},{3,4},{4,3},{5,2},{6,1},{7,0},{8,15},{9,14},{10,... | collective-permute-start | bytes 196616 | tf_op jit(solution)/shard_map/ppermute | solution.py:171
  19.8 1.0 %collective-permute-start.13 = (f32[4,32,128]{2,1,0:T(8,128)S(1)}, f32[4,32,128]{2,1,0:T(8,128)S(1)}, u32[]{:S(2)}, u32[]{:S(2)}) collective-permute-start(f32[4,32,128]{2,1,0:T(8,128)S(1)} %get-tuple-element.12), channel_id=1, source_target_pairs={{0,5},{1,2},{2,1},{3,6},{4,7},{5,0},{6,3},{7,4},{8,13},{9,10},{10,... | collective-permute-start | bytes 196616 | tf_op jit(solution)/shard_map/ppermute | solution.py:171
  20.8 0.7 %collective-permute-start.12 = (f32[4,32,128]{2,1,0:T(8,128)S(1)}, f32[4,32,128]{2,1,0:T(8,128)S(1)}, u32[]{:S(2)}, u32[]{:S(2)}) collective-permute-start(f32[4,32,128]{2,1,0:T(8,128)S(1)} %get-tuple-element.13), channel_id=1, source_target_pairs={{0,3},{1,4},{2,7},{3,0},{4,1},{5,6},{6,5},{7,2},{8,11},{9,12},{10,... | collective-permute-start | bytes 196616 | tf_op jit(solution)/shard_map/ppermute | solution.py:171
  21.5 0.4 %collective-permute-start.10 = (f32[4,32,128]{2,1,0:T(8,128)S(1)}, f32[4,32,128]{2,1,0:T(8,128)S(1)}, u32[]{:S(2)}, u32[]{:S(2)}) collective-permute-start(f32[4,32,128]{2,1,0:T(8,128)S(1)} %get-tuple-element.14), channel_id=1, source_target_pairs={{0,1},{1,0},{2,3},{3,2},{4,5},{5,4},{6,7},{7,6},{8,9},{9,8},{10,11... | collective-permute-start | bytes 196616 | tf_op jit(solution)/shard_map/ppermute | solution.py:171
  21.8 1.7 %collective-permute-done.11 = f32[4,32,128]{2,1,0:T(8,128)S(1)} collective-permute-done((f32[4,32,128]{2,1,0:T(8,128)S(1)}, f32[4,32,128]{2,1,0:T(8,128)S(1)}, u32[]{:S(2)}, u32[]{:S(2)}) %collective-permute-start.11) | collective-permute-done | bytes 65568 | tf_op jit(solution)/shard_map/ppermute | solution.py:171
  23.5 1.1 %collective-permute-done.13 = f32[4,32,128]{2,1,0:T(8,128)S(1)} collective-permute-done((f32[4,32,128]{2,1,0:T(8,128)S(1)}, f32[4,32,128]{2,1,0:T(8,128)S(1)}, u32[]{:S(2)}, u32[]{:S(2)}) %collective-permute-start.13) | collective-permute-done | bytes 65568 | tf_op jit(solution)/shard_map/ppermute | solution.py:171
  24.7 0.3 collective-permute-done.12
  25.0 0.0 collective-permute-done.10
  25.0 1.5 %collective-permute-start.15 = (f32[32,128]{1,0:T(8,128)S(1)}, f32[32,128]{1,0:T(8,128)S(1)}, u32[]{:S(2)}, u32[]{:S(2)}) collective-permute-start(f32[32,128]{1,0:T(8,128)S(1)} %get-tuple-element.15), channel_id=1, source_target_pairs={{0,25},{1,24},{2,27},{3,26},{4,29},{5,28},{6,31},{7,30},{8,17},{9,... | collective-permute-start | bytes 49160 | tf_op jit(solution)/shard_map/ppermute | solution.py:171
  26.5 0.6 %collective-permute-start.17 = (f32[32,128]{1,0:T(8,128)S(1)}, f32[32,128]{1,0:T(8,128)S(1)}, u32[]{:S(2)}, u32[]{:S(2)}) collective-permute-start(f32[32,128]{1,0:T(8,128)S(1)} %get-tuple-element.16), channel_id=1, source_target_pairs={{0,17},{1,16},{2,19},{3,18},{4,21},{5,20},{6,23},{7,22},{8,25},{9,... | collective-permute-start | bytes 49160 | tf_op jit(solution)/shard_map/ppermute | solution.py:171
  27.1 1.8 %collective-permute-start.16 = (f32[32,128]{1,0:T(8,128)S(1)}, f32[32,128]{1,0:T(8,128)S(1)}, u32[]{:S(2)}, u32[]{:S(2)}) collective-permute-start(f32[32,128]{1,0:T(8,128)S(1)} %get-tuple-element.17), channel_id=1, source_target_pairs={{0,9},{1,8},{2,11},{3,10},{4,13},{5,12},{6,15},{7,14},{8,1},{9,0},... | collective-permute-start | bytes 49160 | tf_op jit(solution)/shard_map/ppermute | solution.py:171
  28.9 0.4 %collective-permute-start.14 = (f32[32,128]{1,0:T(8,128)S(1)}, f32[32,128]{1,0:T(8,128)S(1)}, u32[]{:S(2)}, u32[]{:S(2)}) collective-permute-start(f32[32,128]{1,0:T(8,128)S(1)} %get-tuple-element.18), channel_id=1, source_target_pairs={{0,1},{1,0},{2,3},{3,2},{4,5},{5,4},{6,7},{7,6},{8,9},{9,8},{10,11... | collective-permute-start | bytes 49160 | tf_op jit(solution)/shard_map/ppermute | solution.py:171
  29.3 0.7 %collective-permute-done.15 = f32[32,128]{1,0:T(8,128)S(1)} collective-permute-done((f32[32,128]{1,0:T(8,128)S(1)}, f32[32,128]{1,0:T(8,128)S(1)}, u32[]{:S(2)}, u32[]{:S(2)}) %collective-permute-start.15) | collective-permute-done | bytes 16416 | tf_op jit(solution)/shard_map/ppermute | solution.py:171
  30.0 0.6 %collective-permute-done.17 = f32[32,128]{1,0:T(8,128)S(1)} collective-permute-done((f32[32,128]{1,0:T(8,128)S(1)}, f32[32,128]{1,0:T(8,128)S(1)}, u32[]{:S(2)}, u32[]{:S(2)}) %collective-permute-start.17) | collective-permute-done | bytes 16416 | tf_op jit(solution)/shard_map/ppermute | solution.py:171
  30.6 0.1 collective-permute-done.16
  30.7 0.0 collective-permute-done.14
  30.7 0.6 %add_add_fusion.1 = f32[32,128]{1,0:T(8,128)} fusion(f32[32,128]{1,0:T(8,128)S(1)} %collective-permute-done.17, f32[32,128]{1,0:T(8,128)S(1)} %collective-permute-done.16, f32[32,128]{1,0:T(8,128)S(1)} %collective-permute-done.14, f32[32,128]{1,0:T(8,128)S(1)} %collective-permute-done.15), kind=kLoop, calls=%fused_computation.6 | loop fusion | flops 12288 | bytes 81920 | tf_op jit(solution)/shard_map/add | solution.py:177
  (4 shorter events, 0.1 us)
Async XLA Ops:
  0.0 7.2 %collective-permute-start.2 = (f32[32,128]{1,0:T(8,128)}, f32[32,128]{1,0:T(8,128)S(1)}, u32[]{:S(2)}, u32[]{:S(2)}) collective-permute-start(f32[32,128]{1,0:T(8,128)} %bitcast.27), channel_id=1, source_target_pairs={{0,25},{1,24},{2,27},{3,26},{4,29},{5,28},{6,31},{7,30},{8,17},{9,... | collective-permute-start | bytes 49160 | tf_op jit(solution)/shard_map/ppermute | solution.py:171
  4.5 4.4 %collective-permute-start.1 = (f32[32,128]{1,0:T(8,128)}, f32[32,128]{1,0:T(8,128)S(1)}, u32[]{:S(2)}, u32[]{:S(2)}) collective-permute-start(f32[32,128]{1,0:T(8,128)} %bitcast.28), channel_id=1, source_target_pairs={{0,17},{1,16},{2,19},{3,18},{4,21},{5,20},{6,23},{7,22},{8,25},{9,... | collective-permute-start | bytes 49160 | tf_op jit(solution)/shard_map/ppermute | solution.py:171
  4.5 4.4 %collective-permute-start = (f32[32,128]{1,0:T(8,128)}, f32[32,128]{1,0:T(8,128)S(1)}, u32[]{:S(2)}, u32[]{:S(2)}) collective-permute-start(f32[32,128]{1,0:T(8,128)} %bitcast.29), channel_id=1, source_target_pairs={{0,9},{1,8},{2,11},{3,10},{4,13},{5,12},{6,15},{7,14},{8,1},{9,0},... | collective-permute-start | bytes 49160 | tf_op jit(solution)/shard_map/ppermute | solution.py:171
  8.9 5.1 %collective-permute-start.5 = (f32[4,32,128]{2,1,0:T(8,128)S(1)}, f32[4,32,128]{2,1,0:T(8,128)S(1)}, u32[]{:S(2)}, u32[]{:S(2)}) collective-permute-start(f32[4,32,128]{2,1,0:T(8,128)S(1)} %pad_maximum_fusion.refs_2_), channel_id=1, source_target_pairs={{0,7},{1,6},{2,5},{3,4},{4,3},{5,2},{6,1},{7,0},{8,15},{9,14},{10,... | collective-permute-start | bytes 196616 | tf_op jit(solution)/shard_map/ppermute | solution.py:171
  11.6 3.7 %collective-permute-start.4 = (f32[4,32,128]{2,1,0:T(8,128)S(1)}, f32[4,32,128]{2,1,0:T(8,128)S(1)}, u32[]{:S(2)}, u32[]{:S(2)}) collective-permute-start(f32[4,32,128]{2,1,0:T(8,128)S(1)} %pad_maximum_fusion.refs_2_), channel_id=1, source_target_pairs={{0,5},{1,2},{2,1},{3,6},{4,7},{5,0},{6,3},{7,4},{8,13},{9,10},{10,... | collective-permute-start | bytes 196616 | tf_op jit(solution)/shard_map/ppermute | solution.py:171
  11.6 4.4 %collective-permute-start.3 = (f32[4,32,128]{2,1,0:T(8,128)S(1)}, f32[4,32,128]{2,1,0:T(8,128)S(1)}, u32[]{:S(2)}, u32[]{:S(2)}) collective-permute-start(f32[4,32,128]{2,1,0:T(8,128)S(1)} %pad_maximum_fusion.refs_2_), channel_id=1, source_target_pairs={{0,3},{1,4},{2,7},{3,0},{4,1},{5,6},{6,5},{7,2},{8,11},{9,12},{10,... | collective-permute-start | bytes 196616 | tf_op jit(solution)/shard_map/ppermute | solution.py:171
  12.3 3.8 %collective-permute-start.6 = (f32[4,32,128]{2,1,0:T(8,128)S(1)}, f32[4,32,128]{2,1,0:T(8,128)S(1)}, u32[]{:S(2)}, u32[]{:S(2)}) collective-permute-start(f32[4,32,128]{2,1,0:T(8,128)S(1)} %pad_maximum_fusion.refs_2_), channel_id=1, source_target_pairs={{0,1},{1,0},{2,3},{3,2},{4,5},{5,4},{6,7},{7,6},{8,9},{9,8},{10,11... | collective-permute-start | bytes 196616 | tf_op jit(solution)/shard_map/ppermute | solution.py:171
  14.0 2.1 %collective-permute-start.9 = (f32[4,32,128]{2,1,0:T(8,128)S(1)}, f32[4,32,128]{2,1,0:T(8,128)S(1)}, u32[]{:S(2)}, u32[]{:S(2)}) collective-permute-start(f32[4,32,128]{2,1,0:T(8,128)S(1)} %collective-permute-done.5.refs_5_), channel_id=1, source_target_pairs={{0,1},{1,0},{2,3},{3,2},{4,5},{5,4},{6,7},{7,6},{8,9},{9,8},{10,11... | collective-permute-start | bytes 196616 | tf_op jit(solution)/shard_map/ppermute | solution.py:171
  15.3 1.7 %collective-permute-start.8 = (f32[4,32,128]{2,1,0:T(8,128)S(1)}, f32[4,32,128]{2,1,0:T(8,128)S(1)}, u32[]{:S(2)}, u32[]{:S(2)}) collective-permute-start(f32[4,32,128]{2,1,0:T(8,128)S(1)} %collective-permute-done.4.refs_4_), channel_id=1, source_target_pairs={{0,1},{1,0},{2,3},{3,2},{4,5},{5,4},{6,7},{7,6},{8,9},{9,8},{10,11... | collective-permute-start | bytes 196616 | tf_op jit(solution)/shard_map/ppermute | solution.py:171
  16.1 1.3 %collective-permute-start.7 = (f32[4,32,128]{2,1,0:T(8,128)S(1)}, f32[4,32,128]{2,1,0:T(8,128)S(1)}, u32[]{:S(2)}, u32[]{:S(2)}) collective-permute-start(f32[4,32,128]{2,1,0:T(8,128)S(1)} %collective-permute-done.3.refs_3_), channel_id=1, source_target_pairs={{0,1},{1,0},{2,3},{3,2},{4,5},{5,4},{6,7},{7,6},{8,9},{9,8},{10,11... | collective-permute-start | bytes 196616 | tf_op jit(solution)/shard_map/ppermute | solution.py:171
  18.4 5.1 %collective-permute-start.11 = (f32[4,32,128]{2,1,0:T(8,128)S(1)}, f32[4,32,128]{2,1,0:T(8,128)S(1)}, u32[]{:S(2)}, u32[]{:S(2)}) collective-permute-start(f32[4,32,128]{2,1,0:T(8,128)S(1)} %get-tuple-element.11), channel_id=1, source_target_pairs={{0,7},{1,6},{2,5},{3,4},{4,3},{5,2},{6,1},{7,0},{8,15},{9,14},{10,... | collective-permute-start | bytes 196616 | tf_op jit(solution)/shard_map/ppermute | solution.py:171
  19.8 4.9 %collective-permute-start.13 = (f32[4,32,128]{2,1,0:T(8,128)S(1)}, f32[4,32,128]{2,1,0:T(8,128)S(1)}, u32[]{:S(2)}, u32[]{:S(2)}) collective-permute-start(f32[4,32,128]{2,1,0:T(8,128)S(1)} %get-tuple-element.12), channel_id=1, source_target_pairs={{0,5},{1,2},{2,1},{3,6},{4,7},{5,0},{6,3},{7,4},{8,13},{9,10},{10,... | collective-permute-start | bytes 196616 | tf_op jit(solution)/shard_map/ppermute | solution.py:171
  20.8 4.2 %collective-permute-start.12 = (f32[4,32,128]{2,1,0:T(8,128)S(1)}, f32[4,32,128]{2,1,0:T(8,128)S(1)}, u32[]{:S(2)}, u32[]{:S(2)}) collective-permute-start(f32[4,32,128]{2,1,0:T(8,128)S(1)} %get-tuple-element.13), channel_id=1, source_target_pairs={{0,3},{1,4},{2,7},{3,0},{4,1},{5,6},{6,5},{7,2},{8,11},{9,12},{10,... | collective-permute-start | bytes 196616 | tf_op jit(solution)/shard_map/ppermute | solution.py:171
  21.5 3.5 %collective-permute-start.10 = (f32[4,32,128]{2,1,0:T(8,128)S(1)}, f32[4,32,128]{2,1,0:T(8,128)S(1)}, u32[]{:S(2)}, u32[]{:S(2)}) collective-permute-start(f32[4,32,128]{2,1,0:T(8,128)S(1)} %get-tuple-element.14), channel_id=1, source_target_pairs={{0,1},{1,0},{2,3},{3,2},{4,5},{5,4},{6,7},{7,6},{8,9},{9,8},{10,11... | collective-permute-start | bytes 196616 | tf_op jit(solution)/shard_map/ppermute | solution.py:171
  25.0 5.0 %collective-permute-start.15 = (f32[32,128]{1,0:T(8,128)S(1)}, f32[32,128]{1,0:T(8,128)S(1)}, u32[]{:S(2)}, u32[]{:S(2)}) collective-permute-start(f32[32,128]{1,0:T(8,128)S(1)} %get-tuple-element.15), channel_id=1, source_target_pairs={{0,25},{1,24},{2,27},{3,26},{4,29},{5,28},{6,31},{7,30},{8,17},{9,... | collective-permute-start | bytes 49160 | tf_op jit(solution)/shard_map/ppermute | solution.py:171
  26.5 4.1 %collective-permute-start.17 = (f32[32,128]{1,0:T(8,128)S(1)}, f32[32,128]{1,0:T(8,128)S(1)}, u32[]{:S(2)}, u32[]{:S(2)}) collective-permute-start(f32[32,128]{1,0:T(8,128)S(1)} %get-tuple-element.16), channel_id=1, source_target_pairs={{0,17},{1,16},{2,19},{3,18},{4,21},{5,20},{6,23},{7,22},{8,25},{9,... | collective-permute-start | bytes 49160 | tf_op jit(solution)/shard_map/ppermute | solution.py:171
  27.1 3.6 %collective-permute-start.16 = (f32[32,128]{1,0:T(8,128)S(1)}, f32[32,128]{1,0:T(8,128)S(1)}, u32[]{:S(2)}, u32[]{:S(2)}) collective-permute-start(f32[32,128]{1,0:T(8,128)S(1)} %get-tuple-element.17), channel_id=1, source_target_pairs={{0,9},{1,8},{2,11},{3,10},{4,13},{5,12},{6,15},{7,14},{8,1},{9,0},... | collective-permute-start | bytes 49160 | tf_op jit(solution)/shard_map/ppermute | solution.py:171
  28.9 1.8 %collective-permute-start.14 = (f32[32,128]{1,0:T(8,128)S(1)}, f32[32,128]{1,0:T(8,128)S(1)}, u32[]{:S(2)}, u32[]{:S(2)}) collective-permute-start(f32[32,128]{1,0:T(8,128)S(1)} %get-tuple-element.18), channel_id=1, source_target_pairs={{0,1},{1,0},{2,3},{3,2},{4,5},{5,4},{6,7},{7,6},{8,9},{9,8},{10,11... | collective-permute-start | bytes 49160 | tf_op jit(solution)/shard_map/ppermute | solution.py:171

commit v3 on v2

--- a/solution.py
+++ b/solution.py
@@ -85,8 +85,17 @@
     )(live, *operands)
 
 
+def weave(first, second):
+    half = first.shape[0] // 2
+    upper = lax.broadcasted_iota(jnp.int32, first.shape, 0) < half
+    return (
+        jnp.where(upper, first, pltpu.roll(second, half, 0)),
+        jnp.where(upper, pltpu.roll(first, half, 0), second),
+    )
+
+
 def ladder_kernel(virts, codes_here, halves, *refs):
-    blocks, (result, columns, flat, totals, codes, copied) = refs[: virts * NEAR], refs[virts * NEAR :]
+    blocks, (result, columns, totals, codes, copied) = refs[: virts * NEAR], refs[virts * NEAR :]
     fetch = pltpu.make_async_copy(codes_here, codes, copied)
     fetch.start()
     far = blocks[0].shape[0]
@@ -99,16 +108,20 @@
 
     for owner in range(virts):
         for a in range(NEAR):
+            sources = []
             for b in range(far):
                 from_virt = owner ^ int((a > 0) != (b > 0))
-                source = blocks[from_virt * NEAR + (SWITCHED[a] if from_virt % 2 else a)]
-                place = pl.ds((a * far + b) * rows, rows)
-                for tile in range(in_local):
-                    flat[tile, place, :] = source[b, tile * rows : (tile + 1) * rows, :]
-        for tile in range(in_local):
-            high, low = split(flat[tile])
-            columns[owner * in_local + tile, :total_rows, :] = high
-            columns[owner * in_local + tile, total_rows:, :] = low
+                sources.append(blocks[from_virt * NEAR + (SWITCHED[a] if from_virt % 2 else a)])
+            for b in range(0, far, 4):
+                first_row = (a * far + b) * rows
+                for tile in range(0, in_local, 2):
+                    part = slice(tile * rows, (tile + 2) * rows)
+                    four = [sources[b + at][b + at, part, :] for at in range(4)]
+                    for at, pieces in enumerate(zip(weave(*four[:2]), weave(*four[2:]))):
+                        high, low = split(jnp.concatenate(pieces, axis=0))
+                        column = owner * in_local + tile + at
+                        columns[column, first_row : first_row + 4 * rows, :] = high
+                        columns[column, total_rows + first_row : total_rows + first_row + 4 * rows, :] = low
 
     fetch.wait()
 
@@ -125,12 +138,12 @@
         return carry
 
     lax.fori_loop(0, (codes[2, 0] + GROUP - 1) // GROUP, one_group, 0)
-    def give(chunk, carry):
-        for tile in range(out_tiles):
-            result[chunk, tile * rows : (tile + 1) * rows, :] = totals[tile, pl.ds(chunk * rows, rows), :]
-        return carry
-
-    lax.fori_loop(0, chunk_count, give, 0, unroll=min(chunk_count, 16))
+    for chunk in range(0, chunk_count, 2):
+        part = slice(chunk * rows, (chunk + 2) * rows)
+        for tile in range(0, out_tiles, 2):
+            pieces = weave(totals[tile, part, :], totals[tile + 1, part, :])
+            for at, piece in enumerate(pieces):
+                result[chunk + at, tile * rows : (tile + 2) * rows, :] = piece
 
 
 def local_terms(codes, blocks, halves, rows, out_tiles):
@@ -149,7 +162,6 @@
         out_specs=VMEM,
         scratch_shapes=[
             pltpu.VMEM((virts * in_local, 2 * total_rows, W), jnp.bfloat16),
-            pltpu.VMEM((in_local, total_rows, W), jnp.float32),
             pltpu.VMEM((out_tiles + 1, total_rows, W), jnp.float32),
             pltpu.SMEM(codes.shape, jnp.int32),
             pltpu.SemaphoreType.DMA,
@@ -171,9 +183,14 @@
     return lax.ppermute(value, ("pair", "virt"), routes)
 
 
-def swap_sum(parts, pairs, virts, which):
-    last = len(parts) - 1
-    received = [swap(parts[i], pairs, virts, 1, **{which: i}) for i in (0, last, *range(1, last))]
+def far_order(far):
+    return [*range(far - 2), far - 1, far - 2]
+
+
+def swap_sum(parts, pairs, virts, which, marks):
+    last = len(marks) - 1
+    order = (0, last, *range(1, last))
+    received = [swap(parts[marks.index(mark)], pairs, virts, 1, **{which: mark}) for mark in order]
     return sum(received[1:], received[0])
 
 
@@ -191,12 +208,13 @@
         mine,
         local_tiles,
     )
-    line = jnp.stack([own] + [swap(mine, pairs, virts, 1, far=mask) for mask in range(1, pairs // NEAR)])
+    order = far_order(pairs // NEAR)
+    line = jnp.stack([own] + [swap(mine, pairs, virts, 1, far=mask) for mask in order[1:]])
     pieces = [line] + [swap(line, pairs, virts, 1, step=step) for step in range(1, NEAR)]
     blocks = pieces + [swap(piece, pairs, virts, mask) for mask in range(1, virts) for piece in pieces]
     partial_sums = local_terms(codes, blocks, halves, rows, local_tiles)
-    line_sums = swap_sum(partial_sums.reshape((NEAR, pairs // NEAR) + mine.shape), pairs, virts, "step")
-    summed = swap_sum(line_sums, pairs, virts, "far")
+    line_sums = swap_sum(partial_sums.reshape((NEAR, pairs // NEAR) + mine.shape), pairs, virts, "step", list(range(NEAR)))
+    summed = swap_sum(line_sums, pairs, virts, "far", order)
     return summed.reshape(local_tiles, rows, W).transpose(1, 0, 2).reshape(rows, columns)
 
 

time: 31.5 us -> 31.8 us (level)
  transfers between devices with their start and end apart: 18 -> 18, of which waited for: 11 -> 10; matrix products, arithmetic and copies ran while one was open for 0% -> 0% of each run, Pallas kernels for 4% -> 4%
where the time goes in v3:
time: 31.8 us; the launch traced here: 31.7 us
  starting transfers between devices  17.5 us (55%)
  waiting for transfers between devices  10.5 us (33%)
  Pallas kernels  2.27 us (7%)
  between operations  0.72 us (2%)
  other arithmetic  0.64 us (2%)
    ppermute x18, starting transfers between devices, swap(): return lax.ppermute(value, ('pair', 'virt'), routes)  17.5 us
    ppermute x18, waiting for transfers between devices, swap(): return lax.ppermute(value, ('pair', 'virt'), routes)  10.5 us
    pallas_call x1, Pallas kernels, prepare(): pl.pallas_call(kernel, out_shape=(jax.ShapeDtypeStruct((slots, W, 2 * W),...  1.24 us
    pallas_call x1, Pallas kernels, local_terms(): pl.pallas_call(kernel, out_shape=jax.ShapeDtypeStruct((NEAR * far, out_ti...  1.03 us
  transfers between devices with their start and end apart: 18, of which 10 were waited for; matrix products, arithmetic and copies ran while one was open for 0% of the time, Pallas kernels for 4%

profile of v3, /device:TPU:0, one launch (start us, length us, event | category | flops | bytes accessed | tf_op | source)
XLA Modules:
  0.0 31.7 jit_solution(8546335296629722900)
XLA Ops:
  0.0 3.5 %collective-permute-start.2 = (f32[32,128]{1,0:T(8,128)}, f32[32,128]{1,0:T(8,128)S(1)}, u32[]{:S(2)}, u32[]{:S(2)}) collective-permute-start(f32[32,128]{1,0:T(8,128)} %bitcast.27), channel_id=1, source_target_pairs={{0,17},{1,16},{2,19},{3,18},{4,21},{5,20},{6,23},{7,22},{8,25},{9,... | collective-permute-start | bytes 49160 | tf_op jit(solution)/shard_map/ppermute | solution.py:183
  3.5 1.6 %collective-permute-start.1 = (f32[32,128]{1,0:T(8,128)}, f32[32,128]{1,0:T(8,128)S(1)}, u32[]{:S(2)}, u32[]{:S(2)}) collective-permute-start(f32[32,128]{1,0:T(8,128)} %bitcast.28), channel_id=1, source_target_pairs={{0,25},{1,24},{2,27},{3,26},{4,29},{5,28},{6,31},{7,30},{8,17},{9,... | collective-permute-start | bytes 49160 | tf_op jit(solution)/shard_map/ppermute | solution.py:183
  5.1 0.2 collective-permute-start
  6.0 1.2 %shard_map.55 = (bf16[32,128,256]{2,1,0:T(8,128)(2,1)S(1)}, s32[3,32]{1,0:T(4,128)S(1)}, f32[32,128]{1,0:T(8,128)S(1)}) custom-call(s32[1,1]{1,0:T(1,128)S(6)} %copy.8.refs_0_, s32[1,32]{1,0:T(1,128)} %bitcast.34, s32[1,32]{1,0:T(1,128)} %bitcast.35, f32[32,128,128]{2,1,0:T(8,128)} %bitcast.26, f32[32,128]{1,0:T(8,128)} %bitcast.30), custom_call_target="tpu_custom_call" | custom-call | flops 2097152 | bytes 4194304 | tf_op jit(solution)/shard_map/pallas_call | solution.py:68
  7.2 0.0 collective-permute-done.2
  7.2 1.4 %collective-permute-done.1 = f32[32,128]{1,0:T(8,128)S(1)} collective-permute-done((f32[32,128]{1,0:T(8,128)}, f32[32,128]{1,0:T(8,128)S(1)}, u32[]{:S(2)}, u32[]{:S(2)}) %collective-permute-start.1) | collective-permute-done | bytes 16416 | tf_op jit(solution)/shard_map/ppermute | solution.py:183
  8.7 0.0 collective-permute-done
  8.7 2.8 %collective-permute-start.5 = (f32[4,32,128]{2,1,0:T(8,128)S(1)}, f32[4,32,128]{2,1,0:T(8,128)S(1)}, u32[]{:S(2)}, u32[]{:S(2)}) collective-permute-start(f32[4,32,128]{2,1,0:T(8,128)S(1)} %pad_maximum_fusion.refs_2_), channel_id=1, source_target_pairs={{0,7},{1,6},{2,5},{3,4},{4,3},{5,2},{6,1},{7,0},{8,15},{9,14},{10,... | collective-permute-start | bytes 196616 | tf_op jit(solution)/shard_map/ppermute | solution.py:183
  11.5 0.0 collective-permute-start.4
  11.5 0.8 %collective-permute-start.3 = (f32[4,32,128]{2,1,0:T(8,128)S(1)}, f32[4,32,128]{2,1,0:T(8,128)S(1)}, u32[]{:S(2)}, u32[]{:S(2)}) collective-permute-start(f32[4,32,128]{2,1,0:T(8,128)S(1)} %pad_maximum_fusion.refs_2_), channel_id=1, source_target_pairs={{0,3},{1,4},{2,7},{3,0},{4,1},{5,6},{6,5},{7,2},{8,11},{9,12},{10,... | collective-permute-start | bytes 196616 | tf_op jit(solution)/shard_map/ppermute | solution.py:183
  12.3 0.0 collective-permute-start.6
  12.3 1.7 %collective-permute-done.5.refs_5_ = f32[4,32,128]{2,1,0:T(8,128)S(1)} collective-permute-done((f32[4,32,128]{2,1,0:T(8,128)S(1)}, f32[4,32,128]{2,1,0:T(8,128)S(1)}, u32[]{:S(2)}, u32[]{:S(2)}) %collective-permute-start.5) | collective-permute-done | bytes 65568 | tf_op jit(solution)/shard_map/ppermute | solution.py:183
  14.0 0.1 collective-permute-start.9
  14.1 1.2 %collective-permute-done.4.refs_4_ = f32[4,32,128]{2,1,0:T(8,128)S(1)} collective-permute-done((f32[4,32,128]{2,1,0:T(8,128)S(1)}, f32[4,32,128]{2,1,0:T(8,128)S(1)}, u32[]{:S(2)}, u32[]{:S(2)}) %collective-permute-start.4) | collective-permute-done | bytes 65568 | tf_op jit(solution)/shard_map/ppermute | solution.py:183
  15.2 0.7 %collective-permute-start.8 = (f32[4,32,128]{2,1,0:T(8,128)S(1)}, f32[4,32,128]{2,1,0:T(8,128)S(1)}, u32[]{:S(2)}, u32[]{:S(2)}) collective-permute-start(f32[4,32,128]{2,1,0:T(8,128)S(1)} %collective-permute-done.4.refs_4_), channel_id=1, source_target_pairs={{0,1},{1,0},{2,3},{3,2},{4,5},{5,4},{6,7},{7,6},{8,9},{9,8},{10,11... | collective-permute-start | bytes 196616 | tf_op jit(solution)/shard_map/ppermute | solution.py:183
  16.0 0.0 collective-permute-done.3.refs_3_
  16.0 0.0 collective-permute-start.7
  16.0 0.0 collective-permute-done.6.refs_6_
  16.0 0.0 collective-permute-done.9.refs_9_
  16.0 0.9 %collective-permute-done.8.refs_8_ = f32[4,32,128]{2,1,0:T(8,128)S(1)} collective-permute-done((f32[4,32,128]{2,1,0:T(8,128)S(1)}, f32[4,32,128]{2,1,0:T(8,128)S(1)}, u32[]{:S(2)}, u32[]{:S(2)}) %collective-permute-start.8) | collective-permute-done | bytes 65568 | tf_op jit(solution)/shard_map/ppermute | solution.py:183
  16.9 0.4 %collective-permute-done.7.refs_7_ = f32[4,32,128]{2,1,0:T(8,128)S(1)} collective-permute-done((f32[4,32,128]{2,1,0:T(8,128)S(1)}, f32[4,32,128]{2,1,0:T(8,128)S(1)}, u32[]{:S(2)}, u32[]{:S(2)}) %collective-permute-start.7) | collective-permute-done | bytes 65568 | tf_op jit(solution)/shard_map/ppermute | solution.py:183
  17.2 1.0 %shard_map.56 = f32[16,32,128]{2,1,0:T(8,128)S(1)} custom-call(s32[3,32]{1,0:T(4,128)S(1)} %get-tuple-element.8.refs_0_, bf16[32,128,256]{2,1,0:T(8,128)(2,1)S(1)} %get-tuple-element.9.refs_1_, f32[4,32,128]{2,1,0:T(8,128)S(1)} %pad_maximum_fusion.refs_2_, f32[4,32,128]{2,1,0:T(8,128)S(1)} %collective-permute-done.3.refs_3_, ...), custom_call_target="tpu_custom_call" | custom-call | tf_op jit(solution)/shard_map/pallas_call | solution.py:158
  18.3 1.4 %collective-permute-start.11 = (f32[4,32,128]{2,1,0:T(8,128)S(1)}, f32[4,32,128]{2,1,0:T(8,128)S(1)}, u32[]{:S(2)}, u32[]{:S(2)}) collective-permute-start(f32[4,32,128]{2,1,0:T(8,128)S(1)} %get-tuple-element.11), channel_id=1, source_target_pairs={{0,7},{1,6},{2,5},{3,4},{4,3},{5,2},{6,1},{7,0},{8,15},{9,14},{10,... | collective-permute-start | bytes 196616 | tf_op jit(solution)/shard_map/ppermute | solution.py:183
  19.7 1.0 %collective-permute-start.13 = (f32[4,32,128]{2,1,0:T(8,128)S(1)}, f32[4,32,128]{2,1,0:T(8,128)S(1)}, u32[]{:S(2)}, u32[]{:S(2)}) collective-permute-start(f32[4,32,128]{2,1,0:T(8,128)S(1)} %get-tuple-element.12), channel_id=1, source_target_pairs={{0,5},{1,2},{2,1},{3,6},{4,7},{5,0},{6,3},{7,4},{8,13},{9,10},{10,... | collective-permute-start | bytes 196616 | tf_op jit(solution)/shard_map/ppermute | solution.py:183
  20.7 0.6 %collective-permute-start.12 = (f32[4,32,128]{2,1,0:T(8,128)S(1)}, f32[4,32,128]{2,1,0:T(8,128)S(1)}, u32[]{:S(2)}, u32[]{:S(2)}) collective-permute-start(f32[4,32,128]{2,1,0:T(8,128)S(1)} %get-tuple-element.13), channel_id=1, source_target_pairs={{0,3},{1,4},{2,7},{3,0},{4,1},{5,6},{6,5},{7,2},{8,11},{9,12},{10,... | collective-permute-start | bytes 196616 | tf_op jit(solution)/shard_map/ppermute | solution.py:183
  21.3 0.4 %collective-permute-start.10 = (f32[4,32,128]{2,1,0:T(8,128)S(1)}, f32[4,32,128]{2,1,0:T(8,128)S(1)}, u32[]{:S(2)}, u32[]{:S(2)}) collective-permute-start(f32[4,32,128]{2,1,0:T(8,128)S(1)} %get-tuple-element.14), channel_id=1, source_target_pairs={{0,1},{1,0},{2,3},{3,2},{4,5},{5,4},{6,7},{7,6},{8,9},{9,8},{10,11... | collective-permute-start | bytes 196616 | tf_op jit(solution)/shard_map/ppermute | solution.py:183
  21.7 1.7 %collective-permute-done.11 = f32[4,32,128]{2,1,0:T(8,128)S(1)} collective-permute-done((f32[4,32,128]{2,1,0:T(8,128)S(1)}, f32[4,32,128]{2,1,0:T(8,128)S(1)}, u32[]{:S(2)}, u32[]{:S(2)}) %collective-permute-start.11) | collective-permute-done | bytes 65568 | tf_op jit(solution)/shard_map/ppermute | solution.py:183
  23.4 1.1 %collective-permute-done.13 = f32[4,32,128]{2,1,0:T(8,128)S(1)} collective-permute-done((f32[4,32,128]{2,1,0:T(8,128)S(1)}, f32[4,32,128]{2,1,0:T(8,128)S(1)}, u32[]{:S(2)}, u32[]{:S(2)}) %collective-permute-start.13) | collective-permute-done | bytes 65568 | tf_op jit(solution)/shard_map/ppermute | solution.py:183
  24.4 0.5 %collective-permute-done.12 = f32[4,32,128]{2,1,0:T(8,128)S(1)} collective-permute-done((f32[4,32,128]{2,1,0:T(8,128)S(1)}, f32[4,32,128]{2,1,0:T(8,128)S(1)}, u32[]{:S(2)}, u32[]{:S(2)}) %collective-permute-start.12) | collective-permute-done | bytes 65568 | tf_op jit(solution)/shard_map/ppermute | solution.py:183
  24.9 0.0 collective-permute-done.10
  24.9 2.0 %collective-permute-start.15 = (f32[32,128]{1,0:T(8,128)S(1)}, f32[32,128]{1,0:T(8,128)S(1)}, u32[]{:S(2)}, u32[]{:S(2)}) collective-permute-start(f32[32,128]{1,0:T(8,128)S(1)} %get-tuple-element.15), channel_id=1, source_target_pairs={{0,25},{1,24},{2,27},{3,26},{4,29},{5,28},{6,31},{7,30},{8,17},{9,... | collective-permute-start | bytes 49160 | tf_op jit(solution)/shard_map/ppermute | solution.py:183
  27.0 0.0 collective-permute-start.17
  27.0 1.8 %collective-permute-start.16 = (f32[32,128]{1,0:T(8,128)S(1)}, f32[32,128]{1,0:T(8,128)S(1)}, u32[]{:S(2)}, u32[]{:S(2)}) collective-permute-start(f32[32,128]{1,0:T(8,128)S(1)} %get-tuple-element.17), channel_id=1, source_target_pairs={{0,9},{1,8},{2,11},{3,10},{4,13},{5,12},{6,15},{7,14},{8,1},{9,0},... | collective-permute-start | bytes 49160 | tf_op jit(solution)/shard_map/ppermute | solution.py:183
  28.8 0.4 %collective-permute-start.14 = (f32[32,128]{1,0:T(8,128)S(1)}, f32[32,128]{1,0:T(8,128)S(1)}, u32[]{:S(2)}, u32[]{:S(2)}) collective-permute-start(f32[32,128]{1,0:T(8,128)S(1)} %get-tuple-element.18), channel_id=1, source_target_pairs={{0,1},{1,0},{2,3},{3,2},{4,5},{5,4},{6,7},{7,6},{8,9},{9,8},{10,11... | collective-permute-start | bytes 49160 | tf_op jit(solution)/shard_map/ppermute | solution.py:183
  29.3 0.7 %collective-permute-done.15 = f32[32,128]{1,0:T(8,128)S(1)} collective-permute-done((f32[32,128]{1,0:T(8,128)S(1)}, f32[32,128]{1,0:T(8,128)S(1)}, u32[]{:S(2)}, u32[]{:S(2)}) %collective-permute-start.15) | collective-permute-done | bytes 16416 | tf_op jit(solution)/shard_map/ppermute | solution.py:183
  30.0 1.1 %collective-permute-done.17 = f32[32,128]{1,0:T(8,128)S(1)} collective-permute-done((f32[32,128]{1,0:T(8,128)S(1)}, f32[32,128]{1,0:T(8,128)S(1)}, u32[]{:S(2)}, u32[]{:S(2)}) %collective-permute-start.17) | collective-permute-done | bytes 16416 | tf_op jit(solution)/shard_map/ppermute | solution.py:183
  31.1 0.0 collective-permute-done.16
  31.1 0.0 collective-permute-done.14
  31.1 0.6 %add_add_fusion.1 = f32[32,128]{1,0:T(8,128)} fusion(f32[32,128]{1,0:T(8,128)S(1)} %collective-permute-done.17, f32[32,128]{1,0:T(8,128)S(1)} %collective-permute-done.16, f32[32,128]{1,0:T(8,128)S(1)} %collective-permute-done.14, f32[32,128]{1,0:T(8,128)S(1)} %collective-permute-done.15), kind=kLoop, calls=%fused_computation.6 | loop fusion | flops 12288 | bytes 81920 | tf_op jit(solution)/shard_map/add | solution.py:194
  (4 shorter events, 0.1 us)
Async XLA Ops:
  0.0 7.2 %collective-permute-start.2 = (f32[32,128]{1,0:T(8,128)}, f32[32,128]{1,0:T(8,128)S(1)}, u32[]{:S(2)}, u32[]{:S(2)}) collective-permute-start(f32[32,128]{1,0:T(8,128)} %bitcast.27), channel_id=1, source_target_pairs={{0,17},{1,16},{2,19},{3,18},{4,21},{5,20},{6,23},{7,22},{8,25},{9,... | collective-permute-start | bytes 49160 | tf_op jit(solution)/shard_map/ppermute | solution.py:183
  3.5 5.2 %collective-permute-start.1 = (f32[32,128]{1,0:T(8,128)}, f32[32,128]{1,0:T(8,128)S(1)}, u32[]{:S(2)}, u32[]{:S(2)}) collective-permute-start(f32[32,128]{1,0:T(8,128)} %bitcast.28), channel_id=1, source_target_pairs={{0,25},{1,24},{2,27},{3,26},{4,29},{5,28},{6,31},{7,30},{8,17},{9,... | collective-permute-start | bytes 49160 | tf_op jit(solution)/shard_map/ppermute | solution.py:183
  5.1 3.6 %collective-permute-start = (f32[32,128]{1,0:T(8,128)}, f32[32,128]{1,0:T(8,128)S(1)}, u32[]{:S(2)}, u32[]{:S(2)}) collective-permute-start(f32[32,128]{1,0:T(8,128)} %bitcast.29), channel_id=1, source_target_pairs={{0,9},{1,8},{2,11},{3,10},{4,13},{5,12},{6,15},{7,14},{8,1},{9,0},... | collective-permute-start | bytes 49160 | tf_op jit(solution)/shard_map/ppermute | solution.py:183
  8.7 5.3 %collective-permute-start.5 = (f32[4,32,128]{2,1,0:T(8,128)S(1)}, f32[4,32,128]{2,1,0:T(8,128)S(1)}, u32[]{:S(2)}, u32[]{:S(2)}) collective-permute-start(f32[4,32,128]{2,1,0:T(8,128)S(1)} %pad_maximum_fusion.refs_2_), channel_id=1, source_target_pairs={{0,7},{1,6},{2,5},{3,4},{4,3},{5,2},{6,1},{7,0},{8,15},{9,14},{10,... | collective-permute-start | bytes 196616 | tf_op jit(solution)/shard_map/ppermute | solution.py:183
  11.5 3.7 %collective-permute-start.4 = (f32[4,32,128]{2,1,0:T(8,128)S(1)}, f32[4,32,128]{2,1,0:T(8,128)S(1)}, u32[]{:S(2)}, u32[]{:S(2)}) collective-permute-start(f32[4,32,128]{2,1,0:T(8,128)S(1)} %pad_maximum_fusion.refs_2_), channel_id=1, source_target_pairs={{0,5},{1,2},{2,1},{3,6},{4,7},{5,0},{6,3},{7,4},{8,13},{9,10},{10,... | collective-permute-start | bytes 196616 | tf_op jit(solution)/shard_map/ppermute | solution.py:183
  11.5 4.4 %collective-permute-start.3 = (f32[4,32,128]{2,1,0:T(8,128)S(1)}, f32[4,32,128]{2,1,0:T(8,128)S(1)}, u32[]{:S(2)}, u32[]{:S(2)}) collective-permute-start(f32[4,32,128]{2,1,0:T(8,128)S(1)} %pad_maximum_fusion.refs_2_), channel_id=1, source_target_pairs={{0,3},{1,4},{2,7},{3,0},{4,1},{5,6},{6,5},{7,2},{8,11},{9,12},{10,... | collective-permute-start | bytes 196616 | tf_op jit(solution)/shard_map/ppermute | solution.py:183
  12.3 3.7 %collective-permute-start.6 = (f32[4,32,128]{2,1,0:T(8,128)S(1)}, f32[4,32,128]{2,1,0:T(8,128)S(1)}, u32[]{:S(2)}, u32[]{:S(2)}) collective-permute-start(f32[4,32,128]{2,1,0:T(8,128)S(1)} %pad_maximum_fusion.refs_2_), channel_id=1, source_target_pairs={{0,1},{1,0},{2,3},{3,2},{4,5},{5,4},{6,7},{7,6},{8,9},{9,8},{10,11... | collective-permute-start | bytes 196616 | tf_op jit(solution)/shard_map/ppermute | solution.py:183
  14.0 2.0 %collective-permute-start.9 = (f32[4,32,128]{2,1,0:T(8,128)S(1)}, f32[4,32,128]{2,1,0:T(8,128)S(1)}, u32[]{:S(2)}, u32[]{:S(2)}) collective-permute-start(f32[4,32,128]{2,1,0:T(8,128)S(1)} %collective-permute-done.5.refs_5_), channel_id=1, source_target_pairs={{0,1},{1,0},{2,3},{3,2},{4,5},{5,4},{6,7},{7,6},{8,9},{9,8},{10,11... | collective-permute-start | bytes 196616 | tf_op jit(solution)/shard_map/ppermute | solution.py:183
  15.2 1.6 %collective-permute-start.8 = (f32[4,32,128]{2,1,0:T(8,128)S(1)}, f32[4,32,128]{2,1,0:T(8,128)S(1)}, u32[]{:S(2)}, u32[]{:S(2)}) collective-permute-start(f32[4,32,128]{2,1,0:T(8,128)S(1)} %collective-permute-done.4.refs_4_), channel_id=1, source_target_pairs={{0,1},{1,0},{2,3},{3,2},{4,5},{5,4},{6,7},{7,6},{8,9},{9,8},{10,11... | collective-permute-start | bytes 196616 | tf_op jit(solution)/shard_map/ppermute | solution.py:183
  16.0 1.3 %collective-permute-start.7 = (f32[4,32,128]{2,1,0:T(8,128)S(1)}, f32[4,32,128]{2,1,0:T(8,128)S(1)}, u32[]{:S(2)}, u32[]{:S(2)}) collective-permute-start(f32[4,32,128]{2,1,0:T(8,128)S(1)} %collective-permute-done.3.refs_3_), channel_id=1, source_target_pairs={{0,1},{1,0},{2,3},{3,2},{4,5},{5,4},{6,7},{7,6},{8,9},{9,8},{10,11... | collective-permute-start | bytes 196616 | tf_op jit(solution)/shard_map/ppermute | solution.py:183
  18.3 5.1 %collective-permute-start.11 = (f32[4,32,128]{2,1,0:T(8,128)S(1)}, f32[4,32,128]{2,1,0:T(8,128)S(1)}, u32[]{:S(2)}, u32[]{:S(2)}) collective-permute-start(f32[4,32,128]{2,1,0:T(8,128)S(1)} %get-tuple-element.11), channel_id=1, source_target_pairs={{0,7},{1,6},{2,5},{3,4},{4,3},{5,2},{6,1},{7,0},{8,15},{9,14},{10,... | collective-permute-start | bytes 196616 | tf_op jit(solution)/shard_map/ppermute | solution.py:183
  19.7 4.7 %collective-permute-start.13 = (f32[4,32,128]{2,1,0:T(8,128)S(1)}, f32[4,32,128]{2,1,0:T(8,128)S(1)}, u32[]{:S(2)}, u32[]{:S(2)}) collective-permute-start(f32[4,32,128]{2,1,0:T(8,128)S(1)} %get-tuple-element.12), channel_id=1, source_target_pairs={{0,5},{1,2},{2,1},{3,6},{4,7},{5,0},{6,3},{7,4},{8,13},{9,10},{10,... | collective-permute-start | bytes 196616 | tf_op jit(solution)/shard_map/ppermute | solution.py:183
  20.7 4.2 %collective-permute-start.12 = (f32[4,32,128]{2,1,0:T(8,128)S(1)}, f32[4,32,128]{2,1,0:T(8,128)S(1)}, u32[]{:S(2)}, u32[]{:S(2)}) collective-permute-start(f32[4,32,128]{2,1,0:T(8,128)S(1)} %get-tuple-element.13), channel_id=1, source_target_pairs={{0,3},{1,4},{2,7},{3,0},{4,1},{5,6},{6,5},{7,2},{8,11},{9,12},{10,... | collective-permute-start | bytes 196616 | tf_op jit(solution)/shard_map/ppermute | solution.py:183
  21.3 3.6 %collective-permute-start.10 = (f32[4,32,128]{2,1,0:T(8,128)S(1)}, f32[4,32,128]{2,1,0:T(8,128)S(1)}, u32[]{:S(2)}, u32[]{:S(2)}) collective-permute-start(f32[4,32,128]{2,1,0:T(8,128)S(1)} %get-tuple-element.14), channel_id=1, source_target_pairs={{0,1},{1,0},{2,3},{3,2},{4,5},{5,4},{6,7},{7,6},{8,9},{9,8},{10,11... | collective-permute-start | bytes 196616 | tf_op jit(solution)/shard_map/ppermute | solution.py:183
  24.9 5.0 %collective-permute-start.15 = (f32[32,128]{1,0:T(8,128)S(1)}, f32[32,128]{1,0:T(8,128)S(1)}, u32[]{:S(2)}, u32[]{:S(2)}) collective-permute-start(f32[32,128]{1,0:T(8,128)S(1)} %get-tuple-element.15), channel_id=1, source_target_pairs={{0,25},{1,24},{2,27},{3,26},{4,29},{5,28},{6,31},{7,30},{8,17},{9,... | collective-permute-start | bytes 49160 | tf_op jit(solution)/shard_map/ppermute | solution.py:183
  27.0 4.1 %collective-permute-start.17 = (f32[32,128]{1,0:T(8,128)S(1)}, f32[32,128]{1,0:T(8,128)S(1)}, u32[]{:S(2)}, u32[]{:S(2)}) collective-permute-start(f32[32,128]{1,0:T(8,128)S(1)} %get-tuple-element.16), channel_id=1, source_target_pairs={{0,17},{1,16},{2,19},{3,18},{4,21},{5,20},{6,23},{7,22},{8,25},{9,... | collective-permute-start | bytes 49160 | tf_op jit(solution)/shard_map/ppermute | solution.py:183
  27.0 4.1 %collective-permute-start.16 = (f32[32,128]{1,0:T(8,128)S(1)}, f32[32,128]{1,0:T(8,128)S(1)}, u32[]{:S(2)}, u32[]{:S(2)}) collective-permute-start(f32[32,128]{1,0:T(8,128)S(1)} %get-tuple-element.17), channel_id=1, source_target_pairs={{0,9},{1,8},{2,11},{3,10},{4,13},{5,12},{6,15},{7,14},{8,1},{9,0},... | collective-permute-start | bytes 49160 | tf_op jit(solution)/shard_map/ppermute | solution.py:183
  28.8 2.2 %collective-permute-start.14 = (f32[32,128]{1,0:T(8,128)S(1)}, f32[32,128]{1,0:T(8,128)S(1)}, u32[]{:S(2)}, u32[]{:S(2)}) collective-permute-start(f32[32,128]{1,0:T(8,128)S(1)} %get-tuple-element.18), channel_id=1, source_target_pairs={{0,1},{1,0},{2,3},{3,2},{4,5},{5,4},{6,7},{7,6},{8,9},{9,8},{10,11... | collective-permute-start | bytes 49160 | tf_op jit(solution)/shard_map/ppermute | solution.py:183

commit v4 on v3

v4 whole, which is shorter than its diff:
```python
import jax
import jax.numpy as jnp
from jax import lax
from jax.experimental import pallas as pl
from jax.experimental.pallas import tpu as pltpu
from jax.sharding import PartitionSpec as P

W = 128
COPY_GROUP = 8
GROUP = 8
NEAR = 4
SWITCHED = (0, 2, 1, 3)
SMEM = pl.BlockSpec(memory_space=pltpu.SMEM)
VMEM = pl.BlockSpec(memory_space=pltpu.VMEM)


def split(value):
    high = value.astype(jnp.bfloat16)
    low = (value - high.astype(jnp.float32)).astype(jnp.bfloat16)
    return high, low


def slot_list(chosen, rows):
    slots = chosen.shape[1]
    shape = (slots, slots)
    down, across = lax.broadcasted_iota(jnp.int32, shape, 0), lax.broadcasted_iota(jnp.int32, shape, 1)

    def turned(row):
        return jnp.sum(jnp.where(down == across, jnp.broadcast_to(row, shape), 0.0), axis=1, keepdims=True)

    ahead = jnp.sum(jnp.where(across < down, jnp.broadcast_to(chosen, shape), 0.0), axis=1, keepdims=True)
    here = (ahead.astype(jnp.int32) == across) & (turned(chosen) > 0.5)
    return [jnp.sum(jnp.where(here, turned(row), 0.0), axis=0, keepdims=True) for row in rows]


def tile_kernel(out_tiles, live, ins, outs, tiles, halves, codes, held, index_rows, arrived, singles):
    others = [pltpu.make_async_copy(rows, index_rows.at[at], singles.at[at]) for at, rows in enumerate((ins, outs))]
    for copy in others:
        copy.start()
    count = live[0, 0]
    groups = (count + COPY_GROUP - 1) // COPY_GROUP

    def tile_copy(index):
        part = pl.ds(index * COPY_GROUP, COPY_GROUP)
        return pltpu.make_async_copy(tiles.at[part], held.at[part], arrived.at[index])

    def begin(index, carry):
        tile_copy(index).start()
        return carry

    lax.fori_loop(0, groups, begin, 0)
    for copy in others:
        copy.wait()
    slots = lax.broadcasted_iota(jnp.int32, ins.shape, 1)
    tile_in = index_rows[0]
    owner = lax.bitwise_xor(lax.div(tile_in, out_tiles), lax.axis_index("virt"))
    local = lax.rem(tile_in, out_tiles)
    place = lax.rem(index_rows[1], out_tiles)
    for base, is_own in ((0, True), (4, False)):
        chosen = jnp.where((slots < count) & ((owner == 0) == is_own), 1.0, 0.0)
        column = local if is_own else local + (owner - 1) * out_tiles
        rows = [value.astype(jnp.float32) for value in (slots, column, place)]
        slot_row, column_row, place_row = [row.astype(jnp.int32) for row in slot_list(chosen, rows)]
        number = jnp.broadcast_to(jnp.sum(chosen, axis=1, keepdims=True), ins.shape).astype(jnp.int32)
        codes[base : base + 1, :] = slot_row
        codes[base + 1 : base + 2, :] = column_row
        codes[base + 2 : base + 3, :] = jnp.where(slots < number, place_row, out_tiles)
        codes[base + 3 : base + 4, :] = number

    def one_group(index, carry):
        tile_copy(index).wait()
        for step in range(COPY_GROUP):
            slot = index * COPY_GROUP + step
            high, low = split(held[slot])
            halves[slot, :, :W] = high
            halves[slot, :, W:] = low
        return carry

    lax.fori_loop(0, groups, one_group, 0)


def prepare(tiles, ins, outs, live, out_tiles):
    slots = tiles.shape[0]

    def kernel(*refs):
        tile_kernel(out_tiles, *refs)

    operands = [pltpu.with_memory_space_constraint(value, pltpu.HBM) for value in (ins, outs, tiles)]
    return pl.pallas_call(
        kernel,
        out_shape=(
            jax.ShapeDtypeStruct((slots, W, 2 * W), jnp.bfloat16),
            jax.ShapeDtypeStruct((8, slots), jnp.int32),
        ),
        in_specs=[SMEM] + [pl.BlockSpec(memory_space=pltpu.HBM)] * 3,
        out_specs=(VMEM, VMEM),
        scratch_shapes=[
            pltpu.VMEM((slots, W, W), jnp.float32),
            pltpu.VMEM((2, 1, slots), jnp.int32),
            pltpu.SemaphoreType.DMA((slots // COPY_GROUP,)),
            pltpu.SemaphoreType.DMA((2,)),
        ],
        compiler_params=pltpu.CompilerParams(vmem_limit_bytes=32 * 1024 * 1024),
        cost_estimate=pl.CostEstimate(flops=4 * slots * W * W, bytes_accessed=8 * slots * W * W, transcendentals=0),
    )(live, *operands)


def weave(first, second):
    half = first.shape[0] // 2
    upper = lax.broadcasted_iota(jnp.int32, first.shape, 0) < half
    return (
        jnp.where(upper, first, pltpu.roll(second, half, 0)),
        jnp.where(upper, pltpu.roll(first, half, 0), second),
    )


def fill_columns(columns, first_column, lines, rows):
    far, chunk_rows, _ = lines[0].shape
    total_rows = len(lines) * far * rows
    for a, line in enumerate(lines):
        for b in range(0, far, 4):
            first_row = (a * far + b) * rows
            for tile in range(0, chunk_rows // rows, 2):
                part = slice(tile * rows, (tile + 2) * rows)
                four = [line[b + at, part, :] for at in range(4)]
                for at, pieces in enumerate(zip(weave(*four[:2]), weave(*four[2:]))):
                    high, low = split(jnp.concatenate(pieces, axis=0))
                    column = first_column + tile + at
                    columns[column, first_row : first_row + 4 * rows, :] = high
                    columns[column, total_rows + first_row : total_rows + first_row + 4 * rows, :] = low


def add_products(base, codes, columns, halves, totals):
    total_rows = totals.shape[1]

    def one_group(index, carry):
        first = index * GROUP
        products = []
        for step in range(GROUP):
            slot, column = codes[base, first + step], codes[base + 1, first + step]
            got = jnp.dot(columns[column], halves[slot], preferred_element_type=jnp.float32)
            upper, lower = got[:total_rows], got[total_rows:]
            products.append((upper[:, :W] + lower[:, :W]) + (upper[:, W:] + lower[:, W:]))
        for step in range(GROUP):
            place = codes[base + 2, first + step]
            totals[place] = totals[place] + products[step]
        return carry

    lax.fori_loop(0, (codes[base + 3, 0] + GROUP - 1) // GROUP, one_group, 0)


def own_kernel(rows, codes_here, halves, *refs):
    lines, (totals, columns, codes, copied) = refs[:NEAR], refs[NEAR:]
    fetch = pltpu.make_async_copy(codes_here, codes, copied)
    fetch.start()
    totals[...] = jnp.zeros_like(totals)
    fill_columns(columns, 0, lines, rows)
    fetch.wait()
    add_products(0, codes, columns, halves, totals)


def rest_kernel(rows, codes_here, halves, own_totals, *refs):
    lines, (result, columns, totals, codes, copied) = refs[:-5], refs[-5:]
    fetch = pltpu.make_async_copy(codes_here, codes, copied)
    fetch.start()
    totals[...] = own_totals[...]
    in_local = lines[0].shape[1] // rows
    for owner in range(len(lines) // NEAR):
        fill_columns(columns, owner * in_local, lines[owner * NEAR : (owner + 1) * NEAR], rows)
    fetch.wait()
    add_products(4, codes, columns, halves, totals)
    for chunk in range(0, result.shape[0], 2):
        part = slice(chunk * rows, (chunk + 2) * rows)
        for tile in range(0, result.shape[1] // rows, 2):
            pieces = weave(totals[tile, part, :], totals[tile + 1, part, :])
            for at, piece in enumerate(pieces):
                result[chunk + at, tile * rows : (tile + 2) * rows, :] = piece


def local_terms(codes, owners, halves, rows, out_tiles):
    far, chunk_rows, _ = owners[0][0].shape
    total_rows = NEAR * far * rows
    in_local = chunk_rows // rows
    totals = jax.ShapeDtypeStruct((out_tiles + 1, total_rows, W), jnp.float32)

    def scratch(count):
        return [
            pltpu.VMEM((count * in_local, 2 * total_rows, W), jnp.bfloat16),
            pltpu.SMEM(codes.shape, jnp.int32),
            pltpu.SemaphoreType.DMA,
        ]

    def own(*refs):
        own_kernel(rows, *refs)

    def rest(*refs):
        rest_kernel(rows, *refs)

    settings = dict(
        compiler_params=pltpu.CompilerParams(vmem_limit_bytes=32 * 1024 * 1024),
        cost_estimate=pl.CostEstimate(flops=1 << 28, bytes_accessed=1 << 21, transcendentals=0),
    )
    own_totals = pl.pallas_call(
        own, out_shape=totals, in_specs=[VMEM] * (2 + NEAR), out_specs=VMEM, scratch_shapes=scratch(1), **settings
    )(codes, halves, *owners[0])
    others = [line for lines in owners[1:] for line in lines]
    columns, *others_scratch = scratch(len(owners) - 1)
    return pl.pallas_call(
        rest,
        out_shape=jax.ShapeDtypeStruct((NEAR * far, out_tiles * rows, W), jnp.float32),
        in_specs=[VMEM] * (3 + len(others)),
        out_specs=VMEM,
        scratch_shapes=[columns, pltpu.VMEM(totals.shape, totals.dtype)] + others_scratch,
        **settings,
    )(codes, halves, own_totals, *others)


def near_mask(step, a, b):
    return SWITCHED[step] if (a ^ a // 2 ^ b) % 2 else step


def swap(value, pairs, virts, virt_mask, step=0, far=0):
    routes = [
        (a * virts + b, (a ^ far * NEAR ^ near_mask(step, a, b)) * virts + (b ^ virt_mask))
        for a in range(pairs)
        for b in range(virts)
    ]
    return lax.ppermute(value, ("pair", "virt"), routes)


def far_order(far):
    return [*range(far - 2), far - 1, far - 2]


def swap_sum(parts, pairs, virts, which, marks):
    last = len(marks) - 1
    order = (0, last, *range(1, last))
    received = [swap(parts[marks.index(mark)], pairs, virts, 1, **{which: mark}) for mark in order]
    return sum(received[1:], received[0])


def shards(t2_amplitudes, integral_tiles, out_tiles, in_tiles, tile_counts):
    rows, columns = t2_amplitudes.shape
    local_tiles = columns // W
    slots = integral_tiles.shape[2]
    pairs, virts = lax.axis_size("pair"), lax.axis_size("virt")
    mine = t2_amplitudes.reshape(rows, local_tiles, W).transpose(1, 0, 2).reshape(local_tiles * rows, W)
    neighbour = swap(mine, pairs, virts, 1)
    halves, codes = prepare(
        integral_tiles.reshape(slots, W, W),
        in_tiles.reshape(1, slots),
        out_tiles.reshape(1, slots),
        tile_counts,
        local_tiles,
    )
    neighbour, codes = lax.optimization_barrier((neighbour, codes))
    order = far_order(pairs // NEAR)
    line = jnp.stack([neighbour] + [swap(mine, pairs, virts, 1, far=mask) for mask in order[1:]])
    pieces = [line] + [swap(line, pairs, virts, 1, step=step) for step in range(1, NEAR)]
    blocks = [pieces] + [[swap(piece, pairs, virts, mask) for piece in pieces] for mask in range(1, virts)]
    owners = [
        [blocks[mask ^ 1][0]] + [blocks[mask][SWITCHED[a] if mask % 2 else a] for a in range(1, NEAR)]
        for mask in range(virts)
    ]
    partial_sums = local_terms(codes, owners, halves, rows, local_tiles)
    line_sums = swap_sum(partial_sums.reshape((NEAR, pairs // NEAR) + mine.shape), pairs, virts, "step", list(range(NEAR)))
    summed = swap_sum(line_sums, pairs, virts, "far", order)
    return summed.reshape(local_tiles, rows, W).transpose(1, 0, 2).reshape(rows, columns)


def solution(mesh):
    return jax.shard_map(
        shards,
        mesh=mesh,
        in_specs=(
            P("pair", "virt"),
            P("pair", "virt", None, None, None),
            P("pair", "virt", None),
            P("pair", "virt", None),
            P("pair", "virt"),
        ),
        out_specs=P("pair", "virt"),
        check_vma=False,
    )
```

time: 31.8 us -> 31.9 us (level)
  waiting for transfers between devices: 10.5 us -> 8.05 us
  Pallas kernels: 2.27 us -> 4.46 us
    ppermute x18 -> x19, waiting for transfers between devices: 10.5 us -> 8.05 us  [swap(): return lax.ppermute(value, ('pair', 'virt'), routes)]
    pallas_call x1 -> x2, Pallas kernels: 1.03 us -> 2.77 us  [the longest x1 1.52 us: local_terms(): pl.pallas_call(own, out_shape=totals, in_specs=[VMEM] * (2 + NEAR), out_s...]
    pallas_call x1, Pallas kernels: 1.24 us -> 1.69 us  [prepare(): pl.pallas_call(kernel, out_shape=(jax.ShapeDtypeStruct((slots, W, 2 * W),...]
    ppermute x18 -> x19, starting transfers between devices: 17.5 us -> 17.8 us  [swap(): return lax.ppermute(value, ('pair', 'virt'), routes)]
  transfers between devices with their start and end apart: 18 -> 19, of which waited for: 10 -> 8; matrix products, arithmetic and copies ran while one was open for 0% -> 0% of each run, Pallas kernels for 4% -> 10%
where the time goes in v4:
time: 31.9 us; the launch traced here: 31.7 us
  starting transfers between devices  17.8 us (56%)
  waiting for transfers between devices  8.05 us (25%)
  Pallas kernels  4.46 us (14%)
  between operations  0.76 us (2%)
  other arithmetic  0.64 us (2%)
    ppermute x19, starting transfers between devices, swap(): return lax.ppermute(value, ('pair', 'virt'), routes)  17.8 us
    ppermute x19, waiting for transfers between devices, swap(): return lax.ppermute(value, ('pair', 'virt'), routes)  8.05 us
    pallas_call x1, Pallas kernels, prepare(): pl.pallas_call(kernel, out_shape=(jax.ShapeDtypeStruct((slots, W, 2 * W),...  1.69 us
    pallas_call x1, Pallas kernels, local_terms(): pl.pallas_call(own, out_shape=totals, in_specs=[VMEM] * (2 + NEAR), out_s...  1.52 us
    pallas_call x1, Pallas kernels, local_terms(): pl.pallas_call(rest, out_shape=jax.ShapeDtypeStruct((NEAR * far, out_tile...  1.25 us
  transfers between devices with their start and end apart: 19, of which 8 were waited for; matrix products, arithmetic and copies ran while one was open for 0% of the time, Pallas kernels for 10%

profile of v4, /device:TPU:0, one launch (start us, length us, event | category | flops | bytes accessed | tf_op | source)
XLA Modules:
  0.0 31.7 jit_solution(7503256543904476222)
XLA Ops:
  0.0 0.5 %collective-permute-start = (f32[32,128]{1,0:T(8,128)}, f32[32,128]{1,0:T(8,128)S(1)}, u32[]{:S(2)}, u32[]{:S(2)}) collective-permute-start(f32[32,128]{1,0:T(8,128)} %bitcast.32), channel_id=1, source_target_pairs={{0,1},{1,0},{2,3},{3,2},{4,5},{5,4},{6,7},{7,6},{8,9},{9,8},{10,11... | collective-permute-start | bytes 49160 | tf_op jit(solution)/shard_map/ppermute | solution.py:228
  0.5 3.7 %collective-permute-start.3 = (f32[32,128]{1,0:T(8,128)}, f32[32,128]{1,0:T(8,128)S(1)}, u32[]{:S(2)}, u32[]{:S(2)}) collective-permute-start(f32[32,128]{1,0:T(8,128)} %bitcast.33), channel_id=1, source_target_pairs={{0,17},{1,16},{2,19},{3,18},{4,21},{5,20},{6,23},{7,22},{8,25},{9,... | collective-permute-start | bytes 49160 | tf_op jit(solution)/shard_map/ppermute | solution.py:228
  4.2 1.0 %collective-permute-start.2 = (f32[32,128]{1,0:T(8,128)}, f32[32,128]{1,0:T(8,128)S(1)}, u32[]{:S(2)}, u32[]{:S(2)}) collective-permute-start(f32[32,128]{1,0:T(8,128)} %bitcast.34), channel_id=1, source_target_pairs={{0,25},{1,24},{2,27},{3,26},{4,29},{5,28},{6,31},{7,30},{8,17},{9,... | collective-permute-start | bytes 49160 | tf_op jit(solution)/shard_map/ppermute | solution.py:228
  5.2 0.2 collective-permute-start.1
  6.0 1.7 %shard_map.55 = (bf16[32,128,256]{2,1,0:T(8,128)(2,1)S(1)}, s32[8,32]{1,0:T(8,128)S(1)}) custom-call(s32[1,1]{1,0:T(1,128)S(6)} %copy.8.refs_0_, s32[1,32]{1,0:T(1,128)} %bitcast.30, s32[1,32]{1,0:T(1,128)} %bitcast.31, f32[32,128,128]{2,1,0:T(8,128)} %bitcast.25), custom_call_target="tpu_custom_call" | custom-call | flops 2097152 | bytes 4194304 | tf_op jit(solution)/shard_map/pallas_call | solution.py:89
  7.7 0.0 collective-permute-done
  7.7 0.0 collective-permute-done.3
  7.7 1.6 %collective-permute-done.2 = f32[32,128]{1,0:T(8,128)S(1)} collective-permute-done((f32[32,128]{1,0:T(8,128)}, f32[32,128]{1,0:T(8,128)S(1)}, u32[]{:S(2)}, u32[]{:S(2)}) %collective-permute-start.2) | collective-permute-done | bytes 16416 | tf_op jit(solution)/shard_map/ppermute | solution.py:228
  9.3 0.0 collective-permute-done.1
  9.4 2.2 %collective-permute-start.7 = (f32[4,32,128]{2,1,0:T(8,128)S(1)}, f32[4,32,128]{2,1,0:T(8,128)S(1)}, u32[]{:S(2)}, u32[]{:S(2)}) collective-permute-start(f32[4,32,128]{2,1,0:T(8,128)S(1)} %pad_maximum_fusion.refs_3_), channel_id=1, source_target_pairs={{0,7},{1,6},{2,5},{3,4},{4,3},{5,2},{6,1},{7,0},{8,15},{9,14},{10,... | collective-permute-start | bytes 196616 | tf_op jit(solution)/shard_map/ppermute | solution.py:228
  11.6 0.5 %collective-permute-start.6 = (f32[4,32,128]{2,1,0:T(8,128)S(1)}, f32[4,32,128]{2,1,0:T(8,128)S(1)}, u32[]{:S(2)}, u32[]{:S(2)}) collective-permute-start(f32[4,32,128]{2,1,0:T(8,128)S(1)} %pad_maximum_fusion.refs_3_), channel_id=1, source_target_pairs={{0,5},{1,2},{2,1},{3,6},{4,7},{5,0},{6,3},{7,4},{8,13},{9,10},{10,... | collective-permute-start | bytes 196616 | tf_op jit(solution)/shard_map/ppermute | solution.py:228
  12.1 0.2 collective-permute-start.5
  12.3 0.4 %collective-permute-start.4 = (f32[4,32,128]{2,1,0:T(8,128)S(1)}, f32[4,32,128]{2,1,0:T(8,128)S(1)}, u32[]{:S(2)}, u32[]{:S(2)}) collective-permute-start(f32[4,32,128]{2,1,0:T(8,128)S(1)} %pad_maximum_fusion.refs_3_), channel_id=1, source_target_pairs={{0,1},{1,0},{2,3},{3,2},{4,5},{5,4},{6,7},{7,6},{8,9},{9,8},{10,11... | collective-permute-start | bytes 196616 | tf_op jit(solution)/shard_map/ppermute | solution.py:228
  12.8 1.7 %collective-permute-done.7.refs_5_ = f32[4,32,128]{2,1,0:T(8,128)S(1)} collective-permute-done((f32[4,32,128]{2,1,0:T(8,128)S(1)}, f32[4,32,128]{2,1,0:T(8,128)S(1)}, u32[]{:S(2)}, u32[]{:S(2)}) %collective-permute-start.7) | collective-permute-done | bytes 65568 | tf_op jit(solution)/shard_map/ppermute | solution.py:228
  14.4 0.3 %collective-permute-start.10 = (f32[4,32,128]{2,1,0:T(8,128)S(1)}, f32[4,32,128]{2,1,0:T(8,128)S(1)}, u32[]{:S(2)}, u32[]{:S(2)}) collective-permute-start(f32[4,32,128]{2,1,0:T(8,128)S(1)} %collective-permute-done.7.refs_5_), channel_id=1, source_target_pairs={{0,1},{1,0},{2,3},{3,2},{4,5},{5,4},{6,7},{7,6},{8,9},{9,8},{10,11... | collective-permute-start | bytes 196616 | tf_op jit(solution)/shard_map/ppermute | solution.py:228
  14.8 0.8 %collective-permute-done.6.refs_4_ = f32[4,32,128]{2,1,0:T(8,128)S(1)} collective-permute-done((f32[4,32,128]{2,1,0:T(8,128)S(1)}, f32[4,32,128]{2,1,0:T(8,128)S(1)}, u32[]{:S(2)}, u32[]{:S(2)}) %collective-permute-start.6) | collective-permute-done | bytes 65568 | tf_op jit(solution)/shard_map/ppermute | solution.py:228
  15.6 1.0 %collective-permute-start.8 = (f32[4,32,128]{2,1,0:T(8,128)S(1)}, f32[4,32,128]{2,1,0:T(8,128)S(1)}, u32[]{:S(2)}, u32[]{:S(2)}) collective-permute-start(f32[4,32,128]{2,1,0:T(8,128)S(1)} %collective-permute-done.6.refs_4_), channel_id=1, source_target_pairs={{0,1},{1,0},{2,3},{3,2},{4,5},{5,4},{6,7},{7,6},{8,9},{9,8},{10,11... | collective-permute-start | bytes 196616 | tf_op jit(solution)/shard_map/ppermute | solution.py:228
  16.5 0.0 collective-permute-done.5.refs_3_
  16.5 0.0 collective-permute-start.9
  16.5 0.0 collective-permute-done.4.refs_2_
  16.5 1.5 %shard_map.56.refs_2_ = f32[9,64,128]{2,1,0:T(8,128)S(1)} custom-call(s32[8,32]{1,0:T(8,128)S(1)} %get-tuple-element.10.refs_0_, bf16[32,128,256]{2,1,0:T(8,128)(2,1)S(1)} %get-tuple-element.11.refs_1_, f32[4,32,128]{2,1,0:T(8,128)S(1)} %collective-permute-done.4.refs_2_, f32[4,32,128]{2,1,0:T(8,128)S(1)} %collective-permute-done.5.refs_3_, ...), custom_call_target="tpu_custom_call" | custom-call | flops 268435456 | bytes 2097152 | tf_op jit(solution)/shard_map/pallas_call | solution.py:203
  18.1 0.0 collective-permute-done.10.refs_6_
  18.1 0.0 collective-permute-done.8.refs_4_
  18.1 0.0 collective-permute-done.9.refs_5_
  18.1 1.3 %shard_map.57 = f32[16,32,128]{2,1,0:T(8,128)S(1)} custom-call(s32[8,32]{1,0:T(8,128)S(1)} %get-tuple-element.10.refs_0_, bf16[32,128,256]{2,1,0:T(8,128)(2,1)S(1)} %get-tuple-element.11.refs_1_, f32[9,64,128]{2,1,0:T(8,128)S(1)} %shard_map.56.refs_2_, f32[4,32,128]{2,1,0:T(8,128)S(1)} %pad_maximum_fusion.refs_3_, ...), custom_call_target="tpu_custom_call" | custom-call | flops 268435456 | bytes 2097152 | tf_op jit(solution)/shard_map/pallas_call | solution.py:208
  19.4 0.4 %collective-permute-start.12 = (f32[4,32,128]{2,1,0:T(8,128)S(1)}, f32[4,32,128]{2,1,0:T(8,128)S(1)}, u32[]{:S(2)}, u32[]{:S(2)}) collective-permute-start(f32[4,32,128]{2,1,0:T(8,128)S(1)} %get-tuple-element.13), channel_id=1, source_target_pairs={{0,7},{1,6},{2,5},{3,4},{4,3},{5,2},{6,1},{7,0},{8,15},{9,14},{10,... | collective-permute-start | bytes 196616 | tf_op jit(solution)/shard_map/ppermute | solution.py:228
  19.7 1.4 %collective-permute-start.14 = (f32[4,32,128]{2,1,0:T(8,128)S(1)}, f32[4,32,128]{2,1,0:T(8,128)S(1)}, u32[]{:S(2)}, u32[]{:S(2)}) collective-permute-start(f32[4,32,128]{2,1,0:T(8,128)S(1)} %get-tuple-element.14), channel_id=1, source_target_pairs={{0,5},{1,2},{2,1},{3,6},{4,7},{5,0},{6,3},{7,4},{8,13},{9,10},{10,... | collective-permute-start | bytes 196616 | tf_op jit(solution)/shard_map/ppermute | solution.py:228
  21.1 0.8 %collective-permute-start.13 = (f32[4,32,128]{2,1,0:T(8,128)S(1)}, f32[4,32,128]{2,1,0:T(8,128)S(1)}, u32[]{:S(2)}, u32[]{:S(2)}) collective-permute-start(f32[4,32,128]{2,1,0:T(8,128)S(1)} %get-tuple-element.15), channel_id=1, source_target_pairs={{0,3},{1,4},{2,7},{3,0},{4,1},{5,6},{6,5},{7,2},{8,11},{9,12},{10,... | collective-permute-start | bytes 196616 | tf_op jit(solution)/shard_map/ppermute | solution.py:228
  21.9 0.9 %collective-permute-start.11 = (f32[4,32,128]{2,1,0:T(8,128)S(1)}, f32[4,32,128]{2,1,0:T(8,128)S(1)}, u32[]{:S(2)}, u32[]{:S(2)}) collective-permute-start(f32[4,32,128]{2,1,0:T(8,128)S(1)} %get-tuple-element.16), channel_id=1, source_target_pairs={{0,1},{1,0},{2,3},{3,2},{4,5},{5,4},{6,7},{7,6},{8,9},{9,8},{10,11... | collective-permute-start | bytes 196616 | tf_op jit(solution)/shard_map/ppermute | solution.py:228
  22.8 1.9 %collective-permute-done.12 = f32[4,32,128]{2,1,0:T(8,128)S(1)} collective-permute-done((f32[4,32,128]{2,1,0:T(8,128)S(1)}, f32[4,32,128]{2,1,0:T(8,128)S(1)}, u32[]{:S(2)}, u32[]{:S(2)}) %collective-permute-start.12) | collective-permute-done | bytes 65568 | tf_op jit(solution)/shard_map/ppermute | solution.py:228
  24.7 0.3 collective-permute-done.14
  25.0 0.3 %collective-permute-done.13 = f32[4,32,128]{2,1,0:T(8,128)S(1)} collective-permute-done((f32[4,32,128]{2,1,0:T(8,128)S(1)}, f32[4,32,128]{2,1,0:T(8,128)S(1)}, u32[]{:S(2)}, u32[]{:S(2)}) %collective-permute-start.13) | collective-permute-done | bytes 65568 | tf_op jit(solution)/shard_map/ppermute | solution.py:228
  25.3 0.0 collective-permute-done.11
  25.3 1.5 %collective-permute-start.16 = (f32[32,128]{1,0:T(8,128)S(1)}, f32[32,128]{1,0:T(8,128)S(1)}, u32[]{:S(2)}, u32[]{:S(2)}) collective-permute-start(f32[32,128]{1,0:T(8,128)S(1)} %get-tuple-element.17), channel_id=1, source_target_pairs={{0,25},{1,24},{2,27},{3,26},{4,29},{5,28},{6,31},{7,30},{8,17},{9,... | collective-permute-start | bytes 49160 | tf_op jit(solution)/shard_map/ppermute | solution.py:228
  26.8 0.0 collective-permute-start.18
  26.8 2.4 %collective-permute-start.17 = (f32[32,128]{1,0:T(8,128)S(1)}, f32[32,128]{1,0:T(8,128)S(1)}, u32[]{:S(2)}, u32[]{:S(2)}) collective-permute-start(f32[32,128]{1,0:T(8,128)S(1)} %get-tuple-element.19), channel_id=1, source_target_pairs={{0,9},{1,8},{2,11},{3,10},{4,13},{5,12},{6,15},{7,14},{8,1},{9,0},... | collective-permute-start | bytes 49160 | tf_op jit(solution)/shard_map/ppermute | solution.py:228
  29.2 0.4 %collective-permute-start.15 = (f32[32,128]{1,0:T(8,128)S(1)}, f32[32,128]{1,0:T(8,128)S(1)}, u32[]{:S(2)}, u32[]{:S(2)}) collective-permute-start(f32[32,128]{1,0:T(8,128)S(1)} %get-tuple-element.20), channel_id=1, source_target_pairs={{0,1},{1,0},{2,3},{3,2},{4,5},{5,4},{6,7},{7,6},{8,9},{9,8},{10,11... | collective-permute-start | bytes 49160 | tf_op jit(solution)/shard_map/ppermute | solution.py:228
  29.7 0.7 %collective-permute-done.16 = f32[32,128]{1,0:T(8,128)S(1)} collective-permute-done((f32[32,128]{1,0:T(8,128)S(1)}, f32[32,128]{1,0:T(8,128)S(1)}, u32[]{:S(2)}, u32[]{:S(2)}) %collective-permute-start.16) | collective-permute-done | bytes 16416 | tf_op jit(solution)/shard_map/ppermute | solution.py:228
  30.4 0.7 %collective-permute-done.18 = f32[32,128]{1,0:T(8,128)S(1)} collective-permute-done((f32[32,128]{1,0:T(8,128)S(1)}, f32[32,128]{1,0:T(8,128)S(1)}, u32[]{:S(2)}, u32[]{:S(2)}) %collective-permute-start.18) | collective-permute-done | bytes 16416 | tf_op jit(solution)/shard_map/ppermute | solution.py:228
  31.1 0.0 collective-permute-done.17
  31.1 0.0 collective-permute-done.15
  31.1 0.6 %add_add_fusion.1 = f32[32,128]{1,0:T(8,128)} fusion(f32[32,128]{1,0:T(8,128)S(1)} %collective-permute-done.18, f32[32,128]{1,0:T(8,128)S(1)} %collective-permute-done.17, f32[32,128]{1,0:T(8,128)S(1)} %collective-permute-done.15, f32[32,128]{1,0:T(8,128)S(1)} %collective-permute-done.16), kind=kLoop, calls=%fused_computation.6 | loop fusion | flops 12288 | bytes 81920 | tf_op jit(solution)/shard_map/add | solution.py:239
  (4 shorter events, 0.1 us)
Async XLA Ops:
  0.0 7.7 %collective-permute-start = (f32[32,128]{1,0:T(8,128)}, f32[32,128]{1,0:T(8,128)S(1)}, u32[]{:S(2)}, u32[]{:S(2)}) collective-permute-start(f32[32,128]{1,0:T(8,128)} %bitcast.32), channel_id=1, source_target_pairs={{0,1},{1,0},{2,3},{3,2},{4,5},{5,4},{6,7},{7,6},{8,9},{9,8},{10,11... | collective-permute-start | bytes 49160 | tf_op jit(solution)/shard_map/ppermute | solution.py:228
  0.5 7.2 %collective-permute-start.3 = (f32[32,128]{1,0:T(8,128)}, f32[32,128]{1,0:T(8,128)S(1)}, u32[]{:S(2)}, u32[]{:S(2)}) collective-permute-start(f32[32,128]{1,0:T(8,128)} %bitcast.33), channel_id=1, source_target_pairs={{0,17},{1,16},{2,19},{3,18},{4,21},{5,20},{6,23},{7,22},{8,25},{9,... | collective-permute-start | bytes 49160 | tf_op jit(solution)/shard_map/ppermute | solution.py:228
  4.2 5.2 %collective-permute-start.2 = (f32[32,128]{1,0:T(8,128)}, f32[32,128]{1,0:T(8,128)S(1)}, u32[]{:S(2)}, u32[]{:S(2)}) collective-permute-start(f32[32,128]{1,0:T(8,128)} %bitcast.34), channel_id=1, source_target_pairs={{0,25},{1,24},{2,27},{3,26},{4,29},{5,28},{6,31},{7,30},{8,17},{9,... | collective-permute-start | bytes 49160 | tf_op jit(solution)/shard_map/ppermute | solution.py:228
  5.2 4.2 %collective-permute-start.1 = (f32[32,128]{1,0:T(8,128)}, f32[32,128]{1,0:T(8,128)S(1)}, u32[]{:S(2)}, u32[]{:S(2)}) collective-permute-start(f32[32,128]{1,0:T(8,128)} %bitcast.35), channel_id=1, source_target_pairs={{0,9},{1,8},{2,11},{3,10},{4,13},{5,12},{6,15},{7,14},{8,1},{9,0},... | collective-permute-start | bytes 49160 | tf_op jit(solution)/shard_map/ppermute | solution.py:228
  9.4 5.1 %collective-permute-start.7 = (f32[4,32,128]{2,1,0:T(8,128)S(1)}, f32[4,32,128]{2,1,0:T(8,128)S(1)}, u32[]{:S(2)}, u32[]{:S(2)}) collective-permute-start(f32[4,32,128]{2,1,0:T(8,128)S(1)} %pad_maximum_fusion.refs_3_), channel_id=1, source_target_pairs={{0,7},{1,6},{2,5},{3,4},{4,3},{5,2},{6,1},{7,0},{8,15},{9,14},{10,... | collective-permute-start | bytes 196616 | tf_op jit(solution)/shard_map/ppermute | solution.py:228
  11.6 4.0 %collective-permute-start.6 = (f32[4,32,128]{2,1,0:T(8,128)S(1)}, f32[4,32,128]{2,1,0:T(8,128)S(1)}, u32[]{:S(2)}, u32[]{:S(2)}) collective-permute-start(f32[4,32,128]{2,1,0:T(8,128)S(1)} %pad_maximum_fusion.refs_3_), channel_id=1, source_target_pairs={{0,5},{1,2},{2,1},{3,6},{4,7},{5,0},{6,3},{7,4},{8,13},{9,10},{10,... | collective-permute-start | bytes 196616 | tf_op jit(solution)/shard_map/ppermute | solution.py:228
  12.1 4.4 %collective-permute-start.5 = (f32[4,32,128]{2,1,0:T(8,128)S(1)}, f32[4,32,128]{2,1,0:T(8,128)S(1)}, u32[]{:S(2)}, u32[]{:S(2)}) collective-permute-start(f32[4,32,128]{2,1,0:T(8,128)S(1)} %pad_maximum_fusion.refs_3_), channel_id=1, source_target_pairs={{0,3},{1,4},{2,7},{3,0},{4,1},{5,6},{6,5},{7,2},{8,11},{9,12},{10,... | collective-permute-start | bytes 196616 | tf_op jit(solution)/shard_map/ppermute | solution.py:228
  12.3 4.2 %collective-permute-start.4 = (f32[4,32,128]{2,1,0:T(8,128)S(1)}, f32[4,32,128]{2,1,0:T(8,128)S(1)}, u32[]{:S(2)}, u32[]{:S(2)}) collective-permute-start(f32[4,32,128]{2,1,0:T(8,128)S(1)} %pad_maximum_fusion.refs_3_), channel_id=1, source_target_pairs={{0,1},{1,0},{2,3},{3,2},{4,5},{5,4},{6,7},{7,6},{8,9},{9,8},{10,11... | collective-permute-start | bytes 196616 | tf_op jit(solution)/shard_map/ppermute | solution.py:228
  14.4 3.6 %collective-permute-start.10 = (f32[4,32,128]{2,1,0:T(8,128)S(1)}, f32[4,32,128]{2,1,0:T(8,128)S(1)}, u32[]{:S(2)}, u32[]{:S(2)}) collective-permute-start(f32[4,32,128]{2,1,0:T(8,128)S(1)} %collective-permute-done.7.refs_5_), channel_id=1, source_target_pairs={{0,1},{1,0},{2,3},{3,2},{4,5},{5,4},{6,7},{7,6},{8,9},{9,8},{10,11... | collective-permute-start | bytes 196616 | tf_op jit(solution)/shard_map/ppermute | solution.py:228
  15.6 2.5 %collective-permute-start.8 = (f32[4,32,128]{2,1,0:T(8,128)S(1)}, f32[4,32,128]{2,1,0:T(8,128)S(1)}, u32[]{:S(2)}, u32[]{:S(2)}) collective-permute-start(f32[4,32,128]{2,1,0:T(8,128)S(1)} %collective-permute-done.6.refs_4_), channel_id=1, source_target_pairs={{0,1},{1,0},{2,3},{3,2},{4,5},{5,4},{6,7},{7,6},{8,9},{9,8},{10,11... | collective-permute-start | bytes 196616 | tf_op jit(solution)/shard_map/ppermute | solution.py:228
  16.5 1.6 %collective-permute-start.9 = (f32[4,32,128]{2,1,0:T(8,128)S(1)}, f32[4,32,128]{2,1,0:T(8,128)S(1)}, u32[]{:S(2)}, u32[]{:S(2)}) collective-permute-start(f32[4,32,128]{2,1,0:T(8,128)S(1)} %collective-permute-done.5.refs_3_), channel_id=1, source_target_pairs={{0,1},{1,0},{2,3},{3,2},{4,5},{5,4},{6,7},{7,6},{8,9},{9,8},{10,11... | collective-permute-start | bytes 196616 | tf_op jit(solution)/shard_map/ppermute | solution.py:228
  19.4 5.3 %collective-permute-start.12 = (f32[4,32,128]{2,1,0:T(8,128)S(1)}, f32[4,32,128]{2,1,0:T(8,128)S(1)}, u32[]{:S(2)}, u32[]{:S(2)}) collective-permute-start(f32[4,32,128]{2,1,0:T(8,128)S(1)} %get-tuple-element.13), channel_id=1, source_target_pairs={{0,7},{1,6},{2,5},{3,4},{4,3},{5,2},{6,1},{7,0},{8,15},{9,14},{10,... | collective-permute-start | bytes 196616 | tf_op jit(solution)/shard_map/ppermute | solution.py:228
  19.7 5.2 %collective-permute-start.14 = (f32[4,32,128]{2,1,0:T(8,128)S(1)}, f32[4,32,128]{2,1,0:T(8,128)S(1)}, u32[]{:S(2)}, u32[]{:S(2)}) collective-permute-start(f32[4,32,128]{2,1,0:T(8,128)S(1)} %get-tuple-element.14), channel_id=1, source_target_pairs={{0,5},{1,2},{2,1},{3,6},{4,7},{5,0},{6,3},{7,4},{8,13},{9,10},{10,... | collective-permute-start | bytes 196616 | tf_op jit(solution)/shard_map/ppermute | solution.py:228
  21.1 4.2 %collective-permute-start.13 = (f32[4,32,128]{2,1,0:T(8,128)S(1)}, f32[4,32,128]{2,1,0:T(8,128)S(1)}, u32[]{:S(2)}, u32[]{:S(2)}) collective-permute-start(f32[4,32,128]{2,1,0:T(8,128)S(1)} %get-tuple-element.15), channel_id=1, source_target_pairs={{0,3},{1,4},{2,7},{3,0},{4,1},{5,6},{6,5},{7,2},{8,11},{9,12},{10,... | collective-permute-start | bytes 196616 | tf_op jit(solution)/shard_map/ppermute | solution.py:228
  21.9 3.4 %collective-permute-start.11 = (f32[4,32,128]{2,1,0:T(8,128)S(1)}, f32[4,32,128]{2,1,0:T(8,128)S(1)}, u32[]{:S(2)}, u32[]{:S(2)}) collective-permute-start(f32[4,32,128]{2,1,0:T(8,128)S(1)} %get-tuple-element.16), channel_id=1, source_target_pairs={{0,1},{1,0},{2,3},{3,2},{4,5},{5,4},{6,7},{7,6},{8,9},{9,8},{10,11... | collective-permute-start | bytes 196616 | tf_op jit(solution)/shard_map/ppermute | solution.py:228
  25.3 5.0 %collective-permute-start.16 = (f32[32,128]{1,0:T(8,128)S(1)}, f32[32,128]{1,0:T(8,128)S(1)}, u32[]{:S(2)}, u32[]{:S(2)}) collective-permute-start(f32[32,128]{1,0:T(8,128)S(1)} %get-tuple-element.17), channel_id=1, source_target_pairs={{0,25},{1,24},{2,27},{3,26},{4,29},{5,28},{6,31},{7,30},{8,17},{9,... | collective-permute-start | bytes 49160 | tf_op jit(solution)/shard_map/ppermute | solution.py:228
  26.8 4.2 %collective-permute-start.18 = (f32[32,128]{1,0:T(8,128)S(1)}, f32[32,128]{1,0:T(8,128)S(1)}, u32[]{:S(2)}, u32[]{:S(2)}) collective-permute-start(f32[32,128]{1,0:T(8,128)S(1)} %get-tuple-element.18), channel_id=1, source_target_pairs={{0,17},{1,16},{2,19},{3,18},{4,21},{5,20},{6,23},{7,22},{8,25},{9,... | collective-permute-start | bytes 49160 | tf_op jit(solution)/shard_map/ppermute | solution.py:228
  26.8 4.2 %collective-permute-start.17 = (f32[32,128]{1,0:T(8,128)S(1)}, f32[32,128]{1,0:T(8,128)S(1)}, u32[]{:S(2)}, u32[]{:S(2)}) collective-permute-start(f32[32,128]{1,0:T(8,128)S(1)} %get-tuple-element.19), channel_id=1, source_target_pairs={{0,9},{1,8},{2,11},{3,10},{4,13},{5,12},{6,15},{7,14},{8,1},{9,0},... | collective-permute-start | bytes 49160 | tf_op jit(solution)/shard_map/ppermute | solution.py:228
  29.2 1.8 %collective-permute-start.15 = (f32[32,128]{1,0:T(8,128)S(1)}, f32[32,128]{1,0:T(8,128)S(1)}, u32[]{:S(2)}, u32[]{:S(2)}) collective-permute-start(f32[32,128]{1,0:T(8,128)S(1)} %get-tuple-element.20), channel_id=1, source_target_pairs={{0,1},{1,0},{2,3},{3,2},{4,5},{5,4},{6,7},{7,6},{8,9},{9,8},{10,11... | collective-permute-start | bytes 49160 | tf_op jit(solution)/shard_map/ppermute | solution.py:228

commit v5 on v3

--- a/solution.py
+++ b/solution.py
@@ -20,8 +20,8 @@
     return high, low
 
 
-def tile_kernel(out_tiles, live, ins, outs, tiles, mine, halves, codes, own, held, index_rows, arrived, singles):
-    singles_of = ((ins, index_rows.at[0]), (outs, index_rows.at[1]), (mine, own))
+def tile_kernel(out_tiles, live, ins, outs, tiles, mine, halves, codes, own, held, in_row, out_row, arrived, singles):
+    singles_of = ((ins, in_row), (outs, out_row), (mine, own))
     others = [pltpu.make_async_copy(here, there, singles.at[at]) for at, (here, there) in enumerate(singles_of)]
     for copy in others:
         copy.start()
@@ -39,12 +39,13 @@
     lax.fori_loop(0, groups, begin, 0)
     for copy in others:
         copy.wait()
-    slots = lax.broadcasted_iota(jnp.int32, ins.shape, 1)
-    tile_in = index_rows[0]
-    owner = lax.bitwise_xor(lax.div(tile_in, out_tiles), lax.axis_index("virt"))
-    codes[0:1, :] = owner * out_tiles + lax.rem(tile_in, out_tiles)
-    codes[1:2, :] = jnp.where(slots < count, lax.rem(index_rows[1], out_tiles), out_tiles)
-    codes[2:3, :] = jnp.full(ins.shape, count, jnp.int32)
+    me = lax.axis_index("virt")
+    codes[2, 0] = count
+    for slot in range(ins.shape[1]):
+        tile_in = in_row[0, slot]
+        owner = lax.bitwise_xor(lax.div(tile_in, out_tiles), me)
+        codes[0, slot] = owner * out_tiles + lax.rem(tile_in, out_tiles)
+        codes[1, slot] = jnp.where(slot < count, lax.rem(out_row[0, slot], out_tiles), out_tiles)
 
     def one_group(index, carry):
         tile_copy(index).wait()
@@ -69,14 +70,15 @@
         kernel,
         out_shape=(
             jax.ShapeDtypeStruct((slots, W, 2 * W), jnp.bfloat16),
-            jax.ShapeDtypeStruct((3, slots), jnp.int32),
+            pltpu.SMEM((3, slots), jnp.int32),
             jax.ShapeDtypeStruct(mine.shape, mine.dtype),
         ),
         in_specs=[SMEM] + [pl.BlockSpec(memory_space=pltpu.HBM)] * 4,
-        out_specs=(VMEM, VMEM, VMEM),
+        out_specs=(VMEM, SMEM, VMEM),
         scratch_shapes=[
             pltpu.VMEM((slots, W, W), jnp.float32),
-            pltpu.VMEM((2, 1, slots), jnp.int32),
+            pltpu.SMEM((1, slots), jnp.int32),
+            pltpu.SMEM((1, slots), jnp.int32),
             pltpu.SemaphoreType.DMA((slots // COPY_GROUP,)),
             pltpu.SemaphoreType.DMA((3,)),
         ],
@@ -94,10 +96,8 @@
     )
 
 
-def ladder_kernel(virts, codes_here, halves, *refs):
-    blocks, (result, columns, totals, codes, copied) = refs[: virts * NEAR], refs[virts * NEAR :]
-    fetch = pltpu.make_async_copy(codes_here, codes, copied)
-    fetch.start()
+def ladder_kernel(virts, codes, halves, *refs):
+    blocks, (result, columns, totals) = refs[: virts * NEAR], refs[virts * NEAR :]
     far = blocks[0].shape[0]
     chunk_count = NEAR * far
     out_tiles = totals.shape[0] - 1
@@ -123,8 +123,6 @@
                         columns[column, first_row : first_row + 4 * rows, :] = high
                         columns[column, total_rows + first_row : total_rows + first_row + 4 * rows, :] = low
 
-    fetch.wait()
-
     def one_group(index, carry):
         first = index * GROUP
         products = []
@@ -158,16 +156,14 @@
     return pl.pallas_call(
         kernel,
         out_shape=jax.ShapeDtypeStruct((NEAR * far, out_tiles * rows, W), jnp.float32),
-        in_specs=[VMEM, VMEM] + [VMEM] * len(blocks),
+        in_specs=[SMEM, VMEM] + [VMEM] * len(blocks),
         out_specs=VMEM,
         scratch_shapes=[
             pltpu.VMEM((virts * in_local, 2 * total_rows, W), jnp.bfloat16),
             pltpu.VMEM((out_tiles + 1, total_rows, W), jnp.float32),
-            pltpu.SMEM(codes.shape, jnp.int32),
-            pltpu.SemaphoreType.DMA,
         ],
         compiler_params=pltpu.CompilerParams(vmem_limit_bytes=32 * 1024 * 1024),
-    )(codes, halves, *blocks)
+    )(pltpu.with_memory_space_constraint(codes, pltpu.SMEM), halves, *blocks)
 
 
 def near_mask(step, a, b):

time: 31.8 us -> 31.4 us (0.987)
  Pallas kernels: 2.27 us -> 1.76 us
    pallas_call x1, Pallas kernels: 1.03 us -> 0.55 us  [local_terms(): pl.pallas_call(kernel, out_shape=jax.ShapeDtypeStruct((NEAR * far, out_ti...]
where the time goes in v5:
time: 31.4 us; the launch traced here: 31.3 us
  starting transfers between devices  17.5 us (56%)
  waiting for transfers between devices  10.7 us (34%)
  Pallas kernels  1.76 us (6%)
  between operations  0.72 us (2%)
  other arithmetic  0.64 us (2%)
    ppermute x18, starting transfers between devices, swap(): return lax.ppermute(value, ('pair', 'virt'), routes)  17.5 us
    ppermute x18, waiting for transfers between devices, swap(): return lax.ppermute(value, ('pair', 'virt'), routes)  10.7 us
    pallas_call x1, Pallas kernels, prepare(): pl.pallas_call(kernel, out_shape=(jax.ShapeDtypeStruct((slots, W, 2 * W),...  1.21 us
    add x2, other arithmetic, swap_sum(): return sum(received[1:], received[0])  0.63 us
  transfers between devices with their start and end apart: 18, of which 10 were waited for; matrix products, arithmetic and copies ran while one was open for 0% of the time, Pallas kernels for 4%

profile of v5, /device:TPU:0, one launch (start us, length us, event | category | flops | bytes accessed | tf_op | source)
XLA Modules:
  0.0 31.3 jit_solution(4167593939655789783)
XLA Ops:
  0.0 3.5 %collective-permute-start.2 = (f32[32,128]{1,0:T(8,128)}, f32[32,128]{1,0:T(8,128)S(1)}, u32[]{:S(2)}, u32[]{:S(2)}) collective-permute-start(f32[32,128]{1,0:T(8,128)} %bitcast.27), channel_id=1, source_target_pairs={{0,17},{1,16},{2,19},{3,18},{4,21},{5,20},{6,23},{7,22},{8,25},{9,... | collective-permute-start | bytes 49160 | tf_op jit(solution)/shard_map/ppermute | solution.py:179
  3.5 1.6 %collective-permute-start.1 = (f32[32,128]{1,0:T(8,128)}, f32[32,128]{1,0:T(8,128)S(1)}, u32[]{:S(2)}, u32[]{:S(2)}) collective-permute-start(f32[32,128]{1,0:T(8,128)} %bitcast.28), channel_id=1, source_target_pairs={{0,25},{1,24},{2,27},{3,26},{4,29},{5,28},{6,31},{7,30},{8,17},{9,... | collective-permute-start | bytes 49160 | tf_op jit(solution)/shard_map/ppermute | solution.py:179
  5.1 0.2 collective-permute-start
  6.0 1.2 %shard_map.55 = (bf16[32,128,256]{2,1,0:T(8,128)(2,1)S(1)}, s32[3,32]{1,0:T(4,128)S(4)}, f32[32,128]{1,0:T(8,128)S(1)}) custom-call(s32[1,1]{1,0:T(1,128)S(6)} %copy.8.refs_0_, s32[1,32]{1,0:T(1,128)} %bitcast.34, s32[1,32]{1,0:T(1,128)} %bitcast.35, f32[32,128,128]{2,1,0:T(8,128)} %bitcast.26, f32[32,128]{1,0:T(8,128)} %bitcast.30), custom_call_target="tpu_custom_call" | custom-call | flops 2097152 | bytes 4194304 | tf_op jit(solution)/shard_map/pallas_call | solution.py:69
  7.2 0.0 collective-permute-done.2
  7.2 1.4 %collective-permute-done.1 = f32[32,128]{1,0:T(8,128)S(1)} collective-permute-done((f32[32,128]{1,0:T(8,128)}, f32[32,128]{1,0:T(8,128)S(1)}, u32[]{:S(2)}, u32[]{:S(2)}) %collective-permute-start.1) | collective-permute-done | bytes 16416 | tf_op jit(solution)/shard_map/ppermute | solution.py:179
  8.7 0.0 collective-permute-done
  8.7 2.8 %collective-permute-start.5 = (f32[4,32,128]{2,1,0:T(8,128)S(1)}, f32[4,32,128]{2,1,0:T(8,128)S(1)}, u32[]{:S(2)}, u32[]{:S(2)}) collective-permute-start(f32[4,32,128]{2,1,0:T(8,128)S(1)} %pad_maximum_fusion.refs_2_), channel_id=1, source_target_pairs={{0,7},{1,6},{2,5},{3,4},{4,3},{5,2},{6,1},{7,0},{8,15},{9,14},{10,... | collective-permute-start | bytes 196616 | tf_op jit(solution)/shard_map/ppermute | solution.py:179
  11.5 0.0 collective-permute-start.4
  11.5 0.8 %collective-permute-start.3 = (f32[4,32,128]{2,1,0:T(8,128)S(1)}, f32[4,32,128]{2,1,0:T(8,128)S(1)}, u32[]{:S(2)}, u32[]{:S(2)}) collective-permute-start(f32[4,32,128]{2,1,0:T(8,128)S(1)} %pad_maximum_fusion.refs_2_), channel_id=1, source_target_pairs={{0,3},{1,4},{2,7},{3,0},{4,1},{5,6},{6,5},{7,2},{8,11},{9,12},{10,... | collective-permute-start | bytes 196616 | tf_op jit(solution)/shard_map/ppermute | solution.py:179
  12.3 0.0 collective-permute-start.6
  12.3 1.7 %collective-permute-done.5.refs_5_ = f32[4,32,128]{2,1,0:T(8,128)S(1)} collective-permute-done((f32[4,32,128]{2,1,0:T(8,128)S(1)}, f32[4,32,128]{2,1,0:T(8,128)S(1)}, u32[]{:S(2)}, u32[]{:S(2)}) %collective-permute-start.5) | collective-permute-done | bytes 65568 | tf_op jit(solution)/shard_map/ppermute | solution.py:179
  14.0 0.1 collective-permute-start.9
  14.1 1.2 %collective-permute-done.4.refs_4_ = f32[4,32,128]{2,1,0:T(8,128)S(1)} collective-permute-done((f32[4,32,128]{2,1,0:T(8,128)S(1)}, f32[4,32,128]{2,1,0:T(8,128)S(1)}, u32[]{:S(2)}, u32[]{:S(2)}) %collective-permute-start.4) | collective-permute-done | bytes 65568 | tf_op jit(solution)/shard_map/ppermute | solution.py:179
  15.2 0.7 %collective-permute-start.8 = (f32[4,32,128]{2,1,0:T(8,128)S(1)}, f32[4,32,128]{2,1,0:T(8,128)S(1)}, u32[]{:S(2)}, u32[]{:S(2)}) collective-permute-start(f32[4,32,128]{2,1,0:T(8,128)S(1)} %collective-permute-done.4.refs_4_), channel_id=1, source_target_pairs={{0,1},{1,0},{2,3},{3,2},{4,5},{5,4},{6,7},{7,6},{8,9},{9,8},{10,11... | collective-permute-start | bytes 196616 | tf_op jit(solution)/shard_map/ppermute | solution.py:179
  16.0 0.0 collective-permute-done.3.refs_3_
  16.0 0.0 collective-permute-start.7
  16.0 0.0 collective-permute-done.6.refs_6_
  16.0 0.0 collective-permute-done.9.refs_9_
  16.0 0.9 %collective-permute-done.8.refs_8_ = f32[4,32,128]{2,1,0:T(8,128)S(1)} collective-permute-done((f32[4,32,128]{2,1,0:T(8,128)S(1)}, f32[4,32,128]{2,1,0:T(8,128)S(1)}, u32[]{:S(2)}, u32[]{:S(2)}) %collective-permute-start.8) | collective-permute-done | bytes 65568 | tf_op jit(solution)/shard_map/ppermute | solution.py:179
  16.9 0.4 %collective-permute-done.7.refs_7_ = f32[4,32,128]{2,1,0:T(8,128)S(1)} collective-permute-done((f32[4,32,128]{2,1,0:T(8,128)S(1)}, f32[4,32,128]{2,1,0:T(8,128)S(1)}, u32[]{:S(2)}, u32[]{:S(2)}) %collective-permute-start.7) | collective-permute-done | bytes 65568 | tf_op jit(solution)/shard_map/ppermute | solution.py:179
  17.2 0.6 %shard_map.56 = f32[16,32,128]{2,1,0:T(8,128)S(1)} custom-call(s32[3,32]{1,0:T(4,128)S(4)} %get-tuple-element.8.refs_0_, bf16[32,128,256]{2,1,0:T(8,128)(2,1)S(1)} %get-tuple-element.9.refs_1_, f32[4,32,128]{2,1,0:T(8,128)S(1)} %pad_maximum_fusion.refs_2_, f32[4,32,128]{2,1,0:T(8,128)S(1)} %collective-permute-done.3.refs_3_, ...), custom_call_target="tpu_custom_call" | custom-call | tf_op jit(solution)/shard_map/pallas_call | solution.py:156
  17.8 1.4 %collective-permute-start.11 = (f32[4,32,128]{2,1,0:T(8,128)S(1)}, f32[4,32,128]{2,1,0:T(8,128)S(1)}, u32[]{:S(2)}, u32[]{:S(2)}) collective-permute-start(f32[4,32,128]{2,1,0:T(8,128)S(1)} %get-tuple-element.11), channel_id=1, source_target_pairs={{0,7},{1,6},{2,5},{3,4},{4,3},{5,2},{6,1},{7,0},{8,15},{9,14},{10,... | collective-permute-start | bytes 196616 | tf_op jit(solution)/shard_map/ppermute | solution.py:179
  19.2 1.0 %collective-permute-start.13 = (f32[4,32,128]{2,1,0:T(8,128)S(1)}, f32[4,32,128]{2,1,0:T(8,128)S(1)}, u32[]{:S(2)}, u32[]{:S(2)}) collective-permute-start(f32[4,32,128]{2,1,0:T(8,128)S(1)} %get-tuple-element.12), channel_id=1, source_target_pairs={{0,5},{1,2},{2,1},{3,6},{4,7},{5,0},{6,3},{7,4},{8,13},{9,10},{10,... | collective-permute-start | bytes 196616 | tf_op jit(solution)/shard_map/ppermute | solution.py:179
  20.2 0.6 %collective-permute-start.12 = (f32[4,32,128]{2,1,0:T(8,128)S(1)}, f32[4,32,128]{2,1,0:T(8,128)S(1)}, u32[]{:S(2)}, u32[]{:S(2)}) collective-permute-start(f32[4,32,128]{2,1,0:T(8,128)S(1)} %get-tuple-element.13), channel_id=1, source_target_pairs={{0,3},{1,4},{2,7},{3,0},{4,1},{5,6},{6,5},{7,2},{8,11},{9,12},{10,... | collective-permute-start | bytes 196616 | tf_op jit(solution)/shard_map/ppermute | solution.py:179
  20.8 0.4 %collective-permute-start.10 = (f32[4,32,128]{2,1,0:T(8,128)S(1)}, f32[4,32,128]{2,1,0:T(8,128)S(1)}, u32[]{:S(2)}, u32[]{:S(2)}) collective-permute-start(f32[4,32,128]{2,1,0:T(8,128)S(1)} %get-tuple-element.14), channel_id=1, source_target_pairs={{0,1},{1,0},{2,3},{3,2},{4,5},{5,4},{6,7},{7,6},{8,9},{9,8},{10,11... | collective-permute-start | bytes 196616 | tf_op jit(solution)/shard_map/ppermute | solution.py:179
  21.2 1.7 %collective-permute-done.11 = f32[4,32,128]{2,1,0:T(8,128)S(1)} collective-permute-done((f32[4,32,128]{2,1,0:T(8,128)S(1)}, f32[4,32,128]{2,1,0:T(8,128)S(1)}, u32[]{:S(2)}, u32[]{:S(2)}) %collective-permute-start.11) | collective-permute-done | bytes 65568 | tf_op jit(solution)/shard_map/ppermute | solution.py:179
  22.9 1.1 %collective-permute-done.13 = f32[4,32,128]{2,1,0:T(8,128)S(1)} collective-permute-done((f32[4,32,128]{2,1,0:T(8,128)S(1)}, f32[4,32,128]{2,1,0:T(8,128)S(1)}, u32[]{:S(2)}, u32[]{:S(2)}) %collective-permute-start.13) | collective-permute-done | bytes 65568 | tf_op jit(solution)/shard_map/ppermute | solution.py:179
  24.0 0.5 %collective-permute-done.12 = f32[4,32,128]{2,1,0:T(8,128)S(1)} collective-permute-done((f32[4,32,128]{2,1,0:T(8,128)S(1)}, f32[4,32,128]{2,1,0:T(8,128)S(1)}, u32[]{:S(2)}, u32[]{:S(2)}) %collective-permute-start.12) | collective-permute-done | bytes 65568 | tf_op jit(solution)/shard_map/ppermute | solution.py:179
  24.4 0.0 collective-permute-done.10
  24.5 2.2 %collective-permute-start.15 = (f32[32,128]{1,0:T(8,128)S(1)}, f32[32,128]{1,0:T(8,128)S(1)}, u32[]{:S(2)}, u32[]{:S(2)}) collective-permute-start(f32[32,128]{1,0:T(8,128)S(1)} %get-tuple-element.15), channel_id=1, source_target_pairs={{0,25},{1,24},{2,27},{3,26},{4,29},{5,28},{6,31},{7,30},{8,17},{9,... | collective-permute-start | bytes 49160 | tf_op jit(solution)/shard_map/ppermute | solution.py:179
  26.6 0.0 collective-permute-start.17
  26.6 1.7 %collective-permute-start.16 = (f32[32,128]{1,0:T(8,128)S(1)}, f32[32,128]{1,0:T(8,128)S(1)}, u32[]{:S(2)}, u32[]{:S(2)}) collective-permute-start(f32[32,128]{1,0:T(8,128)S(1)} %get-tuple-element.17), channel_id=1, source_target_pairs={{0,9},{1,8},{2,11},{3,10},{4,13},{5,12},{6,15},{7,14},{8,1},{9,0},... | collective-permute-start | bytes 49160 | tf_op jit(solution)/shard_map/ppermute | solution.py:179
  28.4 0.4 %collective-permute-start.14 = (f32[32,128]{1,0:T(8,128)S(1)}, f32[32,128]{1,0:T(8,128)S(1)}, u32[]{:S(2)}, u32[]{:S(2)}) collective-permute-start(f32[32,128]{1,0:T(8,128)S(1)} %get-tuple-element.18), channel_id=1, source_target_pairs={{0,1},{1,0},{2,3},{3,2},{4,5},{5,4},{6,7},{7,6},{8,9},{9,8},{10,11... | collective-permute-start | bytes 49160 | tf_op jit(solution)/shard_map/ppermute | solution.py:179
  28.8 0.7 %collective-permute-done.15 = f32[32,128]{1,0:T(8,128)S(1)} collective-permute-done((f32[32,128]{1,0:T(8,128)S(1)}, f32[32,128]{1,0:T(8,128)S(1)}, u32[]{:S(2)}, u32[]{:S(2)}) %collective-permute-start.15) | collective-permute-done | bytes 16416 | tf_op jit(solution)/shard_map/ppermute | solution.py:179
  29.5 1.2 %collective-permute-done.17 = f32[32,128]{1,0:T(8,128)S(1)} collective-permute-done((f32[32,128]{1,0:T(8,128)S(1)}, f32[32,128]{1,0:T(8,128)S(1)}, u32[]{:S(2)}, u32[]{:S(2)}) %collective-permute-start.17) | collective-permute-done | bytes 16416 | tf_op jit(solution)/shard_map/ppermute | solution.py:179
  30.7 0.0 collective-permute-done.16
  30.7 0.0 collective-permute-done.14
  30.7 0.6 %add_add_fusion.1 = f32[32,128]{1,0:T(8,128)} fusion(f32[32,128]{1,0:T(8,128)S(1)} %collective-permute-done.17, f32[32,128]{1,0:T(8,128)S(1)} %collective-permute-done.16, f32[32,128]{1,0:T(8,128)S(1)} %collective-permute-done.14, f32[32,128]{1,0:T(8,128)S(1)} %collective-permute-done.15), kind=kLoop, calls=%fused_computation.6 | loop fusion | flops 12288 | bytes 81920 | tf_op jit(solution)/shard_map/add | solution.py:190
  (4 shorter events, 0.1 us)
Async XLA Ops:
  0.0 7.2 %collective-permute-start.2 = (f32[32,128]{1,0:T(8,128)}, f32[32,128]{1,0:T(8,128)S(1)}, u32[]{:S(2)}, u32[]{:S(2)}) collective-permute-start(f32[32,128]{1,0:T(8,128)} %bitcast.27), channel_id=1, source_target_pairs={{0,17},{1,16},{2,19},{3,18},{4,21},{5,20},{6,23},{7,22},{8,25},{9,... | collective-permute-start | bytes 49160 | tf_op jit(solution)/shard_map/ppermute | solution.py:179
  3.5 5.2 %collective-permute-start.1 = (f32[32,128]{1,0:T(8,128)}, f32[32,128]{1,0:T(8,128)S(1)}, u32[]{:S(2)}, u32[]{:S(2)}) collective-permute-start(f32[32,128]{1,0:T(8,128)} %bitcast.28), channel_id=1, source_target_pairs={{0,25},{1,24},{2,27},{3,26},{4,29},{5,28},{6,31},{7,30},{8,17},{9,... | collective-permute-start | bytes 49160 | tf_op jit(solution)/shard_map/ppermute | solution.py:179
  5.1 3.6 %collective-permute-start = (f32[32,128]{1,0:T(8,128)}, f32[32,128]{1,0:T(8,128)S(1)}, u32[]{:S(2)}, u32[]{:S(2)}) collective-permute-start(f32[32,128]{1,0:T(8,128)} %bitcast.29), channel_id=1, source_target_pairs={{0,9},{1,8},{2,11},{3,10},{4,13},{5,12},{6,15},{7,14},{8,1},{9,0},... | collective-permute-start | bytes 49160 | tf_op jit(solution)/shard_map/ppermute | solution.py:179
  8.7 5.3 %collective-permute-start.5 = (f32[4,32,128]{2,1,0:T(8,128)S(1)}, f32[4,32,128]{2,1,0:T(8,128)S(1)}, u32[]{:S(2)}, u32[]{:S(2)}) collective-permute-start(f32[4,32,128]{2,1,0:T(8,128)S(1)} %pad_maximum_fusion.refs_2_), channel_id=1, source_target_pairs={{0,7},{1,6},{2,5},{3,4},{4,3},{5,2},{6,1},{7,0},{8,15},{9,14},{10,... | collective-permute-start | bytes 196616 | tf_op jit(solution)/shard_map/ppermute | solution.py:179
  11.5 3.7 %collective-permute-start.4 = (f32[4,32,128]{2,1,0:T(8,128)S(1)}, f32[4,32,128]{2,1,0:T(8,128)S(1)}, u32[]{:S(2)}, u32[]{:S(2)}) collective-permute-start(f32[4,32,128]{2,1,0:T(8,128)S(1)} %pad_maximum_fusion.refs_2_), channel_id=1, source_target_pairs={{0,5},{1,2},{2,1},{3,6},{4,7},{5,0},{6,3},{7,4},{8,13},{9,10},{10,... | collective-permute-start | bytes 196616 | tf_op jit(solution)/shard_map/ppermute | solution.py:179
  11.5 4.4 %collective-permute-start.3 = (f32[4,32,128]{2,1,0:T(8,128)S(1)}, f32[4,32,128]{2,1,0:T(8,128)S(1)}, u32[]{:S(2)}, u32[]{:S(2)}) collective-permute-start(f32[4,32,128]{2,1,0:T(8,128)S(1)} %pad_maximum_fusion.refs_2_), channel_id=1, source_target_pairs={{0,3},{1,4},{2,7},{3,0},{4,1},{5,6},{6,5},{7,2},{8,11},{9,12},{10,... | collective-permute-start | bytes 196616 | tf_op jit(solution)/shard_map/ppermute | solution.py:179
  12.3 3.7 %collective-permute-start.6 = (f32[4,32,128]{2,1,0:T(8,128)S(1)}, f32[4,32,128]{2,1,0:T(8,128)S(1)}, u32[]{:S(2)}, u32[]{:S(2)}) collective-permute-start(f32[4,32,128]{2,1,0:T(8,128)S(1)} %pad_maximum_fusion.refs_2_), channel_id=1, source_target_pairs={{0,1},{1,0},{2,3},{3,2},{4,5},{5,4},{6,7},{7,6},{8,9},{9,8},{10,11... | collective-permute-start | bytes 196616 | tf_op jit(solution)/shard_map/ppermute | solution.py:179
  14.0 2.0 %collective-permute-start.9 = (f32[4,32,128]{2,1,0:T(8,128)S(1)}, f32[4,32,128]{2,1,0:T(8,128)S(1)}, u32[]{:S(2)}, u32[]{:S(2)}) collective-permute-start(f32[4,32,128]{2,1,0:T(8,128)S(1)} %collective-permute-done.5.refs_5_), channel_id=1, source_target_pairs={{0,1},{1,0},{2,3},{3,2},{4,5},{5,4},{6,7},{7,6},{8,9},{9,8},{10,11... | collective-permute-start | bytes 196616 | tf_op jit(solution)/shard_map/ppermute | solution.py:179
  15.2 1.6 %collective-permute-start.8 = (f32[4,32,128]{2,1,0:T(8,128)S(1)}, f32[4,32,128]{2,1,0:T(8,128)S(1)}, u32[]{:S(2)}, u32[]{:S(2)}) collective-permute-start(f32[4,32,128]{2,1,0:T(8,128)S(1)} %collective-permute-done.4.refs_4_), channel_id=1, source_target_pairs={{0,1},{1,0},{2,3},{3,2},{4,5},{5,4},{6,7},{7,6},{8,9},{9,8},{10,11... | collective-permute-start | bytes 196616 | tf_op jit(solution)/shard_map/ppermute | solution.py:179
  16.0 1.3 %collective-permute-start.7 = (f32[4,32,128]{2,1,0:T(8,128)S(1)}, f32[4,32,128]{2,1,0:T(8,128)S(1)}, u32[]{:S(2)}, u32[]{:S(2)}) collective-permute-start(f32[4,32,128]{2,1,0:T(8,128)S(1)} %collective-permute-done.3.refs_3_), channel_id=1, source_target_pairs={{0,1},{1,0},{2,3},{3,2},{4,5},{5,4},{6,7},{7,6},{8,9},{9,8},{10,11... | collective-permute-start | bytes 196616 | tf_op jit(solution)/shard_map/ppermute | solution.py:179
  17.8 5.1 %collective-permute-start.11 = (f32[4,32,128]{2,1,0:T(8,128)S(1)}, f32[4,32,128]{2,1,0:T(8,128)S(1)}, u32[]{:S(2)}, u32[]{:S(2)}) collective-permute-start(f32[4,32,128]{2,1,0:T(8,128)S(1)} %get-tuple-element.11), channel_id=1, source_target_pairs={{0,7},{1,6},{2,5},{3,4},{4,3},{5,2},{6,1},{7,0},{8,15},{9,14},{10,... | collective-permute-start | bytes 196616 | tf_op jit(solution)/shard_map/ppermute | solution.py:179
  19.2 4.7 %collective-permute-start.13 = (f32[4,32,128]{2,1,0:T(8,128)S(1)}, f32[4,32,128]{2,1,0:T(8,128)S(1)}, u32[]{:S(2)}, u32[]{:S(2)}) collective-permute-start(f32[4,32,128]{2,1,0:T(8,128)S(1)} %get-tuple-element.12), channel_id=1, source_target_pairs={{0,5},{1,2},{2,1},{3,6},{4,7},{5,0},{6,3},{7,4},{8,13},{9,10},{10,... | collective-permute-start | bytes 196616 | tf_op jit(solution)/shard_map/ppermute | solution.py:179
  20.2 4.2 %collective-permute-start.12 = (f32[4,32,128]{2,1,0:T(8,128)S(1)}, f32[4,32,128]{2,1,0:T(8,128)S(1)}, u32[]{:S(2)}, u32[]{:S(2)}) collective-permute-start(f32[4,32,128]{2,1,0:T(8,128)S(1)} %get-tuple-element.13), channel_id=1, source_target_pairs={{0,3},{1,4},{2,7},{3,0},{4,1},{5,6},{6,5},{7,2},{8,11},{9,12},{10,... | collective-permute-start | bytes 196616 | tf_op jit(solution)/shard_map/ppermute | solution.py:179
  20.8 3.6 %collective-permute-start.10 = (f32[4,32,128]{2,1,0:T(8,128)S(1)}, f32[4,32,128]{2,1,0:T(8,128)S(1)}, u32[]{:S(2)}, u32[]{:S(2)}) collective-permute-start(f32[4,32,128]{2,1,0:T(8,128)S(1)} %get-tuple-element.14), channel_id=1, source_target_pairs={{0,1},{1,0},{2,3},{3,2},{4,5},{5,4},{6,7},{7,6},{8,9},{9,8},{10,11... | collective-permute-start | bytes 196616 | tf_op jit(solution)/shard_map/ppermute | solution.py:179
  24.5 5.0 %collective-permute-start.15 = (f32[32,128]{1,0:T(8,128)S(1)}, f32[32,128]{1,0:T(8,128)S(1)}, u32[]{:S(2)}, u32[]{:S(2)}) collective-permute-start(f32[32,128]{1,0:T(8,128)S(1)} %get-tuple-element.15), channel_id=1, source_target_pairs={{0,25},{1,24},{2,27},{3,26},{4,29},{5,28},{6,31},{7,30},{8,17},{9,... | collective-permute-start | bytes 49160 | tf_op jit(solution)/shard_map/ppermute | solution.py:179
  26.6 4.1 %collective-permute-start.17 = (f32[32,128]{1,0:T(8,128)S(1)}, f32[32,128]{1,0:T(8,128)S(1)}, u32[]{:S(2)}, u32[]{:S(2)}) collective-permute-start(f32[32,128]{1,0:T(8,128)S(1)} %get-tuple-element.16), channel_id=1, source_target_pairs={{0,17},{1,16},{2,19},{3,18},{4,21},{5,20},{6,23},{7,22},{8,25},{9,... | collective-permute-start | bytes 49160 | tf_op jit(solution)/shard_map/ppermute | solution.py:179
  26.6 4.1 %collective-permute-start.16 = (f32[32,128]{1,0:T(8,128)S(1)}, f32[32,128]{1,0:T(8,128)S(1)}, u32[]{:S(2)}, u32[]{:S(2)}) collective-permute-start(f32[32,128]{1,0:T(8,128)S(1)} %get-tuple-element.17), channel_id=1, source_target_pairs={{0,9},{1,8},{2,11},{3,10},{4,13},{5,12},{6,15},{7,14},{8,1},{9,0},... | collective-permute-start | bytes 49160 | tf_op jit(solution)/shard_map/ppermute | solution.py:179
  28.4 2.3 %collective-permute-start.14 = (f32[32,128]{1,0:T(8,128)S(1)}, f32[32,128]{1,0:T(8,128)S(1)}, u32[]{:S(2)}, u32[]{:S(2)}) collective-permute-start(f32[32,128]{1,0:T(8,128)S(1)} %get-tuple-element.18), channel_id=1, source_target_pairs={{0,1},{1,0},{2,3},{3,2},{4,5},{5,4},{6,7},{7,6},{8,9},{9,8},{10,11... | collective-permute-start | bytes 49160 | tf_op jit(solution)/shard_map/ppermute | solution.py:179

commit v6 on v4

--- a/solution.py
+++ b/solution.py
@@ -20,21 +20,9 @@
     return high, low
 
 
-def slot_list(chosen, rows):
-    slots = chosen.shape[1]
-    shape = (slots, slots)
-    down, across = lax.broadcasted_iota(jnp.int32, shape, 0), lax.broadcasted_iota(jnp.int32, shape, 1)
-
-    def turned(row):
-        return jnp.sum(jnp.where(down == across, jnp.broadcast_to(row, shape), 0.0), axis=1, keepdims=True)
-
-    ahead = jnp.sum(jnp.where(across < down, jnp.broadcast_to(chosen, shape), 0.0), axis=1, keepdims=True)
-    here = (ahead.astype(jnp.int32) == across) & (turned(chosen) > 0.5)
-    return [jnp.sum(jnp.where(here, turned(row), 0.0), axis=0, keepdims=True) for row in rows]
-
-
-def tile_kernel(out_tiles, live, ins, outs, tiles, halves, codes, held, index_rows, arrived, singles):
-    others = [pltpu.make_async_copy(rows, index_rows.at[at], singles.at[at]) for at, rows in enumerate((ins, outs))]
+def tile_kernel(out_tiles, live, ins, outs, tiles, halves, codes, held, in_row, out_row, arrived, singles):
+    indices = ((ins, in_row), (outs, out_row))
+    others = [pltpu.make_async_copy(here, there, singles.at[at]) for at, (here, there) in enumerate(indices)]
     for copy in others:
         copy.start()
     count = live[0, 0]
@@ -51,21 +39,26 @@
     lax.fori_loop(0, groups, begin, 0)
     for copy in others:
         copy.wait()
-    slots = lax.broadcasted_iota(jnp.int32, ins.shape, 1)
-    tile_in = index_rows[0]
-    owner = lax.bitwise_xor(lax.div(tile_in, out_tiles), lax.axis_index("virt"))
-    local = lax.rem(tile_in, out_tiles)
-    place = lax.rem(index_rows[1], out_tiles)
-    for base, is_own in ((0, True), (4, False)):
-        chosen = jnp.where((slots < count) & ((owner == 0) == is_own), 1.0, 0.0)
-        column = local if is_own else local + (owner - 1) * out_tiles
-        rows = [value.astype(jnp.float32) for value in (slots, column, place)]
-        slot_row, column_row, place_row = [row.astype(jnp.int32) for row in slot_list(chosen, rows)]
-        number = jnp.broadcast_to(jnp.sum(chosen, axis=1, keepdims=True), ins.shape).astype(jnp.int32)
-        codes[base : base + 1, :] = slot_row
-        codes[base + 1 : base + 2, :] = column_row
-        codes[base + 2 : base + 3, :] = jnp.where(slots < number, place_row, out_tiles)
-        codes[base + 3 : base + 4, :] = number
+    for at in range(ins.shape[1]):
+        for base in (0, 3):
+            codes[base, at] = 0
+            codes[base + 1, at] = 0
+            codes[base + 2, at] = out_tiles
+    me = lax.axis_index("virt")
+
+    numbers = [jnp.int32(0), jnp.int32(0)]
+    for slot in range(ins.shape[1]):
+        tile_in, is_live = in_row[0, slot], slot < count
+        owner = lax.bitwise_xor(lax.div(tile_in, out_tiles), me)
+        is_own = owner == 0
+        base = jnp.where(is_live, jnp.where(is_own, 0, 3), 6)
+        at = jnp.where(is_own, numbers[0], numbers[1])
+        codes[base, at] = slot
+        codes[base + 1, at] = jnp.where(is_own, 0, owner - 1) * out_tiles + lax.rem(tile_in, out_tiles)
+        codes[base + 2, at] = lax.rem(out_row[0, slot], out_tiles)
+        numbers[0] += (is_live & is_own).astype(jnp.int32)
+        numbers[1] += (is_live & (owner != 0)).astype(jnp.int32)
+    codes[9, 0], codes[9, 1] = numbers
 
     def one_group(index, carry):
         tile_copy(index).wait()
@@ -90,13 +83,14 @@
         kernel,
         out_shape=(
             jax.ShapeDtypeStruct((slots, W, 2 * W), jnp.bfloat16),
-            jax.ShapeDtypeStruct((8, slots), jnp.int32),
+            pltpu.SMEM((10, slots), jnp.int32),
         ),
         in_specs=[SMEM] + [pl.BlockSpec(memory_space=pltpu.HBM)] * 3,
-        out_specs=(VMEM, VMEM),
+        out_specs=(VMEM, SMEM),
         scratch_shapes=[
             pltpu.VMEM((slots, W, W), jnp.float32),
-            pltpu.VMEM((2, 1, slots), jnp.int32),
+            pltpu.SMEM((1, slots), jnp.int32),
+            pltpu.SMEM((1, slots), jnp.int32),
             pltpu.SemaphoreType.DMA((slots // COPY_GROUP,)),
             pltpu.SemaphoreType.DMA((2,)),
         ],
@@ -130,8 +124,9 @@
                     columns[column, total_rows + first_row : total_rows + first_row + 4 * rows, :] = low
 
 
-def add_products(base, codes, columns, halves, totals):
+def add_products(which, codes, columns, halves, totals):
     total_rows = totals.shape[1]
+    base = 3 * which
 
     def one_group(index, carry):
         first = index * GROUP
@@ -146,29 +141,23 @@
             totals[place] = totals[place] + products[step]
         return carry
 
-    lax.fori_loop(0, (codes[base + 3, 0] + GROUP - 1) // GROUP, one_group, 0)
-
-
-def own_kernel(rows, codes_here, halves, *refs):
-    lines, (totals, columns, codes, copied) = refs[:NEAR], refs[NEAR:]
-    fetch = pltpu.make_async_copy(codes_here, codes, copied)
-    fetch.start()
+    lax.fori_loop(0, (codes[9, which] + GROUP - 1) // GROUP, one_group, 0)
+
+
+def own_kernel(rows, codes, halves, *refs):
+    lines, (totals, columns) = refs[:NEAR], refs[NEAR:]
     totals[...] = jnp.zeros_like(totals)
     fill_columns(columns, 0, lines, rows)
-    fetch.wait()
     add_products(0, codes, columns, halves, totals)
 
 
-def rest_kernel(rows, codes_here, halves, own_totals, *refs):
-    lines, (result, columns, totals, codes, copied) = refs[:-5], refs[-5:]
-    fetch = pltpu.make_async_copy(codes_here, codes, copied)
-    fetch.start()
+def rest_kernel(rows, codes, halves, own_totals, *refs):
+    lines, (result, columns, totals) = refs[:-3], refs[-3:]
     totals[...] = own_totals[...]
     in_local = lines[0].shape[1] // rows
     for owner in range(len(lines) // NEAR):
         fill_columns(columns, owner * in_local, lines[owner * NEAR : (owner + 1) * NEAR], rows)
-    fetch.wait()
-    add_products(4, codes, columns, halves, totals)
+    add_products(1, codes, columns, halves, totals)
     for chunk in range(0, result.shape[0], 2):
         part = slice(chunk * rows, (chunk + 2) * rows)
         for tile in range(0, result.shape[1] // rows, 2):
@@ -183,12 +172,8 @@
     in_local = chunk_rows // rows
     totals = jax.ShapeDtypeStruct((out_tiles + 1, total_rows, W), jnp.float32)
 
-    def scratch(count):
-        return [
-            pltpu.VMEM((count * in_local, 2 * total_rows, W), jnp.bfloat16),
-            pltpu.SMEM(codes.shape, jnp.int32),
-            pltpu.SemaphoreType.DMA,
-        ]
+    def columns(count):
+        return pltpu.VMEM((count * in_local, 2 * total_rows, W), jnp.bfloat16)
 
     def own(*refs):
         own_kernel(rows, *refs)
@@ -200,17 +185,22 @@
         compiler_params=pltpu.CompilerParams(vmem_limit_bytes=32 * 1024 * 1024),
         cost_estimate=pl.CostEstimate(flops=1 << 28, bytes_accessed=1 << 21, transcendentals=0),
     )
+    codes = pltpu.with_memory_space_constraint(codes, pltpu.SMEM)
     own_totals = pl.pallas_call(
-        own, out_shape=totals, in_specs=[VMEM] * (2 + NEAR), out_specs=VMEM, scratch_shapes=scratch(1), **settings
+        own,
+        out_shape=totals,
+        in_specs=[SMEM] + [VMEM] * (1 + NEAR),
+        out_specs=VMEM,
+        scratch_shapes=[columns(1)],
+        **settings,
     )(codes, halves, *owners[0])
     others = [line for lines in owners[1:] for line in lines]
-    columns, *others_scratch = scratch(len(owners) - 1)
     return pl.pallas_call(
         rest,
         out_shape=jax.ShapeDtypeStruct((NEAR * far, out_tiles * rows, W), jnp.float32),
-        in_specs=[VMEM] * (3 + len(others)),
+        in_specs=[SMEM] + [VMEM] * (2 + len(others)),
         out_specs=VMEM,
-        scratch_shapes=[columns, pltpu.VMEM(totals.shape, totals.dtype)] + others_scratch,
+        scratch_shapes=[columns(len(owners) - 1), pltpu.VMEM(totals.shape, totals.dtype)],
         **settings,
     )(codes, halves, own_totals, *others)
 
@@ -253,7 +243,7 @@
         tile_counts,
         local_tiles,
     )
-    neighbour, codes = lax.optimization_barrier((neighbour, codes))
+    neighbour, halves = lax.optimization_barrier((neighbour, halves))
     order = far_order(pairs // NEAR)
     line = jnp.stack([neighbour] + [swap(mine, pairs, virts, 1, far=mask) for mask in order[1:]])
     pieces = [line] + [swap(line, pairs, virts, 1, step=step) for step in range(1, NEAR)]

time: 31.9 us -> 31.3 us (0.981)
  Pallas kernels: 4.46 us -> 2.15 us
  waiting for transfers between devices: 8.05 us -> 9.81 us
    ppermute x19, waiting for transfers between devices: 8.05 us -> 9.81 us  [swap(): return lax.ppermute(value, ('pair', 'virt'), routes)]
    pallas_call x1, Pallas kernels: 1.52 us -> 0.35 us  [local_terms(): pl.pallas_call(own, out_shape=totals, in_specs=[SMEM] + [VMEM] * (1 + NEA...]
    pallas_call x1, Pallas kernels: 1.25 us -> 0.37 us  [local_terms(): pl.pallas_call(rest, out_shape=jax.ShapeDtypeStruct((NEAR * far, out_tile...]
  transfers between devices with their start and end apart: 19 -> 19, of which waited for: 8 -> 10; matrix products, arithmetic and copies ran while one was open for 0% -> 0% of each run, Pallas kernels for 10% -> 6%
where the time goes in v6:
time: 31.3 us; the launch traced here: 31.1 us
  starting transfers between devices  17.8 us (57%)
  waiting for transfers between devices  9.81 us (31%)
  Pallas kernels  2.15 us (7%)
  between operations  0.74 us (2%)
  other arithmetic  0.64 us (2%)
    ppermute x19, starting transfers between devices, swap(): return lax.ppermute(value, ('pair', 'virt'), routes)  17.8 us
    ppermute x19, waiting for transfers between devices, swap(): return lax.ppermute(value, ('pair', 'virt'), routes)  9.81 us
    pallas_call x1, Pallas kernels, prepare(): pl.pallas_call(kernel, out_shape=(jax.ShapeDtypeStruct((slots, W, 2 * W),...  1.43 us
    add x2, other arithmetic, swap_sum(): return sum(received[1:], received[0])  0.63 us
  transfers between devices with their start and end apart: 19, of which 10 were waited for; matrix products, arithmetic and copies ran while one was open for 0% of the time, Pallas kernels for 6%

profile of v6, /device:TPU:0, one launch (start us, length us, event | category | flops | bytes accessed | tf_op | source)
XLA Modules:
  0.0 31.1 jit_solution(5835848452780584035)
XLA Ops:
  0.0 0.5 %collective-permute-start = (f32[32,128]{1,0:T(8,128)}, f32[32,128]{1,0:T(8,128)S(1)}, u32[]{:S(2)}, u32[]{:S(2)}) collective-permute-start(f32[32,128]{1,0:T(8,128)} %bitcast.32), channel_id=1, source_target_pairs={{0,1},{1,0},{2,3},{3,2},{4,5},{5,4},{6,7},{7,6},{8,9},{9,8},{10,11... | collective-permute-start | bytes 49160 | tf_op jit(solution)/shard_map/ppermute | solution.py:218
  0.5 3.7 %collective-permute-start.3 = (f32[32,128]{1,0:T(8,128)}, f32[32,128]{1,0:T(8,128)S(1)}, u32[]{:S(2)}, u32[]{:S(2)}) collective-permute-start(f32[32,128]{1,0:T(8,128)} %bitcast.33), channel_id=1, source_target_pairs={{0,17},{1,16},{2,19},{3,18},{4,21},{5,20},{6,23},{7,22},{8,25},{9,... | collective-permute-start | bytes 49160 | tf_op jit(solution)/shard_map/ppermute | solution.py:218
  4.2 1.0 %collective-permute-start.2 = (f32[32,128]{1,0:T(8,128)}, f32[32,128]{1,0:T(8,128)S(1)}, u32[]{:S(2)}, u32[]{:S(2)}) collective-permute-start(f32[32,128]{1,0:T(8,128)} %bitcast.34), channel_id=1, source_target_pairs={{0,25},{1,24},{2,27},{3,26},{4,29},{5,28},{6,31},{7,30},{8,17},{9,... | collective-permute-start | bytes 49160 | tf_op jit(solution)/shard_map/ppermute | solution.py:218
  5.2 0.2 collective-permute-start.1
  6.0 1.4 %shard_map.55 = (bf16[32,128,256]{2,1,0:T(8,128)(2,1)S(1)}, s32[10,32]{1,0:T(8,128)S(4)}) custom-call(s32[1,1]{1,0:T(1,128)S(6)} %copy.8.refs_0_, s32[1,32]{1,0:T(1,128)} %bitcast.30, s32[1,32]{1,0:T(1,128)} %bitcast.31, f32[32,128,128]{2,1,0:T(8,128)} %bitcast.25), custom_call_target="tpu_custom_call" | custom-call | flops 2097152 | bytes 4194304 | tf_op jit(solution)/shard_map/pallas_call | solution.py:82
  7.4 0.0 collective-permute-done
  7.4 0.0 collective-permute-done.3
  7.5 1.9 %collective-permute-done.2 = f32[32,128]{1,0:T(8,128)S(1)} collective-permute-done((f32[32,128]{1,0:T(8,128)}, f32[32,128]{1,0:T(8,128)S(1)}, u32[]{:S(2)}, u32[]{:S(2)}) %collective-permute-start.2) | collective-permute-done | bytes 16416 | tf_op jit(solution)/shard_map/ppermute | solution.py:218
  9.3 0.0 collective-permute-done.1
  9.4 2.2 %collective-permute-start.7 = (f32[4,32,128]{2,1,0:T(8,128)S(1)}, f32[4,32,128]{2,1,0:T(8,128)S(1)}, u32[]{:S(2)}, u32[]{:S(2)}) collective-permute-start(f32[4,32,128]{2,1,0:T(8,128)S(1)} %pad_maximum_fusion.refs_3_), channel_id=1, source_target_pairs={{0,7},{1,6},{2,5},{3,4},{4,3},{5,2},{6,1},{7,0},{8,15},{9,14},{10,... | collective-permute-start | bytes 196616 | tf_op jit(solution)/shard_map/ppermute | solution.py:218
  11.6 0.5 %collective-permute-start.6 = (f32[4,32,128]{2,1,0:T(8,128)S(1)}, f32[4,32,128]{2,1,0:T(8,128)S(1)}, u32[]{:S(2)}, u32[]{:S(2)}) collective-permute-start(f32[4,32,128]{2,1,0:T(8,128)S(1)} %pad_maximum_fusion.refs_3_), channel_id=1, source_target_pairs={{0,5},{1,2},{2,1},{3,6},{4,7},{5,0},{6,3},{7,4},{8,13},{9,10},{10,... | collective-permute-start | bytes 196616 | tf_op jit(solution)/shard_map/ppermute | solution.py:218
  12.1 0.2 collective-permute-start.5
  12.3 0.4 %collective-permute-start.4 = (f32[4,32,128]{2,1,0:T(8,128)S(1)}, f32[4,32,128]{2,1,0:T(8,128)S(1)}, u32[]{:S(2)}, u32[]{:S(2)}) collective-permute-start(f32[4,32,128]{2,1,0:T(8,128)S(1)} %pad_maximum_fusion.refs_3_), channel_id=1, source_target_pairs={{0,1},{1,0},{2,3},{3,2},{4,5},{5,4},{6,7},{7,6},{8,9},{9,8},{10,11... | collective-permute-start | bytes 196616 | tf_op jit(solution)/shard_map/ppermute | solution.py:218
  12.8 1.7 %collective-permute-done.7.refs_5_ = f32[4,32,128]{2,1,0:T(8,128)S(1)} collective-permute-done((f32[4,32,128]{2,1,0:T(8,128)S(1)}, f32[4,32,128]{2,1,0:T(8,128)S(1)}, u32[]{:S(2)}, u32[]{:S(2)}) %collective-permute-start.7) | collective-permute-done | bytes 65568 | tf_op jit(solution)/shard_map/ppermute | solution.py:218
  14.4 0.3 %collective-permute-start.10 = (f32[4,32,128]{2,1,0:T(8,128)S(1)}, f32[4,32,128]{2,1,0:T(8,128)S(1)}, u32[]{:S(2)}, u32[]{:S(2)}) collective-permute-start(f32[4,32,128]{2,1,0:T(8,128)S(1)} %collective-permute-done.7.refs_5_), channel_id=1, source_target_pairs={{0,1},{1,0},{2,3},{3,2},{4,5},{5,4},{6,7},{7,6},{8,9},{9,8},{10,11... | collective-permute-start | bytes 196616 | tf_op jit(solution)/shard_map/ppermute | solution.py:218
  14.8 0.8 %collective-permute-done.6.refs_4_ = f32[4,32,128]{2,1,0:T(8,128)S(1)} collective-permute-done((f32[4,32,128]{2,1,0:T(8,128)S(1)}, f32[4,32,128]{2,1,0:T(8,128)S(1)}, u32[]{:S(2)}, u32[]{:S(2)}) %collective-permute-start.6) | collective-permute-done | bytes 65568 | tf_op jit(solution)/shard_map/ppermute | solution.py:218
  15.6 1.0 %collective-permute-start.8 = (f32[4,32,128]{2,1,0:T(8,128)S(1)}, f32[4,32,128]{2,1,0:T(8,128)S(1)}, u32[]{:S(2)}, u32[]{:S(2)}) collective-permute-start(f32[4,32,128]{2,1,0:T(8,128)S(1)} %collective-permute-done.6.refs_4_), channel_id=1, source_target_pairs={{0,1},{1,0},{2,3},{3,2},{4,5},{5,4},{6,7},{7,6},{8,9},{9,8},{10,11... | collective-permute-start | bytes 196616 | tf_op jit(solution)/shard_map/ppermute | solution.py:218
  16.5 0.0 collective-permute-done.5.refs_3_
  16.5 0.0 collective-permute-start.9
  16.5 0.0 collective-permute-done.4.refs_2_
  16.5 0.3 %shard_map.56.refs_2_ = f32[9,64,128]{2,1,0:T(8,128)S(1)} custom-call(s32[10,32]{1,0:T(8,128)S(4)} %get-tuple-element.9.refs_0_, bf16[32,128,256]{2,1,0:T(8,128)(2,1)S(1)} %get-tuple-element.11.refs_1_, f32[4,32,128]{2,1,0:T(8,128)S(1)} %collective-permute-done.4.refs_2_, f32[4,32,128]{2,1,0:T(8,128)S(1)} %collective-permute-done.5.refs_3_, ...), custom_call_target="tpu_custom_call" | custom-call | flops 268435456 | bytes 2097152 | tf_op jit(solution)/shard_map/pallas_call | solution.py:189
  16.9 0.0 collective-permute-done.10.refs_6_
  16.9 0.5 %collective-permute-done.8.refs_4_ = f32[4,32,128]{2,1,0:T(8,128)S(1)} collective-permute-done((f32[4,32,128]{2,1,0:T(8,128)S(1)}, f32[4,32,128]{2,1,0:T(8,128)S(1)}, u32[]{:S(2)}, u32[]{:S(2)}) %collective-permute-start.8) | collective-permute-done | bytes 65568 | tf_op jit(solution)/shard_map/ppermute | solution.py:218
  17.4 0.4 %collective-permute-done.9.refs_5_ = f32[4,32,128]{2,1,0:T(8,128)S(1)} collective-permute-done((f32[4,32,128]{2,1,0:T(8,128)S(1)}, f32[4,32,128]{2,1,0:T(8,128)S(1)}, u32[]{:S(2)}, u32[]{:S(2)}) %collective-permute-start.9) | collective-permute-done | bytes 65568 | tf_op jit(solution)/shard_map/ppermute | solution.py:218
  17.8 0.4 %shard_map.57 = f32[16,32,128]{2,1,0:T(8,128)S(1)} custom-call(s32[10,32]{1,0:T(8,128)S(4)} %get-tuple-element.9.refs_0_, bf16[32,128,256]{2,1,0:T(8,128)(2,1)S(1)} %get-tuple-element.11.refs_1_, f32[9,64,128]{2,1,0:T(8,128)S(1)} %shard_map.56.refs_2_, f32[4,32,128]{2,1,0:T(8,128)S(1)} %pad_maximum_fusion.refs_3_, ...), custom_call_target="tpu_custom_call" | custom-call | flops 268435456 | bytes 2097152 | tf_op jit(solution)/shard_map/pallas_call | solution.py:198
  18.2 0.9 %collective-permute-start.12 = (f32[4,32,128]{2,1,0:T(8,128)S(1)}, f32[4,32,128]{2,1,0:T(8,128)S(1)}, u32[]{:S(2)}, u32[]{:S(2)}) collective-permute-start(f32[4,32,128]{2,1,0:T(8,128)S(1)} %get-tuple-element.13), channel_id=1, source_target_pairs={{0,7},{1,6},{2,5},{3,4},{4,3},{5,2},{6,1},{7,0},{8,15},{9,14},{10,... | collective-permute-start | bytes 196616 | tf_op jit(solution)/shard_map/ppermute | solution.py:218
  19.1 1.7 %collective-permute-start.14 = (f32[4,32,128]{2,1,0:T(8,128)S(1)}, f32[4,32,128]{2,1,0:T(8,128)S(1)}, u32[]{:S(2)}, u32[]{:S(2)}) collective-permute-start(f32[4,32,128]{2,1,0:T(8,128)S(1)} %get-tuple-element.14), channel_id=1, source_target_pairs={{0,5},{1,2},{2,1},{3,6},{4,7},{5,0},{6,3},{7,4},{8,13},{9,10},{10,... | collective-permute-start | bytes 196616 | tf_op jit(solution)/shard_map/ppermute | solution.py:218
  20.8 0.4 %collective-permute-start.13 = (f32[4,32,128]{2,1,0:T(8,128)S(1)}, f32[4,32,128]{2,1,0:T(8,128)S(1)}, u32[]{:S(2)}, u32[]{:S(2)}) collective-permute-start(f32[4,32,128]{2,1,0:T(8,128)S(1)} %get-tuple-element.15), channel_id=1, source_target_pairs={{0,3},{1,4},{2,7},{3,0},{4,1},{5,6},{6,5},{7,2},{8,11},{9,12},{10,... | collective-permute-start | bytes 196616 | tf_op jit(solution)/shard_map/ppermute | solution.py:218
  21.2 0.3 %collective-permute-start.11 = (f32[4,32,128]{2,1,0:T(8,128)S(1)}, f32[4,32,128]{2,1,0:T(8,128)S(1)}, u32[]{:S(2)}, u32[]{:S(2)}) collective-permute-start(f32[4,32,128]{2,1,0:T(8,128)S(1)} %get-tuple-element.16), channel_id=1, source_target_pairs={{0,1},{1,0},{2,3},{3,2},{4,5},{5,4},{6,7},{7,6},{8,9},{9,8},{10,11... | collective-permute-start | bytes 196616 | tf_op jit(solution)/shard_map/ppermute | solution.py:218
  21.6 1.7 %collective-permute-done.12 = f32[4,32,128]{2,1,0:T(8,128)S(1)} collective-permute-done((f32[4,32,128]{2,1,0:T(8,128)S(1)}, f32[4,32,128]{2,1,0:T(8,128)S(1)}, u32[]{:S(2)}, u32[]{:S(2)}) %collective-permute-start.12) | collective-permute-done | bytes 65568 | tf_op jit(solution)/shard_map/ppermute | solution.py:218
  23.3 1.0 %collective-permute-done.14 = f32[4,32,128]{2,1,0:T(8,128)S(1)} collective-permute-done((f32[4,32,128]{2,1,0:T(8,128)S(1)}, f32[4,32,128]{2,1,0:T(8,128)S(1)}, u32[]{:S(2)}, u32[]{:S(2)}) %collective-permute-start.14) | collective-permute-done | bytes 65568 | tf_op jit(solution)/shard_map/ppermute | solution.py:218
  24.4 0.4 %collective-permute-done.13 = f32[4,32,128]{2,1,0:T(8,128)S(1)} collective-permute-done((f32[4,32,128]{2,1,0:T(8,128)S(1)}, f32[4,32,128]{2,1,0:T(8,128)S(1)}, u32[]{:S(2)}, u32[]{:S(2)}) %collective-permute-start.13) | collective-permute-done | bytes 65568 | tf_op jit(solution)/shard_map/ppermute | solution.py:218
  24.7 0.0 collective-permute-done.11
  24.8 1.6 %collective-permute-start.16 = (f32[32,128]{1,0:T(8,128)S(1)}, f32[32,128]{1,0:T(8,128)S(1)}, u32[]{:S(2)}, u32[]{:S(2)}) collective-permute-start(f32[32,128]{1,0:T(8,128)S(1)} %get-tuple-element.17), channel_id=1, source_target_pairs={{0,25},{1,24},{2,27},{3,26},{4,29},{5,28},{6,31},{7,30},{8,17},{9,... | collective-permute-start | bytes 49160 | tf_op jit(solution)/shard_map/ppermute | solution.py:218
  26.4 0.0 collective-permute-start.18
  26.4 2.3 %collective-permute-start.17 = (f32[32,128]{1,0:T(8,128)S(1)}, f32[32,128]{1,0:T(8,128)S(1)}, u32[]{:S(2)}, u32[]{:S(2)}) collective-permute-start(f32[32,128]{1,0:T(8,128)S(1)} %get-tuple-element.19), channel_id=1, source_target_pairs={{0,9},{1,8},{2,11},{3,10},{4,13},{5,12},{6,15},{7,14},{8,1},{9,0},... | collective-permute-start | bytes 49160 | tf_op jit(solution)/shard_map/ppermute | solution.py:218
  28.7 0.4 %collective-permute-start.15 = (f32[32,128]{1,0:T(8,128)S(1)}, f32[32,128]{1,0:T(8,128)S(1)}, u32[]{:S(2)}, u32[]{:S(2)}) collective-permute-start(f32[32,128]{1,0:T(8,128)S(1)} %get-tuple-element.20), channel_id=1, source_target_pairs={{0,1},{1,0},{2,3},{3,2},{4,5},{5,4},{6,7},{7,6},{8,9},{9,8},{10,11... | collective-permute-start | bytes 49160 | tf_op jit(solution)/shard_map/ppermute | solution.py:218
  29.1 0.7 %collective-permute-done.16 = f32[32,128]{1,0:T(8,128)S(1)} collective-permute-done((f32[32,128]{1,0:T(8,128)S(1)}, f32[32,128]{1,0:T(8,128)S(1)}, u32[]{:S(2)}, u32[]{:S(2)}) %collective-permute-start.16) | collective-permute-done | bytes 16416 | tf_op jit(solution)/shard_map/ppermute | solution.py:218
  29.8 0.7 %collective-permute-done.18 = f32[32,128]{1,0:T(8,128)S(1)} collective-permute-done((f32[32,128]{1,0:T(8,128)S(1)}, f32[32,128]{1,0:T(8,128)S(1)}, u32[]{:S(2)}, u32[]{:S(2)}) %collective-permute-start.18) | collective-permute-done | bytes 16416 | tf_op jit(solution)/shard_map/ppermute | solution.py:218
  30.5 0.0 collective-permute-done.17
  30.5 0.0 collective-permute-done.15
  30.5 0.6 %add_add_fusion.1 = f32[32,128]{1,0:T(8,128)} fusion(f32[32,128]{1,0:T(8,128)S(1)} %collective-permute-done.18, f32[32,128]{1,0:T(8,128)S(1)} %collective-permute-done.17, f32[32,128]{1,0:T(8,128)S(1)} %collective-permute-done.15, f32[32,128]{1,0:T(8,128)S(1)} %collective-permute-done.16), kind=kLoop, calls=%fused_computation.6 | loop fusion | flops 12288 | bytes 81920 | tf_op jit(solution)/shard_map/add | solution.py:229
  (4 shorter events, 0.1 us)
Async XLA Ops:
  0.0 7.4 %collective-permute-start = (f32[32,128]{1,0:T(8,128)}, f32[32,128]{1,0:T(8,128)S(1)}, u32[]{:S(2)}, u32[]{:S(2)}) collective-permute-start(f32[32,128]{1,0:T(8,128)} %bitcast.32), channel_id=1, source_target_pairs={{0,1},{1,0},{2,3},{3,2},{4,5},{5,4},{6,7},{7,6},{8,9},{9,8},{10,11... | collective-permute-start | bytes 49160 | tf_op jit(solution)/shard_map/ppermute | solution.py:218
  0.5 7.0 %collective-permute-start.3 = (f32[32,128]{1,0:T(8,128)}, f32[32,128]{1,0:T(8,128)S(1)}, u32[]{:S(2)}, u32[]{:S(2)}) collective-permute-start(f32[32,128]{1,0:T(8,128)} %bitcast.33), channel_id=1, source_target_pairs={{0,17},{1,16},{2,19},{3,18},{4,21},{5,20},{6,23},{7,22},{8,25},{9,... | collective-permute-start | bytes 49160 | tf_op jit(solution)/shard_map/ppermute | solution.py:218
  4.2 5.2 %collective-permute-start.2 = (f32[32,128]{1,0:T(8,128)}, f32[32,128]{1,0:T(8,128)S(1)}, u32[]{:S(2)}, u32[]{:S(2)}) collective-permute-start(f32[32,128]{1,0:T(8,128)} %bitcast.34), channel_id=1, source_target_pairs={{0,25},{1,24},{2,27},{3,26},{4,29},{5,28},{6,31},{7,30},{8,17},{9,... | collective-permute-start | bytes 49160 | tf_op jit(solution)/shard_map/ppermute | solution.py:218
  5.2 4.2 %collective-permute-start.1 = (f32[32,128]{1,0:T(8,128)}, f32[32,128]{1,0:T(8,128)S(1)}, u32[]{:S(2)}, u32[]{:S(2)}) collective-permute-start(f32[32,128]{1,0:T(8,128)} %bitcast.35), channel_id=1, source_target_pairs={{0,9},{1,8},{2,11},{3,10},{4,13},{5,12},{6,15},{7,14},{8,1},{9,0},... | collective-permute-start | bytes 49160 | tf_op jit(solution)/shard_map/ppermute | solution.py:218
  9.4 5.1 %collective-permute-start.7 = (f32[4,32,128]{2,1,0:T(8,128)S(1)}, f32[4,32,128]{2,1,0:T(8,128)S(1)}, u32[]{:S(2)}, u32[]{:S(2)}) collective-permute-start(f32[4,32,128]{2,1,0:T(8,128)S(1)} %pad_maximum_fusion.refs_3_), channel_id=1, source_target_pairs={{0,7},{1,6},{2,5},{3,4},{4,3},{5,2},{6,1},{7,0},{8,15},{9,14},{10,... | collective-permute-start | bytes 196616 | tf_op jit(solution)/shard_map/ppermute | solution.py:218
  11.6 4.0 %collective-permute-start.6 = (f32[4,32,128]{2,1,0:T(8,128)S(1)}, f32[4,32,128]{2,1,0:T(8,128)S(1)}, u32[]{:S(2)}, u32[]{:S(2)}) collective-permute-start(f32[4,32,128]{2,1,0:T(8,128)S(1)} %pad_maximum_fusion.refs_3_), channel_id=1, source_target_pairs={{0,5},{1,2},{2,1},{3,6},{4,7},{5,0},{6,3},{7,4},{8,13},{9,10},{10,... | collective-permute-start | bytes 196616 | tf_op jit(solution)/shard_map/ppermute | solution.py:218
  12.1 4.4 %collective-permute-start.5 = (f32[4,32,128]{2,1,0:T(8,128)S(1)}, f32[4,32,128]{2,1,0:T(8,128)S(1)}, u32[]{:S(2)}, u32[]{:S(2)}) collective-permute-start(f32[4,32,128]{2,1,0:T(8,128)S(1)} %pad_maximum_fusion.refs_3_), channel_id=1, source_target_pairs={{0,3},{1,4},{2,7},{3,0},{4,1},{5,6},{6,5},{7,2},{8,11},{9,12},{10,... | collective-permute-start | bytes 196616 | tf_op jit(solution)/shard_map/ppermute | solution.py:218
  12.3 4.2 %collective-permute-start.4 = (f32[4,32,128]{2,1,0:T(8,128)S(1)}, f32[4,32,128]{2,1,0:T(8,128)S(1)}, u32[]{:S(2)}, u32[]{:S(2)}) collective-permute-start(f32[4,32,128]{2,1,0:T(8,128)S(1)} %pad_maximum_fusion.refs_3_), channel_id=1, source_target_pairs={{0,1},{1,0},{2,3},{3,2},{4,5},{5,4},{6,7},{7,6},{8,9},{9,8},{10,11... | collective-permute-start | bytes 196616 | tf_op jit(solution)/shard_map/ppermute | solution.py:218
  14.4 2.5 %collective-permute-start.10 = (f32[4,32,128]{2,1,0:T(8,128)S(1)}, f32[4,32,128]{2,1,0:T(8,128)S(1)}, u32[]{:S(2)}, u32[]{:S(2)}) collective-permute-start(f32[4,32,128]{2,1,0:T(8,128)S(1)} %collective-permute-done.7.refs_5_), channel_id=1, source_target_pairs={{0,1},{1,0},{2,3},{3,2},{4,5},{5,4},{6,7},{7,6},{8,9},{9,8},{10,11... | collective-permute-start | bytes 196616 | tf_op jit(solution)/shard_map/ppermute | solution.py:218
  15.6 1.9 %collective-permute-start.8 = (f32[4,32,128]{2,1,0:T(8,128)S(1)}, f32[4,32,128]{2,1,0:T(8,128)S(1)}, u32[]{:S(2)}, u32[]{:S(2)}) collective-permute-start(f32[4,32,128]{2,1,0:T(8,128)S(1)} %collective-permute-done.6.refs_4_), channel_id=1, source_target_pairs={{0,1},{1,0},{2,3},{3,2},{4,5},{5,4},{6,7},{7,6},{8,9},{9,8},{10,11... | collective-permute-start | bytes 196616 | tf_op jit(solution)/shard_map/ppermute | solution.py:218
  16.5 1.3 %collective-permute-start.9 = (f32[4,32,128]{2,1,0:T(8,128)S(1)}, f32[4,32,128]{2,1,0:T(8,128)S(1)}, u32[]{:S(2)}, u32[]{:S(2)}) collective-permute-start(f32[4,32,128]{2,1,0:T(8,128)S(1)} %collective-permute-done.5.refs_3_), channel_id=1, source_target_pairs={{0,1},{1,0},{2,3},{3,2},{4,5},{5,4},{6,7},{7,6},{8,9},{9,8},{10,11... | collective-permute-start | bytes 196616 | tf_op jit(solution)/shard_map/ppermute | solution.py:218
  18.2 5.1 %collective-permute-start.12 = (f32[4,32,128]{2,1,0:T(8,128)S(1)}, f32[4,32,128]{2,1,0:T(8,128)S(1)}, u32[]{:S(2)}, u32[]{:S(2)}) collective-permute-start(f32[4,32,128]{2,1,0:T(8,128)S(1)} %get-tuple-element.13), channel_id=1, source_target_pairs={{0,7},{1,6},{2,5},{3,4},{4,3},{5,2},{6,1},{7,0},{8,15},{9,14},{10,... | collective-permute-start | bytes 196616 | tf_op jit(solution)/shard_map/ppermute | solution.py:218
  19.1 5.2 %collective-permute-start.14 = (f32[4,32,128]{2,1,0:T(8,128)S(1)}, f32[4,32,128]{2,1,0:T(8,128)S(1)}, u32[]{:S(2)}, u32[]{:S(2)}) collective-permute-start(f32[4,32,128]{2,1,0:T(8,128)S(1)} %get-tuple-element.14), channel_id=1, source_target_pairs={{0,5},{1,2},{2,1},{3,6},{4,7},{5,0},{6,3},{7,4},{8,13},{9,10},{10,... | collective-permute-start | bytes 196616 | tf_op jit(solution)/shard_map/ppermute | solution.py:218
  20.8 3.9 %collective-permute-start.13 = (f32[4,32,128]{2,1,0:T(8,128)S(1)}, f32[4,32,128]{2,1,0:T(8,128)S(1)}, u32[]{:S(2)}, u32[]{:S(2)}) collective-permute-start(f32[4,32,128]{2,1,0:T(8,128)S(1)} %get-tuple-element.15), channel_id=1, source_target_pairs={{0,3},{1,4},{2,7},{3,0},{4,1},{5,6},{6,5},{7,2},{8,11},{9,12},{10,... | collective-permute-start | bytes 196616 | tf_op jit(solution)/shard_map/ppermute | solution.py:218
  21.2 3.5 %collective-permute-start.11 = (f32[4,32,128]{2,1,0:T(8,128)S(1)}, f32[4,32,128]{2,1,0:T(8,128)S(1)}, u32[]{:S(2)}, u32[]{:S(2)}) collective-permute-start(f32[4,32,128]{2,1,0:T(8,128)S(1)} %get-tuple-element.16), channel_id=1, source_target_pairs={{0,1},{1,0},{2,3},{3,2},{4,5},{5,4},{6,7},{7,6},{8,9},{9,8},{10,11... | collective-permute-start | bytes 196616 | tf_op jit(solution)/shard_map/ppermute | solution.py:218
  24.8 5.0 %collective-permute-start.16 = (f32[32,128]{1,0:T(8,128)S(1)}, f32[32,128]{1,0:T(8,128)S(1)}, u32[]{:S(2)}, u32[]{:S(2)}) collective-permute-start(f32[32,128]{1,0:T(8,128)S(1)} %get-tuple-element.17), channel_id=1, source_target_pairs={{0,25},{1,24},{2,27},{3,26},{4,29},{5,28},{6,31},{7,30},{8,17},{9,... | collective-permute-start | bytes 49160 | tf_op jit(solution)/shard_map/ppermute | solution.py:218
  26.4 4.1 %collective-permute-start.18 = (f32[32,128]{1,0:T(8,128)S(1)}, f32[32,128]{1,0:T(8,128)S(1)}, u32[]{:S(2)}, u32[]{:S(2)}) collective-permute-start(f32[32,128]{1,0:T(8,128)S(1)} %get-tuple-element.18), channel_id=1, source_target_pairs={{0,17},{1,16},{2,19},{3,18},{4,21},{5,20},{6,23},{7,22},{8,25},{9,... | collective-permute-start | bytes 49160 | tf_op jit(solution)/shard_map/ppermute | solution.py:218
  26.4 4.1 %collective-permute-start.17 = (f32[32,128]{1,0:T(8,128)S(1)}, f32[32,128]{1,0:T(8,128)S(1)}, u32[]{:S(2)}, u32[]{:S(2)}) collective-permute-start(f32[32,128]{1,0:T(8,128)S(1)} %get-tuple-element.19), channel_id=1, source_target_pairs={{0,9},{1,8},{2,11},{3,10},{4,13},{5,12},{6,15},{7,14},{8,1},{9,0},... | collective-permute-start | bytes 49160 | tf_op jit(solution)/shard_map/ppermute | solution.py:218
  28.7 1.8 %collective-permute-start.15 = (f32[32,128]{1,0:T(8,128)S(1)}, f32[32,128]{1,0:T(8,128)S(1)}, u32[]{:S(2)}, u32[]{:S(2)}) collective-permute-start(f32[32,128]{1,0:T(8,128)S(1)} %get-tuple-element.20), channel_id=1, source_target_pairs={{0,1},{1,0},{2,3},{3,2},{4,5},{5,4},{6,7},{7,6},{8,9},{9,8},{10,11... | collective-permute-start | bytes 49160 | tf_op jit(solution)/shard_map/ppermute | solution.py:218

commit v7 on v6

--- a/solution.py
+++ b/solution.py
@@ -222,11 +222,29 @@
     return [*range(far - 2), far - 1, far - 2]
 
 
-def swap_sum(parts, pairs, virts, which, marks):
+def swap_parts(parts, pairs, virts, which, marks):
     last = len(marks) - 1
     order = (0, last, *range(1, last))
-    received = [swap(parts[marks.index(mark)], pairs, virts, 1, **{which: mark}) for mark in order]
-    return sum(received[1:], received[0])
+    return [swap(parts[marks.index(mark)], pairs, virts, 1, **{which: mark}) for mark in order]
+
+
+def sum_kernel(*refs):
+    parts, (result, total, copied) = refs[:-3], refs[-3:]
+    total[...] = sum((part[...] for part in parts[1:]), parts[0][...])
+    copy = pltpu.make_async_copy(total, result, copied)
+    copy.start()
+    copy.wait()
+
+
+def last_sum(parts):
+    shape, dtype = parts[0].shape, parts[0].dtype
+    return pl.pallas_call(
+        sum_kernel,
+        out_shape=jax.ShapeDtypeStruct(shape, dtype),
+        in_specs=[VMEM] * len(parts),
+        out_specs=pl.BlockSpec(memory_space=pltpu.HBM),
+        scratch_shapes=[pltpu.VMEM(shape, dtype), pltpu.SemaphoreType.DMA],
+    )(*parts)
 
 
 def shards(t2_amplitudes, integral_tiles, out_tiles, in_tiles, tile_counts):
@@ -253,8 +271,10 @@
         for mask in range(virts)
     ]
     partial_sums = local_terms(codes, owners, halves, rows, local_tiles)
-    line_sums = swap_sum(partial_sums.reshape((NEAR, pairs // NEAR) + mine.shape), pairs, virts, "step", list(range(NEAR)))
-    summed = swap_sum(line_sums, pairs, virts, "far", order)
+    parts = partial_sums.reshape((NEAR, pairs // NEAR) + mine.shape)
+    line_parts = swap_parts(parts, pairs, virts, "step", list(range(NEAR)))
+    line_sums = sum(line_parts[1:], line_parts[0])
+    summed = last_sum(swap_parts(line_sums, pairs, virts, "far", order))
     return summed.reshape(local_tiles, rows, W).transpose(1, 0, 2).reshape(rows, columns)
 
 

time: 31.3 us -> 34.6 us (1.11)
  Pallas kernels: 2.15 us -> 3.54 us
  waiting for transfers between devices: 9.81 us -> 11 us
  local copies, waits for them, and re-layouts: 0.03 us -> 1.21 us
  other arithmetic: 0.64 us -> 0.02 us
    pallas_call x0 -> x1, Pallas kernels: none -> 1.39 us  [last_sum(): pl.pallas_call(sum_kernel, out_shape=jax.ShapeDtypeStruct(shape, dtype),...]
    unnamed x0 -> x8, local copies, waits for them, and re-layouts: none -> 1.19 us
    ppermute x19, waiting for transfers between devices: 9.81 us -> 11 us  [swap(): return lax.ppermute(value, ('pair', 'virt'), routes)]
    add x2 -> x1, other arithmetic: 0.63 us -> 0.02 us  [shards(): line_sums = sum(line_parts[1:], line_parts[0])]
  transfers between devices with their start and end apart: 19 -> 19, of which waited for: 10 -> 9; matrix products, arithmetic and copies ran while one was open for 0% -> 0% of each run, Pallas kernels for 6% -> 5%
where the time goes in v7:
time: 34.6 us; the launch traced here: 34.3 us
  starting transfers between devices  17.8 us (51%)
  waiting for transfers between devices  11 us (32%)
  Pallas kernels  3.54 us (10%)
  local copies, waits for them, and re-layouts  1.21 us (3%)
  between operations  0.77 us (2%)
    ppermute x19, starting transfers between devices, swap(): return lax.ppermute(value, ('pair', 'virt'), routes)  17.8 us
    ppermute x19, waiting for transfers between devices, swap(): return lax.ppermute(value, ('pair', 'virt'), routes)  11 us
    pallas_call x1, Pallas kernels, prepare(): pl.pallas_call(kernel, out_shape=(jax.ShapeDtypeStruct((slots, W, 2 * W),...  1.43 us
    pallas_call x1, Pallas kernels, last_sum(): pl.pallas_call(sum_kernel, out_shape=jax.ShapeDtypeStruct(shape, dtype),...  1.39 us
    unnamed x8, local copies, waits for them, and re-layouts  1.19 us
  transfers between devices with their start and end apart: 19, of which 9 were waited for; matrix products, arithmetic and copies ran while one was open for 0% of the time, Pallas kernels for 5%

profile of v7, /device:TPU:0, one launch (start us, length us, event | category | flops | bytes accessed | tf_op | source)
XLA Modules:
  0.0 34.3 jit_solution(11337193710344407524)
XLA Ops:
  0.0 0.5 %collective-permute-start = (f32[32,128]{1,0:T(8,128)}, f32[32,128]{1,0:T(8,128)S(1)}, u32[]{:S(2)}, u32[]{:S(2)}) collective-permute-start(f32[32,128]{1,0:T(8,128)} %bitcast.32), channel_id=1, source_target_pairs={{0,1},{1,0},{2,3},{3,2},{4,5},{5,4},{6,7},{7,6},{8,9},{9,8},{10,11... | collective-permute-start | bytes 49160 | tf_op jit(solution)/shard_map/ppermute | solution.py:218
  0.5 3.7 %collective-permute-start.3 = (f32[32,128]{1,0:T(8,128)}, f32[32,128]{1,0:T(8,128)S(1)}, u32[]{:S(2)}, u32[]{:S(2)}) collective-permute-start(f32[32,128]{1,0:T(8,128)} %bitcast.33), channel_id=1, source_target_pairs={{0,17},{1,16},{2,19},{3,18},{4,21},{5,20},{6,23},{7,22},{8,25},{9,... | collective-permute-start | bytes 49160 | tf_op jit(solution)/shard_map/ppermute | solution.py:218
  4.2 1.0 %collective-permute-start.2 = (f32[32,128]{1,0:T(8,128)}, f32[32,128]{1,0:T(8,128)S(1)}, u32[]{:S(2)}, u32[]{:S(2)}) collective-permute-start(f32[32,128]{1,0:T(8,128)} %bitcast.34), channel_id=1, source_target_pairs={{0,25},{1,24},{2,27},{3,26},{4,29},{5,28},{6,31},{7,30},{8,17},{9,... | collective-permute-start | bytes 49160 | tf_op jit(solution)/shard_map/ppermute | solution.py:218
  5.2 0.2 collective-permute-start.1
  6.0 1.4 %shard_map.55 = (bf16[32,128,256]{2,1,0:T(8,128)(2,1)S(1)}, s32[10,32]{1,0:T(8,128)S(4)}) custom-call(s32[1,1]{1,0:T(1,128)S(6)} %copy.8.refs_0_, s32[1,32]{1,0:T(1,128)} %bitcast.30, s32[1,32]{1,0:T(1,128)} %bitcast.31, f32[32,128,128]{2,1,0:T(8,128)} %bitcast.25), custom_call_target="tpu_custom_call" | custom-call | flops 2097152 | bytes 4194304 | tf_op jit(solution)/shard_map/pallas_call | solution.py:82
  7.4 0.0 collective-permute-done
  7.4 0.0 collective-permute-done.3
  7.5 1.9 %collective-permute-done.2 = f32[32,128]{1,0:T(8,128)S(1)} collective-permute-done((f32[32,128]{1,0:T(8,128)}, f32[32,128]{1,0:T(8,128)S(1)}, u32[]{:S(2)}, u32[]{:S(2)}) %collective-permute-start.2) | collective-permute-done | bytes 16416 | tf_op jit(solution)/shard_map/ppermute | solution.py:218
  9.3 0.0 collective-permute-done.1
  9.4 2.2 %collective-permute-start.7 = (f32[4,32,128]{2,1,0:T(8,128)S(1)}, f32[4,32,128]{2,1,0:T(8,128)S(1)}, u32[]{:S(2)}, u32[]{:S(2)}) collective-permute-start(f32[4,32,128]{2,1,0:T(8,128)S(1)} %pad_maximum_fusion.refs_3_), channel_id=1, source_target_pairs={{0,7},{1,6},{2,5},{3,4},{4,3},{5,2},{6,1},{7,0},{8,15},{9,14},{10,... | collective-permute-start | bytes 196616 | tf_op jit(solution)/shard_map/ppermute | solution.py:218
  11.6 0.5 %collective-permute-start.6 = (f32[4,32,128]{2,1,0:T(8,128)S(1)}, f32[4,32,128]{2,1,0:T(8,128)S(1)}, u32[]{:S(2)}, u32[]{:S(2)}) collective-permute-start(f32[4,32,128]{2,1,0:T(8,128)S(1)} %pad_maximum_fusion.refs_3_), channel_id=1, source_target_pairs={{0,5},{1,2},{2,1},{3,6},{4,7},{5,0},{6,3},{7,4},{8,13},{9,10},{10,... | collective-permute-start | bytes 196616 | tf_op jit(solution)/shard_map/ppermute | solution.py:218
  12.1 0.2 collective-permute-start.5
  12.3 0.4 %collective-permute-start.4 = (f32[4,32,128]{2,1,0:T(8,128)S(1)}, f32[4,32,128]{2,1,0:T(8,128)S(1)}, u32[]{:S(2)}, u32[]{:S(2)}) collective-permute-start(f32[4,32,128]{2,1,0:T(8,128)S(1)} %pad_maximum_fusion.refs_3_), channel_id=1, source_target_pairs={{0,1},{1,0},{2,3},{3,2},{4,5},{5,4},{6,7},{7,6},{8,9},{9,8},{10,11... | collective-permute-start | bytes 196616 | tf_op jit(solution)/shard_map/ppermute | solution.py:218
  12.8 1.7 %collective-permute-done.7.refs_5_ = f32[4,32,128]{2,1,0:T(8,128)S(1)} collective-permute-done((f32[4,32,128]{2,1,0:T(8,128)S(1)}, f32[4,32,128]{2,1,0:T(8,128)S(1)}, u32[]{:S(2)}, u32[]{:S(2)}) %collective-permute-start.7) | collective-permute-done | bytes 65568 | tf_op jit(solution)/shard_map/ppermute | solution.py:218
  14.4 0.3 collective-permute-start.10
  14.8 0.8 %collective-permute-done.6.refs_4_ = f32[4,32,128]{2,1,0:T(8,128)S(1)} collective-permute-done((f32[4,32,128]{2,1,0:T(8,128)S(1)}, f32[4,32,128]{2,1,0:T(8,128)S(1)}, u32[]{:S(2)}, u32[]{:S(2)}) %collective-permute-start.6) | collective-permute-done | bytes 65568 | tf_op jit(solution)/shard_map/ppermute | solution.py:218
  15.6 1.0 %collective-permute-start.8 = (f32[4,32,128]{2,1,0:T(8,128)S(1)}, f32[4,32,128]{2,1,0:T(8,128)S(1)}, u32[]{:S(2)}, u32[]{:S(2)}) collective-permute-start(f32[4,32,128]{2,1,0:T(8,128)S(1)} %collective-permute-done.6.refs_4_), channel_id=1, source_target_pairs={{0,1},{1,0},{2,3},{3,2},{4,5},{5,4},{6,7},{7,6},{8,9},{9,8},{10,11... | collective-permute-start | bytes 196616 | tf_op jit(solution)/shard_map/ppermute | solution.py:218
  16.5 0.0 collective-permute-done.5.refs_3_
  16.5 0.0 collective-permute-start.9
  16.5 0.0 collective-permute-done.4.refs_2_
  16.5 0.3 %shard_map.56.refs_2_ = f32[9,64,128]{2,1,0:T(8,128)S(1)} custom-call(s32[10,32]{1,0:T(8,128)S(4)} %get-tuple-element.9.refs_0_, bf16[32,128,256]{2,1,0:T(8,128)(2,1)S(1)} %get-tuple-element.11.refs_1_, f32[4,32,128]{2,1,0:T(8,128)S(1)} %collective-permute-done.4.refs_2_, f32[4,32,128]{2,1,0:T(8,128)S(1)} %collective-permute-done.5.refs_3_, ...), custom_call_target="tpu_custom_call" | custom-call | flops 268435456 | bytes 2097152 | tf_op jit(solution)/shard_map/pallas_call | solution.py:189
  16.9 0.0 collective-permute-done.10.refs_6_
  16.9 0.5 %collective-permute-done.8.refs_4_ = f32[4,32,128]{2,1,0:T(8,128)S(1)} collective-permute-done((f32[4,32,128]{2,1,0:T(8,128)S(1)}, f32[4,32,128]{2,1,0:T(8,128)S(1)}, u32[]{:S(2)}, u32[]{:S(2)}) %collective-permute-start.8) | collective-permute-done | bytes 65568 | tf_op jit(solution)/shard_map/ppermute | solution.py:218
  17.4 0.4 %collective-permute-done.9.refs_5_ = f32[4,32,128]{2,1,0:T(8,128)S(1)} collective-permute-done((f32[4,32,128]{2,1,0:T(8,128)S(1)}, f32[4,32,128]{2,1,0:T(8,128)S(1)}, u32[]{:S(2)}, u32[]{:S(2)}) %collective-permute-start.9) | collective-permute-done | bytes 65568 | tf_op jit(solution)/shard_map/ppermute | solution.py:218
  17.8 0.4 %shard_map.57 = f32[16,32,128]{2,1,0:T(8,128)S(1)} custom-call(s32[10,32]{1,0:T(8,128)S(4)} %get-tuple-element.9.refs_0_, bf16[32,128,256]{2,1,0:T(8,128)(2,1)S(1)} %get-tuple-element.11.refs_1_, f32[9,64,128]{2,1,0:T(8,128)S(1)} %shard_map.56.refs_2_, f32[4,32,128]{2,1,0:T(8,128)S(1)} %pad_maximum_fusion.refs_3_, ...), custom_call_target="tpu_custom_call" | custom-call | flops 268435456 | bytes 2097152 | tf_op jit(solution)/shard_map/pallas_call | solution.py:198
  18.2 0.9 %collective-permute-start.12 = (f32[4,32,128]{2,1,0:T(8,128)S(1)}, f32[4,32,128]{2,1,0:T(8,128)S(1)}, u32[]{:S(2)}, u32[]{:S(2)}) collective-permute-start(f32[4,32,128]{2,1,0:T(8,128)S(1)} %get-tuple-element.13), channel_id=1, source_target_pairs={{0,7},{1,6},{2,5},{3,4},{4,3},{5,2},{6,1},{7,0},{8,15},{9,14},{10,... | collective-permute-start | bytes 196616 | tf_op jit(solution)/shard_map/ppermute | solution.py:218
  19.1 1.4 %collective-permute-start.14 = (f32[4,32,128]{2,1,0:T(8,128)S(1)}, f32[4,32,128]{2,1,0:T(8,128)S(1)}, u32[]{:S(2)}, u32[]{:S(2)}) collective-permute-start(f32[4,32,128]{2,1,0:T(8,128)S(1)} %get-tuple-element.14), channel_id=1, source_target_pairs={{0,5},{1,2},{2,1},{3,6},{4,7},{5,0},{6,3},{7,4},{8,13},{9,10},{10,... | collective-permute-start | bytes 196616 | tf_op jit(solution)/shard_map/ppermute | solution.py:218
  20.5 1.0 %collective-permute-start.13 = (f32[4,32,128]{2,1,0:T(8,128)S(1)}, f32[4,32,128]{2,1,0:T(8,128)S(1)}, u32[]{:S(2)}, u32[]{:S(2)}) collective-permute-start(f32[4,32,128]{2,1,0:T(8,128)S(1)} %get-tuple-element.15), channel_id=1, source_target_pairs={{0,3},{1,4},{2,7},{3,0},{4,1},{5,6},{6,5},{7,2},{8,11},{9,12},{10,... | collective-permute-start | bytes 196616 | tf_op jit(solution)/shard_map/ppermute | solution.py:218
  21.5 0.0 collective-permute-start.11
  21.6 1.5 %collective-permute-done.12 = f32[4,32,128]{2,1,0:T(8,128)S(1)} collective-permute-done((f32[4,32,128]{2,1,0:T(8,128)S(1)}, f32[4,32,128]{2,1,0:T(8,128)S(1)}, u32[]{:S(2)}, u32[]{:S(2)}) %collective-permute-start.12) | collective-permute-done | bytes 65568 | tf_op jit(solution)/shard_map/ppermute | solution.py:218
  23.1 1.1 %collective-permute-done.14 = f32[4,32,128]{2,1,0:T(8,128)S(1)} collective-permute-done((f32[4,32,128]{2,1,0:T(8,128)S(1)}, f32[4,32,128]{2,1,0:T(8,128)S(1)}, u32[]{:S(2)}, u32[]{:S(2)}) %collective-permute-start.14) | collective-permute-done | bytes 65568 | tf_op jit(solution)/shard_map/ppermute | solution.py:218
  24.2 0.5 %collective-permute-done.13 = f32[4,32,128]{2,1,0:T(8,128)S(1)} collective-permute-done((f32[4,32,128]{2,1,0:T(8,128)S(1)}, f32[4,32,128]{2,1,0:T(8,128)S(1)}, u32[]{:S(2)}, u32[]{:S(2)}) %collective-permute-start.13) | collective-permute-done | bytes 65568 | tf_op jit(solution)/shard_map/ppermute | solution.py:218
  24.7 0.0 collective-permute-done.11
  24.8 0.7 %collective-permute-start.18 = (f32[32,128]{1,0:T(8,128)S(1)}, f32[32,128]{1,0:T(8,128)S(1)}, u32[]{:S(2)}, u32[]{:S(2)}) collective-permute-start(f32[32,128]{1,0:T(8,128)S(1)} %get-tuple-element.17), channel_id=1, source_target_pairs={{0,17},{1,16},{2,19},{3,18},{4,21},{5,20},{6,23},{7,22},{8,25},{9,... | collective-permute-start | bytes 49160 | tf_op jit(solution)/shard_map/ppermute | solution.py:218
  25.5 1.2 %collective-permute-start.17 = (f32[32,128]{1,0:T(8,128)S(1)}, f32[32,128]{1,0:T(8,128)S(1)}, u32[]{:S(2)}, u32[]{:S(2)}) collective-permute-start(f32[32,128]{1,0:T(8,128)S(1)} %get-tuple-element.18), channel_id=1, source_target_pairs={{0,9},{1,8},{2,11},{3,10},{4,13},{5,12},{6,15},{7,14},{8,1},{9,0},... | collective-permute-start | bytes 49160 | tf_op jit(solution)/shard_map/ppermute | solution.py:218
  26.7 1.9 %collective-permute-start.16 = (f32[32,128]{1,0:T(8,128)S(1)}, f32[32,128]{1,0:T(8,128)S(1)}, u32[]{:S(2)}, u32[]{:S(2)}) collective-permute-start(f32[32,128]{1,0:T(8,128)S(1)} %get-tuple-element.19), channel_id=1, source_target_pairs={{0,25},{1,24},{2,27},{3,26},{4,29},{5,28},{6,31},{7,30},{8,17},{9,... | collective-permute-start | bytes 49160 | tf_op jit(solution)/shard_map/ppermute | solution.py:218
  28.7 0.4 %collective-permute-start.15 = (f32[32,128]{1,0:T(8,128)S(1)}, f32[32,128]{1,0:T(8,128)S(1)}, u32[]{:S(2)}, u32[]{:S(2)}) collective-permute-start(f32[32,128]{1,0:T(8,128)S(1)} %get-tuple-element.20), channel_id=1, source_target_pairs={{0,1},{1,0},{2,3},{3,2},{4,5},{5,4},{6,7},{7,6},{8,9},{9,8},{10,11... | collective-permute-start | bytes 49160 | tf_op jit(solution)/shard_map/ppermute | solution.py:218
  29.1 0.0 collective-permute-done.18.refs_3_
  29.1 0.0 copy-start
  29.1 0.0 collective-permute-done.17.refs_2_
  29.1 0.0 copy-start.1
  29.1 2.6 %collective-permute-done.16.refs_1_ = f32[32,128]{1,0:T(8,128)S(1)} collective-permute-done((f32[32,128]{1,0:T(8,128)S(1)}, f32[32,128]{1,0:T(8,128)S(1)}, u32[]{:S(2)}, u32[]{:S(2)}) %collective-permute-start.16) | collective-permute-done | bytes 16416 | tf_op jit(solution)/shard_map/ppermute | solution.py:218
  31.7 0.0 copy-start.2
  31.7 0.0 collective-permute-done.15.refs_0_
  31.7 0.0 copy-done
  31.7 0.0 copy-done.1
  31.7 0.6 %copy-done.2 = f32[32,128]{1,0:T(8,128)} copy-done((f32[32,128]{1,0:T(8,128)}, f32[32,128]{1,0:T(8,128)S(1)}, u32[]{:S(2)}) %copy-start.2) | copy-done | bytes 16408
  32.3 0.0 copy-start.3
  32.3 0.6 %copy-done.3 = f32[32,128]{1,0:T(8,128)} copy-done((f32[32,128]{1,0:T(8,128)}, f32[32,128]{1,0:T(8,128)S(1)}, u32[]{:S(2)}) %copy-start.3) | copy-done | bytes 16408
  32.9 1.4 %shard_map.58 = f32[32,128]{1,0:T(8,128)} custom-call(f32[32,128]{1,0:T(8,128)} %copy-done.3, f32[32,128]{1,0:T(8,128)} %copy-done.2, f32[32,128]{1,0:T(8,128)} %copy-done.1, f32[32,128]{1,0:T(8,128)} %copy-done), custom_call_target="tpu_custom_call" | custom-call | tf_op jit(solution)/shard_map/pallas_call | solution.py:241
  (4 shorter events, 0.1 us)
Async XLA Ops:
  0.0 7.4 %collective-permute-start = (f32[32,128]{1,0:T(8,128)}, f32[32,128]{1,0:T(8,128)S(1)}, u32[]{:S(2)}, u32[]{:S(2)}) collective-permute-start(f32[32,128]{1,0:T(8,128)} %bitcast.32), channel_id=1, source_target_pairs={{0,1},{1,0},{2,3},{3,2},{4,5},{5,4},{6,7},{7,6},{8,9},{9,8},{10,11... | collective-permute-start | bytes 49160 | tf_op jit(solution)/shard_map/ppermute | solution.py:218
  0.5 7.0 %collective-permute-start.3 = (f32[32,128]{1,0:T(8,128)}, f32[32,128]{1,0:T(8,128)S(1)}, u32[]{:S(2)}, u32[]{:S(2)}) collective-permute-start(f32[32,128]{1,0:T(8,128)} %bitcast.33), channel_id=1, source_target_pairs={{0,17},{1,16},{2,19},{3,18},{4,21},{5,20},{6,23},{7,22},{8,25},{9,... | collective-permute-start | bytes 49160 | tf_op jit(solution)/shard_map/ppermute | solution.py:218
  4.2 5.2 %collective-permute-start.2 = (f32[32,128]{1,0:T(8,128)}, f32[32,128]{1,0:T(8,128)S(1)}, u32[]{:S(2)}, u32[]{:S(2)}) collective-permute-start(f32[32,128]{1,0:T(8,128)} %bitcast.34), channel_id=1, source_target_pairs={{0,25},{1,24},{2,27},{3,26},{4,29},{5,28},{6,31},{7,30},{8,17},{9,... | collective-permute-start | bytes 49160 | tf_op jit(solution)/shard_map/ppermute | solution.py:218
  5.2 4.2 %collective-permute-start.1 = (f32[32,128]{1,0:T(8,128)}, f32[32,128]{1,0:T(8,128)S(1)}, u32[]{:S(2)}, u32[]{:S(2)}) collective-permute-start(f32[32,128]{1,0:T(8,128)} %bitcast.35), channel_id=1, source_target_pairs={{0,9},{1,8},{2,11},{3,10},{4,13},{5,12},{6,15},{7,14},{8,1},{9,0},... | collective-permute-start | bytes 49160 | tf_op jit(solution)/shard_map/ppermute | solution.py:218
  9.4 5.1 %collective-permute-start.7 = (f32[4,32,128]{2,1,0:T(8,128)S(1)}, f32[4,32,128]{2,1,0:T(8,128)S(1)}, u32[]{:S(2)}, u32[]{:S(2)}) collective-permute-start(f32[4,32,128]{2,1,0:T(8,128)S(1)} %pad_maximum_fusion.refs_3_), channel_id=1, source_target_pairs={{0,7},{1,6},{2,5},{3,4},{4,3},{5,2},{6,1},{7,0},{8,15},{9,14},{10,... | collective-permute-start | bytes 196616 | tf_op jit(solution)/shard_map/ppermute | solution.py:218
  11.6 4.0 %collective-permute-start.6 = (f32[4,32,128]{2,1,0:T(8,128)S(1)}, f32[4,32,128]{2,1,0:T(8,128)S(1)}, u32[]{:S(2)}, u32[]{:S(2)}) collective-permute-start(f32[4,32,128]{2,1,0:T(8,128)S(1)} %pad_maximum_fusion.refs_3_), channel_id=1, source_target_pairs={{0,5},{1,2},{2,1},{3,6},{4,7},{5,0},{6,3},{7,4},{8,13},{9,10},{10,... | collective-permute-start | bytes 196616 | tf_op jit(solution)/shard_map/ppermute | solution.py:218
  12.1 4.4 %collective-permute-start.5 = (f32[4,32,128]{2,1,0:T(8,128)S(1)}, f32[4,32,128]{2,1,0:T(8,128)S(1)}, u32[]{:S(2)}, u32[]{:S(2)}) collective-permute-start(f32[4,32,128]{2,1,0:T(8,128)S(1)} %pad_maximum_fusion.refs_3_), channel_id=1, source_target_pairs={{0,3},{1,4},{2,7},{3,0},{4,1},{5,6},{6,5},{7,2},{8,11},{9,12},{10,... | collective-permute-start | bytes 196616 | tf_op jit(solution)/shard_map/ppermute | solution.py:218
  12.3 4.2 %collective-permute-start.4 = (f32[4,32,128]{2,1,0:T(8,128)S(1)}, f32[4,32,128]{2,1,0:T(8,128)S(1)}, u32[]{:S(2)}, u32[]{:S(2)}) collective-permute-start(f32[4,32,128]{2,1,0:T(8,128)S(1)} %pad_maximum_fusion.refs_3_), channel_id=1, source_target_pairs={{0,1},{1,0},{2,3},{3,2},{4,5},{5,4},{6,7},{7,6},{8,9},{9,8},{10,11... | collective-permute-start | bytes 196616 | tf_op jit(solution)/shard_map/ppermute | solution.py:218
  14.4 2.5 %collective-permute-start.10 = (f32[4,32,128]{2,1,0:T(8,128)S(1)}, f32[4,32,128]{2,1,0:T(8,128)S(1)}, u32[]{:S(2)}, u32[]{:S(2)}) collective-permute-start(f32[4,32,128]{2,1,0:T(8,128)S(1)} %collective-permute-done.7.refs_5_), channel_id=1, source_target_pairs={{0,1},{1,0},{2,3},{3,2},{4,5},{5,4},{6,7},{7,6},{8,9},{9,8},{10,11... | collective-permute-start | bytes 196616 | tf_op jit(solution)/shard_map/ppermute | solution.py:218
  15.6 1.9 %collective-permute-start.8 = (f32[4,32,128]{2,1,0:T(8,128)S(1)}, f32[4,32,128]{2,1,0:T(8,128)S(1)}, u32[]{:S(2)}, u32[]{:S(2)}) collective-permute-start(f32[4,32,128]{2,1,0:T(8,128)S(1)} %collective-permute-done.6.refs_4_), channel_id=1, source_target_pairs={{0,1},{1,0},{2,3},{3,2},{4,5},{5,4},{6,7},{7,6},{8,9},{9,8},{10,11... | collective-permute-start | bytes 196616 | tf_op jit(solution)/shard_map/ppermute | solution.py:218
  16.5 1.3 %collective-permute-start.9 = (f32[4,32,128]{2,1,0:T(8,128)S(1)}, f32[4,32,128]{2,1,0:T(8,128)S(1)}, u32[]{:S(2)}, u32[]{:S(2)}) collective-permute-start(f32[4,32,128]{2,1,0:T(8,128)S(1)} %collective-permute-done.5.refs_3_), channel_id=1, source_target_pairs={{0,1},{1,0},{2,3},{3,2},{4,5},{5,4},{6,7},{7,6},{8,9},{9,8},{10,11... | collective-permute-start | bytes 196616 | tf_op jit(solution)/shard_map/ppermute | solution.py:218
  18.2 4.9 %collective-permute-start.12 = (f32[4,32,128]{2,1,0:T(8,128)S(1)}, f32[4,32,128]{2,1,0:T(8,128)S(1)}, u32[]{:S(2)}, u32[]{:S(2)}) collective-permute-start(f32[4,32,128]{2,1,0:T(8,128)S(1)} %get-tuple-element.13), channel_id=1, source_target_pairs={{0,7},{1,6},{2,5},{3,4},{4,3},{5,2},{6,1},{7,0},{8,15},{9,14},{10,... | collective-permute-start | bytes 196616 | tf_op jit(solution)/shard_map/ppermute | solution.py:218
  19.1 5.1 %collective-permute-start.14 = (f32[4,32,128]{2,1,0:T(8,128)S(1)}, f32[4,32,128]{2,1,0:T(8,128)S(1)}, u32[]{:S(2)}, u32[]{:S(2)}) collective-permute-start(f32[4,32,128]{2,1,0:T(8,128)S(1)} %get-tuple-element.14), channel_id=1, source_target_pairs={{0,5},{1,2},{2,1},{3,6},{4,7},{5,0},{6,3},{7,4},{8,13},{9,10},{10,... | collective-permute-start | bytes 196616 | tf_op jit(solution)/shard_map/ppermute | solution.py:218
  20.5 4.2 %collective-permute-start.13 = (f32[4,32,128]{2,1,0:T(8,128)S(1)}, f32[4,32,128]{2,1,0:T(8,128)S(1)}, u32[]{:S(2)}, u32[]{:S(2)}) collective-permute-start(f32[4,32,128]{2,1,0:T(8,128)S(1)} %get-tuple-element.15), channel_id=1, source_target_pairs={{0,3},{1,4},{2,7},{3,0},{4,1},{5,6},{6,5},{7,2},{8,11},{9,12},{10,... | collective-permute-start | bytes 196616 | tf_op jit(solution)/shard_map/ppermute | solution.py:218
  21.5 3.2 %collective-permute-start.11 = (f32[4,32,128]{2,1,0:T(8,128)S(1)}, f32[4,32,128]{2,1,0:T(8,128)S(1)}, u32[]{:S(2)}, u32[]{:S(2)}) collective-permute-start(f32[4,32,128]{2,1,0:T(8,128)S(1)} %get-tuple-element.16), channel_id=1, source_target_pairs={{0,1},{1,0},{2,3},{3,2},{4,5},{5,4},{6,7},{7,6},{8,9},{9,8},{10,11... | collective-permute-start | bytes 196616 | tf_op jit(solution)/shard_map/ppermute | solution.py:218
  24.8 4.3 %collective-permute-start.18 = (f32[32,128]{1,0:T(8,128)S(1)}, f32[32,128]{1,0:T(8,128)S(1)}, u32[]{:S(2)}, u32[]{:S(2)}) collective-permute-start(f32[32,128]{1,0:T(8,128)S(1)} %get-tuple-element.17), channel_id=1, source_target_pairs={{0,17},{1,16},{2,19},{3,18},{4,21},{5,20},{6,23},{7,22},{8,25},{9,... | collective-permute-start | bytes 49160 | tf_op jit(solution)/shard_map/ppermute | solution.py:218
  25.5 3.6 %collective-permute-start.17 = (f32[32,128]{1,0:T(8,128)S(1)}, f32[32,128]{1,0:T(8,128)S(1)}, u32[]{:S(2)}, u32[]{:S(2)}) collective-permute-start(f32[32,128]{1,0:T(8,128)S(1)} %get-tuple-element.18), channel_id=1, source_target_pairs={{0,9},{1,8},{2,11},{3,10},{4,13},{5,12},{6,15},{7,14},{8,1},{9,0},... | collective-permute-start | bytes 49160 | tf_op jit(solution)/shard_map/ppermute | solution.py:218
  26.7 5.0 %collective-permute-start.16 = (f32[32,128]{1,0:T(8,128)S(1)}, f32[32,128]{1,0:T(8,128)S(1)}, u32[]{:S(2)}, u32[]{:S(2)}) collective-permute-start(f32[32,128]{1,0:T(8,128)S(1)} %get-tuple-element.19), channel_id=1, source_target_pairs={{0,25},{1,24},{2,27},{3,26},{4,29},{5,28},{6,31},{7,30},{8,17},{9,... | collective-permute-start | bytes 49160 | tf_op jit(solution)/shard_map/ppermute | solution.py:218
  28.7 3.0 %collective-permute-start.15 = (f32[32,128]{1,0:T(8,128)S(1)}, f32[32,128]{1,0:T(8,128)S(1)}, u32[]{:S(2)}, u32[]{:S(2)}) collective-permute-start(f32[32,128]{1,0:T(8,128)S(1)} %get-tuple-element.20), channel_id=1, source_target_pairs={{0,1},{1,0},{2,3},{3,2},{4,5},{5,4},{6,7},{7,6},{8,9},{9,8},{10,11... | collective-permute-start | bytes 49160 | tf_op jit(solution)/shard_map/ppermute | solution.py:218
  29.1 2.6 %copy-start = (f32[32,128]{1,0:T(8,128)}, f32[32,128]{1,0:T(8,128)S(1)}, u32[]{:S(2)}) copy-start(f32[32,128]{1,0:T(8,128)S(1)} %collective-permute-done.18.refs_3_) | copy-start | bytes 49156
  29.1 2.6 %copy-start.1 = (f32[32,128]{1,0:T(8,128)}, f32[32,128]{1,0:T(8,128)S(1)}, u32[]{:S(2)}) copy-start(f32[32,128]{1,0:T(8,128)S(1)} %collective-permute-done.17.refs_2_) | copy-start | bytes 49156
  31.7 0.6 %copy-start.2 = (f32[32,128]{1,0:T(8,128)}, f32[32,128]{1,0:T(8,128)S(1)}, u32[]{:S(2)}) copy-start(f32[32,128]{1,0:T(8,128)S(1)} %collective-permute-done.16.refs_1_) | copy-start | bytes 49156
  32.3 0.6 %copy-start.3 = (f32[32,128]{1,0:T(8,128)}, f32[32,128]{1,0:T(8,128)S(1)}, u32[]{:S(2)}) copy-start(f32[32,128]{1,0:T(8,128)S(1)} %collective-permute-done.15.refs_0_) | copy-start | bytes 49156

commit v8 on v7

--- a/solution.py
+++ b/solution.py
@@ -222,9 +222,7 @@
     return [*range(far - 2), far - 1, far - 2]
 
 
-def swap_parts(parts, pairs, virts, which, marks):
-    last = len(marks) - 1
-    order = (0, last, *range(1, last))
+def swap_parts(parts, pairs, virts, which, marks, order):
     return [swap(parts[marks.index(mark)], pairs, virts, 1, **{which: mark}) for mark in order]
 
 
@@ -244,6 +242,7 @@
         in_specs=[VMEM] * len(parts),
         out_specs=pl.BlockSpec(memory_space=pltpu.HBM),
         scratch_shapes=[pltpu.VMEM(shape, dtype), pltpu.SemaphoreType.DMA],
+        compiler_params=pltpu.CompilerParams(vmem_limit_bytes=2 * 1024 * 1024),
     )(*parts)
 
 
@@ -272,9 +271,10 @@
     ]
     partial_sums = local_terms(codes, owners, halves, rows, local_tiles)
     parts = partial_sums.reshape((NEAR, pairs // NEAR) + mine.shape)
-    line_parts = swap_parts(parts, pairs, virts, "step", list(range(NEAR)))
+    steps = list(range(NEAR))
+    line_parts = swap_parts(parts, pairs, virts, "step", steps, (0, 3, 1, 2))
     line_sums = sum(line_parts[1:], line_parts[0])
-    summed = last_sum(swap_parts(line_sums, pairs, virts, "far", order))
+    summed = last_sum(swap_parts(line_sums, pairs, virts, "far", order, range(len(order))))
     return summed.reshape(local_tiles, rows, W).transpose(1, 0, 2).reshape(rows, columns)
 
 

time: 34.6 us -> 31.4 us (0.908); the launches traced: 34.3 us -> 31.4 us
  local copies, waits for them, and re-layouts: 1.21 us -> 0.03 us
  Pallas kernels: 3.54 us -> 2.4 us
  waiting for transfers between devices: 11 us -> 10.5 us
    unnamed x8 -> x0, local copies, waits for them, and re-layouts: 1.19 us -> none
    pallas_call x1, Pallas kernels: 1.39 us -> 0.62 us  [last_sum(): pl.pallas_call(sum_kernel, out_shape=jax.ShapeDtypeStruct(shape, dtype),...]
    ppermute x19, waiting for transfers between devices: 11 us -> 10.5 us  [swap(): return lax.ppermute(value, ('pair', 'virt'), routes)]
  transfers between devices with their start and end apart: 19 -> 19, of which waited for: 9 -> 10; matrix products, arithmetic and copies ran while one was open for 0% -> 0% of each run, Pallas kernels for 5% -> 4%
where the time goes in v8:
time: 31.4 us
  starting transfers between devices  17.7 us (56%)
  waiting for transfers between devices  10.5 us (33%)
  Pallas kernels  2.4 us (8%)
  between operations  0.74 us (2%)
    ppermute x19, starting transfers between devices, swap(): return lax.ppermute(value, ('pair', 'virt'), routes)  17.7 us
    ppermute x19, waiting for transfers between devices, swap(): return lax.ppermute(value, ('pair', 'virt'), routes)  10.5 us
    pallas_call x1, Pallas kernels, prepare(): pl.pallas_call(kernel, out_shape=(jax.ShapeDtypeStruct((slots, W, 2 * W),...  1.34 us
  transfers between devices with their start and end apart: 19, of which 10 were waited for; matrix products, arithmetic and copies ran while one was open for 0% of the time, Pallas kernels for 4%

profile of v8, /device:TPU:0, one launch (start us, length us, event | category | flops | bytes accessed | tf_op | source)
XLA Modules:
  0.0 31.4 jit_solution(16040032696961398191)
XLA Ops:
  0.0 0.5 %collective-permute-start = (f32[32,128]{1,0:T(8,128)}, f32[32,128]{1,0:T(8,128)S(1)}, u32[]{:S(2)}, u32[]{:S(2)}) collective-permute-start(f32[32,128]{1,0:T(8,128)} %bitcast.32), channel_id=1, source_target_pairs={{0,1},{1,0},{2,3},{3,2},{4,5},{5,4},{6,7},{7,6},{8,9},{9,8},{10,11... | collective-permute-start | bytes 49160 | tf_op jit(solution)/shard_map/ppermute | solution.py:218
  0.5 3.7 %collective-permute-start.3 = (f32[32,128]{1,0:T(8,128)}, f32[32,128]{1,0:T(8,128)S(1)}, u32[]{:S(2)}, u32[]{:S(2)}) collective-permute-start(f32[32,128]{1,0:T(8,128)} %bitcast.33), channel_id=1, source_target_pairs={{0,17},{1,16},{2,19},{3,18},{4,21},{5,20},{6,23},{7,22},{8,25},{9,... | collective-permute-start | bytes 49160 | tf_op jit(solution)/shard_map/ppermute | solution.py:218
  4.2 1.0 %collective-permute-start.2 = (f32[32,128]{1,0:T(8,128)}, f32[32,128]{1,0:T(8,128)S(1)}, u32[]{:S(2)}, u32[]{:S(2)}) collective-permute-start(f32[32,128]{1,0:T(8,128)} %bitcast.34), channel_id=1, source_target_pairs={{0,25},{1,24},{2,27},{3,26},{4,29},{5,28},{6,31},{7,30},{8,17},{9,... | collective-permute-start | bytes 49160 | tf_op jit(solution)/shard_map/ppermute | solution.py:218
  5.2 0.2 collective-permute-start.1
  6.0 1.3 %shard_map.55 = (bf16[32,128,256]{2,1,0:T(8,128)(2,1)S(1)}, s32[10,32]{1,0:T(8,128)S(4)}) custom-call(s32[1,1]{1,0:T(1,128)S(6)} %copy.8.refs_0_, s32[1,32]{1,0:T(1,128)} %bitcast.30, s32[1,32]{1,0:T(1,128)} %bitcast.31, f32[32,128,128]{2,1,0:T(8,128)} %bitcast.25), custom_call_target="tpu_custom_call" | custom-call | flops 2097152 | bytes 4194304 | tf_op jit(solution)/shard_map/pallas_call | solution.py:82
  7.3 0.0 collective-permute-done
  7.4 0.0 collective-permute-done.3
  7.4 2.0 %collective-permute-done.2 = f32[32,128]{1,0:T(8,128)S(1)} collective-permute-done((f32[32,128]{1,0:T(8,128)}, f32[32,128]{1,0:T(8,128)S(1)}, u32[]{:S(2)}, u32[]{:S(2)}) %collective-permute-start.2) | collective-permute-done | bytes 16416 | tf_op jit(solution)/shard_map/ppermute | solution.py:218
  9.3 0.0 collective-permute-done.1
  9.4 2.2 %collective-permute-start.7 = (f32[4,32,128]{2,1,0:T(8,128)S(1)}, f32[4,32,128]{2,1,0:T(8,128)S(1)}, u32[]{:S(2)}, u32[]{:S(2)}) collective-permute-start(f32[4,32,128]{2,1,0:T(8,128)S(1)} %pad_maximum_fusion.refs_3_), channel_id=1, source_target_pairs={{0,7},{1,6},{2,5},{3,4},{4,3},{5,2},{6,1},{7,0},{8,15},{9,14},{10,... | collective-permute-start | bytes 196616 | tf_op jit(solution)/shard_map/ppermute | solution.py:218
  11.6 0.5 %collective-permute-start.6 = (f32[4,32,128]{2,1,0:T(8,128)S(1)}, f32[4,32,128]{2,1,0:T(8,128)S(1)}, u32[]{:S(2)}, u32[]{:S(2)}) collective-permute-start(f32[4,32,128]{2,1,0:T(8,128)S(1)} %pad_maximum_fusion.refs_3_), channel_id=1, source_target_pairs={{0,5},{1,2},{2,1},{3,6},{4,7},{5,0},{6,3},{7,4},{8,13},{9,10},{10,... | collective-permute-start | bytes 196616 | tf_op jit(solution)/shard_map/ppermute | solution.py:218
  12.1 0.2 collective-permute-start.5
  12.3 0.4 %collective-permute-start.4 = (f32[4,32,128]{2,1,0:T(8,128)S(1)}, f32[4,32,128]{2,1,0:T(8,128)S(1)}, u32[]{:S(2)}, u32[]{:S(2)}) collective-permute-start(f32[4,32,128]{2,1,0:T(8,128)S(1)} %pad_maximum_fusion.refs_3_), channel_id=1, source_target_pairs={{0,1},{1,0},{2,3},{3,2},{4,5},{5,4},{6,7},{7,6},{8,9},{9,8},{10,11... | collective-permute-start | bytes 196616 | tf_op jit(solution)/shard_map/ppermute | solution.py:218
  12.8 1.7 %collective-permute-done.7.refs_5_ = f32[4,32,128]{2,1,0:T(8,128)S(1)} collective-permute-done((f32[4,32,128]{2,1,0:T(8,128)S(1)}, f32[4,32,128]{2,1,0:T(8,128)S(1)}, u32[]{:S(2)}, u32[]{:S(2)}) %collective-permute-start.7) | collective-permute-done | bytes 65568 | tf_op jit(solution)/shard_map/ppermute | solution.py:218
  14.4 0.3 %collective-permute-start.10 = (f32[4,32,128]{2,1,0:T(8,128)S(1)}, f32[4,32,128]{2,1,0:T(8,128)S(1)}, u32[]{:S(2)}, u32[]{:S(2)}) collective-permute-start(f32[4,32,128]{2,1,0:T(8,128)S(1)} %collective-permute-done.7.refs_5_), channel_id=1, source_target_pairs={{0,1},{1,0},{2,3},{3,2},{4,5},{5,4},{6,7},{7,6},{8,9},{9,8},{10,11... | collective-permute-start | bytes 196616 | tf_op jit(solution)/shard_map/ppermute | solution.py:218
  14.8 0.8 %collective-permute-done.6.refs_4_ = f32[4,32,128]{2,1,0:T(8,128)S(1)} collective-permute-done((f32[4,32,128]{2,1,0:T(8,128)S(1)}, f32[4,32,128]{2,1,0:T(8,128)S(1)}, u32[]{:S(2)}, u32[]{:S(2)}) %collective-permute-start.6) | collective-permute-done | bytes 65568 | tf_op jit(solution)/shard_map/ppermute | solution.py:218
  15.6 1.0 %collective-permute-start.8 = (f32[4,32,128]{2,1,0:T(8,128)S(1)}, f32[4,32,128]{2,1,0:T(8,128)S(1)}, u32[]{:S(2)}, u32[]{:S(2)}) collective-permute-start(f32[4,32,128]{2,1,0:T(8,128)S(1)} %collective-permute-done.6.refs_4_), channel_id=1, source_target_pairs={{0,1},{1,0},{2,3},{3,2},{4,5},{5,4},{6,7},{7,6},{8,9},{9,8},{10,11... | collective-permute-start | bytes 196616 | tf_op jit(solution)/shard_map/ppermute | solution.py:218
  16.5 0.0 collective-permute-done.5.refs_3_
  16.5 0.0 collective-permute-start.9
  16.5 0.0 collective-permute-done.4.refs_2_
  16.5 0.1 shard_map.56.refs_2_
  16.6 0.0 collective-permute-done.10.refs_6_
  16.6 0.8 %collective-permute-done.8.refs_4_ = f32[4,32,128]{2,1,0:T(8,128)S(1)} collective-permute-done((f32[4,32,128]{2,1,0:T(8,128)S(1)}, f32[4,32,128]{2,1,0:T(8,128)S(1)}, u32[]{:S(2)}, u32[]{:S(2)}) %collective-permute-start.8) | collective-permute-done | bytes 65568 | tf_op jit(solution)/shard_map/ppermute | solution.py:218
  17.4 0.4 %collective-permute-done.9.refs_5_ = f32[4,32,128]{2,1,0:T(8,128)S(1)} collective-permute-done((f32[4,32,128]{2,1,0:T(8,128)S(1)}, f32[4,32,128]{2,1,0:T(8,128)S(1)}, u32[]{:S(2)}, u32[]{:S(2)}) %collective-permute-start.9) | collective-permute-done | bytes 65568 | tf_op jit(solution)/shard_map/ppermute | solution.py:218
  17.8 0.4 %shard_map.57 = f32[16,32,128]{2,1,0:T(8,128)S(1)} custom-call(s32[10,32]{1,0:T(8,128)S(4)} %get-tuple-element.9.refs_0_, bf16[32,128,256]{2,1,0:T(8,128)(2,1)S(1)} %get-tuple-element.11.refs_1_, f32[9,64,128]{2,1,0:T(8,128)S(1)} %shard_map.56.refs_2_, f32[4,32,128]{2,1,0:T(8,128)S(1)} %pad_maximum_fusion.refs_3_, ...), custom_call_target="tpu_custom_call" | custom-call | flops 268435456 | bytes 2097152 | tf_op jit(solution)/shard_map/pallas_call | solution.py:198
  18.2 0.9 %collective-permute-start.12 = (f32[4,32,128]{2,1,0:T(8,128)S(1)}, f32[4,32,128]{2,1,0:T(8,128)S(1)}, u32[]{:S(2)}, u32[]{:S(2)}) collective-permute-start(f32[4,32,128]{2,1,0:T(8,128)S(1)} %get-tuple-element.13), channel_id=1, source_target_pairs={{0,7},{1,6},{2,5},{3,4},{4,3},{5,2},{6,1},{7,0},{8,15},{9,14},{10,... | collective-permute-start | bytes 196616 | tf_op jit(solution)/shard_map/ppermute | solution.py:218
  19.1 1.7 %collective-permute-start.14 = (f32[4,32,128]{2,1,0:T(8,128)S(1)}, f32[4,32,128]{2,1,0:T(8,128)S(1)}, u32[]{:S(2)}, u32[]{:S(2)}) collective-permute-start(f32[4,32,128]{2,1,0:T(8,128)S(1)} %get-tuple-element.14), channel_id=1, source_target_pairs={{0,5},{1,2},{2,1},{3,6},{4,7},{5,0},{6,3},{7,4},{8,13},{9,10},{10,... | collective-permute-start | bytes 196616 | tf_op jit(solution)/shard_map/ppermute | solution.py:218
  20.8 0.1 collective-permute-start.13
  21.0 0.6 %collective-permute-start.11 = (f32[4,32,128]{2,1,0:T(8,128)S(1)}, f32[4,32,128]{2,1,0:T(8,128)S(1)}, u32[]{:S(2)}, u32[]{:S(2)}) collective-permute-start(f32[4,32,128]{2,1,0:T(8,128)S(1)} %get-tuple-element.16), channel_id=1, source_target_pairs={{0,1},{1,0},{2,3},{3,2},{4,5},{5,4},{6,7},{7,6},{8,9},{9,8},{10,11... | collective-permute-start | bytes 196616 | tf_op jit(solution)/shard_map/ppermute | solution.py:218
  21.6 2.0 %collective-permute-done.12 = f32[4,32,128]{2,1,0:T(8,128)S(1)} collective-permute-done((f32[4,32,128]{2,1,0:T(8,128)S(1)}, f32[4,32,128]{2,1,0:T(8,128)S(1)}, u32[]{:S(2)}, u32[]{:S(2)}) %collective-permute-start.12) | collective-permute-done | bytes 65568 | tf_op jit(solution)/shard_map/ppermute | solution.py:218
  23.6 0.7 %collective-permute-done.14 = f32[4,32,128]{2,1,0:T(8,128)S(1)} collective-permute-done((f32[4,32,128]{2,1,0:T(8,128)S(1)}, f32[4,32,128]{2,1,0:T(8,128)S(1)}, u32[]{:S(2)}, u32[]{:S(2)}) %collective-permute-start.14) | collective-permute-done | bytes 65568 | tf_op jit(solution)/shard_map/ppermute | solution.py:218
  24.4 0.7 %collective-permute-done.13 = f32[4,32,128]{2,1,0:T(8,128)S(1)} collective-permute-done((f32[4,32,128]{2,1,0:T(8,128)S(1)}, f32[4,32,128]{2,1,0:T(8,128)S(1)}, u32[]{:S(2)}, u32[]{:S(2)}) %collective-permute-start.13) | collective-permute-done | bytes 65568 | tf_op jit(solution)/shard_map/ppermute | solution.py:218
  25.0 0.0 collective-permute-done.11
  25.1 1.2 %collective-permute-start.18 = (f32[32,128]{1,0:T(8,128)S(1)}, f32[32,128]{1,0:T(8,128)S(1)}, u32[]{:S(2)}, u32[]{:S(2)}) collective-permute-start(f32[32,128]{1,0:T(8,128)S(1)} %get-tuple-element.17), channel_id=1, source_target_pairs={{0,25},{1,24},{2,27},{3,26},{4,29},{5,28},{6,31},{7,30},{8,17},{9,... | collective-permute-start | bytes 49160 | tf_op jit(solution)/shard_map/ppermute | solution.py:218
  26.3 0.0 collective-permute-start.17
  26.3 2.6 %collective-permute-start.16 = (f32[32,128]{1,0:T(8,128)S(1)}, f32[32,128]{1,0:T(8,128)S(1)}, u32[]{:S(2)}, u32[]{:S(2)}) collective-permute-start(f32[32,128]{1,0:T(8,128)S(1)} %get-tuple-element.19), channel_id=1, source_target_pairs={{0,9},{1,8},{2,11},{3,10},{4,13},{5,12},{6,15},{7,14},{8,1},{9,0},... | collective-permute-start | bytes 49160 | tf_op jit(solution)/shard_map/ppermute | solution.py:218
  28.8 0.5 %collective-permute-start.15 = (f32[32,128]{1,0:T(8,128)S(1)}, f32[32,128]{1,0:T(8,128)S(1)}, u32[]{:S(2)}, u32[]{:S(2)}) collective-permute-start(f32[32,128]{1,0:T(8,128)S(1)} %get-tuple-element.20), channel_id=1, source_target_pairs={{0,1},{1,0},{2,3},{3,2},{4,5},{5,4},{6,7},{7,6},{8,9},{9,8},{10,11... | collective-permute-start | bytes 49160 | tf_op jit(solution)/shard_map/ppermute | solution.py:218
  29.3 0.7 %collective-permute-done.18.refs_3_ = f32[32,128]{1,0:T(8,128)S(1)} collective-permute-done((f32[32,128]{1,0:T(8,128)S(1)}, f32[32,128]{1,0:T(8,128)S(1)}, u32[]{:S(2)}, u32[]{:S(2)}) %collective-permute-start.18) | collective-permute-done | bytes 16416 | tf_op jit(solution)/shard_map/ppermute | solution.py:218
  30.1 0.7 %collective-permute-done.17.refs_2_ = f32[32,128]{1,0:T(8,128)S(1)} collective-permute-done((f32[32,128]{1,0:T(8,128)S(1)}, f32[32,128]{1,0:T(8,128)S(1)}, u32[]{:S(2)}, u32[]{:S(2)}) %collective-permute-start.17) | collective-permute-done | bytes 16416 | tf_op jit(solution)/shard_map/ppermute | solution.py:218
  30.8 0.0 collective-permute-done.16.refs_1_
  30.8 0.0 collective-permute-done.15.refs_0_
  30.8 0.6 %shard_map.58 = f32[32,128]{1,0:T(8,128)} custom-call(f32[32,128]{1,0:T(8,128)S(1)} %collective-permute-done.15.refs_0_, f32[32,128]{1,0:T(8,128)S(1)} %collective-permute-done.16.refs_1_, f32[32,128]{1,0:T(8,128)S(1)} %collective-permute-done.17.refs_2_, f32[32,128]{1,0:T(8,128)S(1)} %collective-permute-done.18.refs_3_), custom_call_target="tpu_custom_call" | custom-call | tf_op jit(solution)/shard_map/pallas_call | solution.py:239
  (4 shorter events, 0.1 us)
Async XLA Ops:
  0.0 7.3 %collective-permute-start = (f32[32,128]{1,0:T(8,128)}, f32[32,128]{1,0:T(8,128)S(1)}, u32[]{:S(2)}, u32[]{:S(2)}) collective-permute-start(f32[32,128]{1,0:T(8,128)} %bitcast.32), channel_id=1, source_target_pairs={{0,1},{1,0},{2,3},{3,2},{4,5},{5,4},{6,7},{7,6},{8,9},{9,8},{10,11... | collective-permute-start | bytes 49160 | tf_op jit(solution)/shard_map/ppermute | solution.py:218
  0.5 6.9 %collective-permute-start.3 = (f32[32,128]{1,0:T(8,128)}, f32[32,128]{1,0:T(8,128)S(1)}, u32[]{:S(2)}, u32[]{:S(2)}) collective-permute-start(f32[32,128]{1,0:T(8,128)} %bitcast.33), channel_id=1, source_target_pairs={{0,17},{1,16},{2,19},{3,18},{4,21},{5,20},{6,23},{7,22},{8,25},{9,... | collective-permute-start | bytes 49160 | tf_op jit(solution)/shard_map/ppermute | solution.py:218
  4.2 5.2 %collective-permute-start.2 = (f32[32,128]{1,0:T(8,128)}, f32[32,128]{1,0:T(8,128)S(1)}, u32[]{:S(2)}, u32[]{:S(2)}) collective-permute-start(f32[32,128]{1,0:T(8,128)} %bitcast.34), channel_id=1, source_target_pairs={{0,25},{1,24},{2,27},{3,26},{4,29},{5,28},{6,31},{7,30},{8,17},{9,... | collective-permute-start | bytes 49160 | tf_op jit(solution)/shard_map/ppermute | solution.py:218
  5.2 4.2 %collective-permute-start.1 = (f32[32,128]{1,0:T(8,128)}, f32[32,128]{1,0:T(8,128)S(1)}, u32[]{:S(2)}, u32[]{:S(2)}) collective-permute-start(f32[32,128]{1,0:T(8,128)} %bitcast.35), channel_id=1, source_target_pairs={{0,9},{1,8},{2,11},{3,10},{4,13},{5,12},{6,15},{7,14},{8,1},{9,0},... | collective-permute-start | bytes 49160 | tf_op jit(solution)/shard_map/ppermute | solution.py:218
  9.4 5.1 %collective-permute-start.7 = (f32[4,32,128]{2,1,0:T(8,128)S(1)}, f32[4,32,128]{2,1,0:T(8,128)S(1)}, u32[]{:S(2)}, u32[]{:S(2)}) collective-permute-start(f32[4,32,128]{2,1,0:T(8,128)S(1)} %pad_maximum_fusion.refs_3_), channel_id=1, source_target_pairs={{0,7},{1,6},{2,5},{3,4},{4,3},{5,2},{6,1},{7,0},{8,15},{9,14},{10,... | collective-permute-start | bytes 196616 | tf_op jit(solution)/shard_map/ppermute | solution.py:218
  11.6 4.0 %collective-permute-start.6 = (f32[4,32,128]{2,1,0:T(8,128)S(1)}, f32[4,32,128]{2,1,0:T(8,128)S(1)}, u32[]{:S(2)}, u32[]{:S(2)}) collective-permute-start(f32[4,32,128]{2,1,0:T(8,128)S(1)} %pad_maximum_fusion.refs_3_), channel_id=1, source_target_pairs={{0,5},{1,2},{2,1},{3,6},{4,7},{5,0},{6,3},{7,4},{8,13},{9,10},{10,... | collective-permute-start | bytes 196616 | tf_op jit(solution)/shard_map/ppermute | solution.py:218
  12.1 4.4 %collective-permute-start.5 = (f32[4,32,128]{2,1,0:T(8,128)S(1)}, f32[4,32,128]{2,1,0:T(8,128)S(1)}, u32[]{:S(2)}, u32[]{:S(2)}) collective-permute-start(f32[4,32,128]{2,1,0:T(8,128)S(1)} %pad_maximum_fusion.refs_3_), channel_id=1, source_target_pairs={{0,3},{1,4},{2,7},{3,0},{4,1},{5,6},{6,5},{7,2},{8,11},{9,12},{10,... | collective-permute-start | bytes 196616 | tf_op jit(solution)/shard_map/ppermute | solution.py:218
  12.3 4.2 %collective-permute-start.4 = (f32[4,32,128]{2,1,0:T(8,128)S(1)}, f32[4,32,128]{2,1,0:T(8,128)S(1)}, u32[]{:S(2)}, u32[]{:S(2)}) collective-permute-start(f32[4,32,128]{2,1,0:T(8,128)S(1)} %pad_maximum_fusion.refs_3_), channel_id=1, source_target_pairs={{0,1},{1,0},{2,3},{3,2},{4,5},{5,4},{6,7},{7,6},{8,9},{9,8},{10,11... | collective-permute-start | bytes 196616 | tf_op jit(solution)/shard_map/ppermute | solution.py:218
  14.4 2.2 %collective-permute-start.10 = (f32[4,32,128]{2,1,0:T(8,128)S(1)}, f32[4,32,128]{2,1,0:T(8,128)S(1)}, u32[]{:S(2)}, u32[]{:S(2)}) collective-permute-start(f32[4,32,128]{2,1,0:T(8,128)S(1)} %collective-permute-done.7.refs_5_), channel_id=1, source_target_pairs={{0,1},{1,0},{2,3},{3,2},{4,5},{5,4},{6,7},{7,6},{8,9},{9,8},{10,11... | collective-permute-start | bytes 196616 | tf_op jit(solution)/shard_map/ppermute | solution.py:218
  15.6 1.9 %collective-permute-start.8 = (f32[4,32,128]{2,1,0:T(8,128)S(1)}, f32[4,32,128]{2,1,0:T(8,128)S(1)}, u32[]{:S(2)}, u32[]{:S(2)}) collective-permute-start(f32[4,32,128]{2,1,0:T(8,128)S(1)} %collective-permute-done.6.refs_4_), channel_id=1, source_target_pairs={{0,1},{1,0},{2,3},{3,2},{4,5},{5,4},{6,7},{7,6},{8,9},{9,8},{10,11... | collective-permute-start | bytes 196616 | tf_op jit(solution)/shard_map/ppermute | solution.py:218
  16.5 1.3 %collective-permute-start.9 = (f32[4,32,128]{2,1,0:T(8,128)S(1)}, f32[4,32,128]{2,1,0:T(8,128)S(1)}, u32[]{:S(2)}, u32[]{:S(2)}) collective-permute-start(f32[4,32,128]{2,1,0:T(8,128)S(1)} %collective-permute-done.5.refs_3_), channel_id=1, source_target_pairs={{0,1},{1,0},{2,3},{3,2},{4,5},{5,4},{6,7},{7,6},{8,9},{9,8},{10,11... | collective-permute-start | bytes 196616 | tf_op jit(solution)/shard_map/ppermute | solution.py:218
  18.2 5.4 %collective-permute-start.12 = (f32[4,32,128]{2,1,0:T(8,128)S(1)}, f32[4,32,128]{2,1,0:T(8,128)S(1)}, u32[]{:S(2)}, u32[]{:S(2)}) collective-permute-start(f32[4,32,128]{2,1,0:T(8,128)S(1)} %get-tuple-element.13), channel_id=1, source_target_pairs={{0,7},{1,6},{2,5},{3,4},{4,3},{5,2},{6,1},{7,0},{8,15},{9,14},{10,... | collective-permute-start | bytes 196616 | tf_op jit(solution)/shard_map/ppermute | solution.py:218
  19.1 5.2 %collective-permute-start.14 = (f32[4,32,128]{2,1,0:T(8,128)S(1)}, f32[4,32,128]{2,1,0:T(8,128)S(1)}, u32[]{:S(2)}, u32[]{:S(2)}) collective-permute-start(f32[4,32,128]{2,1,0:T(8,128)S(1)} %get-tuple-element.14), channel_id=1, source_target_pairs={{0,5},{1,2},{2,1},{3,6},{4,7},{5,0},{6,3},{7,4},{8,13},{9,10},{10,... | collective-permute-start | bytes 196616 | tf_op jit(solution)/shard_map/ppermute | solution.py:218
  20.8 4.2 %collective-permute-start.13 = (f32[4,32,128]{2,1,0:T(8,128)S(1)}, f32[4,32,128]{2,1,0:T(8,128)S(1)}, u32[]{:S(2)}, u32[]{:S(2)}) collective-permute-start(f32[4,32,128]{2,1,0:T(8,128)S(1)} %get-tuple-element.15), channel_id=1, source_target_pairs={{0,3},{1,4},{2,7},{3,0},{4,1},{5,6},{6,5},{7,2},{8,11},{9,12},{10,... | collective-permute-start | bytes 196616 | tf_op jit(solution)/shard_map/ppermute | solution.py:218
  21.0 4.1 %collective-permute-start.11 = (f32[4,32,128]{2,1,0:T(8,128)S(1)}, f32[4,32,128]{2,1,0:T(8,128)S(1)}, u32[]{:S(2)}, u32[]{:S(2)}) collective-permute-start(f32[4,32,128]{2,1,0:T(8,128)S(1)} %get-tuple-element.16), channel_id=1, source_target_pairs={{0,1},{1,0},{2,3},{3,2},{4,5},{5,4},{6,7},{7,6},{8,9},{9,8},{10,11... | collective-permute-start | bytes 196616 | tf_op jit(solution)/shard_map/ppermute | solution.py:218
  25.1 5.0 %collective-permute-start.18 = (f32[32,128]{1,0:T(8,128)S(1)}, f32[32,128]{1,0:T(8,128)S(1)}, u32[]{:S(2)}, u32[]{:S(2)}) collective-permute-start(f32[32,128]{1,0:T(8,128)S(1)} %get-tuple-element.17), channel_id=1, source_target_pairs={{0,25},{1,24},{2,27},{3,26},{4,29},{5,28},{6,31},{7,30},{8,17},{9,... | collective-permute-start | bytes 49160 | tf_op jit(solution)/shard_map/ppermute | solution.py:218
  26.3 4.6 %collective-permute-start.17 = (f32[32,128]{1,0:T(8,128)S(1)}, f32[32,128]{1,0:T(8,128)S(1)}, u32[]{:S(2)}, u32[]{:S(2)}) collective-permute-start(f32[32,128]{1,0:T(8,128)S(1)} %get-tuple-element.18), channel_id=1, source_target_pairs={{0,17},{1,16},{2,19},{3,18},{4,21},{5,20},{6,23},{7,22},{8,25},{9,... | collective-permute-start | bytes 49160 | tf_op jit(solution)/shard_map/ppermute | solution.py:218
  26.3 4.6 %collective-permute-start.16 = (f32[32,128]{1,0:T(8,128)S(1)}, f32[32,128]{1,0:T(8,128)S(1)}, u32[]{:S(2)}, u32[]{:S(2)}) collective-permute-start(f32[32,128]{1,0:T(8,128)S(1)} %get-tuple-element.19), channel_id=1, source_target_pairs={{0,9},{1,8},{2,11},{3,10},{4,13},{5,12},{6,15},{7,14},{8,1},{9,0},... | collective-permute-start | bytes 49160 | tf_op jit(solution)/shard_map/ppermute | solution.py:218
  28.8 2.0 %collective-permute-start.15 = (f32[32,128]{1,0:T(8,128)S(1)}, f32[32,128]{1,0:T(8,128)S(1)}, u32[]{:S(2)}, u32[]{:S(2)}) collective-permute-start(f32[32,128]{1,0:T(8,128)S(1)} %get-tuple-element.20), channel_id=1, source_target_pairs={{0,1},{1,0},{2,3},{3,2},{4,5},{5,4},{6,7},{7,6},{8,9},{9,8},{10,11... | collective-permute-start | bytes 49160 | tf_op jit(solution)/shard_map/ppermute | solution.py:218

commit v9 on v6

--- a/solution.py
+++ b/solution.py
@@ -243,9 +243,10 @@
         tile_counts,
         local_tiles,
     )
-    neighbour, halves = lax.optimization_barrier((neighbour, halves))
     order = far_order(pairs // NEAR)
-    line = jnp.stack([neighbour] + [swap(mine, pairs, virts, 1, far=mask) for mask in order[1:]])
+    chunks = [neighbour] + [swap(mine, pairs, virts, 1, far=mask) for mask in order[1:]]
+    chunks[-1], halves = lax.optimization_barrier((chunks[-1], halves))
+    line = jnp.stack(chunks)
     pieces = [line] + [swap(line, pairs, virts, 1, step=step) for step in range(1, NEAR)]
     blocks = [pieces] + [[swap(piece, pairs, virts, mask) for piece in pieces] for mask in range(1, virts)]
     owners = [

time: 31.3 us -> 31.3 us (level)
    ppermute x19, waiting for transfers between devices: 9.81 us -> 10.1 us  [swap(): return lax.ppermute(value, ('pair', 'virt'), routes)]
  transfers between devices with their start and end apart: 19 -> 19, of which waited for: 10 -> 10; matrix products, arithmetic and copies ran while one was open for 0% -> 0% of each run, Pallas kernels for 6% -> 5%
where the time goes in v9:
time: 31.3 us; the launch traced here: 31.1 us
  starting transfers between devices  17.5 us (56%)
  waiting for transfers between devices  10.1 us (32%)
  Pallas kernels  2.07 us (7%)
  between operations  0.73 us (2%)
  other arithmetic  0.64 us (2%)
    ppermute x19, starting transfers between devices, swap(): return lax.ppermute(value, ('pair', 'virt'), routes)  17.5 us
    ppermute x19, waiting for transfers between devices, swap(): return lax.ppermute(value, ('pair', 'virt'), routes)  10.1 us
    pallas_call x1, Pallas kernels, prepare(): pl.pallas_call(kernel, out_shape=(jax.ShapeDtypeStruct((slots, W, 2 * W),...  1.34 us
    add x2, other arithmetic, swap_sum(): return sum(received[1:], received[0])  0.63 us
  transfers between devices with their start and end apart: 19, of which 10 were waited for; matrix products, arithmetic and copies ran while one was open for 0% of the time, Pallas kernels for 5%

profile of v9, /device:TPU:0, one launch (start us, length us, event | category | flops | bytes accessed | tf_op | source)
XLA Modules:
  0.0 31.1 jit_solution(4310264078775937116)
XLA Ops:
  0.0 3.5 %collective-permute-start = (f32[32,128]{1,0:T(8,128)}, f32[32,128]{1,0:T(8,128)S(1)}, u32[]{:S(2)}, u32[]{:S(2)}) collective-permute-start(f32[32,128]{1,0:T(8,128)} %bitcast.32), channel_id=1, source_target_pairs={{0,17},{1,16},{2,19},{3,18},{4,21},{5,20},{6,23},{7,22},{8,25},{9,... | collective-permute-start | bytes 49160 | tf_op jit(solution)/shard_map/ppermute | solution.py:218
  3.5 1.6 %collective-permute-start.3 = (f32[32,128]{1,0:T(8,128)}, f32[32,128]{1,0:T(8,128)S(1)}, u32[]{:S(2)}, u32[]{:S(2)}) collective-permute-start(f32[32,128]{1,0:T(8,128)} %bitcast.33), channel_id=1, source_target_pairs={{0,25},{1,24},{2,27},{3,26},{4,29},{5,28},{6,31},{7,30},{8,17},{9,... | collective-permute-start | bytes 49160 | tf_op jit(solution)/shard_map/ppermute | solution.py:218
  5.1 0.2 collective-permute-start.2
  5.3 0.0 collective-permute-start.1
  6.0 1.3 %shard_map.55 = (bf16[32,128,256]{2,1,0:T(8,128)(2,1)S(1)}, s32[10,32]{1,0:T(8,128)S(4)}) custom-call(s32[1,1]{1,0:T(1,128)S(6)} %copy.8.refs_0_, s32[1,32]{1,0:T(1,128)} %bitcast.30, s32[1,32]{1,0:T(1,128)} %bitcast.31, f32[32,128,128]{2,1,0:T(8,128)} %bitcast.25), custom_call_target="tpu_custom_call" | custom-call | flops 2097152 | bytes 4194304 | tf_op jit(solution)/shard_map/pallas_call | solution.py:82
  7.3 0.0 collective-permute-done
  7.4 1.3 %collective-permute-done.3 = f32[32,128]{1,0:T(8,128)S(1)} collective-permute-done((f32[32,128]{1,0:T(8,128)}, f32[32,128]{1,0:T(8,128)S(1)}, u32[]{:S(2)}, u32[]{:S(2)}) %collective-permute-start.3) | collective-permute-done | bytes 16416 | tf_op jit(solution)/shard_map/ppermute | solution.py:218
  8.7 0.0 collective-permute-done.2
  8.7 0.0 collective-permute-done.1
  8.7 2.8 %collective-permute-start.7 = (f32[4,32,128]{2,1,0:T(8,128)S(1)}, f32[4,32,128]{2,1,0:T(8,128)S(1)}, u32[]{:S(2)}, u32[]{:S(2)}) collective-permute-start(f32[4,32,128]{2,1,0:T(8,128)S(1)} %pad_maximum_fusion.refs_3_), channel_id=1, source_target_pairs={{0,7},{1,6},{2,5},{3,4},{4,3},{5,2},{6,1},{7,0},{8,15},{9,14},{10,... | collective-permute-start | bytes 196616 | tf_op jit(solution)/shard_map/ppermute | solution.py:218
  11.5 0.0 collective-permute-start.6
  11.5 0.8 %collective-permute-start.5 = (f32[4,32,128]{2,1,0:T(8,128)S(1)}, f32[4,32,128]{2,1,0:T(8,128)S(1)}, u32[]{:S(2)}, u32[]{:S(2)}) collective-permute-start(f32[4,32,128]{2,1,0:T(8,128)S(1)} %pad_maximum_fusion.refs_3_), channel_id=1, source_target_pairs={{0,3},{1,4},{2,7},{3,0},{4,1},{5,6},{6,5},{7,2},{8,11},{9,12},{10,... | collective-permute-start | bytes 196616 | tf_op jit(solution)/shard_map/ppermute | solution.py:218
  12.3 0.0 collective-permute-start.4
  12.3 1.7 %collective-permute-done.7.refs_5_ = f32[4,32,128]{2,1,0:T(8,128)S(1)} collective-permute-done((f32[4,32,128]{2,1,0:T(8,128)S(1)}, f32[4,32,128]{2,1,0:T(8,128)S(1)}, u32[]{:S(2)}, u32[]{:S(2)}) %collective-permute-start.7) | collective-permute-done | bytes 65568 | tf_op jit(solution)/shard_map/ppermute | solution.py:218
  14.0 0.1 collective-permute-start.10
  14.1 1.2 %collective-permute-done.6.refs_4_ = f32[4,32,128]{2,1,0:T(8,128)S(1)} collective-permute-done((f32[4,32,128]{2,1,0:T(8,128)S(1)}, f32[4,32,128]{2,1,0:T(8,128)S(1)}, u32[]{:S(2)}, u32[]{:S(2)}) %collective-permute-start.6) | collective-permute-done | bytes 65568 | tf_op jit(solution)/shard_map/ppermute | solution.py:218
  15.2 0.7 %collective-permute-start.8 = (f32[4,32,128]{2,1,0:T(8,128)S(1)}, f32[4,32,128]{2,1,0:T(8,128)S(1)}, u32[]{:S(2)}, u32[]{:S(2)}) collective-permute-start(f32[4,32,128]{2,1,0:T(8,128)S(1)} %collective-permute-done.6.refs_4_), channel_id=1, source_target_pairs={{0,1},{1,0},{2,3},{3,2},{4,5},{5,4},{6,7},{7,6},{8,9},{9,8},{10,11... | collective-permute-start | bytes 196616 | tf_op jit(solution)/shard_map/ppermute | solution.py:218
  16.0 0.0 collective-permute-done.5.refs_3_
  16.0 0.0 collective-permute-start.9
  16.0 0.0 collective-permute-done.4.refs_2_
  16.0 0.3 %shard_map.56.refs_2_ = f32[9,64,128]{2,1,0:T(8,128)S(1)} custom-call(s32[10,32]{1,0:T(8,128)S(4)} %get-tuple-element.9.refs_0_, bf16[32,128,256]{2,1,0:T(8,128)(2,1)S(1)} %get-tuple-element.11.refs_1_, f32[4,32,128]{2,1,0:T(8,128)S(1)} %collective-permute-done.4.refs_2_, f32[4,32,128]{2,1,0:T(8,128)S(1)} %collective-permute-done.5.refs_3_, ...), custom_call_target="tpu_custom_call" | custom-call | flops 268435456 | bytes 2097152 | tf_op jit(solution)/shard_map/pallas_call | solution.py:189
  16.4 0.0 collective-permute-done.10.refs_6_
  16.4 0.5 %collective-permute-done.8.refs_4_ = f32[4,32,128]{2,1,0:T(8,128)S(1)} collective-permute-done((f32[4,32,128]{2,1,0:T(8,128)S(1)}, f32[4,32,128]{2,1,0:T(8,128)S(1)}, u32[]{:S(2)}, u32[]{:S(2)}) %collective-permute-start.8) | collective-permute-done | bytes 65568 | tf_op jit(solution)/shard_map/ppermute | solution.py:218
  16.9 0.4 %collective-permute-done.9.refs_5_ = f32[4,32,128]{2,1,0:T(8,128)S(1)} collective-permute-done((f32[4,32,128]{2,1,0:T(8,128)S(1)}, f32[4,32,128]{2,1,0:T(8,128)S(1)}, u32[]{:S(2)}, u32[]{:S(2)}) %collective-permute-start.9) | collective-permute-done | bytes 65568 | tf_op jit(solution)/shard_map/ppermute | solution.py:218
  17.2 0.4 %shard_map.57 = f32[16,32,128]{2,1,0:T(8,128)S(1)} custom-call(s32[10,32]{1,0:T(8,128)S(4)} %get-tuple-element.9.refs_0_, bf16[32,128,256]{2,1,0:T(8,128)(2,1)S(1)} %get-tuple-element.11.refs_1_, f32[9,64,128]{2,1,0:T(8,128)S(1)} %shard_map.56.refs_2_, f32[4,32,128]{2,1,0:T(8,128)S(1)} %pad_maximum_fusion.refs_3_, ...), custom_call_target="tpu_custom_call" | custom-call | flops 268435456 | bytes 2097152 | tf_op jit(solution)/shard_map/pallas_call | solution.py:198
  17.6 1.4 %collective-permute-start.12 = (f32[4,32,128]{2,1,0:T(8,128)S(1)}, f32[4,32,128]{2,1,0:T(8,128)S(1)}, u32[]{:S(2)}, u32[]{:S(2)}) collective-permute-start(f32[4,32,128]{2,1,0:T(8,128)S(1)} %get-tuple-element.13), channel_id=1, source_target_pairs={{0,7},{1,6},{2,5},{3,4},{4,3},{5,2},{6,1},{7,0},{8,15},{9,14},{10,... | collective-permute-start | bytes 196616 | tf_op jit(solution)/shard_map/ppermute | solution.py:218
  19.0 1.0 %collective-permute-start.14 = (f32[4,32,128]{2,1,0:T(8,128)S(1)}, f32[4,32,128]{2,1,0:T(8,128)S(1)}, u32[]{:S(2)}, u32[]{:S(2)}) collective-permute-start(f32[4,32,128]{2,1,0:T(8,128)S(1)} %get-tuple-element.14), channel_id=1, source_target_pairs={{0,5},{1,2},{2,1},{3,6},{4,7},{5,0},{6,3},{7,4},{8,13},{9,10},{10,... | collective-permute-start | bytes 196616 | tf_op jit(solution)/shard_map/ppermute | solution.py:218
  20.0 0.6 %collective-permute-start.13 = (f32[4,32,128]{2,1,0:T(8,128)S(1)}, f32[4,32,128]{2,1,0:T(8,128)S(1)}, u32[]{:S(2)}, u32[]{:S(2)}) collective-permute-start(f32[4,32,128]{2,1,0:T(8,128)S(1)} %get-tuple-element.15), channel_id=1, source_target_pairs={{0,3},{1,4},{2,7},{3,0},{4,1},{5,6},{6,5},{7,2},{8,11},{9,12},{10,... | collective-permute-start | bytes 196616 | tf_op jit(solution)/shard_map/ppermute | solution.py:218
  20.7 0.4 %collective-permute-start.11 = (f32[4,32,128]{2,1,0:T(8,128)S(1)}, f32[4,32,128]{2,1,0:T(8,128)S(1)}, u32[]{:S(2)}, u32[]{:S(2)}) collective-permute-start(f32[4,32,128]{2,1,0:T(8,128)S(1)} %get-tuple-element.16), channel_id=1, source_target_pairs={{0,1},{1,0},{2,3},{3,2},{4,5},{5,4},{6,7},{7,6},{8,9},{9,8},{10,11... | collective-permute-start | bytes 196616 | tf_op jit(solution)/shard_map/ppermute | solution.py:218
  21.0 1.7 %collective-permute-done.12 = f32[4,32,128]{2,1,0:T(8,128)S(1)} collective-permute-done((f32[4,32,128]{2,1,0:T(8,128)S(1)}, f32[4,32,128]{2,1,0:T(8,128)S(1)}, u32[]{:S(2)}, u32[]{:S(2)}) %collective-permute-start.12) | collective-permute-done | bytes 65568 | tf_op jit(solution)/shard_map/ppermute | solution.py:218
  22.7 1.1 %collective-permute-done.14 = f32[4,32,128]{2,1,0:T(8,128)S(1)} collective-permute-done((f32[4,32,128]{2,1,0:T(8,128)S(1)}, f32[4,32,128]{2,1,0:T(8,128)S(1)}, u32[]{:S(2)}, u32[]{:S(2)}) %collective-permute-start.14) | collective-permute-done | bytes 65568 | tf_op jit(solution)/shard_map/ppermute | solution.py:218
  23.8 0.5 %collective-permute-done.13 = f32[4,32,128]{2,1,0:T(8,128)S(1)} collective-permute-done((f32[4,32,128]{2,1,0:T(8,128)S(1)}, f32[4,32,128]{2,1,0:T(8,128)S(1)}, u32[]{:S(2)}, u32[]{:S(2)}) %collective-permute-start.13) | collective-permute-done | bytes 65568 | tf_op jit(solution)/shard_map/ppermute | solution.py:218
  24.3 0.0 collective-permute-done.11
  24.3 2.1 %collective-permute-start.16 = (f32[32,128]{1,0:T(8,128)S(1)}, f32[32,128]{1,0:T(8,128)S(1)}, u32[]{:S(2)}, u32[]{:S(2)}) collective-permute-start(f32[32,128]{1,0:T(8,128)S(1)} %get-tuple-element.17), channel_id=1, source_target_pairs={{0,25},{1,24},{2,27},{3,26},{4,29},{5,28},{6,31},{7,30},{8,17},{9,... | collective-permute-start | bytes 49160 | tf_op jit(solution)/shard_map/ppermute | solution.py:218
  26.4 0.0 collective-permute-start.18
  26.4 1.8 %collective-permute-start.17 = (f32[32,128]{1,0:T(8,128)S(1)}, f32[32,128]{1,0:T(8,128)S(1)}, u32[]{:S(2)}, u32[]{:S(2)}) collective-permute-start(f32[32,128]{1,0:T(8,128)S(1)} %get-tuple-element.19), channel_id=1, source_target_pairs={{0,9},{1,8},{2,11},{3,10},{4,13},{5,12},{6,15},{7,14},{8,1},{9,0},... | collective-permute-start | bytes 49160 | tf_op jit(solution)/shard_map/ppermute | solution.py:218
  28.2 0.4 %collective-permute-start.15 = (f32[32,128]{1,0:T(8,128)S(1)}, f32[32,128]{1,0:T(8,128)S(1)}, u32[]{:S(2)}, u32[]{:S(2)}) collective-permute-start(f32[32,128]{1,0:T(8,128)S(1)} %get-tuple-element.20), channel_id=1, source_target_pairs={{0,1},{1,0},{2,3},{3,2},{4,5},{5,4},{6,7},{7,6},{8,9},{9,8},{10,11... | collective-permute-start | bytes 49160 | tf_op jit(solution)/shard_map/ppermute | solution.py:218
  28.6 0.7 %collective-permute-done.16 = f32[32,128]{1,0:T(8,128)S(1)} collective-permute-done((f32[32,128]{1,0:T(8,128)S(1)}, f32[32,128]{1,0:T(8,128)S(1)}, u32[]{:S(2)}, u32[]{:S(2)}) %collective-permute-start.16) | collective-permute-done | bytes 16416 | tf_op jit(solution)/shard_map/ppermute | solution.py:218
  29.3 1.1 %collective-permute-done.18 = f32[32,128]{1,0:T(8,128)S(1)} collective-permute-done((f32[32,128]{1,0:T(8,128)S(1)}, f32[32,128]{1,0:T(8,128)S(1)}, u32[]{:S(2)}, u32[]{:S(2)}) %collective-permute-start.18) | collective-permute-done | bytes 16416 | tf_op jit(solution)/shard_map/ppermute | solution.py:218
  30.5 0.0 collective-permute-done.17
  30.5 0.0 collective-permute-done.15
  30.5 0.6 %add_add_fusion.1 = f32[32,128]{1,0:T(8,128)} fusion(f32[32,128]{1,0:T(8,128)S(1)} %collective-permute-done.18, f32[32,128]{1,0:T(8,128)S(1)} %collective-permute-done.17, f32[32,128]{1,0:T(8,128)S(1)} %collective-permute-done.15, f32[32,128]{1,0:T(8,128)S(1)} %collective-permute-done.16), kind=kLoop, calls=%fused_computation.6 | loop fusion | flops 12288 | bytes 81920 | tf_op jit(solution)/shard_map/add | solution.py:229
  (4 shorter events, 0.1 us)
Async XLA Ops:
  0.0 7.3 %collective-permute-start = (f32[32,128]{1,0:T(8,128)}, f32[32,128]{1,0:T(8,128)S(1)}, u32[]{:S(2)}, u32[]{:S(2)}) collective-permute-start(f32[32,128]{1,0:T(8,128)} %bitcast.32), channel_id=1, source_target_pairs={{0,17},{1,16},{2,19},{3,18},{4,21},{5,20},{6,23},{7,22},{8,25},{9,... | collective-permute-start | bytes 49160 | tf_op jit(solution)/shard_map/ppermute | solution.py:218
  3.5 5.2 %collective-permute-start.3 = (f32[32,128]{1,0:T(8,128)}, f32[32,128]{1,0:T(8,128)S(1)}, u32[]{:S(2)}, u32[]{:S(2)}) collective-permute-start(f32[32,128]{1,0:T(8,128)} %bitcast.33), channel_id=1, source_target_pairs={{0,25},{1,24},{2,27},{3,26},{4,29},{5,28},{6,31},{7,30},{8,17},{9,... | collective-permute-start | bytes 49160 | tf_op jit(solution)/shard_map/ppermute | solution.py:218
  5.1 3.6 %collective-permute-start.2 = (f32[32,128]{1,0:T(8,128)}, f32[32,128]{1,0:T(8,128)S(1)}, u32[]{:S(2)}, u32[]{:S(2)}) collective-permute-start(f32[32,128]{1,0:T(8,128)} %bitcast.34), channel_id=1, source_target_pairs={{0,9},{1,8},{2,11},{3,10},{4,13},{5,12},{6,15},{7,14},{8,1},{9,0},... | collective-permute-start | bytes 49160 | tf_op jit(solution)/shard_map/ppermute | solution.py:218
  5.3 3.3 %collective-permute-start.1 = (f32[32,128]{1,0:T(8,128)}, f32[32,128]{1,0:T(8,128)S(1)}, u32[]{:S(2)}, u32[]{:S(2)}) collective-permute-start(f32[32,128]{1,0:T(8,128)} %bitcast.35), channel_id=1, source_target_pairs={{0,1},{1,0},{2,3},{3,2},{4,5},{5,4},{6,7},{7,6},{8,9},{9,8},{10,11... | collective-permute-start | bytes 49160 | tf_op jit(solution)/shard_map/ppermute | solution.py:218
  8.7 5.3 %collective-permute-start.7 = (f32[4,32,128]{2,1,0:T(8,128)S(1)}, f32[4,32,128]{2,1,0:T(8,128)S(1)}, u32[]{:S(2)}, u32[]{:S(2)}) collective-permute-start(f32[4,32,128]{2,1,0:T(8,128)S(1)} %pad_maximum_fusion.refs_3_), channel_id=1, source_target_pairs={{0,7},{1,6},{2,5},{3,4},{4,3},{5,2},{6,1},{7,0},{8,15},{9,14},{10,... | collective-permute-start | bytes 196616 | tf_op jit(solution)/shard_map/ppermute | solution.py:218
  11.5 3.7 %collective-permute-start.6 = (f32[4,32,128]{2,1,0:T(8,128)S(1)}, f32[4,32,128]{2,1,0:T(8,128)S(1)}, u32[]{:S(2)}, u32[]{:S(2)}) collective-permute-start(f32[4,32,128]{2,1,0:T(8,128)S(1)} %pad_maximum_fusion.refs_3_), channel_id=1, source_target_pairs={{0,5},{1,2},{2,1},{3,6},{4,7},{5,0},{6,3},{7,4},{8,13},{9,10},{10,... | collective-permute-start | bytes 196616 | tf_op jit(solution)/shard_map/ppermute | solution.py:218
  11.5 4.4 %collective-permute-start.5 = (f32[4,32,128]{2,1,0:T(8,128)S(1)}, f32[4,32,128]{2,1,0:T(8,128)S(1)}, u32[]{:S(2)}, u32[]{:S(2)}) collective-permute-start(f32[4,32,128]{2,1,0:T(8,128)S(1)} %pad_maximum_fusion.refs_3_), channel_id=1, source_target_pairs={{0,3},{1,4},{2,7},{3,0},{4,1},{5,6},{6,5},{7,2},{8,11},{9,12},{10,... | collective-permute-start | bytes 196616 | tf_op jit(solution)/shard_map/ppermute | solution.py:218
  12.3 3.7 %collective-permute-start.4 = (f32[4,32,128]{2,1,0:T(8,128)S(1)}, f32[4,32,128]{2,1,0:T(8,128)S(1)}, u32[]{:S(2)}, u32[]{:S(2)}) collective-permute-start(f32[4,32,128]{2,1,0:T(8,128)S(1)} %pad_maximum_fusion.refs_3_), channel_id=1, source_target_pairs={{0,1},{1,0},{2,3},{3,2},{4,5},{5,4},{6,7},{7,6},{8,9},{9,8},{10,11... | collective-permute-start | bytes 196616 | tf_op jit(solution)/shard_map/ppermute | solution.py:218
  14.0 2.4 %collective-permute-start.10 = (f32[4,32,128]{2,1,0:T(8,128)S(1)}, f32[4,32,128]{2,1,0:T(8,128)S(1)}, u32[]{:S(2)}, u32[]{:S(2)}) collective-permute-start(f32[4,32,128]{2,1,0:T(8,128)S(1)} %collective-permute-done.7.refs_5_), channel_id=1, source_target_pairs={{0,1},{1,0},{2,3},{3,2},{4,5},{5,4},{6,7},{7,6},{8,9},{9,8},{10,11... | collective-permute-start | bytes 196616 | tf_op jit(solution)/shard_map/ppermute | solution.py:218
  15.2 1.6 %collective-permute-start.8 = (f32[4,32,128]{2,1,0:T(8,128)S(1)}, f32[4,32,128]{2,1,0:T(8,128)S(1)}, u32[]{:S(2)}, u32[]{:S(2)}) collective-permute-start(f32[4,32,128]{2,1,0:T(8,128)S(1)} %collective-permute-done.6.refs_4_), channel_id=1, source_target_pairs={{0,1},{1,0},{2,3},{3,2},{4,5},{5,4},{6,7},{7,6},{8,9},{9,8},{10,11... | collective-permute-start | bytes 196616 | tf_op jit(solution)/shard_map/ppermute | solution.py:218
  16.0 1.3 %collective-permute-start.9 = (f32[4,32,128]{2,1,0:T(8,128)S(1)}, f32[4,32,128]{2,1,0:T(8,128)S(1)}, u32[]{:S(2)}, u32[]{:S(2)}) collective-permute-start(f32[4,32,128]{2,1,0:T(8,128)S(1)} %collective-permute-done.5.refs_3_), channel_id=1, source_target_pairs={{0,1},{1,0},{2,3},{3,2},{4,5},{5,4},{6,7},{7,6},{8,9},{9,8},{10,11... | collective-permute-start | bytes 196616 | tf_op jit(solution)/shard_map/ppermute | solution.py:218
  17.6 5.1 %collective-permute-start.12 = (f32[4,32,128]{2,1,0:T(8,128)S(1)}, f32[4,32,128]{2,1,0:T(8,128)S(1)}, u32[]{:S(2)}, u32[]{:S(2)}) collective-permute-start(f32[4,32,128]{2,1,0:T(8,128)S(1)} %get-tuple-element.13), channel_id=1, source_target_pairs={{0,7},{1,6},{2,5},{3,4},{4,3},{5,2},{6,1},{7,0},{8,15},{9,14},{10,... | collective-permute-start | bytes 196616 | tf_op jit(solution)/shard_map/ppermute | solution.py:218
  19.0 4.7 %collective-permute-start.14 = (f32[4,32,128]{2,1,0:T(8,128)S(1)}, f32[4,32,128]{2,1,0:T(8,128)S(1)}, u32[]{:S(2)}, u32[]{:S(2)}) collective-permute-start(f32[4,32,128]{2,1,0:T(8,128)S(1)} %get-tuple-element.14), channel_id=1, source_target_pairs={{0,5},{1,2},{2,1},{3,6},{4,7},{5,0},{6,3},{7,4},{8,13},{9,10},{10,... | collective-permute-start | bytes 196616 | tf_op jit(solution)/shard_map/ppermute | solution.py:218
  20.0 4.2 %collective-permute-start.13 = (f32[4,32,128]{2,1,0:T(8,128)S(1)}, f32[4,32,128]{2,1,0:T(8,128)S(1)}, u32[]{:S(2)}, u32[]{:S(2)}) collective-permute-start(f32[4,32,128]{2,1,0:T(8,128)S(1)} %get-tuple-element.15), channel_id=1, source_target_pairs={{0,3},{1,4},{2,7},{3,0},{4,1},{5,6},{6,5},{7,2},{8,11},{9,12},{10,... | collective-permute-start | bytes 196616 | tf_op jit(solution)/shard_map/ppermute | solution.py:218
  20.7 3.6 %collective-permute-start.11 = (f32[4,32,128]{2,1,0:T(8,128)S(1)}, f32[4,32,128]{2,1,0:T(8,128)S(1)}, u32[]{:S(2)}, u32[]{:S(2)}) collective-permute-start(f32[4,32,128]{2,1,0:T(8,128)S(1)} %get-tuple-element.16), channel_id=1, source_target_pairs={{0,1},{1,0},{2,3},{3,2},{4,5},{5,4},{6,7},{7,6},{8,9},{9,8},{10,11... | collective-permute-start | bytes 196616 | tf_op jit(solution)/shard_map/ppermute | solution.py:218
  24.3 5.0 %collective-permute-start.16 = (f32[32,128]{1,0:T(8,128)S(1)}, f32[32,128]{1,0:T(8,128)S(1)}, u32[]{:S(2)}, u32[]{:S(2)}) collective-permute-start(f32[32,128]{1,0:T(8,128)S(1)} %get-tuple-element.17), channel_id=1, source_target_pairs={{0,25},{1,24},{2,27},{3,26},{4,29},{5,28},{6,31},{7,30},{8,17},{9,... | collective-permute-start | bytes 49160 | tf_op jit(solution)/shard_map/ppermute | solution.py:218
  26.4 4.1 %collective-permute-start.18 = (f32[32,128]{1,0:T(8,128)S(1)}, f32[32,128]{1,0:T(8,128)S(1)}, u32[]{:S(2)}, u32[]{:S(2)}) collective-permute-start(f32[32,128]{1,0:T(8,128)S(1)} %get-tuple-element.18), channel_id=1, source_target_pairs={{0,17},{1,16},{2,19},{3,18},{4,21},{5,20},{6,23},{7,22},{8,25},{9,... | collective-permute-start | bytes 49160 | tf_op jit(solution)/shard_map/ppermute | solution.py:218
  26.4 4.1 %collective-permute-start.17 = (f32[32,128]{1,0:T(8,128)S(1)}, f32[32,128]{1,0:T(8,128)S(1)}, u32[]{:S(2)}, u32[]{:S(2)}) collective-permute-start(f32[32,128]{1,0:T(8,128)S(1)} %get-tuple-element.19), channel_id=1, source_target_pairs={{0,9},{1,8},{2,11},{3,10},{4,13},{5,12},{6,15},{7,14},{8,1},{9,0},... | collective-permute-start | bytes 49160 | tf_op jit(solution)/shard_map/ppermute | solution.py:218
  28.2 2.3 %collective-permute-start.15 = (f32[32,128]{1,0:T(8,128)S(1)}, f32[32,128]{1,0:T(8,128)S(1)}, u32[]{:S(2)}, u32[]{:S(2)}) collective-permute-start(f32[32,128]{1,0:T(8,128)S(1)} %get-tuple-element.20), channel_id=1, source_target_pairs={{0,1},{1,0},{2,3},{3,2},{4,5},{5,4},{6,7},{7,6},{8,9},{9,8},{10,11... | collective-permute-start | bytes 49160 | tf_op jit(solution)/shard_map/ppermute | solution.py:218

commit v10 on v5

--- a/solution.py
+++ b/solution.py
@@ -96,24 +96,22 @@
     )
 
 
-def ladder_kernel(virts, codes, halves, *refs):
-    blocks, (result, columns, totals) = refs[: virts * NEAR], refs[virts * NEAR :]
-    far = blocks[0].shape[0]
-    chunk_count = NEAR * far
+def ladder_kernel(quarters, virts, codes, halves, *refs):
+    blocks, (result, columns, totals) = refs[:-3], refs[-3:]
+    far, chunk_rows, _ = blocks[0].shape
+    chunk_count = len(quarters) * far
     out_tiles = totals.shape[0] - 1
     rows = result.shape[1] // out_tiles
     total_rows = chunk_count * rows
-    in_local = columns.shape[0] // virts
+    in_local = chunk_rows // rows
     totals[...] = jnp.zeros_like(totals)
 
     for owner in range(virts):
-        for a in range(NEAR):
-            sources = []
-            for b in range(far):
-                from_virt = owner ^ int((a > 0) != (b > 0))
-                sources.append(blocks[from_virt * NEAR + (SWITCHED[a] if from_virt % 2 else a)])
+        for at_quarter, quarter in enumerate(quarters):
+            crossed = [int((quarter > 0) != (b > 0)) for b in range(far)]
+            sources = [blocks[at_quarter * virts + (owner ^ cross)] for cross in crossed]
             for b in range(0, far, 4):
-                first_row = (a * far + b) * rows
+                first_row = (at_quarter * far + b) * rows
                 for tile in range(0, in_local, 2):
                     part = slice(tile * rows, (tile + 2) * rows)
                     four = [sources[b + at][b + at, part, :] for at in range(4)]
@@ -144,18 +142,19 @@
                 result[chunk + at, tile * rows : (tile + 2) * rows, :] = piece
 
 
-def local_terms(codes, blocks, halves, rows, out_tiles):
+def quarter_terms(codes, pieces, quarters, halves, rows, out_tiles):
+    virts = len(pieces)
+    blocks = [pieces[c][SWITCHED[a] if c % 2 else a] for a in quarters for c in range(virts)]
     far, chunk_rows, _ = blocks[0].shape
-    virts = len(blocks) // NEAR
-    total_rows = NEAR * far * rows
+    total_rows = len(quarters) * far * rows
     in_local = chunk_rows // rows
 
     def kernel(*refs):
-        ladder_kernel(virts, *refs)
+        ladder_kernel(quarters, virts, *refs)
 
     return pl.pallas_call(
         kernel,
-        out_shape=jax.ShapeDtypeStruct((NEAR * far, out_tiles * rows, W), jnp.float32),
+        out_shape=jax.ShapeDtypeStruct((len(quarters) * far, out_tiles * rows, W), jnp.float32),
         in_specs=[SMEM, VMEM] + [VMEM] * len(blocks),
         out_specs=VMEM,
         scratch_shapes=[
@@ -163,7 +162,8 @@
             pltpu.VMEM((out_tiles + 1, total_rows, W), jnp.float32),
         ],
         compiler_params=pltpu.CompilerParams(vmem_limit_bytes=32 * 1024 * 1024),
-    )(pltpu.with_memory_space_constraint(codes, pltpu.SMEM), halves, *blocks)
+        cost_estimate=pl.CostEstimate(flops=1 << 28, bytes_accessed=1 << 22, transcendentals=0),
+    )(codes, halves, *blocks)
 
 
 def near_mask(step, a, b):
@@ -184,8 +184,7 @@
 
 
 def swap_sum(parts, pairs, virts, which, marks):
-    last = len(marks) - 1
-    order = (0, last, *range(1, last))
+    order = (1, 2, 0, 3) if which == "step" else (1, 0, *range(2, len(marks)))
     received = [swap(parts[marks.index(mark)], pairs, virts, 1, **{which: mark}) for mark in order]
     return sum(received[1:], received[0])
 
@@ -207,9 +206,14 @@
     order = far_order(pairs // NEAR)
     line = jnp.stack([own] + [swap(mine, pairs, virts, 1, far=mask) for mask in order[1:]])
     pieces = [line] + [swap(line, pairs, virts, 1, step=step) for step in range(1, NEAR)]
-    blocks = pieces + [swap(piece, pairs, virts, mask) for mask in range(1, virts) for piece in pieces]
-    partial_sums = local_terms(codes, blocks, halves, rows, local_tiles)
-    line_sums = swap_sum(partial_sums.reshape((NEAR, pairs // NEAR) + mine.shape), pairs, virts, "step", list(range(NEAR)))
+    pieces = [pieces] + [[swap(piece, pairs, virts, mask) for piece in pieces] for mask in range(1, virts)]
+    codes = pltpu.with_memory_space_constraint(codes, pltpu.SMEM)
+    parts, order_size = {}, len(order)
+    for quarters in ((0, 3), (1, 2)):
+        sums = quarter_terms(codes, pieces, quarters, halves, rows, local_tiles)
+        halves, sums = lax.optimization_barrier((halves, sums))
+        parts.update({a: sums[at * order_size : (at + 1) * order_size] for at, a in enumerate(quarters)})
+    line_sums = swap_sum(parts, pairs, virts, "step", list(range(NEAR)))
     summed = swap_sum(line_sums, pairs, virts, "far", order)
     return summed.reshape(local_tiles, rows, W).transpose(1, 0, 2).reshape(rows, columns)
 

time: 31.4 us -> 30.7 us (0.978)
  waiting for transfers between devices: 10.7 us -> 9.56 us
    ppermute x18, waiting for transfers between devices: 10.7 us -> 9.56 us  [swap(): return lax.ppermute(value, ('pair', 'virt'), routes)]
    pallas_call x1 -> x2, Pallas kernels: 0.55 us -> 0.75 us  [quarter_terms(): pl.pallas_call(kernel, out_shape=jax.ShapeDtypeStruct((len(quarters) * fa...]
  transfers between devices with their start and end apart: 18 -> 18, of which waited for: 10 -> 8; matrix products, arithmetic and copies ran while one was open for 0% -> 0% of each run, Pallas kernels for 4% -> 6%
where the time goes in v10:
time: 30.7 us; the launch traced here: 30.4 us
  starting transfers between devices  17.5 us (57%)
  waiting for transfers between devices  9.56 us (31%)
  Pallas kernels  1.96 us (6%)
  between operations  0.73 us (2%)
  other arithmetic  0.64 us (2%)
    ppermute x18, starting transfers between devices, swap(): return lax.ppermute(value, ('pair', 'virt'), routes)  17.5 us
    ppermute x18, waiting for transfers between devices, swap(): return lax.ppermute(value, ('pair', 'virt'), routes)  9.56 us
    pallas_call x1, Pallas kernels, prepare(): pl.pallas_call(kernel, out_shape=(jax.ShapeDtypeStruct((slots, W, 2 * W),...  1.21 us
    pallas_call x2, Pallas kernels, quarter_terms(): pl.pallas_call(kernel, out_shape=jax.ShapeDtypeStruct((len(quarters) * fa...  0.75 us
    add x2, other arithmetic, swap_sum(): return sum(received[1:], received[0])  0.63 us
  transfers between devices with their start and end apart: 18, of which 8 were waited for; matrix products, arithmetic and copies ran while one was open for 0% of the time, Pallas kernels for 6%

profile of v10, /device:TPU:0, one launch (start us, length us, event | category | flops | bytes accessed | tf_op | source)
XLA Modules:
  0.0 30.4 jit_solution(107567802479938133)
XLA Ops:
  0.0 3.5 %collective-permute-start.2 = (f32[32,128]{1,0:T(8,128)}, f32[32,128]{1,0:T(8,128)S(1)}, u32[]{:S(2)}, u32[]{:S(2)}) collective-permute-start(f32[32,128]{1,0:T(8,128)} %bitcast.27), channel_id=1, source_target_pairs={{0,17},{1,16},{2,19},{3,18},{4,21},{5,20},{6,23},{7,22},{8,25},{9,... | collective-permute-start | bytes 49160 | tf_op jit(solution)/shard_map/ppermute | solution.py:179
  3.5 1.6 %collective-permute-start.1 = (f32[32,128]{1,0:T(8,128)}, f32[32,128]{1,0:T(8,128)S(1)}, u32[]{:S(2)}, u32[]{:S(2)}) collective-permute-start(f32[32,128]{1,0:T(8,128)} %bitcast.28), channel_id=1, source_target_pairs={{0,25},{1,24},{2,27},{3,26},{4,29},{5,28},{6,31},{7,30},{8,17},{9,... | collective-permute-start | bytes 49160 | tf_op jit(solution)/shard_map/ppermute | solution.py:179
  5.1 0.2 collective-permute-start
  6.0 1.2 %shard_map.55 = (bf16[32,128,256]{2,1,0:T(8,128)(2,1)S(1)}, s32[3,32]{1,0:T(4,128)S(4)}, f32[32,128]{1,0:T(8,128)S(1)}) custom-call(s32[1,1]{1,0:T(1,128)S(6)} %copy.8.refs_0_, s32[1,32]{1,0:T(1,128)} %bitcast.34, s32[1,32]{1,0:T(1,128)} %bitcast.35, f32[32,128,128]{2,1,0:T(8,128)} %bitcast.26, f32[32,128]{1,0:T(8,128)} %bitcast.30), custom_call_target="tpu_custom_call" | custom-call | flops 2097152 | bytes 4194304 | tf_op jit(solution)/shard_map/pallas_call | solution.py:69
  7.2 0.0 collective-permute-done.2
  7.2 1.4 %collective-permute-done.1 = f32[32,128]{1,0:T(8,128)S(1)} collective-permute-done((f32[32,128]{1,0:T(8,128)}, f32[32,128]{1,0:T(8,128)S(1)}, u32[]{:S(2)}, u32[]{:S(2)}) %collective-permute-start.1) | collective-permute-done | bytes 16416 | tf_op jit(solution)/shard_map/ppermute | solution.py:179
  8.7 0.0 collective-permute-done
  8.7 2.8 %collective-permute-start.4 = (f32[4,32,128]{2,1,0:T(8,128)S(1)}, f32[4,32,128]{2,1,0:T(8,128)S(1)}, u32[]{:S(2)}, u32[]{:S(2)}) collective-permute-start(f32[4,32,128]{2,1,0:T(8,128)S(1)} %pad_maximum_fusion.refs_2_), channel_id=1, source_target_pairs={{0,7},{1,6},{2,5},{3,4},{4,3},{5,2},{6,1},{7,0},{8,15},{9,14},{10,... | collective-permute-start | bytes 196616 | tf_op jit(solution)/shard_map/ppermute | solution.py:179
  11.5 0.0 collective-permute-start.7
  11.5 0.8 %collective-permute-start.6 = (f32[4,32,128]{2,1,0:T(8,128)S(1)}, f32[4,32,128]{2,1,0:T(8,128)S(1)}, u32[]{:S(2)}, u32[]{:S(2)}) collective-permute-start(f32[4,32,128]{2,1,0:T(8,128)S(1)} %pad_maximum_fusion.refs_2_), channel_id=1, source_target_pairs={{0,3},{1,4},{2,7},{3,0},{4,1},{5,6},{6,5},{7,2},{8,11},{9,12},{10,... | collective-permute-start | bytes 196616 | tf_op jit(solution)/shard_map/ppermute | solution.py:179
  12.3 0.0 collective-permute-start.3
  12.3 1.7 %collective-permute-done.4.refs_4_ = f32[4,32,128]{2,1,0:T(8,128)S(1)} collective-permute-done((f32[4,32,128]{2,1,0:T(8,128)S(1)}, f32[4,32,128]{2,1,0:T(8,128)S(1)}, u32[]{:S(2)}, u32[]{:S(2)}) %collective-permute-start.4) | collective-permute-done | bytes 65568 | tf_op jit(solution)/shard_map/ppermute | solution.py:179
  14.0 0.1 collective-permute-start.5
  14.1 1.2 %collective-permute-done.7.refs_4_ = f32[4,32,128]{2,1,0:T(8,128)S(1)} collective-permute-done((f32[4,32,128]{2,1,0:T(8,128)S(1)}, f32[4,32,128]{2,1,0:T(8,128)S(1)}, u32[]{:S(2)}, u32[]{:S(2)}) %collective-permute-start.7) | collective-permute-done | bytes 65568 | tf_op jit(solution)/shard_map/ppermute | solution.py:179
  15.2 0.7 %collective-permute-start.8 = (f32[4,32,128]{2,1,0:T(8,128)S(1)}, f32[4,32,128]{2,1,0:T(8,128)S(1)}, u32[]{:S(2)}, u32[]{:S(2)}) collective-permute-start(f32[4,32,128]{2,1,0:T(8,128)S(1)} %collective-permute-done.7.refs_4_), channel_id=1, source_target_pairs={{0,1},{1,0},{2,3},{3,2},{4,5},{5,4},{6,7},{7,6},{8,9},{9,8},{10,11... | collective-permute-start | bytes 196616 | tf_op jit(solution)/shard_map/ppermute | solution.py:179
  16.0 0.0 collective-permute-done.6.refs_2_
  16.0 0.0 collective-permute-start.9
  16.0 0.0 collective-permute-done.3.refs_3_
  16.0 0.0 collective-permute-done.5.refs_5_
  16.0 0.4 %shard_map.56 = f32[8,32,128]{2,1,0:T(8,128)S(1)} custom-call(s32[3,32]{1,0:T(4,128)S(4)} %get-tuple-element.12.refs_0_, bf16[32,128,256]{2,1,0:T(8,128)(2,1)S(1)} %get-tuple-element.14.refs_1_, f32[4,32,128]{2,1,0:T(8,128)S(1)} %pad_maximum_fusion.refs_2_, f32[4,32,128]{2,1,0:T(8,128)S(1)} %collective-permute-done.3.refs_3_, ...), custom_call_target="tpu_custom_call" | custom-call | flops 268435456 | bytes 4194304 | tf_op jit(solution)/shard_map/pallas_call | solution.py:155
  16.4 2.1 %collective-permute-start.13 = (f32[4,32,128]{2,1,0:T(8,128)S(1)}, f32[4,32,128]{2,1,0:T(8,128)S(1)}, u32[]{:S(2)}, u32[]{:S(2)}) collective-permute-start(f32[4,32,128]{2,1,0:T(8,128)S(1)} %get-tuple-element.20), channel_id=1, source_target_pairs={{0,7},{1,6},{2,5},{3,4},{4,3},{5,2},{6,1},{7,0},{8,15},{9,14},{10,... | collective-permute-start | bytes 196616 | tf_op jit(solution)/shard_map/ppermute | solution.py:179
  18.5 0.2 collective-permute-start.12
  18.7 0.0 collective-permute-done.8.refs_3_
  18.7 0.0 collective-permute-done.9.refs_5_
  18.7 0.4 %shard_map.57 = f32[8,32,128]{2,1,0:T(8,128)S(1)} custom-call(s32[3,32]{1,0:T(4,128)S(4)} %get-tuple-element.12.refs_0_, bf16[32,128,256]{2,1,0:T(8,128)(2,1)S(1)} %get-tuple-element.14.refs_1_, f32[4,32,128]{2,1,0:T(8,128)S(1)} %collective-permute-done.6.refs_2_, f32[4,32,128]{2,1,0:T(8,128)S(1)} %collective-permute-done.8.refs_3_, ...), custom_call_target="tpu_custom_call" | custom-call | flops 268435456 | bytes 4194304 | tf_op jit(solution)/shard_map/pallas_call | solution.py:155
  19.1 0.8 %collective-permute-start.10 = (f32[4,32,128]{2,1,0:T(8,128)S(1)}, f32[4,32,128]{2,1,0:T(8,128)S(1)}, u32[]{:S(2)}, u32[]{:S(2)}) collective-permute-start(f32[4,32,128]{2,1,0:T(8,128)S(1)} %get-tuple-element.18), channel_id=1, source_target_pairs={{0,3},{1,4},{2,7},{3,0},{4,1},{5,6},{6,5},{7,2},{8,11},{9,12},{10,... | collective-permute-start | bytes 196616 | tf_op jit(solution)/shard_map/ppermute | solution.py:179
  19.9 0.3 %collective-permute-start.11 = (f32[4,32,128]{2,1,0:T(8,128)S(1)}, f32[4,32,128]{2,1,0:T(8,128)S(1)}, u32[]{:S(2)}, u32[]{:S(2)}) collective-permute-start(f32[4,32,128]{2,1,0:T(8,128)S(1)} %get-tuple-element.17), channel_id=1, source_target_pairs={{0,5},{1,2},{2,1},{3,6},{4,7},{5,0},{6,3},{7,4},{8,13},{9,10},{10,... | collective-permute-start | bytes 196616 | tf_op jit(solution)/shard_map/ppermute | solution.py:179
  20.3 0.9 %collective-permute-done.13 = f32[4,32,128]{2,1,0:T(8,128)S(1)} collective-permute-done((f32[4,32,128]{2,1,0:T(8,128)S(1)}, f32[4,32,128]{2,1,0:T(8,128)S(1)}, u32[]{:S(2)}, u32[]{:S(2)}) %collective-permute-start.13) | collective-permute-done | bytes 65568 | tf_op jit(solution)/shard_map/ppermute | solution.py:179
  21.2 0.0 collective-permute-done.12
  21.2 1.7 %collective-permute-done.10 = f32[4,32,128]{2,1,0:T(8,128)S(1)} collective-permute-done((f32[4,32,128]{2,1,0:T(8,128)S(1)}, f32[4,32,128]{2,1,0:T(8,128)S(1)}, u32[]{:S(2)}, u32[]{:S(2)}) %collective-permute-start.10) | collective-permute-done | bytes 65568 | tf_op jit(solution)/shard_map/ppermute | solution.py:179
  22.8 1.2 %collective-permute-done.11 = f32[4,32,128]{2,1,0:T(8,128)S(1)} collective-permute-done((f32[4,32,128]{2,1,0:T(8,128)S(1)}, f32[4,32,128]{2,1,0:T(8,128)S(1)}, u32[]{:S(2)}, u32[]{:S(2)}) %collective-permute-start.11) | collective-permute-done | bytes 65568 | tf_op jit(solution)/shard_map/ppermute | solution.py:179
  24.1 1.6 %collective-permute-start.17 = (f32[32,128]{1,0:T(8,128)S(1)}, f32[32,128]{1,0:T(8,128)S(1)}, u32[]{:S(2)}, u32[]{:S(2)}) collective-permute-start(f32[32,128]{1,0:T(8,128)S(1)} %get-tuple-element.22), channel_id=1, source_target_pairs={{0,25},{1,24},{2,27},{3,26},{4,29},{5,28},{6,31},{7,30},{8,17},{9,... | collective-permute-start | bytes 49160 | tf_op jit(solution)/shard_map/ppermute | solution.py:179
  25.7 0.0 collective-permute-start.16
  25.7 2.0 %collective-permute-start.14 = (f32[32,128]{1,0:T(8,128)S(1)}, f32[32,128]{1,0:T(8,128)S(1)}, u32[]{:S(2)}, u32[]{:S(2)}) collective-permute-start(f32[32,128]{1,0:T(8,128)S(1)} %get-tuple-element.24), channel_id=1, source_target_pairs={{0,9},{1,8},{2,11},{3,10},{4,13},{5,12},{6,15},{7,14},{8,1},{9,0},... | collective-permute-start | bytes 49160 | tf_op jit(solution)/shard_map/ppermute | solution.py:179
  27.8 0.6 %collective-permute-start.15 = (f32[32,128]{1,0:T(8,128)S(1)}, f32[32,128]{1,0:T(8,128)S(1)}, u32[]{:S(2)}, u32[]{:S(2)}) collective-permute-start(f32[32,128]{1,0:T(8,128)S(1)} %get-tuple-element.21), channel_id=1, source_target_pairs={{0,1},{1,0},{2,3},{3,2},{4,5},{5,4},{6,7},{7,6},{8,9},{9,8},{10,11... | collective-permute-start | bytes 49160 | tf_op jit(solution)/shard_map/ppermute | solution.py:179
  28.4 0.9 %collective-permute-done.17 = f32[32,128]{1,0:T(8,128)S(1)} collective-permute-done((f32[32,128]{1,0:T(8,128)S(1)}, f32[32,128]{1,0:T(8,128)S(1)}, u32[]{:S(2)}, u32[]{:S(2)}) %collective-permute-start.17) | collective-permute-done | bytes 16416 | tf_op jit(solution)/shard_map/ppermute | solution.py:179
  29.3 0.6 %collective-permute-done.16 = f32[32,128]{1,0:T(8,128)S(1)} collective-permute-done((f32[32,128]{1,0:T(8,128)S(1)}, f32[32,128]{1,0:T(8,128)S(1)}, u32[]{:S(2)}, u32[]{:S(2)}) %collective-permute-start.16) | collective-permute-done | bytes 16416 | tf_op jit(solution)/shard_map/ppermute | solution.py:179
  29.8 0.0 collective-permute-done.14
  29.8 0.0 collective-permute-done.15
  29.8 0.6 %add_add_fusion.1 = f32[32,128]{1,0:T(8,128)} fusion(f32[32,128]{1,0:T(8,128)S(1)} %collective-permute-done.17, f32[32,128]{1,0:T(8,128)S(1)} %collective-permute-done.16, f32[32,128]{1,0:T(8,128)S(1)} %collective-permute-done.14, f32[32,128]{1,0:T(8,128)S(1)} %collective-permute-done.15), kind=kLoop, calls=%fused_computation.6 | loop fusion | flops 12288 | bytes 81920 | tf_op jit(solution)/shard_map/add | solution.py:189
  (5 shorter events, 0.1 us)
Async XLA Ops:
  0.0 7.2 %collective-permute-start.2 = (f32[32,128]{1,0:T(8,128)}, f32[32,128]{1,0:T(8,128)S(1)}, u32[]{:S(2)}, u32[]{:S(2)}) collective-permute-start(f32[32,128]{1,0:T(8,128)} %bitcast.27), channel_id=1, source_target_pairs={{0,17},{1,16},{2,19},{3,18},{4,21},{5,20},{6,23},{7,22},{8,25},{9,... | collective-permute-start | bytes 49160 | tf_op jit(solution)/shard_map/ppermute | solution.py:179
  3.5 5.2 %collective-permute-start.1 = (f32[32,128]{1,0:T(8,128)}, f32[32,128]{1,0:T(8,128)S(1)}, u32[]{:S(2)}, u32[]{:S(2)}) collective-permute-start(f32[32,128]{1,0:T(8,128)} %bitcast.28), channel_id=1, source_target_pairs={{0,25},{1,24},{2,27},{3,26},{4,29},{5,28},{6,31},{7,30},{8,17},{9,... | collective-permute-start | bytes 49160 | tf_op jit(solution)/shard_map/ppermute | solution.py:179
  5.1 3.6 %collective-permute-start = (f32[32,128]{1,0:T(8,128)}, f32[32,128]{1,0:T(8,128)S(1)}, u32[]{:S(2)}, u32[]{:S(2)}) collective-permute-start(f32[32,128]{1,0:T(8,128)} %bitcast.29), channel_id=1, source_target_pairs={{0,9},{1,8},{2,11},{3,10},{4,13},{5,12},{6,15},{7,14},{8,1},{9,0},... | collective-permute-start | bytes 49160 | tf_op jit(solution)/shard_map/ppermute | solution.py:179
  8.7 5.3 %collective-permute-start.4 = (f32[4,32,128]{2,1,0:T(8,128)S(1)}, f32[4,32,128]{2,1,0:T(8,128)S(1)}, u32[]{:S(2)}, u32[]{:S(2)}) collective-permute-start(f32[4,32,128]{2,1,0:T(8,128)S(1)} %pad_maximum_fusion.refs_2_), channel_id=1, source_target_pairs={{0,7},{1,6},{2,5},{3,4},{4,3},{5,2},{6,1},{7,0},{8,15},{9,14},{10,... | collective-permute-start | bytes 196616 | tf_op jit(solution)/shard_map/ppermute | solution.py:179
  11.5 3.7 %collective-permute-start.7 = (f32[4,32,128]{2,1,0:T(8,128)S(1)}, f32[4,32,128]{2,1,0:T(8,128)S(1)}, u32[]{:S(2)}, u32[]{:S(2)}) collective-permute-start(f32[4,32,128]{2,1,0:T(8,128)S(1)} %pad_maximum_fusion.refs_2_), channel_id=1, source_target_pairs={{0,5},{1,2},{2,1},{3,6},{4,7},{5,0},{6,3},{7,4},{8,13},{9,10},{10,... | collective-permute-start | bytes 196616 | tf_op jit(solution)/shard_map/ppermute | solution.py:179
  11.5 4.4 %collective-permute-start.6 = (f32[4,32,128]{2,1,0:T(8,128)S(1)}, f32[4,32,128]{2,1,0:T(8,128)S(1)}, u32[]{:S(2)}, u32[]{:S(2)}) collective-permute-start(f32[4,32,128]{2,1,0:T(8,128)S(1)} %pad_maximum_fusion.refs_2_), channel_id=1, source_target_pairs={{0,3},{1,4},{2,7},{3,0},{4,1},{5,6},{6,5},{7,2},{8,11},{9,12},{10,... | collective-permute-start | bytes 196616 | tf_op jit(solution)/shard_map/ppermute | solution.py:179
  12.3 3.7 %collective-permute-start.3 = (f32[4,32,128]{2,1,0:T(8,128)S(1)}, f32[4,32,128]{2,1,0:T(8,128)S(1)}, u32[]{:S(2)}, u32[]{:S(2)}) collective-permute-start(f32[4,32,128]{2,1,0:T(8,128)S(1)} %pad_maximum_fusion.refs_2_), channel_id=1, source_target_pairs={{0,1},{1,0},{2,3},{3,2},{4,5},{5,4},{6,7},{7,6},{8,9},{9,8},{10,11... | collective-permute-start | bytes 196616 | tf_op jit(solution)/shard_map/ppermute | solution.py:179
  14.0 2.0 %collective-permute-start.5 = (f32[4,32,128]{2,1,0:T(8,128)S(1)}, f32[4,32,128]{2,1,0:T(8,128)S(1)}, u32[]{:S(2)}, u32[]{:S(2)}) collective-permute-start(f32[4,32,128]{2,1,0:T(8,128)S(1)} %collective-permute-done.4.refs_4_), channel_id=1, source_target_pairs={{0,1},{1,0},{2,3},{3,2},{4,5},{5,4},{6,7},{7,6},{8,9},{9,8},{10,11... | collective-permute-start | bytes 196616 | tf_op jit(solution)/shard_map/ppermute | solution.py:179
  15.2 3.4 %collective-permute-start.8 = (f32[4,32,128]{2,1,0:T(8,128)S(1)}, f32[4,32,128]{2,1,0:T(8,128)S(1)}, u32[]{:S(2)}, u32[]{:S(2)}) collective-permute-start(f32[4,32,128]{2,1,0:T(8,128)S(1)} %collective-permute-done.7.refs_4_), channel_id=1, source_target_pairs={{0,1},{1,0},{2,3},{3,2},{4,5},{5,4},{6,7},{7,6},{8,9},{9,8},{10,11... | collective-permute-start | bytes 196616 | tf_op jit(solution)/shard_map/ppermute | solution.py:179
  16.0 2.7 %collective-permute-start.9 = (f32[4,32,128]{2,1,0:T(8,128)S(1)}, f32[4,32,128]{2,1,0:T(8,128)S(1)}, u32[]{:S(2)}, u32[]{:S(2)}) collective-permute-start(f32[4,32,128]{2,1,0:T(8,128)S(1)} %collective-permute-done.6.refs_2_), channel_id=1, source_target_pairs={{0,1},{1,0},{2,3},{3,2},{4,5},{5,4},{6,7},{7,6},{8,9},{9,8},{10,11... | collective-permute-start | bytes 196616 | tf_op jit(solution)/shard_map/ppermute | solution.py:179
  16.4 4.8 %collective-permute-start.13 = (f32[4,32,128]{2,1,0:T(8,128)S(1)}, f32[4,32,128]{2,1,0:T(8,128)S(1)}, u32[]{:S(2)}, u32[]{:S(2)}) collective-permute-start(f32[4,32,128]{2,1,0:T(8,128)S(1)} %get-tuple-element.20), channel_id=1, source_target_pairs={{0,7},{1,6},{2,5},{3,4},{4,3},{5,2},{6,1},{7,0},{8,15},{9,14},{10,... | collective-permute-start | bytes 196616 | tf_op jit(solution)/shard_map/ppermute | solution.py:179
  18.5 2.7 %collective-permute-start.12 = (f32[4,32,128]{2,1,0:T(8,128)S(1)}, f32[4,32,128]{2,1,0:T(8,128)S(1)}, u32[]{:S(2)}, u32[]{:S(2)}) collective-permute-start(f32[4,32,128]{2,1,0:T(8,128)S(1)} %get-tuple-element.19), channel_id=1, source_target_pairs={{0,1},{1,0},{2,3},{3,2},{4,5},{5,4},{6,7},{7,6},{8,9},{9,8},{10,11... | collective-permute-start | bytes 196616 | tf_op jit(solution)/shard_map/ppermute | solution.py:179
  19.1 3.8 %collective-permute-start.10 = (f32[4,32,128]{2,1,0:T(8,128)S(1)}, f32[4,32,128]{2,1,0:T(8,128)S(1)}, u32[]{:S(2)}, u32[]{:S(2)}) collective-permute-start(f32[4,32,128]{2,1,0:T(8,128)S(1)} %get-tuple-element.18), channel_id=1, source_target_pairs={{0,3},{1,4},{2,7},{3,0},{4,1},{5,6},{6,5},{7,2},{8,11},{9,12},{10,... | collective-permute-start | bytes 196616 | tf_op jit(solution)/shard_map/ppermute | solution.py:179
  19.9 4.2 %collective-permute-start.11 = (f32[4,32,128]{2,1,0:T(8,128)S(1)}, f32[4,32,128]{2,1,0:T(8,128)S(1)}, u32[]{:S(2)}, u32[]{:S(2)}) collective-permute-start(f32[4,32,128]{2,1,0:T(8,128)S(1)} %get-tuple-element.17), channel_id=1, source_target_pairs={{0,5},{1,2},{2,1},{3,6},{4,7},{5,0},{6,3},{7,4},{8,13},{9,10},{10,... | collective-permute-start | bytes 196616 | tf_op jit(solution)/shard_map/ppermute | solution.py:179
  24.1 5.2 %collective-permute-start.17 = (f32[32,128]{1,0:T(8,128)S(1)}, f32[32,128]{1,0:T(8,128)S(1)}, u32[]{:S(2)}, u32[]{:S(2)}) collective-permute-start(f32[32,128]{1,0:T(8,128)S(1)} %get-tuple-element.22), channel_id=1, source_target_pairs={{0,25},{1,24},{2,27},{3,26},{4,29},{5,28},{6,31},{7,30},{8,17},{9,... | collective-permute-start | bytes 49160 | tf_op jit(solution)/shard_map/ppermute | solution.py:179
  25.7 4.1 %collective-permute-start.16 = (f32[32,128]{1,0:T(8,128)S(1)}, f32[32,128]{1,0:T(8,128)S(1)}, u32[]{:S(2)}, u32[]{:S(2)}) collective-permute-start(f32[32,128]{1,0:T(8,128)S(1)} %get-tuple-element.23), channel_id=1, source_target_pairs={{0,17},{1,16},{2,19},{3,18},{4,21},{5,20},{6,23},{7,22},{8,25},{9,... | collective-permute-start | bytes 49160 | tf_op jit(solution)/shard_map/ppermute | solution.py:179
  25.7 4.1 %collective-permute-start.14 = (f32[32,128]{1,0:T(8,128)S(1)}, f32[32,128]{1,0:T(8,128)S(1)}, u32[]{:S(2)}, u32[]{:S(2)}) collective-permute-start(f32[32,128]{1,0:T(8,128)S(1)} %get-tuple-element.24), channel_id=1, source_target_pairs={{0,9},{1,8},{2,11},{3,10},{4,13},{5,12},{6,15},{7,14},{8,1},{9,0},... | collective-permute-start | bytes 49160 | tf_op jit(solution)/shard_map/ppermute | solution.py:179
  27.8 2.1 %collective-permute-start.15 = (f32[32,128]{1,0:T(8,128)S(1)}, f32[32,128]{1,0:T(8,128)S(1)}, u32[]{:S(2)}, u32[]{:S(2)}) collective-permute-start(f32[32,128]{1,0:T(8,128)S(1)} %get-tuple-element.21), channel_id=1, source_target_pairs={{0,1},{1,0},{2,3},{3,2},{4,5},{5,4},{6,7},{7,6},{8,9},{9,8},{10,11... | collective-permute-start | bytes 49160 | tf_op jit(solution)/shard_map/ppermute | solution.py:179

commit v11 on v10

--- a/solution.py
+++ b/solution.py
@@ -121,19 +121,18 @@
                         columns[column, first_row : first_row + 4 * rows, :] = high
                         columns[column, total_rows + first_row : total_rows + first_row + 4 * rows, :] = low
 
-    def one_group(index, carry):
-        first = index * GROUP
+    def add_slots(number):
         products = []
-        for step in range(GROUP):
-            got = jnp.dot(columns[codes[0, first + step]], halves[first + step], preferred_element_type=jnp.float32)
+        for slot in range(number):
+            got = jnp.dot(columns[codes[0, slot]], halves[slot], preferred_element_type=jnp.float32)
             upper, lower = got[:total_rows], got[total_rows:]
             products.append((upper[:, :W] + lower[:, :W]) + (upper[:, W:] + lower[:, W:]))
-        for step in range(GROUP):
-            place = codes[1, first + step]
-            totals[place] = totals[place] + products[step]
-        return carry
-
-    lax.fori_loop(0, (codes[2, 0] + GROUP - 1) // GROUP, one_group, 0)
+        for slot, product in enumerate(products):
+            place = codes[1, slot]
+            totals[place] = totals[place] + product
+
+    pl.when(codes[2, 0] <= GROUP)(lambda: add_slots(GROUP))
+    pl.when(codes[2, 0] > GROUP)(lambda: add_slots(halves.shape[0]))
     for chunk in range(0, chunk_count, 2):
         part = slice(chunk * rows, (chunk + 2) * rows)
         for tile in range(0, out_tiles, 2):

time: 30.7 us -> 30.6 us (level)
  transfers between devices with their start and end apart: 18 -> 18, of which waited for: 8 -> 8; matrix products, arithmetic and copies ran while one was open for 0% -> 0% of each run, Pallas kernels for 6% -> 7%
where the time goes in v11:
time: 30.6 us; the launch traced here: 30.5 us
  starting transfers between devices  17.5 us (57%)
  waiting for transfers between devices  9.52 us (31%)
  Pallas kernels  2.07 us (7%)
  between operations  0.73 us (2%)
  other arithmetic  0.64 us (2%)
    ppermute x18, starting transfers between devices, swap(): return lax.ppermute(value, ('pair', 'virt'), routes)  17.5 us
    ppermute x18, waiting for transfers between devices, swap(): return lax.ppermute(value, ('pair', 'virt'), routes)  9.52 us
    pallas_call x1, Pallas kernels, prepare(): pl.pallas_call(kernel, out_shape=(jax.ShapeDtypeStruct((slots, W, 2 * W),...  1.37 us
    pallas_call x2, Pallas kernels, quarter_terms(): pl.pallas_call(kernel, out_shape=jax.ShapeDtypeStruct((len(quarters) * fa...  0.71 us
    add x2, other arithmetic, swap_sum(): return sum(received[1:], received[0])  0.63 us
  transfers between devices with their start and end apart: 18, of which 8 were waited for; matrix products, arithmetic and copies ran while one was open for 0% of the time, Pallas kernels for 7%

profile of v11, /device:TPU:0, one launch (start us, length us, event | category | flops | bytes accessed | tf_op | source)
XLA Modules:
  0.0 30.5 jit_solution(10855099064405010282)
XLA Ops:
  0.0 3.5 %collective-permute-start.2 = (f32[32,128]{1,0:T(8,128)}, f32[32,128]{1,0:T(8,128)S(1)}, u32[]{:S(2)}, u32[]{:S(2)}) collective-permute-start(f32[32,128]{1,0:T(8,128)} %bitcast.27), channel_id=1, source_target_pairs={{0,17},{1,16},{2,19},{3,18},{4,21},{5,20},{6,23},{7,22},{8,25},{9,... | collective-permute-start | bytes 49160 | tf_op jit(solution)/shard_map/ppermute | solution.py:178
  3.5 1.6 %collective-permute-start.1 = (f32[32,128]{1,0:T(8,128)}, f32[32,128]{1,0:T(8,128)S(1)}, u32[]{:S(2)}, u32[]{:S(2)}) collective-permute-start(f32[32,128]{1,0:T(8,128)} %bitcast.28), channel_id=1, source_target_pairs={{0,25},{1,24},{2,27},{3,26},{4,29},{5,28},{6,31},{7,30},{8,17},{9,... | collective-permute-start | bytes 49160 | tf_op jit(solution)/shard_map/ppermute | solution.py:178
  5.1 0.2 collective-permute-start
  6.0 1.4 %shard_map.55 = (bf16[32,128,256]{2,1,0:T(8,128)(2,1)S(1)}, s32[3,32]{1,0:T(4,128)S(4)}, f32[32,128]{1,0:T(8,128)S(1)}) custom-call(s32[1,1]{1,0:T(1,128)S(6)} %copy.8.refs_0_, s32[1,32]{1,0:T(1,128)} %bitcast.34, s32[1,32]{1,0:T(1,128)} %bitcast.35, f32[32,128,128]{2,1,0:T(8,128)} %bitcast.26, f32[32,128]{1,0:T(8,128)} %bitcast.30), custom_call_target="tpu_custom_call" | custom-call | flops 2097152 | bytes 4194304 | tf_op jit(solution)/shard_map/pallas_call | solution.py:69
  7.4 0.0 collective-permute-done.2
  7.4 1.3 %collective-permute-done.1 = f32[32,128]{1,0:T(8,128)S(1)} collective-permute-done((f32[32,128]{1,0:T(8,128)}, f32[32,128]{1,0:T(8,128)S(1)}, u32[]{:S(2)}, u32[]{:S(2)}) %collective-permute-start.1) | collective-permute-done | bytes 16416 | tf_op jit(solution)/shard_map/ppermute | solution.py:178
  8.7 0.0 collective-permute-done
  8.7 2.8 %collective-permute-start.4 = (f32[4,32,128]{2,1,0:T(8,128)S(1)}, f32[4,32,128]{2,1,0:T(8,128)S(1)}, u32[]{:S(2)}, u32[]{:S(2)}) collective-permute-start(f32[4,32,128]{2,1,0:T(8,128)S(1)} %pad_maximum_fusion.refs_2_), channel_id=1, source_target_pairs={{0,7},{1,6},{2,5},{3,4},{4,3},{5,2},{6,1},{7,0},{8,15},{9,14},{10,... | collective-permute-start | bytes 196616 | tf_op jit(solution)/shard_map/ppermute | solution.py:178
  11.5 0.0 collective-permute-start.7
  11.5 0.8 %collective-permute-start.6 = (f32[4,32,128]{2,1,0:T(8,128)S(1)}, f32[4,32,128]{2,1,0:T(8,128)S(1)}, u32[]{:S(2)}, u32[]{:S(2)}) collective-permute-start(f32[4,32,128]{2,1,0:T(8,128)S(1)} %pad_maximum_fusion.refs_2_), channel_id=1, source_target_pairs={{0,3},{1,4},{2,7},{3,0},{4,1},{5,6},{6,5},{7,2},{8,11},{9,12},{10,... | collective-permute-start | bytes 196616 | tf_op jit(solution)/shard_map/ppermute | solution.py:178
  12.3 0.0 collective-permute-start.3
  12.3 1.7 %collective-permute-done.4.refs_4_ = f32[4,32,128]{2,1,0:T(8,128)S(1)} collective-permute-done((f32[4,32,128]{2,1,0:T(8,128)S(1)}, f32[4,32,128]{2,1,0:T(8,128)S(1)}, u32[]{:S(2)}, u32[]{:S(2)}) %collective-permute-start.4) | collective-permute-done | bytes 65568 | tf_op jit(solution)/shard_map/ppermute | solution.py:178
  14.0 0.1 collective-permute-start.5
  14.1 1.2 %collective-permute-done.7.refs_4_ = f32[4,32,128]{2,1,0:T(8,128)S(1)} collective-permute-done((f32[4,32,128]{2,1,0:T(8,128)S(1)}, f32[4,32,128]{2,1,0:T(8,128)S(1)}, u32[]{:S(2)}, u32[]{:S(2)}) %collective-permute-start.7) | collective-permute-done | bytes 65568 | tf_op jit(solution)/shard_map/ppermute | solution.py:178
  15.2 0.7 %collective-permute-start.8 = (f32[4,32,128]{2,1,0:T(8,128)S(1)}, f32[4,32,128]{2,1,0:T(8,128)S(1)}, u32[]{:S(2)}, u32[]{:S(2)}) collective-permute-start(f32[4,32,128]{2,1,0:T(8,128)S(1)} %collective-permute-done.7.refs_4_), channel_id=1, source_target_pairs={{0,1},{1,0},{2,3},{3,2},{4,5},{5,4},{6,7},{7,6},{8,9},{9,8},{10,11... | collective-permute-start | bytes 196616 | tf_op jit(solution)/shard_map/ppermute | solution.py:178
  16.0 0.0 collective-permute-done.6.refs_2_
  16.0 0.0 collective-permute-start.9
  16.0 0.0 collective-permute-done.3.refs_3_
  16.0 0.0 collective-permute-done.5.refs_5_
  16.0 0.4 %shard_map.56 = f32[8,32,128]{2,1,0:T(8,128)S(1)} custom-call(s32[3,32]{1,0:T(4,128)S(4)} %get-tuple-element.12.refs_0_, bf16[32,128,256]{2,1,0:T(8,128)(2,1)S(1)} %get-tuple-element.14.refs_1_, f32[4,32,128]{2,1,0:T(8,128)S(1)} %pad_maximum_fusion.refs_2_, f32[4,32,128]{2,1,0:T(8,128)S(1)} %collective-permute-done.3.refs_3_, ...), custom_call_target="tpu_custom_call" | custom-call | flops 268435456 | bytes 4194304 | tf_op jit(solution)/shard_map/pallas_call | solution.py:154
  16.4 2.1 %collective-permute-start.13 = (f32[4,32,128]{2,1,0:T(8,128)S(1)}, f32[4,32,128]{2,1,0:T(8,128)S(1)}, u32[]{:S(2)}, u32[]{:S(2)}) collective-permute-start(f32[4,32,128]{2,1,0:T(8,128)S(1)} %get-tuple-element.20), channel_id=1, source_target_pairs={{0,7},{1,6},{2,5},{3,4},{4,3},{5,2},{6,1},{7,0},{8,15},{9,14},{10,... | collective-permute-start | bytes 196616 | tf_op jit(solution)/shard_map/ppermute | solution.py:178
  18.5 0.2 collective-permute-start.12
  18.6 0.0 collective-permute-done.8.refs_3_
  18.6 0.0 collective-permute-done.9.refs_5_
  18.7 0.4 %shard_map.57 = f32[8,32,128]{2,1,0:T(8,128)S(1)} custom-call(s32[3,32]{1,0:T(4,128)S(4)} %get-tuple-element.12.refs_0_, bf16[32,128,256]{2,1,0:T(8,128)(2,1)S(1)} %get-tuple-element.14.refs_1_, f32[4,32,128]{2,1,0:T(8,128)S(1)} %collective-permute-done.6.refs_2_, f32[4,32,128]{2,1,0:T(8,128)S(1)} %collective-permute-done.8.refs_3_, ...), custom_call_target="tpu_custom_call" | custom-call | flops 268435456 | bytes 4194304 | tf_op jit(solution)/shard_map/pallas_call | solution.py:154
  19.0 1.0 %collective-permute-start.10 = (f32[4,32,128]{2,1,0:T(8,128)S(1)}, f32[4,32,128]{2,1,0:T(8,128)S(1)}, u32[]{:S(2)}, u32[]{:S(2)}) collective-permute-start(f32[4,32,128]{2,1,0:T(8,128)S(1)} %get-tuple-element.18), channel_id=1, source_target_pairs={{0,3},{1,4},{2,7},{3,0},{4,1},{5,6},{6,5},{7,2},{8,11},{9,12},{10,... | collective-permute-start | bytes 196616 | tf_op jit(solution)/shard_map/ppermute | solution.py:178
  20.0 0.2 collective-permute-start.11
  20.2 0.9 %collective-permute-done.13 = f32[4,32,128]{2,1,0:T(8,128)S(1)} collective-permute-done((f32[4,32,128]{2,1,0:T(8,128)S(1)}, f32[4,32,128]{2,1,0:T(8,128)S(1)}, u32[]{:S(2)}, u32[]{:S(2)}) %collective-permute-start.13) | collective-permute-done | bytes 65568 | tf_op jit(solution)/shard_map/ppermute | solution.py:178
  21.1 0.0 collective-permute-done.12
  21.1 1.6 %collective-permute-done.10 = f32[4,32,128]{2,1,0:T(8,128)S(1)} collective-permute-done((f32[4,32,128]{2,1,0:T(8,128)S(1)}, f32[4,32,128]{2,1,0:T(8,128)S(1)}, u32[]{:S(2)}, u32[]{:S(2)}) %collective-permute-start.10) | collective-permute-done | bytes 65568 | tf_op jit(solution)/shard_map/ppermute | solution.py:178
  22.8 1.2 %collective-permute-done.11 = f32[4,32,128]{2,1,0:T(8,128)S(1)} collective-permute-done((f32[4,32,128]{2,1,0:T(8,128)S(1)}, f32[4,32,128]{2,1,0:T(8,128)S(1)}, u32[]{:S(2)}, u32[]{:S(2)}) %collective-permute-start.11) | collective-permute-done | bytes 65568 | tf_op jit(solution)/shard_map/ppermute | solution.py:178
  24.1 1.8 %collective-permute-start.17 = (f32[32,128]{1,0:T(8,128)S(1)}, f32[32,128]{1,0:T(8,128)S(1)}, u32[]{:S(2)}, u32[]{:S(2)}) collective-permute-start(f32[32,128]{1,0:T(8,128)S(1)} %get-tuple-element.22), channel_id=1, source_target_pairs={{0,25},{1,24},{2,27},{3,26},{4,29},{5,28},{6,31},{7,30},{8,17},{9,... | collective-permute-start | bytes 49160 | tf_op jit(solution)/shard_map/ppermute | solution.py:178
  25.8 0.0 collective-permute-start.16
  25.8 1.8 %collective-permute-start.14 = (f32[32,128]{1,0:T(8,128)S(1)}, f32[32,128]{1,0:T(8,128)S(1)}, u32[]{:S(2)}, u32[]{:S(2)}) collective-permute-start(f32[32,128]{1,0:T(8,128)S(1)} %get-tuple-element.24), channel_id=1, source_target_pairs={{0,9},{1,8},{2,11},{3,10},{4,13},{5,12},{6,15},{7,14},{8,1},{9,0},... | collective-permute-start | bytes 49160 | tf_op jit(solution)/shard_map/ppermute | solution.py:178
  27.7 0.7 %collective-permute-start.15 = (f32[32,128]{1,0:T(8,128)S(1)}, f32[32,128]{1,0:T(8,128)S(1)}, u32[]{:S(2)}, u32[]{:S(2)}) collective-permute-start(f32[32,128]{1,0:T(8,128)S(1)} %get-tuple-element.21), channel_id=1, source_target_pairs={{0,1},{1,0},{2,3},{3,2},{4,5},{5,4},{6,7},{7,6},{8,9},{9,8},{10,11... | collective-permute-start | bytes 49160 | tf_op jit(solution)/shard_map/ppermute | solution.py:178
  28.4 1.0 %collective-permute-done.17 = f32[32,128]{1,0:T(8,128)S(1)} collective-permute-done((f32[32,128]{1,0:T(8,128)S(1)}, f32[32,128]{1,0:T(8,128)S(1)}, u32[]{:S(2)}, u32[]{:S(2)}) %collective-permute-start.17) | collective-permute-done | bytes 16416 | tf_op jit(solution)/shard_map/ppermute | solution.py:178
  29.4 0.5 %collective-permute-done.16 = f32[32,128]{1,0:T(8,128)S(1)} collective-permute-done((f32[32,128]{1,0:T(8,128)S(1)}, f32[32,128]{1,0:T(8,128)S(1)}, u32[]{:S(2)}, u32[]{:S(2)}) %collective-permute-start.16) | collective-permute-done | bytes 16416 | tf_op jit(solution)/shard_map/ppermute | solution.py:178
  29.9 0.0 collective-permute-done.14
  29.9 0.0 collective-permute-done.15
  29.9 0.6 %add_add_fusion.1 = f32[32,128]{1,0:T(8,128)} fusion(f32[32,128]{1,0:T(8,128)S(1)} %collective-permute-done.17, f32[32,128]{1,0:T(8,128)S(1)} %collective-permute-done.16, f32[32,128]{1,0:T(8,128)S(1)} %collective-permute-done.14, f32[32,128]{1,0:T(8,128)S(1)} %collective-permute-done.15), kind=kLoop, calls=%fused_computation.6 | loop fusion | flops 12288 | bytes 81920 | tf_op jit(solution)/shard_map/add | solution.py:188
  (5 shorter events, 0.1 us)
Async XLA Ops:
  0.0 7.4 %collective-permute-start.2 = (f32[32,128]{1,0:T(8,128)}, f32[32,128]{1,0:T(8,128)S(1)}, u32[]{:S(2)}, u32[]{:S(2)}) collective-permute-start(f32[32,128]{1,0:T(8,128)} %bitcast.27), channel_id=1, source_target_pairs={{0,17},{1,16},{2,19},{3,18},{4,21},{5,20},{6,23},{7,22},{8,25},{9,... | collective-permute-start | bytes 49160 | tf_op jit(solution)/shard_map/ppermute | solution.py:178
  3.5 5.2 %collective-permute-start.1 = (f32[32,128]{1,0:T(8,128)}, f32[32,128]{1,0:T(8,128)S(1)}, u32[]{:S(2)}, u32[]{:S(2)}) collective-permute-start(f32[32,128]{1,0:T(8,128)} %bitcast.28), channel_id=1, source_target_pairs={{0,25},{1,24},{2,27},{3,26},{4,29},{5,28},{6,31},{7,30},{8,17},{9,... | collective-permute-start | bytes 49160 | tf_op jit(solution)/shard_map/ppermute | solution.py:178
  5.1 3.6 %collective-permute-start = (f32[32,128]{1,0:T(8,128)}, f32[32,128]{1,0:T(8,128)S(1)}, u32[]{:S(2)}, u32[]{:S(2)}) collective-permute-start(f32[32,128]{1,0:T(8,128)} %bitcast.29), channel_id=1, source_target_pairs={{0,9},{1,8},{2,11},{3,10},{4,13},{5,12},{6,15},{7,14},{8,1},{9,0},... | collective-permute-start | bytes 49160 | tf_op jit(solution)/shard_map/ppermute | solution.py:178
  8.7 5.3 %collective-permute-start.4 = (f32[4,32,128]{2,1,0:T(8,128)S(1)}, f32[4,32,128]{2,1,0:T(8,128)S(1)}, u32[]{:S(2)}, u32[]{:S(2)}) collective-permute-start(f32[4,32,128]{2,1,0:T(8,128)S(1)} %pad_maximum_fusion.refs_2_), channel_id=1, source_target_pairs={{0,7},{1,6},{2,5},{3,4},{4,3},{5,2},{6,1},{7,0},{8,15},{9,14},{10,... | collective-permute-start | bytes 196616 | tf_op jit(solution)/shard_map/ppermute | solution.py:178
  11.5 3.7 %collective-permute-start.7 = (f32[4,32,128]{2,1,0:T(8,128)S(1)}, f32[4,32,128]{2,1,0:T(8,128)S(1)}, u32[]{:S(2)}, u32[]{:S(2)}) collective-permute-start(f32[4,32,128]{2,1,0:T(8,128)S(1)} %pad_maximum_fusion.refs_2_), channel_id=1, source_target_pairs={{0,5},{1,2},{2,1},{3,6},{4,7},{5,0},{6,3},{7,4},{8,13},{9,10},{10,... | collective-permute-start | bytes 196616 | tf_op jit(solution)/shard_map/ppermute | solution.py:178
  11.5 4.4 %collective-permute-start.6 = (f32[4,32,128]{2,1,0:T(8,128)S(1)}, f32[4,32,128]{2,1,0:T(8,128)S(1)}, u32[]{:S(2)}, u32[]{:S(2)}) collective-permute-start(f32[4,32,128]{2,1,0:T(8,128)S(1)} %pad_maximum_fusion.refs_2_), channel_id=1, source_target_pairs={{0,3},{1,4},{2,7},{3,0},{4,1},{5,6},{6,5},{7,2},{8,11},{9,12},{10,... | collective-permute-start | bytes 196616 | tf_op jit(solution)/shard_map/ppermute | solution.py:178
  12.3 3.7 %collective-permute-start.3 = (f32[4,32,128]{2,1,0:T(8,128)S(1)}, f32[4,32,128]{2,1,0:T(8,128)S(1)}, u32[]{:S(2)}, u32[]{:S(2)}) collective-permute-start(f32[4,32,128]{2,1,0:T(8,128)S(1)} %pad_maximum_fusion.refs_2_), channel_id=1, source_target_pairs={{0,1},{1,0},{2,3},{3,2},{4,5},{5,4},{6,7},{7,6},{8,9},{9,8},{10,11... | collective-permute-start | bytes 196616 | tf_op jit(solution)/shard_map/ppermute | solution.py:178
  14.0 2.0 %collective-permute-start.5 = (f32[4,32,128]{2,1,0:T(8,128)S(1)}, f32[4,32,128]{2,1,0:T(8,128)S(1)}, u32[]{:S(2)}, u32[]{:S(2)}) collective-permute-start(f32[4,32,128]{2,1,0:T(8,128)S(1)} %collective-permute-done.4.refs_4_), channel_id=1, source_target_pairs={{0,1},{1,0},{2,3},{3,2},{4,5},{5,4},{6,7},{7,6},{8,9},{9,8},{10,11... | collective-permute-start | bytes 196616 | tf_op jit(solution)/shard_map/ppermute | solution.py:178
  15.2 3.4 %collective-permute-start.8 = (f32[4,32,128]{2,1,0:T(8,128)S(1)}, f32[4,32,128]{2,1,0:T(8,128)S(1)}, u32[]{:S(2)}, u32[]{:S(2)}) collective-permute-start(f32[4,32,128]{2,1,0:T(8,128)S(1)} %collective-permute-done.7.refs_4_), channel_id=1, source_target_pairs={{0,1},{1,0},{2,3},{3,2},{4,5},{5,4},{6,7},{7,6},{8,9},{9,8},{10,11... | collective-permute-start | bytes 196616 | tf_op jit(solution)/shard_map/ppermute | solution.py:178
  16.0 2.7 %collective-permute-start.9 = (f32[4,32,128]{2,1,0:T(8,128)S(1)}, f32[4,32,128]{2,1,0:T(8,128)S(1)}, u32[]{:S(2)}, u32[]{:S(2)}) collective-permute-start(f32[4,32,128]{2,1,0:T(8,128)S(1)} %collective-permute-done.6.refs_2_), channel_id=1, source_target_pairs={{0,1},{1,0},{2,3},{3,2},{4,5},{5,4},{6,7},{7,6},{8,9},{9,8},{10,11... | collective-permute-start | bytes 196616 | tf_op jit(solution)/shard_map/ppermute | solution.py:178
  16.4 4.7 %collective-permute-start.13 = (f32[4,32,128]{2,1,0:T(8,128)S(1)}, f32[4,32,128]{2,1,0:T(8,128)S(1)}, u32[]{:S(2)}, u32[]{:S(2)}) collective-permute-start(f32[4,32,128]{2,1,0:T(8,128)S(1)} %get-tuple-element.20), channel_id=1, source_target_pairs={{0,7},{1,6},{2,5},{3,4},{4,3},{5,2},{6,1},{7,0},{8,15},{9,14},{10,... | collective-permute-start | bytes 196616 | tf_op jit(solution)/shard_map/ppermute | solution.py:178
  18.5 2.6 %collective-permute-start.12 = (f32[4,32,128]{2,1,0:T(8,128)S(1)}, f32[4,32,128]{2,1,0:T(8,128)S(1)}, u32[]{:S(2)}, u32[]{:S(2)}) collective-permute-start(f32[4,32,128]{2,1,0:T(8,128)S(1)} %get-tuple-element.19), channel_id=1, source_target_pairs={{0,1},{1,0},{2,3},{3,2},{4,5},{5,4},{6,7},{7,6},{8,9},{9,8},{10,11... | collective-permute-start | bytes 196616 | tf_op jit(solution)/shard_map/ppermute | solution.py:178
  19.0 3.8 %collective-permute-start.10 = (f32[4,32,128]{2,1,0:T(8,128)S(1)}, f32[4,32,128]{2,1,0:T(8,128)S(1)}, u32[]{:S(2)}, u32[]{:S(2)}) collective-permute-start(f32[4,32,128]{2,1,0:T(8,128)S(1)} %get-tuple-element.18), channel_id=1, source_target_pairs={{0,3},{1,4},{2,7},{3,0},{4,1},{5,6},{6,5},{7,2},{8,11},{9,12},{10,... | collective-permute-start | bytes 196616 | tf_op jit(solution)/shard_map/ppermute | solution.py:178
  20.0 4.0 %collective-permute-start.11 = (f32[4,32,128]{2,1,0:T(8,128)S(1)}, f32[4,32,128]{2,1,0:T(8,128)S(1)}, u32[]{:S(2)}, u32[]{:S(2)}) collective-permute-start(f32[4,32,128]{2,1,0:T(8,128)S(1)} %get-tuple-element.17), channel_id=1, source_target_pairs={{0,5},{1,2},{2,1},{3,6},{4,7},{5,0},{6,3},{7,4},{8,13},{9,10},{10,... | collective-permute-start | bytes 196616 | tf_op jit(solution)/shard_map/ppermute | solution.py:178
  24.1 5.3 %collective-permute-start.17 = (f32[32,128]{1,0:T(8,128)S(1)}, f32[32,128]{1,0:T(8,128)S(1)}, u32[]{:S(2)}, u32[]{:S(2)}) collective-permute-start(f32[32,128]{1,0:T(8,128)S(1)} %get-tuple-element.22), channel_id=1, source_target_pairs={{0,25},{1,24},{2,27},{3,26},{4,29},{5,28},{6,31},{7,30},{8,17},{9,... | collective-permute-start | bytes 49160 | tf_op jit(solution)/shard_map/ppermute | solution.py:178
  25.8 4.1 %collective-permute-start.16 = (f32[32,128]{1,0:T(8,128)S(1)}, f32[32,128]{1,0:T(8,128)S(1)}, u32[]{:S(2)}, u32[]{:S(2)}) collective-permute-start(f32[32,128]{1,0:T(8,128)S(1)} %get-tuple-element.23), channel_id=1, source_target_pairs={{0,17},{1,16},{2,19},{3,18},{4,21},{5,20},{6,23},{7,22},{8,25},{9,... | collective-permute-start | bytes 49160 | tf_op jit(solution)/shard_map/ppermute | solution.py:178
  25.8 4.1 %collective-permute-start.14 = (f32[32,128]{1,0:T(8,128)S(1)}, f32[32,128]{1,0:T(8,128)S(1)}, u32[]{:S(2)}, u32[]{:S(2)}) collective-permute-start(f32[32,128]{1,0:T(8,128)S(1)} %get-tuple-element.24), channel_id=1, source_target_pairs={{0,9},{1,8},{2,11},{3,10},{4,13},{5,12},{6,15},{7,14},{8,1},{9,0},... | collective-permute-start | bytes 49160 | tf_op jit(solution)/shard_map/ppermute | solution.py:178
  27.7 2.2 %collective-permute-start.15 = (f32[32,128]{1,0:T(8,128)S(1)}, f32[32,128]{1,0:T(8,128)S(1)}, u32[]{:S(2)}, u32[]{:S(2)}) collective-permute-start(f32[32,128]{1,0:T(8,128)S(1)} %get-tuple-element.21), channel_id=1, source_target_pairs={{0,1},{1,0},{2,3},{3,2},{4,5},{5,4},{6,7},{7,6},{8,9},{9,8},{10,11... | collective-permute-start | bytes 49160 | tf_op jit(solution)/shard_map/ppermute | solution.py:178

commit v12 on v11

--- a/solution.py
+++ b/solution.py
@@ -183,7 +183,7 @@
 
 
 def swap_sum(parts, pairs, virts, which, marks):
-    order = (1, 2, 0, 3) if which == "step" else (1, 0, *range(2, len(marks)))
+    order = (1, 0, 2, 3) if which == "step" else (1, 0, *range(2, len(marks)))
     received = [swap(parts[marks.index(mark)], pairs, virts, 1, **{which: mark}) for mark in order]
     return sum(received[1:], received[0])
 
@@ -208,7 +208,7 @@
     pieces = [pieces] + [[swap(piece, pairs, virts, mask) for piece in pieces] for mask in range(1, virts)]
     codes = pltpu.with_memory_space_constraint(codes, pltpu.SMEM)
     parts, order_size = {}, len(order)
-    for quarters in ((0, 3), (1, 2)):
+    for quarters in ((3,), (0, 1, 2)):
         sums = quarter_terms(codes, pieces, quarters, halves, rows, local_tiles)
         halves, sums = lax.optimization_barrier((halves, sums))
         parts.update({a: sums[at * order_size : (at + 1) * order_size] for at, a in enumerate(quarters)})

time: 30.6 us -> 30.5 us (level)
  waiting for transfers between devices: 9.52 us -> 8.93 us
  starting transfers between devices: 17.5 us -> 18 us
    ppermute x18, waiting for transfers between devices: 9.52 us -> 8.93 us  [swap(): return lax.ppermute(value, ('pair', 'virt'), routes)]
    ppermute x18, starting transfers between devices: 17.5 us -> 18 us  [swap(): return lax.ppermute(value, ('pair', 'virt'), routes)]
where the time goes in v12:
time: 30.5 us; the launch traced here: 30.3 us
  starting transfers between devices  18 us (59%)
  waiting for transfers between devices  8.93 us (29%)
  Pallas kernels  1.99 us (7%)
  between operations  0.72 us (2%)
  other arithmetic  0.64 us (2%)
    ppermute x18, starting transfers between devices, swap(): return lax.ppermute(value, ('pair', 'virt'), routes)  18 us
    ppermute x18, waiting for transfers between devices, swap(): return lax.ppermute(value, ('pair', 'virt'), routes)  8.93 us
    pallas_call x1, Pallas kernels, prepare(): pl.pallas_call(kernel, out_shape=(jax.ShapeDtypeStruct((slots, W, 2 * W),...  1.21 us
    pallas_call x2, Pallas kernels, quarter_terms(): pl.pallas_call(kernel, out_shape=jax.ShapeDtypeStruct((len(quarters) * fa...  0.78 us
    add x2, other arithmetic, swap_sum(): return sum(received[1:], received[0])  0.64 us
  transfers between devices with their start and end apart: 18, of which 8 were waited for; matrix products, arithmetic and copies ran while one was open for 0% of the time, Pallas kernels for 7%

profile of v12, /device:TPU:0, one launch (start us, length us, event | category | flops | bytes accessed | tf_op | source)
XLA Modules:
  0.0 30.3 jit_solution(16602421699858402748)
XLA Ops:
  0.0 3.5 %collective-permute-start.2 = (f32[32,128]{1,0:T(8,128)}, f32[32,128]{1,0:T(8,128)S(1)}, u32[]{:S(2)}, u32[]{:S(2)}) collective-permute-start(f32[32,128]{1,0:T(8,128)} %bitcast.27), channel_id=1, source_target_pairs={{0,17},{1,16},{2,19},{3,18},{4,21},{5,20},{6,23},{7,22},{8,25},{9,... | collective-permute-start | bytes 49160 | tf_op jit(solution)/shard_map/ppermute | solution.py:178
  3.5 1.6 %collective-permute-start.1 = (f32[32,128]{1,0:T(8,128)}, f32[32,128]{1,0:T(8,128)S(1)}, u32[]{:S(2)}, u32[]{:S(2)}) collective-permute-start(f32[32,128]{1,0:T(8,128)} %bitcast.28), channel_id=1, source_target_pairs={{0,25},{1,24},{2,27},{3,26},{4,29},{5,28},{6,31},{7,30},{8,17},{9,... | collective-permute-start | bytes 49160 | tf_op jit(solution)/shard_map/ppermute | solution.py:178
  5.1 0.2 collective-permute-start
  6.0 1.2 %shard_map.55 = (bf16[32,128,256]{2,1,0:T(8,128)(2,1)S(1)}, s32[3,32]{1,0:T(4,128)S(4)}, f32[32,128]{1,0:T(8,128)S(1)}) custom-call(s32[1,1]{1,0:T(1,128)S(6)} %copy.8.refs_0_, s32[1,32]{1,0:T(1,128)} %bitcast.34, s32[1,32]{1,0:T(1,128)} %bitcast.35, f32[32,128,128]{2,1,0:T(8,128)} %bitcast.26, f32[32,128]{1,0:T(8,128)} %bitcast.30), custom_call_target="tpu_custom_call" | custom-call | flops 2097152 | bytes 4194304 | tf_op jit(solution)/shard_map/pallas_call | solution.py:69
  7.2 0.0 collective-permute-done.2
  7.2 1.4 %collective-permute-done.1 = f32[32,128]{1,0:T(8,128)S(1)} collective-permute-done((f32[32,128]{1,0:T(8,128)}, f32[32,128]{1,0:T(8,128)S(1)}, u32[]{:S(2)}, u32[]{:S(2)}) %collective-permute-start.1) | collective-permute-done | bytes 16416 | tf_op jit(solution)/shard_map/ppermute | solution.py:178
  8.7 0.0 collective-permute-done
  8.7 2.8 %collective-permute-start.3 = (f32[4,32,128]{2,1,0:T(8,128)S(1)}, f32[4,32,128]{2,1,0:T(8,128)S(1)}, u32[]{:S(2)}, u32[]{:S(2)}) collective-permute-start(f32[4,32,128]{2,1,0:T(8,128)S(1)} %pad_maximum_fusion.refs_2_), channel_id=1, source_target_pairs={{0,7},{1,6},{2,5},{3,4},{4,3},{5,2},{6,1},{7,0},{8,15},{9,14},{10,... | collective-permute-start | bytes 196616 | tf_op jit(solution)/shard_map/ppermute | solution.py:178
  11.5 0.0 collective-permute-start.7
  11.5 0.8 %collective-permute-start.6 = (f32[4,32,128]{2,1,0:T(8,128)S(1)}, f32[4,32,128]{2,1,0:T(8,128)S(1)}, u32[]{:S(2)}, u32[]{:S(2)}) collective-permute-start(f32[4,32,128]{2,1,0:T(8,128)S(1)} %pad_maximum_fusion.refs_2_), channel_id=1, source_target_pairs={{0,3},{1,4},{2,7},{3,0},{4,1},{5,6},{6,5},{7,2},{8,11},{9,12},{10,... | collective-permute-start | bytes 196616 | tf_op jit(solution)/shard_map/ppermute | solution.py:178
  12.3 1.7 %collective-permute-done.3.refs_2_ = f32[4,32,128]{2,1,0:T(8,128)S(1)} collective-permute-done((f32[4,32,128]{2,1,0:T(8,128)S(1)}, f32[4,32,128]{2,1,0:T(8,128)S(1)}, u32[]{:S(2)}, u32[]{:S(2)}) %collective-permute-start.3) | collective-permute-done | bytes 65568 | tf_op jit(solution)/shard_map/ppermute | solution.py:178
  14.0 0.1 collective-permute-start.4
  14.1 0.4 %collective-permute-start.5 = (f32[4,32,128]{2,1,0:T(8,128)S(1)}, f32[4,32,128]{2,1,0:T(8,128)S(1)}, u32[]{:S(2)}, u32[]{:S(2)}) collective-permute-start(f32[4,32,128]{2,1,0:T(8,128)S(1)} %pad_maximum_fusion.refs_2_), channel_id=1, source_target_pairs={{0,1},{1,0},{2,3},{3,2},{4,5},{5,4},{6,7},{7,6},{8,9},{9,8},{10,11... | collective-permute-start | bytes 196616 | tf_op jit(solution)/shard_map/ppermute | solution.py:178
  14.5 0.7 %collective-permute-done.7.refs_6_ = f32[4,32,128]{2,1,0:T(8,128)S(1)} collective-permute-done((f32[4,32,128]{2,1,0:T(8,128)S(1)}, f32[4,32,128]{2,1,0:T(8,128)S(1)}, u32[]{:S(2)}, u32[]{:S(2)}) %collective-permute-start.7) | collective-permute-done | bytes 65568 | tf_op jit(solution)/shard_map/ppermute | solution.py:178
  15.2 0.7 %collective-permute-start.8 = (f32[4,32,128]{2,1,0:T(8,128)S(1)}, f32[4,32,128]{2,1,0:T(8,128)S(1)}, u32[]{:S(2)}, u32[]{:S(2)}) collective-permute-start(f32[4,32,128]{2,1,0:T(8,128)S(1)} %collective-permute-done.7.refs_6_), channel_id=1, source_target_pairs={{0,1},{1,0},{2,3},{3,2},{4,5},{5,4},{6,7},{7,6},{8,9},{9,8},{10,11... | collective-permute-start | bytes 196616 | tf_op jit(solution)/shard_map/ppermute | solution.py:178
  16.0 0.0 collective-permute-done.6.refs_4_
  16.0 0.0 collective-permute-start.9
  16.0 0.0 collective-permute-done.4.refs_3_
  16.0 0.3 %shard_map.56 = f32[4,32,128]{2,1,0:T(8,128)S(1)} custom-call(s32[3,32]{1,0:T(4,128)S(4)} %get-tuple-element.12.refs_0_, bf16[32,128,256]{2,1,0:T(8,128)(2,1)S(1)} %get-tuple-element.14.refs_1_, f32[4,32,128]{2,1,0:T(8,128)S(1)} %collective-permute-done.3.refs_2_, f32[4,32,128]{2,1,0:T(8,128)S(1)} %collective-permute-done.4.refs_3_), custom_call_target="tpu_custom_call" | custom-call | flops 268435456 | bytes 4194304 | tf_op jit(solution)/shard_map/pallas_call | solution.py:154
  16.3 2.1 %collective-permute-start.13 = (f32[4,32,128]{2,1,0:T(8,128)S(1)}, f32[4,32,128]{2,1,0:T(8,128)S(1)}, u32[]{:S(2)}, u32[]{:S(2)}) collective-permute-start(f32[4,32,128]{2,1,0:T(8,128)S(1)} %shard_map.56), channel_id=1, source_target_pairs={{0,7},{1,6},{2,5},{3,4},{4,3},{5,2},{6,1},{7,0},{8,15},{9,14},{10,... | collective-permute-start | bytes 196616 | tf_op jit(solution)/shard_map/ppermute | solution.py:178
  18.4 0.0 collective-permute-done.5.refs_3_
  18.4 0.0 collective-permute-done.8.refs_5_
  18.4 0.0 collective-permute-done.9.refs_7_
  18.4 0.5 %shard_map.57 = f32[12,32,128]{2,1,0:T(8,128)S(1)} custom-call(s32[3,32]{1,0:T(4,128)S(4)} %get-tuple-element.12.refs_0_, bf16[32,128,256]{2,1,0:T(8,128)(2,1)S(1)} %get-tuple-element.14.refs_1_, f32[4,32,128]{2,1,0:T(8,128)S(1)} %pad_maximum_fusion.refs_2_, f32[4,32,128]{2,1,0:T(8,128)S(1)} %collective-permute-done.5.refs_3_, ...), custom_call_target="tpu_custom_call" | custom-call | flops 268435456 | bytes 4194304 | tf_op jit(solution)/shard_map/pallas_call | solution.py:154
  18.9 0.4 %collective-permute-start.12 = (f32[4,32,128]{2,1,0:T(8,128)S(1)}, f32[4,32,128]{2,1,0:T(8,128)S(1)}, u32[]{:S(2)}, u32[]{:S(2)}) collective-permute-start(f32[4,32,128]{2,1,0:T(8,128)S(1)} %get-tuple-element.18), channel_id=1, source_target_pairs={{0,5},{1,2},{2,1},{3,6},{4,7},{5,0},{6,3},{7,4},{8,13},{9,10},{10,... | collective-permute-start | bytes 196616 | tf_op jit(solution)/shard_map/ppermute | solution.py:178
  19.4 0.9 %collective-permute-start.10 = (f32[4,32,128]{2,1,0:T(8,128)S(1)}, f32[4,32,128]{2,1,0:T(8,128)S(1)}, u32[]{:S(2)}, u32[]{:S(2)}) collective-permute-start(f32[4,32,128]{2,1,0:T(8,128)S(1)} %get-tuple-element.19), channel_id=1, source_target_pairs={{0,3},{1,4},{2,7},{3,0},{4,1},{5,6},{6,5},{7,2},{8,11},{9,12},{10,... | collective-permute-start | bytes 196616 | tf_op jit(solution)/shard_map/ppermute | solution.py:178
  20.2 0.0 collective-permute-start.11
  20.3 0.8 %collective-permute-done.13 = f32[4,32,128]{2,1,0:T(8,128)S(1)} collective-permute-done((f32[4,32,128]{2,1,0:T(8,128)S(1)}, f32[4,32,128]{2,1,0:T(8,128)S(1)}, u32[]{:S(2)}, u32[]{:S(2)}) %collective-permute-start.13) | collective-permute-done | bytes 65568 | tf_op jit(solution)/shard_map/ppermute | solution.py:178
  21.1 1.6 %collective-permute-done.12 = f32[4,32,128]{2,1,0:T(8,128)S(1)} collective-permute-done((f32[4,32,128]{2,1,0:T(8,128)S(1)}, f32[4,32,128]{2,1,0:T(8,128)S(1)}, u32[]{:S(2)}, u32[]{:S(2)}) %collective-permute-start.12) | collective-permute-done | bytes 65568 | tf_op jit(solution)/shard_map/ppermute | solution.py:178
  22.7 1.0 %collective-permute-done.10 = f32[4,32,128]{2,1,0:T(8,128)S(1)} collective-permute-done((f32[4,32,128]{2,1,0:T(8,128)S(1)}, f32[4,32,128]{2,1,0:T(8,128)S(1)}, u32[]{:S(2)}, u32[]{:S(2)}) %collective-permute-start.10) | collective-permute-done | bytes 65568 | tf_op jit(solution)/shard_map/ppermute | solution.py:178
  23.7 0.0 collective-permute-done.11
  23.8 1.8 %collective-permute-start.17 = (f32[32,128]{1,0:T(8,128)S(1)}, f32[32,128]{1,0:T(8,128)S(1)}, u32[]{:S(2)}, u32[]{:S(2)}) collective-permute-start(f32[32,128]{1,0:T(8,128)S(1)} %get-tuple-element.21), channel_id=1, source_target_pairs={{0,25},{1,24},{2,27},{3,26},{4,29},{5,28},{6,31},{7,30},{8,17},{9,... | collective-permute-start | bytes 49160 | tf_op jit(solution)/shard_map/ppermute | solution.py:178
  25.6 0.0 collective-permute-start.16
  25.6 2.0 %collective-permute-start.14 = (f32[32,128]{1,0:T(8,128)S(1)}, f32[32,128]{1,0:T(8,128)S(1)}, u32[]{:S(2)}, u32[]{:S(2)}) collective-permute-start(f32[32,128]{1,0:T(8,128)S(1)} %get-tuple-element.23), channel_id=1, source_target_pairs={{0,9},{1,8},{2,11},{3,10},{4,13},{5,12},{6,15},{7,14},{8,1},{9,0},... | collective-permute-start | bytes 49160 | tf_op jit(solution)/shard_map/ppermute | solution.py:178
  27.6 0.4 %collective-permute-start.15 = (f32[32,128]{1,0:T(8,128)S(1)}, f32[32,128]{1,0:T(8,128)S(1)}, u32[]{:S(2)}, u32[]{:S(2)}) collective-permute-start(f32[32,128]{1,0:T(8,128)S(1)} %get-tuple-element.20), channel_id=1, source_target_pairs={{0,1},{1,0},{2,3},{3,2},{4,5},{5,4},{6,7},{7,6},{8,9},{9,8},{10,11... | collective-permute-start | bytes 49160 | tf_op jit(solution)/shard_map/ppermute | solution.py:178
  28.1 0.7 %collective-permute-done.17 = f32[32,128]{1,0:T(8,128)S(1)} collective-permute-done((f32[32,128]{1,0:T(8,128)S(1)}, f32[32,128]{1,0:T(8,128)S(1)}, u32[]{:S(2)}, u32[]{:S(2)}) %collective-permute-start.17) | collective-permute-done | bytes 16416 | tf_op jit(solution)/shard_map/ppermute | solution.py:178
  28.8 0.9 %collective-permute-done.16 = f32[32,128]{1,0:T(8,128)S(1)} collective-permute-done((f32[32,128]{1,0:T(8,128)S(1)}, f32[32,128]{1,0:T(8,128)S(1)}, u32[]{:S(2)}, u32[]{:S(2)}) %collective-permute-start.16) | collective-permute-done | bytes 16416 | tf_op jit(solution)/shard_map/ppermute | solution.py:178
  29.7 0.0 collective-permute-done.14
  29.7 0.0 collective-permute-done.15
  29.7 0.6 %add_add_fusion.1 = f32[32,128]{1,0:T(8,128)} fusion(f32[32,128]{1,0:T(8,128)S(1)} %collective-permute-done.17, f32[32,128]{1,0:T(8,128)S(1)} %collective-permute-done.16, f32[32,128]{1,0:T(8,128)S(1)} %collective-permute-done.14, f32[32,128]{1,0:T(8,128)S(1)} %collective-permute-done.15), kind=kLoop, calls=%fused_computation.6 | loop fusion | flops 12288 | bytes 81920 | tf_op jit(solution)/shard_map/add | solution.py:188
  (4 shorter events, 0.0 us)
Async XLA Ops:
  0.0 7.2 %collective-permute-start.2 = (f32[32,128]{1,0:T(8,128)}, f32[32,128]{1,0:T(8,128)S(1)}, u32[]{:S(2)}, u32[]{:S(2)}) collective-permute-start(f32[32,128]{1,0:T(8,128)} %bitcast.27), channel_id=1, source_target_pairs={{0,17},{1,16},{2,19},{3,18},{4,21},{5,20},{6,23},{7,22},{8,25},{9,... | collective-permute-start | bytes 49160 | tf_op jit(solution)/shard_map/ppermute | solution.py:178
  3.5 5.2 %collective-permute-start.1 = (f32[32,128]{1,0:T(8,128)}, f32[32,128]{1,0:T(8,128)S(1)}, u32[]{:S(2)}, u32[]{:S(2)}) collective-permute-start(f32[32,128]{1,0:T(8,128)} %bitcast.28), channel_id=1, source_target_pairs={{0,25},{1,24},{2,27},{3,26},{4,29},{5,28},{6,31},{7,30},{8,17},{9,... | collective-permute-start | bytes 49160 | tf_op jit(solution)/shard_map/ppermute | solution.py:178
  5.1 3.6 %collective-permute-start = (f32[32,128]{1,0:T(8,128)}, f32[32,128]{1,0:T(8,128)S(1)}, u32[]{:S(2)}, u32[]{:S(2)}) collective-permute-start(f32[32,128]{1,0:T(8,128)} %bitcast.29), channel_id=1, source_target_pairs={{0,9},{1,8},{2,11},{3,10},{4,13},{5,12},{6,15},{7,14},{8,1},{9,0},... | collective-permute-start | bytes 49160 | tf_op jit(solution)/shard_map/ppermute | solution.py:178
  8.7 5.3 %collective-permute-start.3 = (f32[4,32,128]{2,1,0:T(8,128)S(1)}, f32[4,32,128]{2,1,0:T(8,128)S(1)}, u32[]{:S(2)}, u32[]{:S(2)}) collective-permute-start(f32[4,32,128]{2,1,0:T(8,128)S(1)} %pad_maximum_fusion.refs_2_), channel_id=1, source_target_pairs={{0,7},{1,6},{2,5},{3,4},{4,3},{5,2},{6,1},{7,0},{8,15},{9,14},{10,... | collective-permute-start | bytes 196616 | tf_op jit(solution)/shard_map/ppermute | solution.py:178
  11.5 3.7 %collective-permute-start.7 = (f32[4,32,128]{2,1,0:T(8,128)S(1)}, f32[4,32,128]{2,1,0:T(8,128)S(1)}, u32[]{:S(2)}, u32[]{:S(2)}) collective-permute-start(f32[4,32,128]{2,1,0:T(8,128)S(1)} %pad_maximum_fusion.refs_2_), channel_id=1, source_target_pairs={{0,5},{1,2},{2,1},{3,6},{4,7},{5,0},{6,3},{7,4},{8,13},{9,10},{10,... | collective-permute-start | bytes 196616 | tf_op jit(solution)/shard_map/ppermute | solution.py:178
  11.5 4.4 %collective-permute-start.6 = (f32[4,32,128]{2,1,0:T(8,128)S(1)}, f32[4,32,128]{2,1,0:T(8,128)S(1)}, u32[]{:S(2)}, u32[]{:S(2)}) collective-permute-start(f32[4,32,128]{2,1,0:T(8,128)S(1)} %pad_maximum_fusion.refs_2_), channel_id=1, source_target_pairs={{0,3},{1,4},{2,7},{3,0},{4,1},{5,6},{6,5},{7,2},{8,11},{9,12},{10,... | collective-permute-start | bytes 196616 | tf_op jit(solution)/shard_map/ppermute | solution.py:178
  14.0 2.0 %collective-permute-start.4 = (f32[4,32,128]{2,1,0:T(8,128)S(1)}, f32[4,32,128]{2,1,0:T(8,128)S(1)}, u32[]{:S(2)}, u32[]{:S(2)}) collective-permute-start(f32[4,32,128]{2,1,0:T(8,128)S(1)} %collective-permute-done.3.refs_2_), channel_id=1, source_target_pairs={{0,1},{1,0},{2,3},{3,2},{4,5},{5,4},{6,7},{7,6},{8,9},{9,8},{10,11... | collective-permute-start | bytes 196616 | tf_op jit(solution)/shard_map/ppermute | solution.py:178
  14.1 4.4 %collective-permute-start.5 = (f32[4,32,128]{2,1,0:T(8,128)S(1)}, f32[4,32,128]{2,1,0:T(8,128)S(1)}, u32[]{:S(2)}, u32[]{:S(2)}) collective-permute-start(f32[4,32,128]{2,1,0:T(8,128)S(1)} %pad_maximum_fusion.refs_2_), channel_id=1, source_target_pairs={{0,1},{1,0},{2,3},{3,2},{4,5},{5,4},{6,7},{7,6},{8,9},{9,8},{10,11... | collective-permute-start | bytes 196616 | tf_op jit(solution)/shard_map/ppermute | solution.py:178
  15.2 3.2 %collective-permute-start.8 = (f32[4,32,128]{2,1,0:T(8,128)S(1)}, f32[4,32,128]{2,1,0:T(8,128)S(1)}, u32[]{:S(2)}, u32[]{:S(2)}) collective-permute-start(f32[4,32,128]{2,1,0:T(8,128)S(1)} %collective-permute-done.7.refs_6_), channel_id=1, source_target_pairs={{0,1},{1,0},{2,3},{3,2},{4,5},{5,4},{6,7},{7,6},{8,9},{9,8},{10,11... | collective-permute-start | bytes 196616 | tf_op jit(solution)/shard_map/ppermute | solution.py:178
  16.0 2.5 %collective-permute-start.9 = (f32[4,32,128]{2,1,0:T(8,128)S(1)}, f32[4,32,128]{2,1,0:T(8,128)S(1)}, u32[]{:S(2)}, u32[]{:S(2)}) collective-permute-start(f32[4,32,128]{2,1,0:T(8,128)S(1)} %collective-permute-done.6.refs_4_), channel_id=1, source_target_pairs={{0,1},{1,0},{2,3},{3,2},{4,5},{5,4},{6,7},{7,6},{8,9},{9,8},{10,11... | collective-permute-start | bytes 196616 | tf_op jit(solution)/shard_map/ppermute | solution.py:178
  16.3 4.8 %collective-permute-start.13 = (f32[4,32,128]{2,1,0:T(8,128)S(1)}, f32[4,32,128]{2,1,0:T(8,128)S(1)}, u32[]{:S(2)}, u32[]{:S(2)}) collective-permute-start(f32[4,32,128]{2,1,0:T(8,128)S(1)} %shard_map.56), channel_id=1, source_target_pairs={{0,7},{1,6},{2,5},{3,4},{4,3},{5,2},{6,1},{7,0},{8,15},{9,14},{10,... | collective-permute-start | bytes 196616 | tf_op jit(solution)/shard_map/ppermute | solution.py:178
  18.9 3.8 %collective-permute-start.12 = (f32[4,32,128]{2,1,0:T(8,128)S(1)}, f32[4,32,128]{2,1,0:T(8,128)S(1)}, u32[]{:S(2)}, u32[]{:S(2)}) collective-permute-start(f32[4,32,128]{2,1,0:T(8,128)S(1)} %get-tuple-element.18), channel_id=1, source_target_pairs={{0,5},{1,2},{2,1},{3,6},{4,7},{5,0},{6,3},{7,4},{8,13},{9,10},{10,... | collective-permute-start | bytes 196616 | tf_op jit(solution)/shard_map/ppermute | solution.py:178
  19.4 4.3 %collective-permute-start.10 = (f32[4,32,128]{2,1,0:T(8,128)S(1)}, f32[4,32,128]{2,1,0:T(8,128)S(1)}, u32[]{:S(2)}, u32[]{:S(2)}) collective-permute-start(f32[4,32,128]{2,1,0:T(8,128)S(1)} %get-tuple-element.19), channel_id=1, source_target_pairs={{0,3},{1,4},{2,7},{3,0},{4,1},{5,6},{6,5},{7,2},{8,11},{9,12},{10,... | collective-permute-start | bytes 196616 | tf_op jit(solution)/shard_map/ppermute | solution.py:178
  20.2 3.5 %collective-permute-start.11 = (f32[4,32,128]{2,1,0:T(8,128)S(1)}, f32[4,32,128]{2,1,0:T(8,128)S(1)}, u32[]{:S(2)}, u32[]{:S(2)}) collective-permute-start(f32[4,32,128]{2,1,0:T(8,128)S(1)} %get-tuple-element.17), channel_id=1, source_target_pairs={{0,1},{1,0},{2,3},{3,2},{4,5},{5,4},{6,7},{7,6},{8,9},{9,8},{10,11... | collective-permute-start | bytes 196616 | tf_op jit(solution)/shard_map/ppermute | solution.py:178
  23.8 5.0 %collective-permute-start.17 = (f32[32,128]{1,0:T(8,128)S(1)}, f32[32,128]{1,0:T(8,128)S(1)}, u32[]{:S(2)}, u32[]{:S(2)}) collective-permute-start(f32[32,128]{1,0:T(8,128)S(1)} %get-tuple-element.21), channel_id=1, source_target_pairs={{0,25},{1,24},{2,27},{3,26},{4,29},{5,28},{6,31},{7,30},{8,17},{9,... | collective-permute-start | bytes 49160 | tf_op jit(solution)/shard_map/ppermute | solution.py:178
  25.6 4.1 %collective-permute-start.16 = (f32[32,128]{1,0:T(8,128)S(1)}, f32[32,128]{1,0:T(8,128)S(1)}, u32[]{:S(2)}, u32[]{:S(2)}) collective-permute-start(f32[32,128]{1,0:T(8,128)S(1)} %get-tuple-element.22), channel_id=1, source_target_pairs={{0,17},{1,16},{2,19},{3,18},{4,21},{5,20},{6,23},{7,22},{8,25},{9,... | collective-permute-start | bytes 49160 | tf_op jit(solution)/shard_map/ppermute | solution.py:178
  25.6 4.1 %collective-permute-start.14 = (f32[32,128]{1,0:T(8,128)S(1)}, f32[32,128]{1,0:T(8,128)S(1)}, u32[]{:S(2)}, u32[]{:S(2)}) collective-permute-start(f32[32,128]{1,0:T(8,128)S(1)} %get-tuple-element.23), channel_id=1, source_target_pairs={{0,9},{1,8},{2,11},{3,10},{4,13},{5,12},{6,15},{7,14},{8,1},{9,0},... | collective-permute-start | bytes 49160 | tf_op jit(solution)/shard_map/ppermute | solution.py:178
  27.6 2.0 %collective-permute-start.15 = (f32[32,128]{1,0:T(8,128)S(1)}, f32[32,128]{1,0:T(8,128)S(1)}, u32[]{:S(2)}, u32[]{:S(2)}) collective-permute-start(f32[32,128]{1,0:T(8,128)S(1)} %get-tuple-element.20), channel_id=1, source_target_pairs={{0,1},{1,0},{2,3},{3,2},{4,5},{5,4},{6,7},{7,6},{8,9},{9,8},{10,11... | collective-permute-start | bytes 49160 | tf_op jit(solution)/shard_map/ppermute | solution.py:178

commit v13 on v12

--- a/solution.py
+++ b/solution.py
@@ -9,7 +9,7 @@
 COPY_GROUP = 8
 GROUP = 16
 NEAR = 4
-SWITCHED = (0, 2, 1, 3)
+SWITCHED = (0, 1, 2, 3)
 SMEM = pl.BlockSpec(memory_space=pltpu.SMEM)
 VMEM = pl.BlockSpec(memory_space=pltpu.VMEM)
 

time: 30.5 us -> 30.6 us (level)
  no operation moved by 1% of the time
where the time goes in v13:
time: 30.6 us; the launch traced here: 30.4 us
  starting transfers between devices  18 us (59%)
  waiting for transfers between devices  9.11 us (30%)
  Pallas kernels  1.98 us (6%)
  between operations  0.72 us (2%)
  other arithmetic  0.64 us (2%)
    ppermute x18, starting transfers between devices, swap(): return lax.ppermute(value, ('pair', 'virt'), routes)  18 us
    ppermute x18, waiting for transfers between devices, swap(): return lax.ppermute(value, ('pair', 'virt'), routes)  9.11 us
    pallas_call x1, Pallas kernels, prepare(): pl.pallas_call(kernel, out_shape=(jax.ShapeDtypeStruct((slots, W, 2 * W),...  1.21 us
    pallas_call x2, Pallas kernels, quarter_terms(): pl.pallas_call(kernel, out_shape=jax.ShapeDtypeStruct((len(quarters) * fa...  0.77 us
    add x2, other arithmetic, swap_sum(): return sum(received[1:], received[0])  0.64 us
  transfers between devices with their start and end apart: 18, of which 8 were waited for; matrix products, arithmetic and copies ran while one was open for 0% of the time, Pallas kernels for 7%

profile of v13, /device:TPU:0, one launch (start us, length us, event | category | flops | bytes accessed | tf_op | source)
XLA Modules:
  0.0 30.4 jit_solution(740828908287816769)
XLA Ops:
  0.0 3.5 %collective-permute-start.2 = (f32[32,128]{1,0:T(8,128)}, f32[32,128]{1,0:T(8,128)S(1)}, u32[]{:S(2)}, u32[]{:S(2)}) collective-permute-start(f32[32,128]{1,0:T(8,128)} %bitcast.27), channel_id=1, source_target_pairs={{0,17},{1,16},{2,19},{3,18},{4,21},{5,20},{6,23},{7,22},{8,25},{9,... | collective-permute-start | bytes 49160 | tf_op jit(solution)/shard_map/ppermute | solution.py:178
  3.5 1.6 %collective-permute-start.1 = (f32[32,128]{1,0:T(8,128)}, f32[32,128]{1,0:T(8,128)S(1)}, u32[]{:S(2)}, u32[]{:S(2)}) collective-permute-start(f32[32,128]{1,0:T(8,128)} %bitcast.28), channel_id=1, source_target_pairs={{0,25},{1,24},{2,27},{3,26},{4,29},{5,28},{6,31},{7,30},{8,17},{9,... | collective-permute-start | bytes 49160 | tf_op jit(solution)/shard_map/ppermute | solution.py:178
  5.1 0.2 collective-permute-start
  6.0 1.2 %shard_map.55 = (bf16[32,128,256]{2,1,0:T(8,128)(2,1)S(1)}, s32[3,32]{1,0:T(4,128)S(4)}, f32[32,128]{1,0:T(8,128)S(1)}) custom-call(s32[1,1]{1,0:T(1,128)S(6)} %copy.8.refs_0_, s32[1,32]{1,0:T(1,128)} %bitcast.34, s32[1,32]{1,0:T(1,128)} %bitcast.35, f32[32,128,128]{2,1,0:T(8,128)} %bitcast.26, f32[32,128]{1,0:T(8,128)} %bitcast.30), custom_call_target="tpu_custom_call" | custom-call | flops 2097152 | bytes 4194304 | tf_op jit(solution)/shard_map/pallas_call | solution.py:69
  7.2 0.0 collective-permute-done.2
  7.2 1.4 %collective-permute-done.1 = f32[32,128]{1,0:T(8,128)S(1)} collective-permute-done((f32[32,128]{1,0:T(8,128)}, f32[32,128]{1,0:T(8,128)S(1)}, u32[]{:S(2)}, u32[]{:S(2)}) %collective-permute-start.1) | collective-permute-done | bytes 16416 | tf_op jit(solution)/shard_map/ppermute | solution.py:178
  8.7 0.0 collective-permute-done
  8.7 2.8 %collective-permute-start.3 = (f32[4,32,128]{2,1,0:T(8,128)S(1)}, f32[4,32,128]{2,1,0:T(8,128)S(1)}, u32[]{:S(2)}, u32[]{:S(2)}) collective-permute-start(f32[4,32,128]{2,1,0:T(8,128)S(1)} %pad_maximum_fusion.refs_2_), channel_id=1, source_target_pairs={{0,7},{1,6},{2,5},{3,4},{4,3},{5,2},{6,1},{7,0},{8,15},{9,14},{10,... | collective-permute-start | bytes 196616 | tf_op jit(solution)/shard_map/ppermute | solution.py:178
  11.5 0.0 collective-permute-start.6
  11.5 0.8 %collective-permute-start.8 = (f32[4,32,128]{2,1,0:T(8,128)S(1)}, f32[4,32,128]{2,1,0:T(8,128)S(1)}, u32[]{:S(2)}, u32[]{:S(2)}) collective-permute-start(f32[4,32,128]{2,1,0:T(8,128)S(1)} %pad_maximum_fusion.refs_2_), channel_id=1, source_target_pairs={{0,5},{1,4},{2,7},{3,6},{4,1},{5,0},{6,3},{7,2},{8,13},{9,12},{10,... | collective-permute-start | bytes 196616 | tf_op jit(solution)/shard_map/ppermute | solution.py:178
  12.3 1.7 %collective-permute-done.3.refs_2_ = f32[4,32,128]{2,1,0:T(8,128)S(1)} collective-permute-done((f32[4,32,128]{2,1,0:T(8,128)S(1)}, f32[4,32,128]{2,1,0:T(8,128)S(1)}, u32[]{:S(2)}, u32[]{:S(2)}) %collective-permute-start.3) | collective-permute-done | bytes 65568 | tf_op jit(solution)/shard_map/ppermute | solution.py:178
  14.0 0.1 collective-permute-start.4
  14.1 0.4 %collective-permute-start.5 = (f32[4,32,128]{2,1,0:T(8,128)S(1)}, f32[4,32,128]{2,1,0:T(8,128)S(1)}, u32[]{:S(2)}, u32[]{:S(2)}) collective-permute-start(f32[4,32,128]{2,1,0:T(8,128)S(1)} %pad_maximum_fusion.refs_2_), channel_id=1, source_target_pairs={{0,1},{1,0},{2,3},{3,2},{4,5},{5,4},{6,7},{7,6},{8,9},{9,8},{10,11... | collective-permute-start | bytes 196616 | tf_op jit(solution)/shard_map/ppermute | solution.py:178
  14.5 1.4 %collective-permute-done.6.refs_4_ = f32[4,32,128]{2,1,0:T(8,128)S(1)} collective-permute-done((f32[4,32,128]{2,1,0:T(8,128)S(1)}, f32[4,32,128]{2,1,0:T(8,128)S(1)}, u32[]{:S(2)}, u32[]{:S(2)}) %collective-permute-start.6) | collective-permute-done | bytes 65568 | tf_op jit(solution)/shard_map/ppermute | solution.py:178
  15.9 0.1 collective-permute-start.7
  16.0 0.0 collective-permute-done.8.refs_6_
  16.0 0.4 %collective-permute-start.9 = (f32[4,32,128]{2,1,0:T(8,128)S(1)}, f32[4,32,128]{2,1,0:T(8,128)S(1)}, u32[]{:S(2)}, u32[]{:S(2)}) collective-permute-start(f32[4,32,128]{2,1,0:T(8,128)S(1)} %collective-permute-done.8.refs_6_), channel_id=1, source_target_pairs={{0,1},{1,0},{2,3},{3,2},{4,5},{5,4},{6,7},{7,6},{8,9},{9,8},{10,11... | collective-permute-start | bytes 196616 | tf_op jit(solution)/shard_map/ppermute | solution.py:178
  16.4 0.0 collective-permute-done.4.refs_3_
  16.4 0.3 %shard_map.56 = f32[4,32,128]{2,1,0:T(8,128)S(1)} custom-call(s32[3,32]{1,0:T(4,128)S(4)} %get-tuple-element.12.refs_0_, bf16[32,128,256]{2,1,0:T(8,128)(2,1)S(1)} %get-tuple-element.14.refs_1_, f32[4,32,128]{2,1,0:T(8,128)S(1)} %collective-permute-done.3.refs_2_, f32[4,32,128]{2,1,0:T(8,128)S(1)} %collective-permute-done.4.refs_3_), custom_call_target="tpu_custom_call" | custom-call | flops 268435456 | bytes 4194304 | tf_op jit(solution)/shard_map/pallas_call | solution.py:154
  16.7 1.9 %collective-permute-start.13 = (f32[4,32,128]{2,1,0:T(8,128)S(1)}, f32[4,32,128]{2,1,0:T(8,128)S(1)}, u32[]{:S(2)}, u32[]{:S(2)}) collective-permute-start(f32[4,32,128]{2,1,0:T(8,128)S(1)} %shard_map.56), channel_id=1, source_target_pairs={{0,7},{1,6},{2,5},{3,4},{4,3},{5,2},{6,1},{7,0},{8,15},{9,14},{10,... | collective-permute-start | bytes 196616 | tf_op jit(solution)/shard_map/ppermute | solution.py:178
  18.7 0.0 collective-permute-done.5.refs_3_
  18.7 0.0 collective-permute-done.7.refs_5_
  18.7 0.0 collective-permute-done.9.refs_7_
  18.7 0.5 %shard_map.57 = f32[12,32,128]{2,1,0:T(8,128)S(1)} custom-call(s32[3,32]{1,0:T(4,128)S(4)} %get-tuple-element.12.refs_0_, bf16[32,128,256]{2,1,0:T(8,128)(2,1)S(1)} %get-tuple-element.14.refs_1_, f32[4,32,128]{2,1,0:T(8,128)S(1)} %pad_maximum_fusion.refs_2_, f32[4,32,128]{2,1,0:T(8,128)S(1)} %collective-permute-done.5.refs_3_, ...), custom_call_target="tpu_custom_call" | custom-call | flops 268435456 | bytes 4194304 | tf_op jit(solution)/shard_map/pallas_call | solution.py:154
  19.2 0.4 %collective-permute-start.12 = (f32[4,32,128]{2,1,0:T(8,128)S(1)}, f32[4,32,128]{2,1,0:T(8,128)S(1)}, u32[]{:S(2)}, u32[]{:S(2)}) collective-permute-start(f32[4,32,128]{2,1,0:T(8,128)S(1)} %get-tuple-element.18), channel_id=1, source_target_pairs={{0,5},{1,4},{2,7},{3,6},{4,1},{5,0},{6,3},{7,2},{8,13},{9,12},{10,... | collective-permute-start | bytes 196616 | tf_op jit(solution)/shard_map/ppermute | solution.py:178
  19.5 0.7 %collective-permute-start.10 = (f32[4,32,128]{2,1,0:T(8,128)S(1)}, f32[4,32,128]{2,1,0:T(8,128)S(1)}, u32[]{:S(2)}, u32[]{:S(2)}) collective-permute-start(f32[4,32,128]{2,1,0:T(8,128)S(1)} %get-tuple-element.19), channel_id=1, source_target_pairs={{0,3},{1,2},{2,1},{3,0},{4,7},{5,6},{6,5},{7,4},{8,11},{9,10},{10,... | collective-permute-start | bytes 196616 | tf_op jit(solution)/shard_map/ppermute | solution.py:178
  20.2 0.7 %collective-permute-start.11 = (f32[4,32,128]{2,1,0:T(8,128)S(1)}, f32[4,32,128]{2,1,0:T(8,128)S(1)}, u32[]{:S(2)}, u32[]{:S(2)}) collective-permute-start(f32[4,32,128]{2,1,0:T(8,128)S(1)} %get-tuple-element.17), channel_id=1, source_target_pairs={{0,1},{1,0},{2,3},{3,2},{4,5},{5,4},{6,7},{7,6},{8,9},{9,8},{10,11... | collective-permute-start | bytes 196616 | tf_op jit(solution)/shard_map/ppermute | solution.py:178
  20.9 0.9 %collective-permute-done.13 = f32[4,32,128]{2,1,0:T(8,128)S(1)} collective-permute-done((f32[4,32,128]{2,1,0:T(8,128)S(1)}, f32[4,32,128]{2,1,0:T(8,128)S(1)}, u32[]{:S(2)}, u32[]{:S(2)}) %collective-permute-start.13) | collective-permute-done | bytes 65568 | tf_op jit(solution)/shard_map/ppermute | solution.py:178
  21.8 1.6 %collective-permute-done.12 = f32[4,32,128]{2,1,0:T(8,128)S(1)} collective-permute-done((f32[4,32,128]{2,1,0:T(8,128)S(1)}, f32[4,32,128]{2,1,0:T(8,128)S(1)}, u32[]{:S(2)}, u32[]{:S(2)}) %collective-permute-start.12) | collective-permute-done | bytes 65568 | tf_op jit(solution)/shard_map/ppermute | solution.py:178
  23.4 0.2 collective-permute-done.10
  23.6 0.0 collective-permute-done.11
  23.7 2.1 %collective-permute-start.17 = (f32[32,128]{1,0:T(8,128)S(1)}, f32[32,128]{1,0:T(8,128)S(1)}, u32[]{:S(2)}, u32[]{:S(2)}) collective-permute-start(f32[32,128]{1,0:T(8,128)S(1)} %get-tuple-element.21), channel_id=1, source_target_pairs={{0,25},{1,24},{2,27},{3,26},{4,29},{5,28},{6,31},{7,30},{8,17},{9,... | collective-permute-start | bytes 49160 | tf_op jit(solution)/shard_map/ppermute | solution.py:178
  25.7 0.0 collective-permute-start.16
  25.7 1.8 %collective-permute-start.14 = (f32[32,128]{1,0:T(8,128)S(1)}, f32[32,128]{1,0:T(8,128)S(1)}, u32[]{:S(2)}, u32[]{:S(2)}) collective-permute-start(f32[32,128]{1,0:T(8,128)S(1)} %get-tuple-element.23), channel_id=1, source_target_pairs={{0,9},{1,8},{2,11},{3,10},{4,13},{5,12},{6,15},{7,14},{8,1},{9,0},... | collective-permute-start | bytes 49160 | tf_op jit(solution)/shard_map/ppermute | solution.py:178
  27.6 0.4 %collective-permute-start.15 = (f32[32,128]{1,0:T(8,128)S(1)}, f32[32,128]{1,0:T(8,128)S(1)}, u32[]{:S(2)}, u32[]{:S(2)}) collective-permute-start(f32[32,128]{1,0:T(8,128)S(1)} %get-tuple-element.20), channel_id=1, source_target_pairs={{0,1},{1,0},{2,3},{3,2},{4,5},{5,4},{6,7},{7,6},{8,9},{9,8},{10,11... | collective-permute-start | bytes 49160 | tf_op jit(solution)/shard_map/ppermute | solution.py:178
  28.0 0.7 %collective-permute-done.17 = f32[32,128]{1,0:T(8,128)S(1)} collective-permute-done((f32[32,128]{1,0:T(8,128)S(1)}, f32[32,128]{1,0:T(8,128)S(1)}, u32[]{:S(2)}, u32[]{:S(2)}) %collective-permute-start.17) | collective-permute-done | bytes 16416 | tf_op jit(solution)/shard_map/ppermute | solution.py:178
  28.7 1.1 %collective-permute-done.16 = f32[32,128]{1,0:T(8,128)S(1)} collective-permute-done((f32[32,128]{1,0:T(8,128)S(1)}, f32[32,128]{1,0:T(8,128)S(1)}, u32[]{:S(2)}, u32[]{:S(2)}) %collective-permute-start.16) | collective-permute-done | bytes 16416 | tf_op jit(solution)/shard_map/ppermute | solution.py:178
  29.8 0.0 collective-permute-done.14
  29.8 0.0 collective-permute-done.15
  29.8 0.6 %add_add_fusion.1 = f32[32,128]{1,0:T(8,128)} fusion(f32[32,128]{1,0:T(8,128)S(1)} %collective-permute-done.17, f32[32,128]{1,0:T(8,128)S(1)} %collective-permute-done.16, f32[32,128]{1,0:T(8,128)S(1)} %collective-permute-done.14, f32[32,128]{1,0:T(8,128)S(1)} %collective-permute-done.15), kind=kLoop, calls=%fused_computation.6 | loop fusion | flops 12288 | bytes 81920 | tf_op jit(solution)/shard_map/add | solution.py:188
  (4 shorter events, 0.0 us)
Async XLA Ops:
  0.0 7.2 %collective-permute-start.2 = (f32[32,128]{1,0:T(8,128)}, f32[32,128]{1,0:T(8,128)S(1)}, u32[]{:S(2)}, u32[]{:S(2)}) collective-permute-start(f32[32,128]{1,0:T(8,128)} %bitcast.27), channel_id=1, source_target_pairs={{0,17},{1,16},{2,19},{3,18},{4,21},{5,20},{6,23},{7,22},{8,25},{9,... | collective-permute-start | bytes 49160 | tf_op jit(solution)/shard_map/ppermute | solution.py:178
  3.5 5.2 %collective-permute-start.1 = (f32[32,128]{1,0:T(8,128)}, f32[32,128]{1,0:T(8,128)S(1)}, u32[]{:S(2)}, u32[]{:S(2)}) collective-permute-start(f32[32,128]{1,0:T(8,128)} %bitcast.28), channel_id=1, source_target_pairs={{0,25},{1,24},{2,27},{3,26},{4,29},{5,28},{6,31},{7,30},{8,17},{9,... | collective-permute-start | bytes 49160 | tf_op jit(solution)/shard_map/ppermute | solution.py:178
  5.1 3.6 %collective-permute-start = (f32[32,128]{1,0:T(8,128)}, f32[32,128]{1,0:T(8,128)S(1)}, u32[]{:S(2)}, u32[]{:S(2)}) collective-permute-start(f32[32,128]{1,0:T(8,128)} %bitcast.29), channel_id=1, source_target_pairs={{0,9},{1,8},{2,11},{3,10},{4,13},{5,12},{6,15},{7,14},{8,1},{9,0},... | collective-permute-start | bytes 49160 | tf_op jit(solution)/shard_map/ppermute | solution.py:178
  8.7 5.3 %collective-permute-start.3 = (f32[4,32,128]{2,1,0:T(8,128)S(1)}, f32[4,32,128]{2,1,0:T(8,128)S(1)}, u32[]{:S(2)}, u32[]{:S(2)}) collective-permute-start(f32[4,32,128]{2,1,0:T(8,128)S(1)} %pad_maximum_fusion.refs_2_), channel_id=1, source_target_pairs={{0,7},{1,6},{2,5},{3,4},{4,3},{5,2},{6,1},{7,0},{8,15},{9,14},{10,... | collective-permute-start | bytes 196616 | tf_op jit(solution)/shard_map/ppermute | solution.py:178
  11.5 4.4 %collective-permute-start.6 = (f32[4,32,128]{2,1,0:T(8,128)S(1)}, f32[4,32,128]{2,1,0:T(8,128)S(1)}, u32[]{:S(2)}, u32[]{:S(2)}) collective-permute-start(f32[4,32,128]{2,1,0:T(8,128)S(1)} %pad_maximum_fusion.refs_2_), channel_id=1, source_target_pairs={{0,3},{1,2},{2,1},{3,0},{4,7},{5,6},{6,5},{7,4},{8,11},{9,10},{10,... | collective-permute-start | bytes 196616 | tf_op jit(solution)/shard_map/ppermute | solution.py:178
  11.5 4.4 %collective-permute-start.8 = (f32[4,32,128]{2,1,0:T(8,128)S(1)}, f32[4,32,128]{2,1,0:T(8,128)S(1)}, u32[]{:S(2)}, u32[]{:S(2)}) collective-permute-start(f32[4,32,128]{2,1,0:T(8,128)S(1)} %pad_maximum_fusion.refs_2_), channel_id=1, source_target_pairs={{0,5},{1,4},{2,7},{3,6},{4,1},{5,0},{6,3},{7,2},{8,13},{9,12},{10,... | collective-permute-start | bytes 196616 | tf_op jit(solution)/shard_map/ppermute | solution.py:178
  14.0 2.4 %collective-permute-start.4 = (f32[4,32,128]{2,1,0:T(8,128)S(1)}, f32[4,32,128]{2,1,0:T(8,128)S(1)}, u32[]{:S(2)}, u32[]{:S(2)}) collective-permute-start(f32[4,32,128]{2,1,0:T(8,128)S(1)} %collective-permute-done.3.refs_2_), channel_id=1, source_target_pairs={{0,1},{1,0},{2,3},{3,2},{4,5},{5,4},{6,7},{7,6},{8,9},{9,8},{10,11... | collective-permute-start | bytes 196616 | tf_op jit(solution)/shard_map/ppermute | solution.py:178
  14.1 4.6 %collective-permute-start.5 = (f32[4,32,128]{2,1,0:T(8,128)S(1)}, f32[4,32,128]{2,1,0:T(8,128)S(1)}, u32[]{:S(2)}, u32[]{:S(2)}) collective-permute-start(f32[4,32,128]{2,1,0:T(8,128)S(1)} %pad_maximum_fusion.refs_2_), channel_id=1, source_target_pairs={{0,1},{1,0},{2,3},{3,2},{4,5},{5,4},{6,7},{7,6},{8,9},{9,8},{10,11... | collective-permute-start | bytes 196616 | tf_op jit(solution)/shard_map/ppermute | solution.py:178
  15.9 2.8 %collective-permute-start.7 = (f32[4,32,128]{2,1,0:T(8,128)S(1)}, f32[4,32,128]{2,1,0:T(8,128)S(1)}, u32[]{:S(2)}, u32[]{:S(2)}) collective-permute-start(f32[4,32,128]{2,1,0:T(8,128)S(1)} %collective-permute-done.6.refs_4_), channel_id=1, source_target_pairs={{0,1},{1,0},{2,3},{3,2},{4,5},{5,4},{6,7},{7,6},{8,9},{9,8},{10,11... | collective-permute-start | bytes 196616 | tf_op jit(solution)/shard_map/ppermute | solution.py:178
  16.0 2.7 %collective-permute-start.9 = (f32[4,32,128]{2,1,0:T(8,128)S(1)}, f32[4,32,128]{2,1,0:T(8,128)S(1)}, u32[]{:S(2)}, u32[]{:S(2)}) collective-permute-start(f32[4,32,128]{2,1,0:T(8,128)S(1)} %collective-permute-done.8.refs_6_), channel_id=1, source_target_pairs={{0,1},{1,0},{2,3},{3,2},{4,5},{5,4},{6,7},{7,6},{8,9},{9,8},{10,11... | collective-permute-start | bytes 196616 | tf_op jit(solution)/shard_map/ppermute | solution.py:178
  16.7 5.1 %collective-permute-start.13 = (f32[4,32,128]{2,1,0:T(8,128)S(1)}, f32[4,32,128]{2,1,0:T(8,128)S(1)}, u32[]{:S(2)}, u32[]{:S(2)}) collective-permute-start(f32[4,32,128]{2,1,0:T(8,128)S(1)} %shard_map.56), channel_id=1, source_target_pairs={{0,7},{1,6},{2,5},{3,4},{4,3},{5,2},{6,1},{7,0},{8,15},{9,14},{10,... | collective-permute-start | bytes 196616 | tf_op jit(solution)/shard_map/ppermute | solution.py:178
  19.2 4.3 %collective-permute-start.12 = (f32[4,32,128]{2,1,0:T(8,128)S(1)}, f32[4,32,128]{2,1,0:T(8,128)S(1)}, u32[]{:S(2)}, u32[]{:S(2)}) collective-permute-start(f32[4,32,128]{2,1,0:T(8,128)S(1)} %get-tuple-element.18), channel_id=1, source_target_pairs={{0,5},{1,4},{2,7},{3,6},{4,1},{5,0},{6,3},{7,2},{8,13},{9,12},{10,... | collective-permute-start | bytes 196616 | tf_op jit(solution)/shard_map/ppermute | solution.py:178
  19.5 4.1 %collective-permute-start.10 = (f32[4,32,128]{2,1,0:T(8,128)S(1)}, f32[4,32,128]{2,1,0:T(8,128)S(1)}, u32[]{:S(2)}, u32[]{:S(2)}) collective-permute-start(f32[4,32,128]{2,1,0:T(8,128)S(1)} %get-tuple-element.19), channel_id=1, source_target_pairs={{0,3},{1,2},{2,1},{3,0},{4,7},{5,6},{6,5},{7,4},{8,11},{9,10},{10,... | collective-permute-start | bytes 196616 | tf_op jit(solution)/shard_map/ppermute | solution.py:178
  20.2 3.4 %collective-permute-start.11 = (f32[4,32,128]{2,1,0:T(8,128)S(1)}, f32[4,32,128]{2,1,0:T(8,128)S(1)}, u32[]{:S(2)}, u32[]{:S(2)}) collective-permute-start(f32[4,32,128]{2,1,0:T(8,128)S(1)} %get-tuple-element.17), channel_id=1, source_target_pairs={{0,1},{1,0},{2,3},{3,2},{4,5},{5,4},{6,7},{7,6},{8,9},{9,8},{10,11... | collective-permute-start | bytes 196616 | tf_op jit(solution)/shard_map/ppermute | solution.py:178
  23.7 5.0 %collective-permute-start.17 = (f32[32,128]{1,0:T(8,128)S(1)}, f32[32,128]{1,0:T(8,128)S(1)}, u32[]{:S(2)}, u32[]{:S(2)}) collective-permute-start(f32[32,128]{1,0:T(8,128)S(1)} %get-tuple-element.21), channel_id=1, source_target_pairs={{0,25},{1,24},{2,27},{3,26},{4,29},{5,28},{6,31},{7,30},{8,17},{9,... | collective-permute-start | bytes 49160 | tf_op jit(solution)/shard_map/ppermute | solution.py:178
  25.7 4.1 %collective-permute-start.16 = (f32[32,128]{1,0:T(8,128)S(1)}, f32[32,128]{1,0:T(8,128)S(1)}, u32[]{:S(2)}, u32[]{:S(2)}) collective-permute-start(f32[32,128]{1,0:T(8,128)S(1)} %get-tuple-element.22), channel_id=1, source_target_pairs={{0,17},{1,16},{2,19},{3,18},{4,21},{5,20},{6,23},{7,22},{8,25},{9,... | collective-permute-start | bytes 49160 | tf_op jit(solution)/shard_map/ppermute | solution.py:178
  25.7 4.1 %collective-permute-start.14 = (f32[32,128]{1,0:T(8,128)S(1)}, f32[32,128]{1,0:T(8,128)S(1)}, u32[]{:S(2)}, u32[]{:S(2)}) collective-permute-start(f32[32,128]{1,0:T(8,128)S(1)} %get-tuple-element.23), channel_id=1, source_target_pairs={{0,9},{1,8},{2,11},{3,10},{4,13},{5,12},{6,15},{7,14},{8,1},{9,0},... | collective-permute-start | bytes 49160 | tf_op jit(solution)/shard_map/ppermute | solution.py:178
  27.6 2.2 %collective-permute-start.15 = (f32[32,128]{1,0:T(8,128)S(1)}, f32[32,128]{1,0:T(8,128)S(1)}, u32[]{:S(2)}, u32[]{:S(2)}) collective-permute-start(f32[32,128]{1,0:T(8,128)S(1)} %get-tuple-element.20), channel_id=1, source_target_pairs={{0,1},{1,0},{2,3},{3,2},{4,5},{5,4},{6,7},{7,6},{8,9},{9,8},{10,11... | collective-permute-start | bytes 49160 | tf_op jit(solution)/shard_map/ppermute | solution.py:178

commit v14 on v12

--- a/solution.py
+++ b/solution.py
@@ -131,8 +131,10 @@
             place = codes[1, slot]
             totals[place] = totals[place] + product
 
-    pl.when(codes[2, 0] <= GROUP)(lambda: add_slots(GROUP))
-    pl.when(codes[2, 0] > GROUP)(lambda: add_slots(halves.shape[0]))
+    count = codes[2, 0]
+    pl.when(count <= GROUP // 2)(lambda: add_slots(GROUP // 2))
+    pl.when((count > GROUP // 2) & (count <= GROUP))(lambda: add_slots(GROUP))
+    pl.when(count > GROUP)(lambda: add_slots(halves.shape[0]))
     for chunk in range(0, chunk_count, 2):
         part = slice(chunk * rows, (chunk + 2) * rows)
         for tile in range(0, out_tiles, 2):

time: 30.5 us -> 30.4 us (level)
  transfers between devices with their start and end apart: 18 -> 18, of which waited for: 8 -> 8; matrix products, arithmetic and copies ran while one was open for 0% -> 0% of each run, Pallas kernels for 7% -> 6%
where the time goes in v14:
time: 30.4 us; the launch traced here: 30.2 us
  starting transfers between devices  18.1 us (60%)
  waiting for transfers between devices  8.87 us (29%)
  Pallas kernels  1.8 us (6%)
  between operations  0.73 us (2%)
  other arithmetic  0.64 us (2%)
    ppermute x18, starting transfers between devices, swap(): return lax.ppermute(value, ('pair', 'virt'), routes)  18.1 us
    ppermute x18, waiting for transfers between devices, swap(): return lax.ppermute(value, ('pair', 'virt'), routes)  8.87 us
    pallas_call x1, Pallas kernels, prepare(): pl.pallas_call(kernel, out_shape=(jax.ShapeDtypeStruct((slots, W, 2 * W),...  1.21 us
    add x2, other arithmetic, swap_sum(): return sum(received[1:], received[0])  0.64 us
  transfers between devices with their start and end apart: 18, of which 8 were waited for; matrix products, arithmetic and copies ran while one was open for 0% of the time, Pallas kernels for 6%

profile of v14, /device:TPU:0, one launch (start us, length us, event | category | flops | bytes accessed | tf_op | source)
XLA Modules:
  0.0 30.2 jit_solution(2893227642573734124)
XLA Ops:
  0.0 3.5 %collective-permute-start.2 = (f32[32,128]{1,0:T(8,128)}, f32[32,128]{1,0:T(8,128)S(1)}, u32[]{:S(2)}, u32[]{:S(2)}) collective-permute-start(f32[32,128]{1,0:T(8,128)} %bitcast.27), channel_id=1, source_target_pairs={{0,17},{1,16},{2,19},{3,18},{4,21},{5,20},{6,23},{7,22},{8,25},{9,... | collective-permute-start | bytes 49160 | tf_op jit(solution)/shard_map/ppermute | solution.py:180
  3.5 1.6 %collective-permute-start.1 = (f32[32,128]{1,0:T(8,128)}, f32[32,128]{1,0:T(8,128)S(1)}, u32[]{:S(2)}, u32[]{:S(2)}) collective-permute-start(f32[32,128]{1,0:T(8,128)} %bitcast.28), channel_id=1, source_target_pairs={{0,25},{1,24},{2,27},{3,26},{4,29},{5,28},{6,31},{7,30},{8,17},{9,... | collective-permute-start | bytes 49160 | tf_op jit(solution)/shard_map/ppermute | solution.py:180
  5.1 0.2 collective-permute-start
  6.0 1.2 %shard_map.55 = (bf16[32,128,256]{2,1,0:T(8,128)(2,1)S(1)}, s32[3,32]{1,0:T(4,128)S(4)}, f32[32,128]{1,0:T(8,128)S(1)}) custom-call(s32[1,1]{1,0:T(1,128)S(6)} %copy.8.refs_0_, s32[1,32]{1,0:T(1,128)} %bitcast.34, s32[1,32]{1,0:T(1,128)} %bitcast.35, f32[32,128,128]{2,1,0:T(8,128)} %bitcast.26, f32[32,128]{1,0:T(8,128)} %bitcast.30), custom_call_target="tpu_custom_call" | custom-call | flops 2097152 | bytes 4194304 | tf_op jit(solution)/shard_map/pallas_call | solution.py:69
  7.2 0.0 collective-permute-done.2
  7.2 1.4 %collective-permute-done.1 = f32[32,128]{1,0:T(8,128)S(1)} collective-permute-done((f32[32,128]{1,0:T(8,128)}, f32[32,128]{1,0:T(8,128)S(1)}, u32[]{:S(2)}, u32[]{:S(2)}) %collective-permute-start.1) | collective-permute-done | bytes 16416 | tf_op jit(solution)/shard_map/ppermute | solution.py:180
  8.7 0.0 collective-permute-done
  8.7 2.8 %collective-permute-start.3 = (f32[4,32,128]{2,1,0:T(8,128)S(1)}, f32[4,32,128]{2,1,0:T(8,128)S(1)}, u32[]{:S(2)}, u32[]{:S(2)}) collective-permute-start(f32[4,32,128]{2,1,0:T(8,128)S(1)} %pad_maximum_fusion.refs_2_), channel_id=1, source_target_pairs={{0,7},{1,6},{2,5},{3,4},{4,3},{5,2},{6,1},{7,0},{8,15},{9,14},{10,... | collective-permute-start | bytes 196616 | tf_op jit(solution)/shard_map/ppermute | solution.py:180
  11.5 0.0 collective-permute-start.7
  11.5 0.8 %collective-permute-start.6 = (f32[4,32,128]{2,1,0:T(8,128)S(1)}, f32[4,32,128]{2,1,0:T(8,128)S(1)}, u32[]{:S(2)}, u32[]{:S(2)}) collective-permute-start(f32[4,32,128]{2,1,0:T(8,128)S(1)} %pad_maximum_fusion.refs_2_), channel_id=1, source_target_pairs={{0,3},{1,4},{2,7},{3,0},{4,1},{5,6},{6,5},{7,2},{8,11},{9,12},{10,... | collective-permute-start | bytes 196616 | tf_op jit(solution)/shard_map/ppermute | solution.py:180
  12.3 1.7 %collective-permute-done.3.refs_2_ = f32[4,32,128]{2,1,0:T(8,128)S(1)} collective-permute-done((f32[4,32,128]{2,1,0:T(8,128)S(1)}, f32[4,32,128]{2,1,0:T(8,128)S(1)}, u32[]{:S(2)}, u32[]{:S(2)}) %collective-permute-start.3) | collective-permute-done | bytes 65568 | tf_op jit(solution)/shard_map/ppermute | solution.py:180
  14.0 0.1 collective-permute-start.4
  14.1 0.4 %collective-permute-start.5 = (f32[4,32,128]{2,1,0:T(8,128)S(1)}, f32[4,32,128]{2,1,0:T(8,128)S(1)}, u32[]{:S(2)}, u32[]{:S(2)}) collective-permute-start(f32[4,32,128]{2,1,0:T(8,128)S(1)} %pad_maximum_fusion.refs_2_), channel_id=1, source_target_pairs={{0,1},{1,0},{2,3},{3,2},{4,5},{5,4},{6,7},{7,6},{8,9},{9,8},{10,11... | collective-permute-start | bytes 196616 | tf_op jit(solution)/shard_map/ppermute | solution.py:180
  14.5 0.7 %collective-permute-done.7.refs_6_ = f32[4,32,128]{2,1,0:T(8,128)S(1)} collective-permute-done((f32[4,32,128]{2,1,0:T(8,128)S(1)}, f32[4,32,128]{2,1,0:T(8,128)S(1)}, u32[]{:S(2)}, u32[]{:S(2)}) %collective-permute-start.7) | collective-permute-done | bytes 65568 | tf_op jit(solution)/shard_map/ppermute | solution.py:180
  15.2 0.7 %collective-permute-start.8 = (f32[4,32,128]{2,1,0:T(8,128)S(1)}, f32[4,32,128]{2,1,0:T(8,128)S(1)}, u32[]{:S(2)}, u32[]{:S(2)}) collective-permute-start(f32[4,32,128]{2,1,0:T(8,128)S(1)} %collective-permute-done.7.refs_6_), channel_id=1, source_target_pairs={{0,1},{1,0},{2,3},{3,2},{4,5},{5,4},{6,7},{7,6},{8,9},{9,8},{10,11... | collective-permute-start | bytes 196616 | tf_op jit(solution)/shard_map/ppermute | solution.py:180
  16.0 0.0 collective-permute-done.6.refs_4_
  16.0 0.0 collective-permute-start.9
  16.0 0.0 collective-permute-done.4.refs_3_
  16.0 0.2 shard_map.56
  16.2 2.2 %collective-permute-start.13 = (f32[4,32,128]{2,1,0:T(8,128)S(1)}, f32[4,32,128]{2,1,0:T(8,128)S(1)}, u32[]{:S(2)}, u32[]{:S(2)}) collective-permute-start(f32[4,32,128]{2,1,0:T(8,128)S(1)} %shard_map.56), channel_id=1, source_target_pairs={{0,7},{1,6},{2,5},{3,4},{4,3},{5,2},{6,1},{7,0},{8,15},{9,14},{10,... | collective-permute-start | bytes 196616 | tf_op jit(solution)/shard_map/ppermute | solution.py:180
  18.4 0.0 collective-permute-done.5.refs_3_
  18.4 0.0 collective-permute-done.8.refs_5_
  18.4 0.0 collective-permute-done.9.refs_7_
  18.5 0.4 %shard_map.57 = f32[12,32,128]{2,1,0:T(8,128)S(1)} custom-call(s32[3,32]{1,0:T(4,128)S(4)} %get-tuple-element.12.refs_0_, bf16[32,128,256]{2,1,0:T(8,128)(2,1)S(1)} %get-tuple-element.14.refs_1_, f32[4,32,128]{2,1,0:T(8,128)S(1)} %pad_maximum_fusion.refs_2_, f32[4,32,128]{2,1,0:T(8,128)S(1)} %collective-permute-done.5.refs_3_, ...), custom_call_target="tpu_custom_call" | custom-call | flops 268435456 | bytes 4194304 | tf_op jit(solution)/shard_map/pallas_call | solution.py:156
  18.8 0.5 %collective-permute-start.12 = (f32[4,32,128]{2,1,0:T(8,128)S(1)}, f32[4,32,128]{2,1,0:T(8,128)S(1)}, u32[]{:S(2)}, u32[]{:S(2)}) collective-permute-start(f32[4,32,128]{2,1,0:T(8,128)S(1)} %get-tuple-element.18), channel_id=1, source_target_pairs={{0,5},{1,2},{2,1},{3,6},{4,7},{5,0},{6,3},{7,4},{8,13},{9,10},{10,... | collective-permute-start | bytes 196616 | tf_op jit(solution)/shard_map/ppermute | solution.py:180
  19.3 0.8 %collective-permute-start.10 = (f32[4,32,128]{2,1,0:T(8,128)S(1)}, f32[4,32,128]{2,1,0:T(8,128)S(1)}, u32[]{:S(2)}, u32[]{:S(2)}) collective-permute-start(f32[4,32,128]{2,1,0:T(8,128)S(1)} %get-tuple-element.19), channel_id=1, source_target_pairs={{0,3},{1,4},{2,7},{3,0},{4,1},{5,6},{6,5},{7,2},{8,11},{9,12},{10,... | collective-permute-start | bytes 196616 | tf_op jit(solution)/shard_map/ppermute | solution.py:180
  20.1 0.1 collective-permute-start.11
  20.2 0.7 %collective-permute-done.13 = f32[4,32,128]{2,1,0:T(8,128)S(1)} collective-permute-done((f32[4,32,128]{2,1,0:T(8,128)S(1)}, f32[4,32,128]{2,1,0:T(8,128)S(1)}, u32[]{:S(2)}, u32[]{:S(2)}) %collective-permute-start.13) | collective-permute-done | bytes 65568 | tf_op jit(solution)/shard_map/ppermute | solution.py:180
  20.9 1.7 %collective-permute-done.12 = f32[4,32,128]{2,1,0:T(8,128)S(1)} collective-permute-done((f32[4,32,128]{2,1,0:T(8,128)S(1)}, f32[4,32,128]{2,1,0:T(8,128)S(1)}, u32[]{:S(2)}, u32[]{:S(2)}) %collective-permute-start.12) | collective-permute-done | bytes 65568 | tf_op jit(solution)/shard_map/ppermute | solution.py:180
  22.6 1.1 %collective-permute-done.10 = f32[4,32,128]{2,1,0:T(8,128)S(1)} collective-permute-done((f32[4,32,128]{2,1,0:T(8,128)S(1)}, f32[4,32,128]{2,1,0:T(8,128)S(1)}, u32[]{:S(2)}, u32[]{:S(2)}) %collective-permute-start.10) | collective-permute-done | bytes 65568 | tf_op jit(solution)/shard_map/ppermute | solution.py:180
  23.6 0.0 collective-permute-done.11
  23.7 1.8 %collective-permute-start.17 = (f32[32,128]{1,0:T(8,128)S(1)}, f32[32,128]{1,0:T(8,128)S(1)}, u32[]{:S(2)}, u32[]{:S(2)}) collective-permute-start(f32[32,128]{1,0:T(8,128)S(1)} %get-tuple-element.21), channel_id=1, source_target_pairs={{0,25},{1,24},{2,27},{3,26},{4,29},{5,28},{6,31},{7,30},{8,17},{9,... | collective-permute-start | bytes 49160 | tf_op jit(solution)/shard_map/ppermute | solution.py:180
  25.5 0.0 collective-permute-start.16
  25.5 2.1 %collective-permute-start.14 = (f32[32,128]{1,0:T(8,128)S(1)}, f32[32,128]{1,0:T(8,128)S(1)}, u32[]{:S(2)}, u32[]{:S(2)}) collective-permute-start(f32[32,128]{1,0:T(8,128)S(1)} %get-tuple-element.23), channel_id=1, source_target_pairs={{0,9},{1,8},{2,11},{3,10},{4,13},{5,12},{6,15},{7,14},{8,1},{9,0},... | collective-permute-start | bytes 49160 | tf_op jit(solution)/shard_map/ppermute | solution.py:180
  27.6 0.4 %collective-permute-start.15 = (f32[32,128]{1,0:T(8,128)S(1)}, f32[32,128]{1,0:T(8,128)S(1)}, u32[]{:S(2)}, u32[]{:S(2)}) collective-permute-start(f32[32,128]{1,0:T(8,128)S(1)} %get-tuple-element.20), channel_id=1, source_target_pairs={{0,1},{1,0},{2,3},{3,2},{4,5},{5,4},{6,7},{7,6},{8,9},{9,8},{10,11... | collective-permute-start | bytes 49160 | tf_op jit(solution)/shard_map/ppermute | solution.py:180
  28.0 0.7 %collective-permute-done.17 = f32[32,128]{1,0:T(8,128)S(1)} collective-permute-done((f32[32,128]{1,0:T(8,128)S(1)}, f32[32,128]{1,0:T(8,128)S(1)}, u32[]{:S(2)}, u32[]{:S(2)}) %collective-permute-start.17) | collective-permute-done | bytes 16416 | tf_op jit(solution)/shard_map/ppermute | solution.py:180
  28.7 0.8 %collective-permute-done.16 = f32[32,128]{1,0:T(8,128)S(1)} collective-permute-done((f32[32,128]{1,0:T(8,128)S(1)}, f32[32,128]{1,0:T(8,128)S(1)}, u32[]{:S(2)}, u32[]{:S(2)}) %collective-permute-start.16) | collective-permute-done | bytes 16416 | tf_op jit(solution)/shard_map/ppermute | solution.py:180
  29.6 0.0 collective-permute-done.14
  29.6 0.0 collective-permute-done.15
  29.6 0.6 %add_add_fusion.1 = f32[32,128]{1,0:T(8,128)} fusion(f32[32,128]{1,0:T(8,128)S(1)} %collective-permute-done.17, f32[32,128]{1,0:T(8,128)S(1)} %collective-permute-done.16, f32[32,128]{1,0:T(8,128)S(1)} %collective-permute-done.14, f32[32,128]{1,0:T(8,128)S(1)} %collective-permute-done.15), kind=kLoop, calls=%fused_computation.6 | loop fusion | flops 12288 | bytes 81920 | tf_op jit(solution)/shard_map/add | solution.py:190
  (4 shorter events, 0.0 us)
Async XLA Ops:
  0.0 7.2 %collective-permute-start.2 = (f32[32,128]{1,0:T(8,128)}, f32[32,128]{1,0:T(8,128)S(1)}, u32[]{:S(2)}, u32[]{:S(2)}) collective-permute-start(f32[32,128]{1,0:T(8,128)} %bitcast.27), channel_id=1, source_target_pairs={{0,17},{1,16},{2,19},{3,18},{4,21},{5,20},{6,23},{7,22},{8,25},{9,... | collective-permute-start | bytes 49160 | tf_op jit(solution)/shard_map/ppermute | solution.py:180
  3.5 5.2 %collective-permute-start.1 = (f32[32,128]{1,0:T(8,128)}, f32[32,128]{1,0:T(8,128)S(1)}, u32[]{:S(2)}, u32[]{:S(2)}) collective-permute-start(f32[32,128]{1,0:T(8,128)} %bitcast.28), channel_id=1, source_target_pairs={{0,25},{1,24},{2,27},{3,26},{4,29},{5,28},{6,31},{7,30},{8,17},{9,... | collective-permute-start | bytes 49160 | tf_op jit(solution)/shard_map/ppermute | solution.py:180
  5.1 3.6 %collective-permute-start = (f32[32,128]{1,0:T(8,128)}, f32[32,128]{1,0:T(8,128)S(1)}, u32[]{:S(2)}, u32[]{:S(2)}) collective-permute-start(f32[32,128]{1,0:T(8,128)} %bitcast.29), channel_id=1, source_target_pairs={{0,9},{1,8},{2,11},{3,10},{4,13},{5,12},{6,15},{7,14},{8,1},{9,0},... | collective-permute-start | bytes 49160 | tf_op jit(solution)/shard_map/ppermute | solution.py:180
  8.7 5.3 %collective-permute-start.3 = (f32[4,32,128]{2,1,0:T(8,128)S(1)}, f32[4,32,128]{2,1,0:T(8,128)S(1)}, u32[]{:S(2)}, u32[]{:S(2)}) collective-permute-start(f32[4,32,128]{2,1,0:T(8,128)S(1)} %pad_maximum_fusion.refs_2_), channel_id=1, source_target_pairs={{0,7},{1,6},{2,5},{3,4},{4,3},{5,2},{6,1},{7,0},{8,15},{9,14},{10,... | collective-permute-start | bytes 196616 | tf_op jit(solution)/shard_map/ppermute | solution.py:180
  11.5 3.7 %collective-permute-start.7 = (f32[4,32,128]{2,1,0:T(8,128)S(1)}, f32[4,32,128]{2,1,0:T(8,128)S(1)}, u32[]{:S(2)}, u32[]{:S(2)}) collective-permute-start(f32[4,32,128]{2,1,0:T(8,128)S(1)} %pad_maximum_fusion.refs_2_), channel_id=1, source_target_pairs={{0,5},{1,2},{2,1},{3,6},{4,7},{5,0},{6,3},{7,4},{8,13},{9,10},{10,... | collective-permute-start | bytes 196616 | tf_op jit(solution)/shard_map/ppermute | solution.py:180
  11.5 4.4 %collective-permute-start.6 = (f32[4,32,128]{2,1,0:T(8,128)S(1)}, f32[4,32,128]{2,1,0:T(8,128)S(1)}, u32[]{:S(2)}, u32[]{:S(2)}) collective-permute-start(f32[4,32,128]{2,1,0:T(8,128)S(1)} %pad_maximum_fusion.refs_2_), channel_id=1, source_target_pairs={{0,3},{1,4},{2,7},{3,0},{4,1},{5,6},{6,5},{7,2},{8,11},{9,12},{10,... | collective-permute-start | bytes 196616 | tf_op jit(solution)/shard_map/ppermute | solution.py:180
  14.0 2.0 %collective-permute-start.4 = (f32[4,32,128]{2,1,0:T(8,128)S(1)}, f32[4,32,128]{2,1,0:T(8,128)S(1)}, u32[]{:S(2)}, u32[]{:S(2)}) collective-permute-start(f32[4,32,128]{2,1,0:T(8,128)S(1)} %collective-permute-done.3.refs_2_), channel_id=1, source_target_pairs={{0,1},{1,0},{2,3},{3,2},{4,5},{5,4},{6,7},{7,6},{8,9},{9,8},{10,11... | collective-permute-start | bytes 196616 | tf_op jit(solution)/shard_map/ppermute | solution.py:180
  14.1 4.4 %collective-permute-start.5 = (f32[4,32,128]{2,1,0:T(8,128)S(1)}, f32[4,32,128]{2,1,0:T(8,128)S(1)}, u32[]{:S(2)}, u32[]{:S(2)}) collective-permute-start(f32[4,32,128]{2,1,0:T(8,128)S(1)} %pad_maximum_fusion.refs_2_), channel_id=1, source_target_pairs={{0,1},{1,0},{2,3},{3,2},{4,5},{5,4},{6,7},{7,6},{8,9},{9,8},{10,11... | collective-permute-start | bytes 196616 | tf_op jit(solution)/shard_map/ppermute | solution.py:180
  15.2 3.2 %collective-permute-start.8 = (f32[4,32,128]{2,1,0:T(8,128)S(1)}, f32[4,32,128]{2,1,0:T(8,128)S(1)}, u32[]{:S(2)}, u32[]{:S(2)}) collective-permute-start(f32[4,32,128]{2,1,0:T(8,128)S(1)} %collective-permute-done.7.refs_6_), channel_id=1, source_target_pairs={{0,1},{1,0},{2,3},{3,2},{4,5},{5,4},{6,7},{7,6},{8,9},{9,8},{10,11... | collective-permute-start | bytes 196616 | tf_op jit(solution)/shard_map/ppermute | solution.py:180
  16.0 2.5 %collective-permute-start.9 = (f32[4,32,128]{2,1,0:T(8,128)S(1)}, f32[4,32,128]{2,1,0:T(8,128)S(1)}, u32[]{:S(2)}, u32[]{:S(2)}) collective-permute-start(f32[4,32,128]{2,1,0:T(8,128)S(1)} %collective-permute-done.6.refs_4_), channel_id=1, source_target_pairs={{0,1},{1,0},{2,3},{3,2},{4,5},{5,4},{6,7},{7,6},{8,9},{9,8},{10,11... | collective-permute-start | bytes 196616 | tf_op jit(solution)/shard_map/ppermute | solution.py:180
  16.2 4.7 %collective-permute-start.13 = (f32[4,32,128]{2,1,0:T(8,128)S(1)}, f32[4,32,128]{2,1,0:T(8,128)S(1)}, u32[]{:S(2)}, u32[]{:S(2)}) collective-permute-start(f32[4,32,128]{2,1,0:T(8,128)S(1)} %shard_map.56), channel_id=1, source_target_pairs={{0,7},{1,6},{2,5},{3,4},{4,3},{5,2},{6,1},{7,0},{8,15},{9,14},{10,... | collective-permute-start | bytes 196616 | tf_op jit(solution)/shard_map/ppermute | solution.py:180
  18.8 3.8 %collective-permute-start.12 = (f32[4,32,128]{2,1,0:T(8,128)S(1)}, f32[4,32,128]{2,1,0:T(8,128)S(1)}, u32[]{:S(2)}, u32[]{:S(2)}) collective-permute-start(f32[4,32,128]{2,1,0:T(8,128)S(1)} %get-tuple-element.18), channel_id=1, source_target_pairs={{0,5},{1,2},{2,1},{3,6},{4,7},{5,0},{6,3},{7,4},{8,13},{9,10},{10,... | collective-permute-start | bytes 196616 | tf_op jit(solution)/shard_map/ppermute | solution.py:180
  19.3 4.3 %collective-permute-start.10 = (f32[4,32,128]{2,1,0:T(8,128)S(1)}, f32[4,32,128]{2,1,0:T(8,128)S(1)}, u32[]{:S(2)}, u32[]{:S(2)}) collective-permute-start(f32[4,32,128]{2,1,0:T(8,128)S(1)} %get-tuple-element.19), channel_id=1, source_target_pairs={{0,3},{1,4},{2,7},{3,0},{4,1},{5,6},{6,5},{7,2},{8,11},{9,12},{10,... | collective-permute-start | bytes 196616 | tf_op jit(solution)/shard_map/ppermute | solution.py:180
  20.1 3.5 %collective-permute-start.11 = (f32[4,32,128]{2,1,0:T(8,128)S(1)}, f32[4,32,128]{2,1,0:T(8,128)S(1)}, u32[]{:S(2)}, u32[]{:S(2)}) collective-permute-start(f32[4,32,128]{2,1,0:T(8,128)S(1)} %get-tuple-element.17), channel_id=1, source_target_pairs={{0,1},{1,0},{2,3},{3,2},{4,5},{5,4},{6,7},{7,6},{8,9},{9,8},{10,11... | collective-permute-start | bytes 196616 | tf_op jit(solution)/shard_map/ppermute | solution.py:180
  23.7 5.0 %collective-permute-start.17 = (f32[32,128]{1,0:T(8,128)S(1)}, f32[32,128]{1,0:T(8,128)S(1)}, u32[]{:S(2)}, u32[]{:S(2)}) collective-permute-start(f32[32,128]{1,0:T(8,128)S(1)} %get-tuple-element.21), channel_id=1, source_target_pairs={{0,25},{1,24},{2,27},{3,26},{4,29},{5,28},{6,31},{7,30},{8,17},{9,... | collective-permute-start | bytes 49160 | tf_op jit(solution)/shard_map/ppermute | solution.py:180
  25.5 4.1 %collective-permute-start.16 = (f32[32,128]{1,0:T(8,128)S(1)}, f32[32,128]{1,0:T(8,128)S(1)}, u32[]{:S(2)}, u32[]{:S(2)}) collective-permute-start(f32[32,128]{1,0:T(8,128)S(1)} %get-tuple-element.22), channel_id=1, source_target_pairs={{0,17},{1,16},{2,19},{3,18},{4,21},{5,20},{6,23},{7,22},{8,25},{9,... | collective-permute-start | bytes 49160 | tf_op jit(solution)/shard_map/ppermute | solution.py:180
  25.5 4.1 %collective-permute-start.14 = (f32[32,128]{1,0:T(8,128)S(1)}, f32[32,128]{1,0:T(8,128)S(1)}, u32[]{:S(2)}, u32[]{:S(2)}) collective-permute-start(f32[32,128]{1,0:T(8,128)S(1)} %get-tuple-element.23), channel_id=1, source_target_pairs={{0,9},{1,8},{2,11},{3,10},{4,13},{5,12},{6,15},{7,14},{8,1},{9,0},... | collective-permute-start | bytes 49160 | tf_op jit(solution)/shard_map/ppermute | solution.py:180
  27.6 2.0 %collective-permute-start.15 = (f32[32,128]{1,0:T(8,128)S(1)}, f32[32,128]{1,0:T(8,128)S(1)}, u32[]{:S(2)}, u32[]{:S(2)}) collective-permute-start(f32[32,128]{1,0:T(8,128)S(1)} %get-tuple-element.20), channel_id=1, source_target_pairs={{0,1},{1,0},{2,3},{3,2},{4,5},{5,4},{6,7},{7,6},{8,9},{9,8},{10,11... | collective-permute-start | bytes 49160 | tf_op jit(solution)/shard_map/ppermute | solution.py:180

commit v15 on v12

--- a/solution.py
+++ b/solution.py
@@ -183,7 +183,7 @@
 
 
 def swap_sum(parts, pairs, virts, which, marks):
-    order = (1, 0, 2, 3) if which == "step" else (1, 0, *range(2, len(marks)))
+    order = (2, 0, 1, 3) if which == "step" else (1, 0, *range(2, len(marks)))
     received = [swap(parts[marks.index(mark)], pairs, virts, 1, **{which: mark}) for mark in order]
     return sum(received[1:], received[0])
 

time: 30.5 us -> 30.3 us (level)
  Pallas kernels: 1.99 us -> 2.83 us
  waiting for transfers between devices: 8.93 us -> 8.19 us
    ppermute x18, waiting for transfers between devices: 8.93 us -> 8.19 us  [swap(): return lax.ppermute(value, ('pair', 'virt'), routes)]
    pallas_call x1, Pallas kernels: 1.21 us -> 1.69 us  [prepare(): pl.pallas_call(kernel, out_shape=(jax.ShapeDtypeStruct((slots, W, 2 * W),...]
    pallas_call x2, Pallas kernels: 0.78 us -> 1.14 us  [quarter_terms(): pl.pallas_call(kernel, out_shape=jax.ShapeDtypeStruct((len(quarters) * fa...]
  transfers between devices with their start and end apart: 18 -> 18, of which waited for: 8 -> 8; matrix products, arithmetic and copies ran while one was open for 0% -> 0% of each run, Pallas kernels for 7% -> 9%
where the time goes in v15:
time: 30.3 us; the launch traced here: 30.2 us
  starting transfers between devices  17.8 us (59%)
  waiting for transfers between devices  8.19 us (27%)
  Pallas kernels  2.83 us (9%)
  between operations  0.73 us (2%)
  other arithmetic  0.64 us (2%)
    ppermute x18, starting transfers between devices, swap(): return lax.ppermute(value, ('pair', 'virt'), routes)  17.8 us
    ppermute x18, waiting for transfers between devices, swap(): return lax.ppermute(value, ('pair', 'virt'), routes)  8.19 us
    pallas_call x1, Pallas kernels, prepare(): pl.pallas_call(kernel, out_shape=(jax.ShapeDtypeStruct((slots, W, 2 * W),...  1.69 us
    pallas_call x2, Pallas kernels, quarter_terms(): pl.pallas_call(kernel, out_shape=jax.ShapeDtypeStruct((len(quarters) * fa...  1.14 us
    add x2, other arithmetic, swap_sum(): return sum(received[1:], received[0])  0.64 us
  transfers between devices with their start and end apart: 18, of which 8 were waited for; matrix products, arithmetic and copies ran while one was open for 0% of the time, Pallas kernels for 9%

profile of v15, /device:TPU:0, one launch (start us, length us, event | category | flops | bytes accessed | tf_op | source)
XLA Modules:
  0.0 30.2 jit_solution(8379374416718910860)
XLA Ops:
  0.0 3.5 %collective-permute-start.2 = (f32[32,128]{1,0:T(8,128)}, f32[32,128]{1,0:T(8,128)S(1)}, u32[]{:S(2)}, u32[]{:S(2)}) collective-permute-start(f32[32,128]{1,0:T(8,128)} %bitcast.27), channel_id=1, source_target_pairs={{0,17},{1,16},{2,19},{3,18},{4,21},{5,20},{6,23},{7,22},{8,25},{9,... | collective-permute-start | bytes 49160 | tf_op jit(solution)/shard_map/ppermute | solution.py:178
  3.5 1.6 %collective-permute-start.1 = (f32[32,128]{1,0:T(8,128)}, f32[32,128]{1,0:T(8,128)S(1)}, u32[]{:S(2)}, u32[]{:S(2)}) collective-permute-start(f32[32,128]{1,0:T(8,128)} %bitcast.28), channel_id=1, source_target_pairs={{0,25},{1,24},{2,27},{3,26},{4,29},{5,28},{6,31},{7,30},{8,17},{9,... | collective-permute-start | bytes 49160 | tf_op jit(solution)/shard_map/ppermute | solution.py:178
  5.1 0.2 collective-permute-start
  6.0 1.7 %shard_map.55 = (bf16[32,128,256]{2,1,0:T(8,128)(2,1)S(1)}, s32[3,32]{1,0:T(4,128)S(4)}, f32[32,128]{1,0:T(8,128)S(1)}) custom-call(s32[1,1]{1,0:T(1,128)S(6)} %copy.8.refs_0_, s32[1,32]{1,0:T(1,128)} %bitcast.34, s32[1,32]{1,0:T(1,128)} %bitcast.35, f32[32,128,128]{2,1,0:T(8,128)} %bitcast.26, f32[32,128]{1,0:T(8,128)} %bitcast.30), custom_call_target="tpu_custom_call" | custom-call | flops 2097152 | bytes 4194304 | tf_op jit(solution)/shard_map/pallas_call | solution.py:69
  7.7 0.0 collective-permute-done.2
  7.7 1.0 %collective-permute-done.1 = f32[32,128]{1,0:T(8,128)S(1)} collective-permute-done((f32[32,128]{1,0:T(8,128)}, f32[32,128]{1,0:T(8,128)S(1)}, u32[]{:S(2)}, u32[]{:S(2)}) %collective-permute-start.1) | collective-permute-done | bytes 16416 | tf_op jit(solution)/shard_map/ppermute | solution.py:178
  8.7 0.0 collective-permute-done
  8.7 2.8 %collective-permute-start.3 = (f32[4,32,128]{2,1,0:T(8,128)S(1)}, f32[4,32,128]{2,1,0:T(8,128)S(1)}, u32[]{:S(2)}, u32[]{:S(2)}) collective-permute-start(f32[4,32,128]{2,1,0:T(8,128)S(1)} %pad_maximum_fusion.refs_2_), channel_id=1, source_target_pairs={{0,7},{1,6},{2,5},{3,4},{4,3},{5,2},{6,1},{7,0},{8,15},{9,14},{10,... | collective-permute-start | bytes 196616 | tf_op jit(solution)/shard_map/ppermute | solution.py:178
  11.5 0.0 collective-permute-start.7
  11.5 0.8 %collective-permute-start.6 = (f32[4,32,128]{2,1,0:T(8,128)S(1)}, f32[4,32,128]{2,1,0:T(8,128)S(1)}, u32[]{:S(2)}, u32[]{:S(2)}) collective-permute-start(f32[4,32,128]{2,1,0:T(8,128)S(1)} %pad_maximum_fusion.refs_2_), channel_id=1, source_target_pairs={{0,3},{1,4},{2,7},{3,0},{4,1},{5,6},{6,5},{7,2},{8,11},{9,12},{10,... | collective-permute-start | bytes 196616 | tf_op jit(solution)/shard_map/ppermute | solution.py:178
  12.3 1.7 %collective-permute-done.3.refs_2_ = f32[4,32,128]{2,1,0:T(8,128)S(1)} collective-permute-done((f32[4,32,128]{2,1,0:T(8,128)S(1)}, f32[4,32,128]{2,1,0:T(8,128)S(1)}, u32[]{:S(2)}, u32[]{:S(2)}) %collective-permute-start.3) | collective-permute-done | bytes 65568 | tf_op jit(solution)/shard_map/ppermute | solution.py:178
  14.0 0.1 collective-permute-start.4
  14.1 0.4 %collective-permute-start.5 = (f32[4,32,128]{2,1,0:T(8,128)S(1)}, f32[4,32,128]{2,1,0:T(8,128)S(1)}, u32[]{:S(2)}, u32[]{:S(2)}) collective-permute-start(f32[4,32,128]{2,1,0:T(8,128)S(1)} %pad_maximum_fusion.refs_2_), channel_id=1, source_target_pairs={{0,1},{1,0},{2,3},{3,2},{4,5},{5,4},{6,7},{7,6},{8,9},{9,8},{10,11... | collective-permute-start | bytes 196616 | tf_op jit(solution)/shard_map/ppermute | solution.py:178
  14.5 0.7 %collective-permute-done.7.refs_6_ = f32[4,32,128]{2,1,0:T(8,128)S(1)} collective-permute-done((f32[4,32,128]{2,1,0:T(8,128)S(1)}, f32[4,32,128]{2,1,0:T(8,128)S(1)}, u32[]{:S(2)}, u32[]{:S(2)}) %collective-permute-start.7) | collective-permute-done | bytes 65568 | tf_op jit(solution)/shard_map/ppermute | solution.py:178
  15.2 0.7 %collective-permute-start.8 = (f32[4,32,128]{2,1,0:T(8,128)S(1)}, f32[4,32,128]{2,1,0:T(8,128)S(1)}, u32[]{:S(2)}, u32[]{:S(2)}) collective-permute-start(f32[4,32,128]{2,1,0:T(8,128)S(1)} %collective-permute-done.7.refs_6_), channel_id=1, source_target_pairs={{0,1},{1,0},{2,3},{3,2},{4,5},{5,4},{6,7},{7,6},{8,9},{9,8},{10,11... | collective-permute-start | bytes 196616 | tf_op jit(solution)/shard_map/ppermute | solution.py:178
  16.0 0.0 collective-permute-done.6.refs_4_
  16.0 0.0 collective-permute-start.9
  16.0 0.0 collective-permute-done.4.refs_3_
  16.0 0.5 %shard_map.56 = f32[4,32,128]{2,1,0:T(8,128)S(1)} custom-call(s32[3,32]{1,0:T(4,128)S(4)} %get-tuple-element.12.refs_0_, bf16[32,128,256]{2,1,0:T(8,128)(2,1)S(1)} %get-tuple-element.14.refs_1_, f32[4,32,128]{2,1,0:T(8,128)S(1)} %collective-permute-done.3.refs_2_, f32[4,32,128]{2,1,0:T(8,128)S(1)} %collective-permute-done.4.refs_3_), custom_call_target="tpu_custom_call" | custom-call | flops 268435456 | bytes 4194304 | tf_op jit(solution)/shard_map/pallas_call | solution.py:154
  16.5 2.0 %collective-permute-start.13 = (f32[4,32,128]{2,1,0:T(8,128)S(1)}, f32[4,32,128]{2,1,0:T(8,128)S(1)}, u32[]{:S(2)}, u32[]{:S(2)}) collective-permute-start(f32[4,32,128]{2,1,0:T(8,128)S(1)} %shard_map.56), channel_id=1, source_target_pairs={{0,7},{1,6},{2,5},{3,4},{4,3},{5,2},{6,1},{7,0},{8,15},{9,14},{10,... | collective-permute-start | bytes 196616 | tf_op jit(solution)/shard_map/ppermute | solution.py:178
  18.4 0.0 collective-permute-done.5.refs_3_
  18.4 0.0 collective-permute-done.8.refs_5_
  18.4 0.0 collective-permute-done.9.refs_7_
  18.4 0.7 %shard_map.57 = f32[12,32,128]{2,1,0:T(8,128)S(1)} custom-call(s32[3,32]{1,0:T(4,128)S(4)} %get-tuple-element.12.refs_0_, bf16[32,128,256]{2,1,0:T(8,128)(2,1)S(1)} %get-tuple-element.14.refs_1_, f32[4,32,128]{2,1,0:T(8,128)S(1)} %pad_maximum_fusion.refs_2_, f32[4,32,128]{2,1,0:T(8,128)S(1)} %collective-permute-done.5.refs_3_, ...), custom_call_target="tpu_custom_call" | custom-call | flops 268435456 | bytes 4194304 | tf_op jit(solution)/shard_map/pallas_call | solution.py:154
  19.1 0.3 %collective-permute-start.12 = (f32[4,32,128]{2,1,0:T(8,128)S(1)}, f32[4,32,128]{2,1,0:T(8,128)S(1)}, u32[]{:S(2)}, u32[]{:S(2)}) collective-permute-start(f32[4,32,128]{2,1,0:T(8,128)S(1)} %get-tuple-element.18), channel_id=1, source_target_pairs={{0,3},{1,4},{2,7},{3,0},{4,1},{5,6},{6,5},{7,2},{8,11},{9,12},{10,... | collective-permute-start | bytes 196616 | tf_op jit(solution)/shard_map/ppermute | solution.py:178
  19.5 0.7 %collective-permute-start.10 = (f32[4,32,128]{2,1,0:T(8,128)S(1)}, f32[4,32,128]{2,1,0:T(8,128)S(1)}, u32[]{:S(2)}, u32[]{:S(2)}) collective-permute-start(f32[4,32,128]{2,1,0:T(8,128)S(1)} %get-tuple-element.19), channel_id=1, source_target_pairs={{0,5},{1,2},{2,1},{3,6},{4,7},{5,0},{6,3},{7,4},{8,13},{9,10},{10,... | collective-permute-start | bytes 196616 | tf_op jit(solution)/shard_map/ppermute | solution.py:178
  20.2 0.2 collective-permute-start.11
  20.4 1.0 %collective-permute-done.13 = f32[4,32,128]{2,1,0:T(8,128)S(1)} collective-permute-done((f32[4,32,128]{2,1,0:T(8,128)S(1)}, f32[4,32,128]{2,1,0:T(8,128)S(1)}, u32[]{:S(2)}, u32[]{:S(2)}) %collective-permute-start.13) | collective-permute-done | bytes 65568 | tf_op jit(solution)/shard_map/ppermute | solution.py:178
  21.4 1.5 %collective-permute-done.12 = f32[4,32,128]{2,1,0:T(8,128)S(1)} collective-permute-done((f32[4,32,128]{2,1,0:T(8,128)S(1)}, f32[4,32,128]{2,1,0:T(8,128)S(1)}, u32[]{:S(2)}, u32[]{:S(2)}) %collective-permute-start.12) | collective-permute-done | bytes 65568 | tf_op jit(solution)/shard_map/ppermute | solution.py:178
  22.9 0.8 %collective-permute-done.10 = f32[4,32,128]{2,1,0:T(8,128)S(1)} collective-permute-done((f32[4,32,128]{2,1,0:T(8,128)S(1)}, f32[4,32,128]{2,1,0:T(8,128)S(1)}, u32[]{:S(2)}, u32[]{:S(2)}) %collective-permute-start.10) | collective-permute-done | bytes 65568 | tf_op jit(solution)/shard_map/ppermute | solution.py:178
  23.7 0.0 collective-permute-done.11
  23.8 1.7 %collective-permute-start.17 = (f32[32,128]{1,0:T(8,128)S(1)}, f32[32,128]{1,0:T(8,128)S(1)}, u32[]{:S(2)}, u32[]{:S(2)}) collective-permute-start(f32[32,128]{1,0:T(8,128)S(1)} %get-tuple-element.21), channel_id=1, source_target_pairs={{0,25},{1,24},{2,27},{3,26},{4,29},{5,28},{6,31},{7,30},{8,17},{9,... | collective-permute-start | bytes 49160 | tf_op jit(solution)/shard_map/ppermute | solution.py:178
  25.5 0.0 collective-permute-start.16
  25.5 2.1 %collective-permute-start.14 = (f32[32,128]{1,0:T(8,128)S(1)}, f32[32,128]{1,0:T(8,128)S(1)}, u32[]{:S(2)}, u32[]{:S(2)}) collective-permute-start(f32[32,128]{1,0:T(8,128)S(1)} %get-tuple-element.23), channel_id=1, source_target_pairs={{0,9},{1,8},{2,11},{3,10},{4,13},{5,12},{6,15},{7,14},{8,1},{9,0},... | collective-permute-start | bytes 49160 | tf_op jit(solution)/shard_map/ppermute | solution.py:178
  27.6 0.5 %collective-permute-start.15 = (f32[32,128]{1,0:T(8,128)S(1)}, f32[32,128]{1,0:T(8,128)S(1)}, u32[]{:S(2)}, u32[]{:S(2)}) collective-permute-start(f32[32,128]{1,0:T(8,128)S(1)} %get-tuple-element.20), channel_id=1, source_target_pairs={{0,1},{1,0},{2,3},{3,2},{4,5},{5,4},{6,7},{7,6},{8,9},{9,8},{10,11... | collective-permute-start | bytes 49160 | tf_op jit(solution)/shard_map/ppermute | solution.py:178
  28.0 0.7 %collective-permute-done.17 = f32[32,128]{1,0:T(8,128)S(1)} collective-permute-done((f32[32,128]{1,0:T(8,128)S(1)}, f32[32,128]{1,0:T(8,128)S(1)}, u32[]{:S(2)}, u32[]{:S(2)}) %collective-permute-start.17) | collective-permute-done | bytes 16416 | tf_op jit(solution)/shard_map/ppermute | solution.py:178
  28.8 0.8 %collective-permute-done.16 = f32[32,128]{1,0:T(8,128)S(1)} collective-permute-done((f32[32,128]{1,0:T(8,128)S(1)}, f32[32,128]{1,0:T(8,128)S(1)}, u32[]{:S(2)}, u32[]{:S(2)}) %collective-permute-start.16) | collective-permute-done | bytes 16416 | tf_op jit(solution)/shard_map/ppermute | solution.py:178
  29.5 0.0 collective-permute-done.14
  29.5 0.0 collective-permute-done.15
  29.5 0.6 %add_add_fusion.1 = f32[32,128]{1,0:T(8,128)} fusion(f32[32,128]{1,0:T(8,128)S(1)} %collective-permute-done.17, f32[32,128]{1,0:T(8,128)S(1)} %collective-permute-done.16, f32[32,128]{1,0:T(8,128)S(1)} %collective-permute-done.14, f32[32,128]{1,0:T(8,128)S(1)} %collective-permute-done.15), kind=kLoop, calls=%fused_computation.6 | loop fusion | flops 12288 | bytes 81920 | tf_op jit(solution)/shard_map/add | solution.py:188
  (4 shorter events, 0.0 us)
Async XLA Ops:
  0.0 7.7 %collective-permute-start.2 = (f32[32,128]{1,0:T(8,128)}, f32[32,128]{1,0:T(8,128)S(1)}, u32[]{:S(2)}, u32[]{:S(2)}) collective-permute-start(f32[32,128]{1,0:T(8,128)} %bitcast.27), channel_id=1, source_target_pairs={{0,17},{1,16},{2,19},{3,18},{4,21},{5,20},{6,23},{7,22},{8,25},{9,... | collective-permute-start | bytes 49160 | tf_op jit(solution)/shard_map/ppermute | solution.py:178
  3.5 5.2 %collective-permute-start.1 = (f32[32,128]{1,0:T(8,128)}, f32[32,128]{1,0:T(8,128)S(1)}, u32[]{:S(2)}, u32[]{:S(2)}) collective-permute-start(f32[32,128]{1,0:T(8,128)} %bitcast.28), channel_id=1, source_target_pairs={{0,25},{1,24},{2,27},{3,26},{4,29},{5,28},{6,31},{7,30},{8,17},{9,... | collective-permute-start | bytes 49160 | tf_op jit(solution)/shard_map/ppermute | solution.py:178
  5.1 3.6 %collective-permute-start = (f32[32,128]{1,0:T(8,128)}, f32[32,128]{1,0:T(8,128)S(1)}, u32[]{:S(2)}, u32[]{:S(2)}) collective-permute-start(f32[32,128]{1,0:T(8,128)} %bitcast.29), channel_id=1, source_target_pairs={{0,9},{1,8},{2,11},{3,10},{4,13},{5,12},{6,15},{7,14},{8,1},{9,0},... | collective-permute-start | bytes 49160 | tf_op jit(solution)/shard_map/ppermute | solution.py:178
  8.7 5.3 %collective-permute-start.3 = (f32[4,32,128]{2,1,0:T(8,128)S(1)}, f32[4,32,128]{2,1,0:T(8,128)S(1)}, u32[]{:S(2)}, u32[]{:S(2)}) collective-permute-start(f32[4,32,128]{2,1,0:T(8,128)S(1)} %pad_maximum_fusion.refs_2_), channel_id=1, source_target_pairs={{0,7},{1,6},{2,5},{3,4},{4,3},{5,2},{6,1},{7,0},{8,15},{9,14},{10,... | collective-permute-start | bytes 196616 | tf_op jit(solution)/shard_map/ppermute | solution.py:178
  11.5 3.7 %collective-permute-start.7 = (f32[4,32,128]{2,1,0:T(8,128)S(1)}, f32[4,32,128]{2,1,0:T(8,128)S(1)}, u32[]{:S(2)}, u32[]{:S(2)}) collective-permute-start(f32[4,32,128]{2,1,0:T(8,128)S(1)} %pad_maximum_fusion.refs_2_), channel_id=1, source_target_pairs={{0,5},{1,2},{2,1},{3,6},{4,7},{5,0},{6,3},{7,4},{8,13},{9,10},{10,... | collective-permute-start | bytes 196616 | tf_op jit(solution)/shard_map/ppermute | solution.py:178
  11.5 4.4 %collective-permute-start.6 = (f32[4,32,128]{2,1,0:T(8,128)S(1)}, f32[4,32,128]{2,1,0:T(8,128)S(1)}, u32[]{:S(2)}, u32[]{:S(2)}) collective-permute-start(f32[4,32,128]{2,1,0:T(8,128)S(1)} %pad_maximum_fusion.refs_2_), channel_id=1, source_target_pairs={{0,3},{1,4},{2,7},{3,0},{4,1},{5,6},{6,5},{7,2},{8,11},{9,12},{10,... | collective-permute-start | bytes 196616 | tf_op jit(solution)/shard_map/ppermute | solution.py:178
  14.0 2.0 %collective-permute-start.4 = (f32[4,32,128]{2,1,0:T(8,128)S(1)}, f32[4,32,128]{2,1,0:T(8,128)S(1)}, u32[]{:S(2)}, u32[]{:S(2)}) collective-permute-start(f32[4,32,128]{2,1,0:T(8,128)S(1)} %collective-permute-done.3.refs_2_), channel_id=1, source_target_pairs={{0,1},{1,0},{2,3},{3,2},{4,5},{5,4},{6,7},{7,6},{8,9},{9,8},{10,11... | collective-permute-start | bytes 196616 | tf_op jit(solution)/shard_map/ppermute | solution.py:178
  14.1 4.4 %collective-permute-start.5 = (f32[4,32,128]{2,1,0:T(8,128)S(1)}, f32[4,32,128]{2,1,0:T(8,128)S(1)}, u32[]{:S(2)}, u32[]{:S(2)}) collective-permute-start(f32[4,32,128]{2,1,0:T(8,128)S(1)} %pad_maximum_fusion.refs_2_), channel_id=1, source_target_pairs={{0,1},{1,0},{2,3},{3,2},{4,5},{5,4},{6,7},{7,6},{8,9},{9,8},{10,11... | collective-permute-start | bytes 196616 | tf_op jit(solution)/shard_map/ppermute | solution.py:178
  15.2 3.2 %collective-permute-start.8 = (f32[4,32,128]{2,1,0:T(8,128)S(1)}, f32[4,32,128]{2,1,0:T(8,128)S(1)}, u32[]{:S(2)}, u32[]{:S(2)}) collective-permute-start(f32[4,32,128]{2,1,0:T(8,128)S(1)} %collective-permute-done.7.refs_6_), channel_id=1, source_target_pairs={{0,1},{1,0},{2,3},{3,2},{4,5},{5,4},{6,7},{7,6},{8,9},{9,8},{10,11... | collective-permute-start | bytes 196616 | tf_op jit(solution)/shard_map/ppermute | solution.py:178
  16.0 2.5 %collective-permute-start.9 = (f32[4,32,128]{2,1,0:T(8,128)S(1)}, f32[4,32,128]{2,1,0:T(8,128)S(1)}, u32[]{:S(2)}, u32[]{:S(2)}) collective-permute-start(f32[4,32,128]{2,1,0:T(8,128)S(1)} %collective-permute-done.6.refs_4_), channel_id=1, source_target_pairs={{0,1},{1,0},{2,3},{3,2},{4,5},{5,4},{6,7},{7,6},{8,9},{9,8},{10,11... | collective-permute-start | bytes 196616 | tf_op jit(solution)/shard_map/ppermute | solution.py:178
  16.5 4.9 %collective-permute-start.13 = (f32[4,32,128]{2,1,0:T(8,128)S(1)}, f32[4,32,128]{2,1,0:T(8,128)S(1)}, u32[]{:S(2)}, u32[]{:S(2)}) collective-permute-start(f32[4,32,128]{2,1,0:T(8,128)S(1)} %shard_map.56), channel_id=1, source_target_pairs={{0,7},{1,6},{2,5},{3,4},{4,3},{5,2},{6,1},{7,0},{8,15},{9,14},{10,... | collective-permute-start | bytes 196616 | tf_op jit(solution)/shard_map/ppermute | solution.py:178
  19.1 3.8 %collective-permute-start.12 = (f32[4,32,128]{2,1,0:T(8,128)S(1)}, f32[4,32,128]{2,1,0:T(8,128)S(1)}, u32[]{:S(2)}, u32[]{:S(2)}) collective-permute-start(f32[4,32,128]{2,1,0:T(8,128)S(1)} %get-tuple-element.18), channel_id=1, source_target_pairs={{0,3},{1,4},{2,7},{3,0},{4,1},{5,6},{6,5},{7,2},{8,11},{9,12},{10,... | collective-permute-start | bytes 196616 | tf_op jit(solution)/shard_map/ppermute | solution.py:178
  19.5 4.2 %collective-permute-start.10 = (f32[4,32,128]{2,1,0:T(8,128)S(1)}, f32[4,32,128]{2,1,0:T(8,128)S(1)}, u32[]{:S(2)}, u32[]{:S(2)}) collective-permute-start(f32[4,32,128]{2,1,0:T(8,128)S(1)} %get-tuple-element.19), channel_id=1, source_target_pairs={{0,5},{1,2},{2,1},{3,6},{4,7},{5,0},{6,3},{7,4},{8,13},{9,10},{10,... | collective-permute-start | bytes 196616 | tf_op jit(solution)/shard_map/ppermute | solution.py:178
  20.2 3.5 %collective-permute-start.11 = (f32[4,32,128]{2,1,0:T(8,128)S(1)}, f32[4,32,128]{2,1,0:T(8,128)S(1)}, u32[]{:S(2)}, u32[]{:S(2)}) collective-permute-start(f32[4,32,128]{2,1,0:T(8,128)S(1)} %get-tuple-element.17), channel_id=1, source_target_pairs={{0,1},{1,0},{2,3},{3,2},{4,5},{5,4},{6,7},{7,6},{8,9},{9,8},{10,11... | collective-permute-start | bytes 196616 | tf_op jit(solution)/shard_map/ppermute | solution.py:178
  23.8 5.0 %collective-permute-start.17 = (f32[32,128]{1,0:T(8,128)S(1)}, f32[32,128]{1,0:T(8,128)S(1)}, u32[]{:S(2)}, u32[]{:S(2)}) collective-permute-start(f32[32,128]{1,0:T(8,128)S(1)} %get-tuple-element.21), channel_id=1, source_target_pairs={{0,25},{1,24},{2,27},{3,26},{4,29},{5,28},{6,31},{7,30},{8,17},{9,... | collective-permute-start | bytes 49160 | tf_op jit(solution)/shard_map/ppermute | solution.py:178
  25.5 4.1 %collective-permute-start.16 = (f32[32,128]{1,0:T(8,128)S(1)}, f32[32,128]{1,0:T(8,128)S(1)}, u32[]{:S(2)}, u32[]{:S(2)}) collective-permute-start(f32[32,128]{1,0:T(8,128)S(1)} %get-tuple-element.22), channel_id=1, source_target_pairs={{0,17},{1,16},{2,19},{3,18},{4,21},{5,20},{6,23},{7,22},{8,25},{9,... | collective-permute-start | bytes 49160 | tf_op jit(solution)/shard_map/ppermute | solution.py:178
  25.5 4.1 %collective-permute-start.14 = (f32[32,128]{1,0:T(8,128)S(1)}, f32[32,128]{1,0:T(8,128)S(1)}, u32[]{:S(2)}, u32[]{:S(2)}) collective-permute-start(f32[32,128]{1,0:T(8,128)S(1)} %get-tuple-element.23), channel_id=1, source_target_pairs={{0,9},{1,8},{2,11},{3,10},{4,13},{5,12},{6,15},{7,14},{8,1},{9,0},... | collective-permute-start | bytes 49160 | tf_op jit(solution)/shard_map/ppermute | solution.py:178
  27.6 2.0 %collective-permute-start.15 = (f32[32,128]{1,0:T(8,128)S(1)}, f32[32,128]{1,0:T(8,128)S(1)}, u32[]{:S(2)}, u32[]{:S(2)}) collective-permute-start(f32[32,128]{1,0:T(8,128)S(1)} %get-tuple-element.20), channel_id=1, source_target_pairs={{0,1},{1,0},{2,3},{3,2},{4,5},{5,4},{6,7},{7,6},{8,9},{9,8},{10,11... | collective-permute-start | bytes 49160 | tf_op jit(solution)/shard_map/ppermute | solution.py:178
